TPU v7x, 32 devices: a whole 2x2x4 slice. The times are simulated.
32 devices in a mesh: tm: 4 (over y, x), space: 4 (over z), mp: 2 (over core).
Axes of the slice: x: 2, y: 2, z: 4, core: 2. Of those that a mesh axis runs over, the one named last changes fastest.
Arguments:
- video: bfloat16 [2, 8, 16, 16, 1024], P(None, 'tm', 'space')
- cotangent: bfloat16 [2, 8, 16, 16, 1024], P(None, 'tm', 'space'), may hold values from -6 to 6
- text: bfloat16 [2, 128, 4096], P(None, ('tm', 'space')), may hold values from -6 to 6
- video_ids: int32 [2, 8], replicated, may hold values from 0 to 2, as said below
- timesteps: int32 [2, 3], replicated, may hold values from 0 to 999
- text_lengths: int32 [2], replicated, may hold values from 16 to 128
- group_gain: float32 [1024], replicated, may hold values from 0.5 to 1.5
- group_bias: float32 [1024], replicated, may hold values from -2 to 2
- first_conv: bfloat16 [1024, 9, 1024], P('space', None, 'mp'), may hold values from -0.0625 to 0.0625
- film_weight: bfloat16 [1024, 2, 1024], P('space', None, 'mp'), may hold values from -0.1875 to 0.1875
- second_conv: bfloat16 [1024, 9, 1024], P('mp', None, 'space'), may hold values from -0.0625 to 0.0625
- spatial_norm: float32 [1024], replicated, may hold values from 0.5 to 1.5
- spatial_qkv: bfloat16 [1024, 3, 1024], P('space', None, 'mp'), may hold values from -0.1875 to 0.1875
- spatial_out: bfloat16 [1024, 1024], P('mp', 'space'), may hold values from -0.5 to 0.5
- cross_norm: float32 [1024], replicated, may hold values from 0.5 to 1.5
- cross_query: bfloat16 [1024, 1024], P('space', 'mp'), may hold values from -0.1875 to 0.1875
- cross_kv: bfloat16 [4096, 2, 1024], P('space', None, 'mp'), may hold values from -0.09375 to 0.09375
- cross_out: bfloat16 [1024, 1024], P('mp', 'space'), may hold values from -0.5 to 0.5
- temporal_norm: float32 [1024], replicated, may hold values from 0.5 to 1.5
- temporal_qkv: bfloat16 [1024, 3, 1024], P('space', None, 'mp'), may hold values from -0.1875 to 0.1875
- temporal_out: bfloat16 [1024, 1024], P('mp', 'space'), may hold values from -0.375 to 0.375
- offset_bias: float32 [128, 16], P(None, 'mp'), may hold values from -4 to 4
- feed_norm: float32 [1024], replicated, may hold values from 0.5 to 1.5
- feed_in: bfloat16 [1024, 4096], P('space', 'mp'), may hold values from -0.1875 to 0.1875
- feed_out: bfloat16 [4096, 1024], P('mp', 'space'), may hold values from -0.09375 to 0.09375
Outputs:
- mixed: bfloat16 [2, 8, 16, 16, 1024], P(None, 'tm', 'space')
- video_grad: float32 [2, 8, 16, 16, 1024], P(None, 'tm', 'space')
- text_grad: float32 [2, 128, 4096], P(None, ('tm', 'space'), 'mp')
- group_gain_grad: float32 [1024], P(('tm', 'space'))
- group_bias_grad: float32 [1024], P(('tm', 'space'))
- first_conv_grad: float32 [1024, 9, 1024], P(('tm', 'space'), None, 'mp')
- film_weight_grad: float32 [1024, 2, 1024], P(('tm', 'space'), None, 'mp')
- second_conv_grad: float32 [1024, 9, 1024], P('mp', None, ('tm', 'space'))
- spatial_norm_grad: float32 [1024], P(('tm', 'space'))
- spatial_qkv_grad: float32 [1024, 3, 1024], P(('tm', 'space'), None, 'mp')
- spatial_out_grad: float32 [1024, 1024], P('mp', ('tm', 'space'))
- cross_norm_grad: float32 [1024], P(('tm', 'space'))
- cross_query_grad: float32 [1024, 1024], P(('tm', 'space'), 'mp')
- cross_kv_grad: float32 [4096, 2, 1024], P(('tm', 'space'), None, 'mp')
- cross_out_grad: float32 [1024, 1024], P('mp', ('tm', 'space'))
- temporal_norm_grad: float32 [1024], P(('tm', 'space'))
- temporal_qkv_grad: float32 [1024, 3, 1024], P(('tm', 'space'), None, 'mp')
- temporal_out_grad: float32 [1024, 1024], P('mp', ('tm', 'space'))
- offset_bias_grad: float32 [128, 16], P(('tm', 'space'), 'mp')
- feed_norm_grad: float32 [1024], P(('tm', 'space'))
- feed_in_grad: float32 [1024, 4096], P(('tm', 'space'), 'mp')
- feed_out_grad: float32 [4096, 1024], P('mp', ('tm', 'space'))
Inputs may be any that keep to these rules, and one draw needn't show every extreme that they name: `video_ids`: within each slot the video number starts at 0 and rises by 0 or 1 from one frame to the next. Some slot holds a single video of all 8 frames, and some slot holds 3 videos.
All inputs are finite; a program needn't handle non-finite values.
Results may differ from a plain program's by a relative error of at most 0.03.
Values may be sent and summed in bfloat16 or wider, within the bound.
A program may use at most 256 MiB of HBM per device.

v0:
```python
import math

import jax
import jax.numpy as jnp
from jax import lax
from jax.sharding import PartitionSpec as P

D = 1024
HDIM = 64
TXT = 128
G = 32
R = 128
VIDS = 3
H = 16
W = 16


epsilon = 1e-05
highest = lax.Precision.HIGHEST
masked = -1e30


def with_halo(block, sides, width):
    for axis, dim in sides:
        count = lax.axis_size(axis)
        forward = [(i, i + 1) for i in range(count - 1)]
        backward = [(target, source) for source, target in forward]
        low = lax.ppermute(
            lax.slice_in_dim(block, block.shape[dim] - width, None, axis=dim), axis, forward
        )
        high = lax.ppermute(lax.slice_in_dim(block, 0, width, axis=dim), axis, backward)
        block = jnp.concatenate([low, block, high], axis=dim)
    return block


def over_heads(partial_sum, gather_back):
    portion = lax.psum_scatter(
        partial_sum.astype(jnp.bfloat16), "mp", scatter_dimension=1, tiled=True
    ).astype(jnp.float32)
    if gather_back:
        return lax.all_gather(portion.astype(jnp.bfloat16), "mp", axis=1, tiled=True).astype(
            portion.dtype
        )
    return portion


def space_sum(statistics):
    return lax.psum(statistics, "space")


def with_rims(source):
    padded = with_halo(source, (("space", 2),), 1)
    return jnp.pad(padded, ((0, 0), (0, 0), (0, 0), (1, 1), (0, 0)))


def to_clips(source):
    return lax.all_to_all(source, "tm", split_axis=2, concat_axis=1, tiled=True)


def from_clips(source):
    return lax.all_to_all(source, "tm", split_axis=1, concat_axis=2, tiled=True)


def tap_tiles(padded, flipped):
    row_count = padded.shape[2] - 2
    col_count = padded.shape[3] - 2
    tile_list = []
    for tap_row in range(3):
        for tap_col in range(3):
            first_row = 2 - tap_row if flipped else tap_row
            first_col = 2 - tap_col if flipped else tap_col
            tile_list.append(
                padded[:, :, first_row : first_row + row_count, first_col : first_col + col_count]
            )
    return jnp.stack(tile_list, axis=4)


def grouped_view(source):
    group_size = D // G
    dims_all = source.shape
    return source.reshape(
        dims_all[0], dims_all[1], dims_all[2] * dims_all[3], dims_all[4] // group_size, group_size
    )


def group_forward(source):
    grouped = grouped_view(source)
    counted = H * W * (D // G)
    totals = space_sum(jnp.sum(grouped, axis=(2, 4)))
    centered = grouped - (totals / counted)[:, :, None, :, None]
    spread = space_sum(jnp.sum(centered * centered, axis=(2, 4)))
    inverse = lax.rsqrt(spread / counted + epsilon)
    return ((centered * inverse[:, :, None, :, None]).reshape(source.shape), inverse)


def group_backward(upstream, normal, inverse):
    counted = H * W * (D // G)
    grouped_up = grouped_view(upstream)
    grouped_norm = grouped_view(normal)
    first_sum, second_sum = space_sum(
        (jnp.sum(grouped_up, axis=(2, 4)), jnp.sum(grouped_up * grouped_norm, axis=(2, 4)))
    )
    result = inverse[:, :, None, :, None] * (
        grouped_up
        - first_sum[:, :, None, :, None] / counted
        - grouped_norm * second_sum[:, :, None, :, None] / counted
    )
    return result.reshape(upstream.shape)


def layer_norm(source, norm_gain):
    average = jnp.mean(source, axis=-1, keepdims=True)
    centered = source - average
    variance = jnp.mean(centered * centered, axis=-1, keepdims=True)
    return centered * lax.rsqrt(variance + epsilon) * norm_gain


def layer_back(source, norm_gain, upstream):
    _, pullback = jax.vjp(layer_norm, source, norm_gain)
    return pullback(upstream)


def sinusoid(steps_int):
    counted = D // 2
    freqs = jnp.exp(-math.log(10000.0) * jnp.arange(counted, dtype=jnp.float32) / counted)
    angles = steps_int.astype(jnp.float32)[..., None] * freqs
    return jnp.concatenate([jnp.sin(angles), jnp.cos(angles)], axis=-1)


def offset_onehot(query_start, query_count, key_count):
    distance = (
        query_start
        + jnp.arange(query_count, dtype=jnp.int32)[:, None]
        - jnp.arange(key_count, dtype=jnp.int32)[None, :]
    )
    position = jnp.clip(distance, -(R // 2), R // 2 - 1) + R // 2
    return (position[:, :, None] == jnp.arange(R, dtype=jnp.int32)[None, None, :]).astype(
        jnp.float32
    )


def scores_of(queries, keys, forms, bias, valid):
    query_form, key_form, score_form = forms
    raw_scores = jnp.einsum(
        query_form + "," + key_form + "->" + score_form,
        queries,
        keys,
        preferred_element_type=jnp.float32,
    ) * (1.0 / math.sqrt(HDIM))
    if bias is not None:
        raw_scores = raw_scores + bias
    if valid is not None:
        raw_scores = jnp.where(valid, raw_scores, masked)
    return raw_scores


def attend_forward(queries, keys, values_in, forms, bias, valid):
    query_form, key_form, score_form = forms
    raw_scores = scores_of(queries, keys, forms, bias, valid)
    largest = jnp.max(raw_scores, axis=-1, keepdims=True)
    expos = jnp.exp(raw_scores - largest)
    totals = jnp.sum(expos, axis=-1, keepdims=True)
    probs = (expos / totals).astype(jnp.bfloat16)
    log_total = (largest + jnp.log(totals))[..., 0]
    result = jnp.einsum(
        score_form + "," + key_form + "->" + query_form,
        probs,
        values_in,
        preferred_element_type=jnp.float32,
    )
    return (result.astype(jnp.bfloat16), log_total)


def attend_backward(queries, keys, values_in, forms, bias, valid, log_total, upstream):
    query_form, key_form, score_form = forms
    score_scale = 1.0 / math.sqrt(HDIM)
    raw_scores = scores_of(queries, keys, forms, bias, valid)
    probs = jnp.exp(raw_scores - log_total[..., None])
    low_probs = probs.astype(jnp.bfloat16)
    prob_grad = jnp.einsum(
        query_form + "," + key_form + "->" + score_form,
        upstream,
        values_in,
        preferred_element_type=jnp.float32,
    )
    inner = jnp.sum(probs * prob_grad, axis=-1, keepdims=True)
    score_grad = (probs * (prob_grad - inner)).astype(jnp.bfloat16)
    query_grad = (
        jnp.einsum(
            score_form + "," + key_form + "->" + query_form,
            score_grad,
            keys,
            preferred_element_type=jnp.float32,
        )
        * score_scale
    )
    key_grad = (
        jnp.einsum(
            score_form + "," + query_form + "->" + key_form,
            score_grad,
            queries,
            preferred_element_type=jnp.float32,
        )
        * score_scale
    )
    value_grad = jnp.einsum(
        score_form + "," + query_form + "->" + key_form,
        low_probs,
        upstream,
        preferred_element_type=jnp.float32,
    )
    return (query_grad, key_grad, value_grad, score_grad)


def on_device(
    video,
    cotangent,
    text,
    video_ids,
    timesteps,
    text_lengths,
    group_gain,
    group_bias,
    first_conv,
    film_weight,
    second_conv,
    spatial_norm,
    spatial_qkv,
    spatial_out,
    cross_norm,
    cross_query,
    cross_kv,
    cross_out,
    temporal_norm,
    temporal_qkv,
    temporal_out,
    offset_bias,
    feed_norm,
    feed_in,
    feed_out,
):
    (
        first_conv,
        film_weight,
        second_conv,
        spatial_qkv,
        spatial_out,
        cross_query,
        cross_kv,
        cross_out,
        temporal_qkv,
        temporal_out,
        feed_in,
        feed_out,
    ) = (
        lax.all_gather(first_conv, "space", axis=0, tiled=True),
        lax.all_gather(film_weight, "space", axis=0, tiled=True),
        lax.all_gather(second_conv, "space", axis=2, tiled=True),
        lax.all_gather(spatial_qkv, "space", axis=0, tiled=True),
        lax.all_gather(spatial_out, "space", axis=1, tiled=True),
        lax.all_gather(cross_query, "space", axis=0, tiled=True),
        lax.all_gather(cross_kv, "space", axis=0, tiled=True),
        lax.all_gather(cross_out, "space", axis=1, tiled=True),
        lax.all_gather(temporal_qkv, "space", axis=0, tiled=True),
        lax.all_gather(temporal_out, "space", axis=1, tiled=True),
        lax.all_gather(feed_in, "space", axis=0, tiled=True),
        lax.all_gather(feed_out, "space", axis=1, tiled=True),
    )
    slots, frame_dev, row_dev, columns, channels = video.shape
    half_width = first_conv.shape[2]
    head_local = half_width // HDIM
    pixels_dev = row_dev * columns
    frames_all = frame_dev * lax.axis_size("tm")
    token_rows = slots * frame_dev * pixels_dev
    text_local = text.shape[1]
    pixel_form = ("nqhe", "nkhe", "nhqk")
    frame_form = ("bfphe", "bgphe", "bphfg")
    stream_zero = video.astype(jnp.float32)
    normal_one, inverse_one = group_forward(stream_zero)
    affine_one = normal_one * group_gain + group_bias
    first_in = jax.nn.silu(affine_one).astype(jnp.bfloat16)
    first_tiles = tap_tiles(with_rims(first_in), False)
    hidden = jnp.einsum(
        "bfhwtc,ctk->bfhwk", first_tiles, first_conv, preferred_element_type=jnp.float32
    )
    normal_two, inverse_two = group_forward(hidden)
    embed = sinusoid(timesteps).astype(jnp.bfloat16)
    film = jnp.einsum("bvc,cjk->bvjk", embed, film_weight, preferred_element_type=jnp.float32)
    frame_ids = lax.dynamic_slice_in_dim(video_ids, lax.axis_index("tm") * frame_dev, frame_dev, 1)
    choose = (frame_ids[:, :, None] == jnp.arange(VIDS, dtype=jnp.int32)[None, None, :]).astype(
        jnp.float32
    )
    frame_film = jnp.einsum("bfv,bvjk->bfjk", choose, film, precision=highest)
    modulated = (
        normal_two * (1.0 + frame_film[:, :, None, None, 0]) + frame_film[:, :, None, None, 1]
    )
    second_in = jax.nn.silu(modulated).astype(jnp.bfloat16)
    second_tiles = tap_tiles(with_rims(second_in), False)
    conv_part = jnp.einsum(
        "bfhwtc,ctk->bfhwk", second_tiles, second_conv, preferred_element_type=jnp.float32
    )
    stream_one = stream_zero.reshape(token_rows, channels) + over_heads(
        conv_part.reshape(token_rows, channels), True
    )
    spatial_in = layer_norm(stream_one, spatial_norm).astype(jnp.bfloat16)
    spatial_triple = (
        jnp.einsum("rd,djk->rjk", spatial_in, spatial_qkv, preferred_element_type=jnp.float32)
        .astype(jnp.bfloat16)
        .reshape(slots, frame_dev, pixels_dev, 3, half_width)
    )
    frame_pairs = lax.all_gather(spatial_triple[:, :, :, 1:], "space", axis=2, tiled=True)
    spatial_query = spatial_triple[:, :, :, 0].reshape(
        slots * frame_dev, pixels_dev, head_local, HDIM
    )
    spatial_key = frame_pairs[:, :, :, 0].reshape(slots * frame_dev, H * W, head_local, HDIM)
    spatial_value = frame_pairs[:, :, :, 1].reshape(slots * frame_dev, H * W, head_local, HDIM)
    spatial_mix, spatial_total = attend_forward(
        spatial_query, spatial_key, spatial_value, pixel_form, None, None
    )
    spatial_mix = spatial_mix.reshape(token_rows, half_width)
    stream_two = stream_one + over_heads(
        jnp.dot(spatial_mix, spatial_out, preferred_element_type=jnp.float32), True
    )
    cross_in = layer_norm(stream_two, cross_norm).astype(jnp.bfloat16)
    cross_rows = jnp.dot(cross_in, cross_query, preferred_element_type=jnp.float32).astype(
        jnp.bfloat16
    )
    text_pairs = jnp.einsum(
        "btc,cjk->btjk", text, cross_kv, preferred_element_type=jnp.float32
    ).astype(jnp.bfloat16)
    text_all = lax.all_gather(text_pairs, ("tm", "space"), axis=1, tiled=True)
    cross_queries = cross_rows.reshape(slots, frame_dev * pixels_dev, head_local, HDIM)
    text_key = text_all[:, :, 0].reshape(slots, TXT, head_local, HDIM)
    text_value = text_all[:, :, 1].reshape(slots, TXT, head_local, HDIM)
    text_valid = (jnp.arange(TXT, dtype=jnp.int32)[None, :] < text_lengths[:, None])[
        :, None, None, :
    ]
    cross_mix, cross_total = attend_forward(
        cross_queries, text_key, text_value, pixel_form, None, text_valid
    )
    cross_mix = cross_mix.reshape(token_rows, half_width)
    stream_three = stream_two + over_heads(
        jnp.dot(cross_mix, cross_out, preferred_element_type=jnp.float32), True
    )
    temporal_in = layer_norm(stream_three, temporal_norm).astype(jnp.bfloat16)
    temporal_triple = (
        jnp.einsum("rd,djk->rjk", temporal_in, temporal_qkv, preferred_element_type=jnp.float32)
        .astype(jnp.bfloat16)
        .reshape(slots, frame_dev, pixels_dev, 3, half_width)
    )
    clip_triple = to_clips(temporal_triple)
    clip_pixels = clip_triple.shape[2]
    clip_query = clip_triple[:, :, :, 0].reshape(slots, frames_all, clip_pixels, head_local, HDIM)
    clip_key = clip_triple[:, :, :, 1].reshape(slots, frames_all, clip_pixels, head_local, HDIM)
    clip_value = clip_triple[:, :, :, 2].reshape(slots, frames_all, clip_pixels, head_local, HDIM)
    query_start = 0
    offset_table = offset_onehot(query_start, video_ids.shape[1], frames_all)
    clip_bias = jnp.einsum("qkr,rh->hqk", offset_table, offset_bias, precision=highest)[None, None]
    clip_valid = (video_ids[:, :, None] == video_ids[:, None, :])[:, None, None]
    clip_mix, clip_total = attend_forward(
        clip_query, clip_key, clip_value, frame_form, clip_bias, clip_valid
    )
    temporal_mix = from_clips(clip_mix.reshape(slots, frames_all, clip_pixels, half_width))
    temporal_mix = temporal_mix.reshape(token_rows, half_width)
    stream_four = stream_three + over_heads(
        jnp.dot(temporal_mix, temporal_out, preferred_element_type=jnp.float32), True
    )
    feed_rows = layer_norm(stream_four, feed_norm).astype(jnp.bfloat16)
    upper = jnp.dot(feed_rows, feed_in, preferred_element_type=jnp.float32)
    active = jax.nn.gelu(upper).astype(jnp.bfloat16)
    final = stream_four + over_heads(
        jnp.dot(active, feed_out, preferred_element_type=jnp.float32), True
    )
    mixed = final.astype(jnp.bfloat16).reshape(video.shape)
    upstream = cotangent.astype(jnp.float32).reshape(token_rows, channels)
    branch_grad = upstream.astype(jnp.bfloat16)
    feed_out_grad = jnp.einsum("rf,rd->fd", active, branch_grad, preferred_element_type=jnp.float32)
    active_grad = jnp.einsum("rd,fd->rf", branch_grad, feed_out, preferred_element_type=jnp.float32)
    upper_grad = jax.vjp(jax.nn.gelu, upper)[1](active_grad)[0].astype(jnp.bfloat16)
    feed_in_grad = jnp.einsum(
        "rd,rf->df", feed_rows, upper_grad, preferred_element_type=jnp.float32
    )
    normed_grad = over_heads(
        jnp.einsum("rf,df->rd", upper_grad, feed_in, preferred_element_type=jnp.float32), True
    )
    stream_grad, feed_norm_grad = layer_back(stream_four, feed_norm, normed_grad)
    upstream = upstream + stream_grad
    branch_grad = upstream.astype(jnp.bfloat16)
    temporal_out_grad = jnp.einsum(
        "rc,rd->cd", temporal_mix, branch_grad, preferred_element_type=jnp.float32
    )
    mix_grad = jnp.einsum(
        "rd,cd->rc", branch_grad, temporal_out, preferred_element_type=jnp.float32
    ).astype(jnp.bfloat16)
    clip_up = to_clips(mix_grad.reshape(slots, frame_dev, pixels_dev, half_width)).reshape(
        slots, frames_all, clip_pixels, head_local, HDIM
    )
    query_grad, key_grad, value_grad, score_grad = attend_backward(
        clip_query, clip_key, clip_value, frame_form, clip_bias, clip_valid, clip_total, clip_up
    )
    score_total = jnp.sum(score_grad.astype(jnp.float32), axis=(0, 1))
    offset_bias_grad = jnp.einsum("hqk,qkr->rh", score_total, offset_table, precision=highest)
    clip_grads = (
        jnp.stack([query_grad, key_grad, value_grad], axis=3)
        .astype(jnp.bfloat16)
        .reshape(slots, frames_all, clip_pixels, 3, half_width)
    )
    triple_grad = from_clips(clip_grads)
    triple_grad = triple_grad.reshape(token_rows, 3, half_width)
    temporal_qkv_grad = jnp.einsum(
        "rd,rjk->djk", temporal_in, triple_grad, preferred_element_type=jnp.float32
    )
    normed_grad = over_heads(
        jnp.einsum("rjk,djk->rd", triple_grad, temporal_qkv, preferred_element_type=jnp.float32),
        True,
    )
    stream_grad, temporal_norm_grad = layer_back(stream_three, temporal_norm, normed_grad)
    upstream = upstream + stream_grad
    branch_grad = upstream.astype(jnp.bfloat16)
    cross_out_grad = jnp.einsum(
        "rc,rd->cd", cross_mix, branch_grad, preferred_element_type=jnp.float32
    )
    mix_grad = (
        jnp.einsum("rd,cd->rc", branch_grad, cross_out, preferred_element_type=jnp.float32)
        .astype(jnp.bfloat16)
        .reshape(slots, frame_dev * pixels_dev, head_local, HDIM)
    )
    query_grad, key_grad, value_grad, score_grad = attend_backward(
        cross_queries, text_key, text_value, pixel_form, None, text_valid, cross_total, mix_grad
    )
    text_pair_grad = lax.psum_scatter(
        jnp.stack([key_grad, value_grad], axis=2).reshape(slots, TXT, 2, half_width),
        ("tm", "space"),
        scatter_dimension=1,
        tiled=True,
    ).astype(jnp.bfloat16)
    cross_kv_grad = jnp.einsum(
        "btc,btjk->cjk", text, text_pair_grad, preferred_element_type=jnp.float32
    )
    text_part = jnp.einsum(
        "btjk,cjk->btc", text_pair_grad, cross_kv, preferred_element_type=jnp.float32
    )
    text_grad = over_heads(text_part.reshape(slots * text_local, text.shape[2]), False).reshape(
        slots, text_local, text.shape[2] // lax.axis_size("mp")
    )
    query_rows_grad = query_grad.astype(jnp.bfloat16).reshape(token_rows, half_width)
    cross_query_grad = jnp.einsum(
        "rd,rk->dk", cross_in, query_rows_grad, preferred_element_type=jnp.float32
    )
    normed_grad = over_heads(
        jnp.einsum("rk,dk->rd", query_rows_grad, cross_query, preferred_element_type=jnp.float32),
        True,
    )
    stream_grad, cross_norm_grad = layer_back(stream_two, cross_norm, normed_grad)
    upstream = upstream + stream_grad
    branch_grad = upstream.astype(jnp.bfloat16)
    spatial_out_grad = jnp.einsum(
        "rc,rd->cd", spatial_mix, branch_grad, preferred_element_type=jnp.float32
    )
    mix_grad = (
        jnp.einsum("rd,cd->rc", branch_grad, spatial_out, preferred_element_type=jnp.float32)
        .astype(jnp.bfloat16)
        .reshape(slots * frame_dev, pixels_dev, head_local, HDIM)
    )
    query_grad, key_grad, value_grad, score_grad = attend_backward(
        spatial_query, spatial_key, spatial_value, pixel_form, None, None, spatial_total, mix_grad
    )
    frame_pair_grad = lax.psum_scatter(
        jnp.stack([key_grad, value_grad], axis=2)
        .reshape(slots, frame_dev, H * W, 2, half_width)
        .astype(jnp.bfloat16),
        "space",
        scatter_dimension=2,
        tiled=True,
    )
    triple_grad = jnp.concatenate(
        [
            query_grad.astype(jnp.bfloat16).reshape(slots, frame_dev, pixels_dev, 1, half_width),
            frame_pair_grad,
        ],
        axis=3,
    ).reshape(token_rows, 3, half_width)
    spatial_qkv_grad = jnp.einsum(
        "rd,rjk->djk", spatial_in, triple_grad, preferred_element_type=jnp.float32
    )
    normed_grad = over_heads(
        jnp.einsum("rjk,djk->rd", triple_grad, spatial_qkv, preferred_element_type=jnp.float32),
        True,
    )
    stream_grad, spatial_norm_grad = layer_back(stream_one, spatial_norm, normed_grad)
    upstream = upstream + stream_grad
    branch_grad = upstream.astype(jnp.bfloat16).reshape(video.shape)
    second_conv_grad = jnp.einsum(
        "bfhwtc,bfhwk->ctk", second_tiles, branch_grad, preferred_element_type=jnp.float32
    )
    second_in_grad = jnp.einsum(
        "bfhwtk,ctk->bfhwc",
        tap_tiles(with_rims(branch_grad), True),
        second_conv,
        preferred_element_type=jnp.float32,
    )
    modulated_grad = jax.vjp(jax.nn.silu, modulated)[1](second_in_grad)[0]
    frame_grads = jnp.stack(
        [jnp.sum(modulated_grad * normal_two, axis=(2, 3)), jnp.sum(modulated_grad, axis=(2, 3))],
        axis=2,
    )
    video_film_grad = jnp.einsum("bfv,bfjk->bvjk", choose, frame_grads, precision=highest)
    film_weight_grad = jnp.einsum(
        "bvc,bvjk->cjk", embed.astype(jnp.float32), video_film_grad, precision=highest
    )
    hidden_grad = group_backward(
        modulated_grad * (1.0 + frame_film[:, :, None, None, 0]), normal_two, inverse_two
    ).astype(jnp.bfloat16)
    first_conv_grad = jnp.einsum(
        "bfhwtc,bfhwk->ctk", first_tiles, hidden_grad, preferred_element_type=jnp.float32
    )
    first_in_part = jnp.einsum(
        "bfhwtk,ctk->bfhwc",
        tap_tiles(with_rims(hidden_grad), True),
        first_conv,
        preferred_element_type=jnp.float32,
    )
    first_in_grad = over_heads(first_in_part.reshape(token_rows, channels), True).reshape(
        video.shape
    )
    affine_grad = jax.vjp(jax.nn.silu, affine_one)[1](first_in_grad)[0]
    group_gain_grad = jnp.sum(affine_grad * normal_one, axis=(0, 1, 2, 3))
    group_bias_grad = jnp.sum(affine_grad, axis=(0, 1, 2, 3))
    video_grad = upstream.reshape(video.shape) + group_backward(
        affine_grad * group_gain, normal_one, inverse_one
    )
    weight_set = (
        lax.psum_scatter(group_gain_grad, ("tm", "space"), scatter_dimension=0, tiled=True),
        lax.psum_scatter(group_bias_grad, ("tm", "space"), scatter_dimension=0, tiled=True),
        lax.psum_scatter(first_conv_grad, ("tm", "space"), scatter_dimension=0, tiled=True),
        lax.psum_scatter(film_weight_grad, ("tm", "space"), scatter_dimension=0, tiled=True),
        lax.psum_scatter(second_conv_grad, ("tm", "space"), scatter_dimension=2, tiled=True),
        lax.psum_scatter(spatial_norm_grad, ("tm", "space"), scatter_dimension=0, tiled=True),
        lax.psum_scatter(spatial_qkv_grad, ("tm", "space"), scatter_dimension=0, tiled=True),
        lax.psum_scatter(spatial_out_grad, ("tm", "space"), scatter_dimension=1, tiled=True),
        lax.psum_scatter(cross_norm_grad, ("tm", "space"), scatter_dimension=0, tiled=True),
        lax.psum_scatter(cross_query_grad, ("tm", "space"), scatter_dimension=0, tiled=True),
        lax.psum_scatter(cross_kv_grad, ("tm", "space"), scatter_dimension=0, tiled=True),
        lax.psum_scatter(cross_out_grad, ("tm", "space"), scatter_dimension=1, tiled=True),
        lax.psum_scatter(temporal_norm_grad, ("tm", "space"), scatter_dimension=0, tiled=True),
        lax.psum_scatter(temporal_qkv_grad, ("tm", "space"), scatter_dimension=0, tiled=True),
        lax.psum_scatter(temporal_out_grad, ("tm", "space"), scatter_dimension=1, tiled=True),
        lax.psum_scatter(offset_bias_grad, ("tm", "space"), scatter_dimension=0, tiled=True),
        lax.psum_scatter(feed_norm_grad, ("tm", "space"), scatter_dimension=0, tiled=True),
        lax.psum_scatter(feed_in_grad, ("tm", "space"), scatter_dimension=0, tiled=True),
        lax.psum_scatter(feed_out_grad, ("tm", "space"), scatter_dimension=1, tiled=True),
    )
    return (mixed, video_grad, text_grad) + tuple(weight_set)


def solution(mesh):
    return jax.shard_map(
        on_device,
        mesh=mesh,
        in_specs=(
            P(None, "tm", "space", None, None),
            P(None, "tm", "space", None, None),
            P(None, ("tm", "space"), None),
            P(),
            P(),
            P(),
            P(),
            P(),
            P("space", None, "mp"),
            P("space", None, "mp"),
            P("mp", None, "space"),
            P(),
            P("space", None, "mp"),
            P("mp", "space"),
            P(),
            P("space", "mp"),
            P("space", None, "mp"),
            P("mp", "space"),
            P(),
            P("space", None, "mp"),
            P("mp", "space"),
            P(None, "mp"),
            P(),
            P("space", "mp"),
            P("mp", "space"),
        ),
        out_specs=(
            P(None, "tm", "space", None, None),
            P(None, "tm", "space", None, None),
            P(None, ("tm", "space"), "mp"),
            P(("tm", "space")),
            P(("tm", "space")),
            P(("tm", "space"), None, "mp"),
            P(("tm", "space"), None, "mp"),
            P("mp", None, ("tm", "space")),
            P(("tm", "space")),
            P(("tm", "space"), None, "mp"),
            P("mp", ("tm", "space")),
            P(("tm", "space")),
            P(("tm", "space"), "mp"),
            P(("tm", "space"), None, "mp"),
            P("mp", ("tm", "space")),
            P(("tm", "space")),
            P(("tm", "space"), None, "mp"),
            P("mp", ("tm", "space")),
            P(("tm", "space"), "mp"),
            P(("tm", "space")),
            P(("tm", "space"), "mp"),
            P("mp", ("tm", "space")),
        ),
        check_vma=False,
    )
```

profile of v0, /device:TPU:2, one launch (start us, length us, event | category | flops | bytes accessed | tf_op | source)
XLA Modules:
  0.0 3947.8 jit_solution(10452632931363446045)
XLA Ops:
  11.1 12.1 psum.56
  23.8 8.7 psum.57
  42.2 7.8 collective-permute-done.1
  62.6 164.9 %all-gather.14.cloned.1.call-done = bf16[1024,9,512]{2,0,1:T(8,128)(2,1)} async-done(((bf16[256,9,512]{2,0,1:T(8,128)(2,1)}), bf16[1024,9,512]{2,0,1:T(8,128)(2,1)}) %all-gather.14.cloned.1.call-update) | async-done | bytes 9437200 | tf_op jit(solution)/shard_map/all_gather | solution.py:256
  227.5 6.7 fusion.227
  234.4 9.0 psum.58
  243.8 13.9 psum.59
  258.1 13.3 collective-permute-start.2
  274.9 20.4 collective-permute-done.3
  302.4 92.9 %all-gather.18.cloned.1.call-done = bf16[512,9,1024]{2,0,1:T(8,128)(2,1)} async-done(((bf16[512,9,256]{2,0,1:T(8,128)(2,1)}), bf16[512,9,1024]{2,0,1:T(8,128)(2,1)}) %all-gather.18.cloned.1.call-update) | async-done | bytes 9437200 | tf_op jit(solution)/shard_map/all_gather | solution.py:258
  395.3 7.0 fusion.4
  414.1 61.6 %all-gather.20.cloned.1.call-done = bf16[1024,3,512]{2,0,1:T(8,128)(2,1)} async-done(((bf16[256,3,512]{2,0,1:T(8,128)(2,1)}), bf16[1024,3,512]{2,0,1:T(8,128)(2,1)}) %all-gather.20.cloned.1.call-update) | async-done | bytes 3145744 | tf_op jit(solution)/shard_map/all_gather | solution.py:259
  484.1 40.1 %all-gather.22.cloned.1.call-done = bf16[2,2,256,2,512]{4,2,1,0,3:T(8,128)(2,1)} async-done(((bf16[2,2,64,2,512]{4,2,1,0,3:T(8,128)(2,1)}), bf16[2,2,256,2,512]{4,2,1,0,3:T(8,128)(2,1)}) %all-gather.22.cloned.1.call-update) | async-done | bytes 2097168 | tf_op jit(solution)/shard_map/all_gather | solution.py:311
  535.0 18.7 all-gather.24.cloned.1.call-done
  557.6 146.7 %all-gather.26.cloned.1.call-done = bf16[4096,2,512]{2,0,1:T(8,128)(2,1)} async-done(((bf16[1024,2,512]{2,0,1:T(8,128)(2,1)}), bf16[4096,2,512]{2,0,1:T(8,128)(2,1)}) %all-gather.26.cloned.1.call-update) | async-done | bytes 8388624 | tf_op jit(solution)/shard_map/all_gather | solution.py:262
  708.9 41.1 %all_gather.81 = bf16[2,128,2,512]{3,1,2,0:T(8,128)(2,1)S(1)} all-gather(bf16[2,8,2,512]{3,1,2,0:T(8,128)(2,1)S(1)} %fusion.68), channel_id=1, replica_groups=mesh['tm'=4,'space'=4,'mp'=2] {'tm','space'}, dimensions={1}, use_global_device_ids=true | all-gather | bytes 557056 | tf_op jit(solution)/shard_map/all_gather | solution.py:331
  758.7 20.8 all-gather.30.cloned.1.call-done
  792.6 63.2 %all-gather.32.cloned.1.call-done = bf16[1024,3,512]{2,0,1:T(8,128)(2,1)} async-done(((bf16[256,3,512]{2,0,1:T(8,128)(2,1)}), bf16[1024,3,512]{2,0,1:T(8,128)(2,1)}) %all-gather.32.cloned.1.call-update) | async-done | bytes 3145744 | tf_op jit(solution)/shard_map/all_gather | solution.py:264
  866.7 9.2 all-to-all-done
  888.9 7.8 all_to_all.63
  899.9 66.4 %all-gather.38.cloned.1.call-done = bf16[2048,1024]{1,0:T(8,128)(2,1)} async-done(((bf16[2048,256]{1,0:T(8,128)(2,1)}), bf16[2048,1024]{1,0:T(8,128)(2,1)}) %all-gather.38.cloned.1.call-update) | async-done | bytes 4194320 | tf_op jit(solution)/shard_map/all_gather | solution.py:267
  979.3 79.4 %all-gather.36.cloned.1.call-done = bf16[1024,2048]{1,0:T(8,128)(2,1)} async-done(((bf16[256,2048]{1,0:T(8,128)(2,1)}), bf16[1024,2048]{1,0:T(8,128)(2,1)}) %all-gather.36.cloned.1.call-update) | async-done | bytes 4194320 | tf_op jit(solution)/shard_map/all_gather | solution.py:266
  1058.7 7.1 fusion.30
  1081.2 6.6 reduce-scatter.33.cloned.1.call-done
  1128.4 13.4 all_to_all.64
  1144.7 8.5 reduce-scatter.37.cloned.1.call-done
  1166.7 8.4 reduce-scatter.39.cloned.1.call-done
  1204.5 6.7 pad_maximum_fusion
  1216.3 82.5 %all-reduce.17.cloned.1.call-done = bf16[2,2,256,2,512]{4,3,1,0,2:T(2,128)(2,1)} async-done(((bf16[2,2,256,2,512]{4,3,1,0,2:T(2,128)(2,1)}), bf16[2,2,256,2,512]{4,3,1,0,2:T(2,128)(2,1)}) %all-reduce.17.cloned.1.call-update) | async-done | bytes 2097168
  1337.0 9.9 all-reduce.14
  1351.1 47.4 %reduce-scatter.45.cloned.1.call-done = f32[2,8,2,512]{3,1,0,2:T(8,128)} async-done(((f32[2,128,2,512]{3,1,0,2:T(8,128)}), f32[2,8,2,512]{3,1,0,2:T(8,128)}) %reduce-scatter.45.cloned.1.call-update) | async-done | bytes 65552 | tf_op jit(solution)/shard_map/reduce_scatter | solution.py:431
  1417.9 8.1 convolution_bitcast_fusion
  1426.3 10.4 convolution_bitcast_fusion.2
  1436.7 27.1 copy.643
  1496.8 9.6 convolution_bitcast_fusion.1
  1514.4 82.6 %all-reduce.12 = (f32[1024]{0:T(1024)S(1)}, f32[1024]{0:T(1024)S(1)}, f32[1024]{0:T(1024)S(1)}, f32[1024]{0:T(1024)S(1)}, f32[1024]{0:T(1024)S(1)}, /*index=5*/f32[128,8]{1,0:T(8,128)S(1)}, f32[1024]{0:T(1024)S(1)}) all-reduce(f32[1024]{0:T(1024)S(1)} %get-tuple-element.198, ...), channel_id=15, replica_groups=mesh['tm'=4,'space'=4,'mp'=2] {'tm','space'}, use_global_device_ids=true, to_apply=%region_63.64.clone | all-reduce | flops 7168 | bytes 57344
  1601.0 13.0 all-reduce.13
  1618.2 261.0 %reduce-scatter.61.cloned.1.call-done = f32[256,2,512]{0,2,1:T(8,128)} async-done(((f32[4096,2,512]{0,2,1:T(8,128)}), f32[256,2,512]{0,2,1:T(8,128)}) %reduce-scatter.61.cloned.1.call-update) | async-done | bytes 1048592 | tf_op jit(solution)/shard_map/reduce_scatter | solution.py:543
  1881.4 689.2 %reduce-scatter.49.cloned.1.call-done = f32[64,9,512]{2,1,0:T(8,128)} async-done(((f32[1024,9,512]{2,1,0:T(8,128)}), f32[64,9,512]{2,1,0:T(8,128)}) %reduce-scatter.49.cloned.1.call-update) | async-done | bytes 1179664 | tf_op jit(solution)/shard_map/reduce_scatter | solution.py:535
  2573.9 78.3 %reduce-scatter.67.cloned.1.call-done = f32[512,64]{0,1:T(8,128)} async-done(((f32[512,1024]{0,1:T(8,128)}), f32[512,64]{0,1:T(8,128)}) %reduce-scatter.67.cloned.1.call-update) | async-done | bytes 131088 | tf_op jit(solution)/shard_map/reduce_scatter | solution.py:547
  2652.2 83.7 %reduce-scatter.59.cloned.1.call-done = f32[64,512]{1,0:T(8,128)} async-done(((f32[1024,512]{1,0:T(8,128)}), f32[64,512]{1,0:T(8,128)}) %reduce-scatter.59.cloned.1.call-update) | async-done | bytes 131088 | tf_op jit(solution)/shard_map/reduce_scatter | solution.py:542
  2735.9 83.7 %reduce-scatter.63.cloned.1.call-done = f32[512,64]{0,1:T(8,128)} async-done(((f32[512,1024]{0,1:T(8,128)}), f32[512,64]{0,1:T(8,128)}) %reduce-scatter.63.cloned.1.call-update) | async-done | bytes 131088 | tf_op jit(solution)/shard_map/reduce_scatter | solution.py:544
  2819.7 83.8 %reduce-scatter.57.cloned.1.call-done = f32[512,64]{0,1:T(8,128)} async-done(((f32[512,1024]{0,1:T(8,128)}), f32[512,64]{0,1:T(8,128)}) %reduce-scatter.57.cloned.1.call-update) | async-done | bytes 131088 | tf_op jit(solution)/shard_map/reduce_scatter | solution.py:540
  2903.5 142.1 %reduce-scatter.65.cloned.1.call-done = f32[64,3,512]{2,0,1:T(8,128)} async-done(((f32[1024,3,512]{2,0,1:T(8,128)}), f32[64,3,512]{2,0,1:T(8,128)}) %reduce-scatter.65.cloned.1.call-update) | async-done | bytes 393232 | tf_op jit(solution)/shard_map/reduce_scatter | solution.py:546
  3045.6 182.4 %reduce-scatter.69.cloned.1.call-done = f32[64,2048]{1,0:T(8,128)} async-done(((f32[1024,2048]{1,0:T(8,128)}), f32[64,2048]{1,0:T(8,128)}) %reduce-scatter.69.cloned.1.call-update) | async-done | bytes 524304 | tf_op jit(solution)/shard_map/reduce_scatter | solution.py:550
  3228.0 182.6 %reduce-scatter.71.cloned.1.call-done = f32[2048,64]{0,1:T(8,128)} async-done(((f32[2048,1024]{0,1:T(8,128)}), f32[2048,64]{0,1:T(8,128)}) %reduce-scatter.71.cloned.1.call-update) | async-done | bytes 524304 | tf_op jit(solution)/shard_map/reduce_scatter | solution.py:551
  3410.6 138.5 %reduce-scatter.55.cloned.1.call-done = f32[64,3,512]{2,0,1:T(8,128)} async-done(((f32[1024,3,512]{2,0,1:T(8,128)}), f32[64,3,512]{2,0,1:T(8,128)}) %reduce-scatter.55.cloned.1.call-update) | async-done | bytes 393232 | tf_op jit(solution)/shard_map/reduce_scatter | solution.py:539
  3549.1 392.0 %reduce-scatter.53.cloned.1.call-done = f32[512,9,64]{0,2,1:T(8,128)} async-done(((f32[512,9,1024]{0,2,1:T(8,128)}), f32[512,9,64]{0,2,1:T(8,128)}) %reduce-scatter.53.cloned.1.call-update) | async-done | bytes 1179664 | tf_op jit(solution)/shard_map/reduce_scatter | solution.py:537
  (711 shorter events, 358.7 us)
Async XLA Ops:
  7.2 53.2 %all-gather.16.cloned.1.call-start = ((), (), s32[]{:S(2)}) async-start(), calls=%async_computation.29 | async-start | bytes 2621440 | tf_op jit(solution)/shard_map/all_gather | solution.py:257
  9.2 218.3 %all-gather.14.cloned.1.call-start = ((), (), s32[]{:S(2)}) async-start(), calls=%async_computation.28 | async-start | bytes 11796480 | tf_op jit(solution)/shard_map/all_gather | solution.py:256
  10.0 385.3 %all-gather.18.cloned.1.call-start = ((), (), s32[]{:S(2)}) async-start(), calls=%async_computation.30 | async-start | bytes 11796480 | tf_op jit(solution)/shard_map/all_gather | solution.py:258
  10.7 399.0 %reduce-scatter.25.cloned.1.call-start = ((), (), s32[]{:S(2)}) async-start(), calls=%async_computation.31 | async-start | bytes 786432 | tf_op jit(solution)/shard_map/reduce_scatter | solution.py:37
  33.2 9.1 collective-permute-start
  37.0 13.1 collective-permute-start.1
  258.1 16.7 collective-permute-start.2
  271.5 23.8 collective-permute-start.3
  403.2 72.4 %all-gather.20.cloned.1.call-start = ((), (), s32[]{:S(2)}) async-start(), calls=%async_computation.32 | async-start | bytes 3932160 | tf_op jit(solution)/shard_map/all_gather | solution.py:259
  403.8 120.4 %all-gather.22.cloned.1.call-start = ((), (), s32[]{:S(2)}) async-start(), calls=%async_computation.33 | async-start | bytes 2621440 | tf_op jit(solution)/shard_map/all_gather | solution.py:311
  479.4 74.3 %all-gather.24.cloned.1.call-start = ((), (), s32[]{:S(2)}) async-start(), calls=%async_computation.34 | async-start | bytes 1310720 | tf_op jit(solution)/shard_map/all_gather | solution.py:260
  480.1 224.2 %all-gather.26.cloned.1.call-start = ((), (), s32[]{:S(2)}) async-start(), calls=%async_computation.36 | async-start | bytes 10485760 | tf_op jit(solution)/shard_map/all_gather | solution.py:262
  483.5 266.9 %reduce-scatter.27.cloned.1.call-start = ((), (), s32[]{:S(2)}) async-start(), calls=%async_computation.35 | async-start | bytes 786432 | tf_op jit(solution)/shard_map/reduce_scatter | solution.py:37
  556.2 197.9 %all-gather.28.cloned.1.call-start = ((), (), s32[]{:S(2)}) async-start(), calls=%async_computation.37 | async-start | bytes 1310720 | tf_op jit(solution)/shard_map/all_gather | solution.py:261
  556.8 222.7 %all-gather.30.cloned.1.call-start = ((), (), s32[]{:S(2)}) async-start(), calls=%async_computation.38 | async-start | bytes 1310720 | tf_op jit(solution)/shard_map/all_gather | solution.py:263
  557.5 232.2 %reduce-scatter.29.cloned.1.call-start = ((), (), s32[]{:S(2)}) async-start(), calls=%async_computation.39 | async-start | bytes 786432 | tf_op jit(solution)/shard_map/reduce_scatter | solution.py:37
  782.0 73.8 %all-gather.32.cloned.1.call-start = ((), (), s32[]{:S(2)}) async-start(), calls=%async_computation.40 | async-start | bytes 3932160 | tf_op jit(solution)/shard_map/all_gather | solution.py:264
  782.8 113.9 %all-gather.34.cloned.1.call-start = ((), (), s32[]{:S(2)}) async-start(), calls=%async_computation.41 | async-start | bytes 1310720 | tf_op jit(solution)/shard_map/all_gather | solution.py:265
  783.4 183.0 %all-gather.38.cloned.1.call-start = ((), (), s32[]{:S(2)}) async-start(), calls=%async_computation.44 | async-start | bytes 5242880 | tf_op jit(solution)/shard_map/all_gather | solution.py:267
  860.5 15.3 all-to-all-start
  865.2 110.3 %reduce-scatter.31.cloned.1.call-start = ((), (), s32[]{:S(2)}) async-start(), calls=%async_computation.42 | async-start | bytes 786432 | tf_op jit(solution)/shard_map/reduce_scatter | solution.py:37
  899.3 159.4 %all-gather.36.cloned.1.call-start = ((), (), s32[]{:S(2)}) async-start(), calls=%async_computation.43 | async-start | bytes 5242880 | tf_op jit(solution)/shard_map/all_gather | solution.py:266
  899.9 175.9 %reduce-scatter.35.cloned.1.call-start = ((), (), s32[]{:S(2)}) async-start(), calls=%async_computation.46 | async-start | bytes 786432 | tf_op jit(solution)/shard_map/reduce_scatter | solution.py:37
  1068.9 18.9 reduce-scatter.33.cloned.1.call-start
  1096.6 9.8 all-to-all-start.2
  1100.9 52.3 %reduce-scatter.37.cloned.1.call-start = ((), (), s32[]{:S(2)}) async-start(), calls=%async_computation.47 | async-start | bytes 786432 | tf_op jit(solution)/shard_map/reduce_scatter | solution.py:37
  1144.6 30.5 reduce-scatter.39.cloned.1.call-start
  1165.8 133.0 %all-reduce.17.cloned.1.call-start = ((), (), s32[]{:S(2)}) async-start(), calls=%async_computation.65 | async-start | bytes 4194304
  1211.2 101.2 %reduce-scatter.41.cloned.1.call-start = ((), (), s32[]{:S(2)}) async-start(), calls=%async_computation.49 | async-start | bytes 786432 | tf_op jit(solution)/shard_map/reduce_scatter | solution.py:37
  1305.1 93.5 %reduce-scatter.45.cloned.1.call-start = ((), (), s32[]{:S(2)}) async-start(), calls=%async_computation.51 | async-start | bytes 1114112 | tf_op jit(solution)/shard_map/reduce_scatter | solution.py:431
  1317.8 6.6 collective-permute-start.4
  1321.2 7.4 collective-permute-start.5
  1323.6 185.9 %reduce-scatter.47.cloned.1.call-start = ((), (), s32[]{:S(2)}) async-start(), calls=%async_computation.52 | async-start | bytes 196608 | tf_op jit(solution)/shard_map/reduce_scatter | solution.py:37
  1347.4 57.6 %collective-permute-start.6 = (bf16[2,2,1,16,512]{4,3,2,1,0:T(8,128)(2,1)S(1)}, bf16[2,2,1,16,512]{4,3,2,1,0:T(8,128)(2,1)S(1)}, u32[]{:S(2)}, u32[]{:S(2)}) collective-permute-start(bf16[2,2,1,16,512]{4,3,2,1,0:T(8,128)(2,1)S(1)} %get-tuple-element.250), channel_id=1, source_target_pairs={{0,2},{2,4},{4,6},{1,3},{3,5},{5,7},{8,10},{10,12},{12,14},{9,11},... | collective-permute-start | bytes 196616 | tf_op jit(solution)/shard_map/ppermute | solution.py:28
  1349.8 55.1 %collective-permute-start.7 = (bf16[2,2,1,16,512]{4,3,2,1,0:T(8,128)(2,1)S(1)}, bf16[2,2,1,16,512]{4,3,2,1,0:T(8,128)(2,1)S(1)}, u32[]{:S(2)}, u32[]{:S(2)}) collective-permute-start(bf16[2,2,1,16,512]{4,3,2,1,0:T(8,128)(2,1)S(1)} %get-tuple-element.251), channel_id=1, source_target_pairs={{2,0},{4,2},{6,4},{3,1},{5,3},{7,5},{10,8},{12,10},{14,12},{11,9},... | collective-permute-start | bytes 196616 | tf_op jit(solution)/shard_map/ppermute | solution.py:31
  1404.9 106.2 %reduce-scatter.43.cloned.1.call-start = ((), (), s32[]{:S(2)}) async-start(), calls=%async_computation.50 | async-start | bytes 786432 | tf_op jit(solution)/shard_map/reduce_scatter | solution.py:37
  1412.9 203.4 %reduce-scatter.51.cloned.1.call-start = ((), (), s32[]{:S(2)}) async-start(), calls=%async_computation.54 | async-start | bytes 4456448 | tf_op jit(solution)/shard_map/reduce_scatter | solution.py:536
  1417.1 462.1 %reduce-scatter.61.cloned.1.call-start = ((), (), s32[]{:S(2)}) async-start(), calls=%async_computation.59 | async-start | bytes 17825792 | tf_op jit(solution)/shard_map/reduce_scatter | solution.py:543
  1426.1 1144.5 %reduce-scatter.49.cloned.1.call-start = ((), (), s32[]{:S(2)}) async-start(), calls=%async_computation.53 | async-start | bytes 35651584 | tf_op jit(solution)/shard_map/reduce_scatter | solution.py:535
  1463.8 1188.3 %reduce-scatter.67.cloned.1.call-start = ((), (), s32[]{:S(2)}) async-start(), calls=%async_computation.62 | async-start | bytes 2228224 | tf_op jit(solution)/shard_map/reduce_scatter | solution.py:547
  1466.7 1269.2 %reduce-scatter.59.cloned.1.call-start = ((), (), s32[]{:S(2)}) async-start(), calls=%async_computation.58 | async-start | bytes 2228224 | tf_op jit(solution)/shard_map/reduce_scatter | solution.py:542
  1468.8 1350.9 %reduce-scatter.63.cloned.1.call-start = ((), (), s32[]{:S(2)}) async-start(), calls=%async_computation.60 | async-start | bytes 2228224 | tf_op jit(solution)/shard_map/reduce_scatter | solution.py:544
  1470.8 1432.7 %reduce-scatter.57.cloned.1.call-start = ((), (), s32[]{:S(2)}) async-start(), calls=%async_computation.57 | async-start | bytes 2228224 | tf_op jit(solution)/shard_map/reduce_scatter | solution.py:540
  1474.0 1571.7 %reduce-scatter.65.cloned.1.call-start = ((), (), s32[]{:S(2)}) async-start(), calls=%async_computation.61 | async-start | bytes 6684672 | tf_op jit(solution)/shard_map/reduce_scatter | solution.py:546
  1477.9 1750.1 %reduce-scatter.69.cloned.1.call-start = ((), (), s32[]{:S(2)}) async-start(), calls=%async_computation.63 | async-start | bytes 8912896 | tf_op jit(solution)/shard_map/reduce_scatter | solution.py:550
  1484.2 1926.4 %reduce-scatter.71.cloned.1.call-start = ((), (), s32[]{:S(2)}) async-start(), calls=%async_computation.64 | async-start | bytes 8912896 | tf_op jit(solution)/shard_map/reduce_scatter | solution.py:551
  1490.7 2058.3 %reduce-scatter.55.cloned.1.call-start = ((), (), s32[]{:S(2)}) async-start(), calls=%async_computation.56 | async-start | bytes 6684672 | tf_op jit(solution)/shard_map/reduce_scatter | solution.py:539
  1495.7 2445.3 %reduce-scatter.53.cloned.1.call-start = ((), (), s32[]{:S(2)}) async-start(), calls=%async_computation.55 | async-start | bytes 20054016 | tf_op jit(solution)/shard_map/reduce_scatter | solution.py:537
  (166 other events, 6368.3 us)
Sparse Core Ops, SparseCore 0:
  10.2 50.1 all-gather.15
  61.9 165.5 all-gather.13
  229.1 166.2 all-gather.17
  403.3 6.3 reduce-scatter.24
  411.2 64.3 all-gather.19
  479.5 44.5 all-gather.21
  525.8 27.8 all-gather.23
  555.4 148.9 all-gather.25
  707.3 6.3 reduce-scatter.26
  715.1 34.3 all-gather.27
  751.0 28.4 all-gather.29
  782.2 7.4 reduce-scatter.28
  791.4 64.3 all-gather.31
  857.3 27.8 all-gather.33
  886.7 79.6 all-gather.37
  969.1 6.3 reduce-scatter.30
  976.9 81.7 all-gather.35
  1069.0 6.6 reduce-scatter.34
  1078.6 9.0 reduce-scatter.32
  1144.7 8.4 reduce-scatter.36
  1165.9 9.1 reduce-scatter.38
  1211.3 87.4 all-reduce.16
  1305.2 7.1 reduce-scatter.40
  1323.8 74.7 reduce-scatter.44
  1405.0 10.6 reduce-scatter.46
  1417.9 9.0 reduce-scatter.42
  1429.2 95.7 reduce-scatter.50
  1527.3 351.8 reduce-scatter.60
  1881.5 688.9 reduce-scatter.48
  2573.3 78.8 reduce-scatter.66
  2655.0 80.8 reduce-scatter.58
  2738.8 80.8 reduce-scatter.62
  2822.4 81.0 reduce-scatter.56
  2906.4 139.2 reduce-scatter.64
  3048.5 179.4 reduce-scatter.68
  3230.7 179.8 reduce-scatter.70
  3413.3 135.7 reduce-scatter.54
  3551.9 389.0 reduce-scatter.52
where the time goes:
time: 3960 us; the launch traced here: 3950 us
  waiting for transfers between devices  3310 us (84%)
  blocking collectives  236 us (6%)
  matrix products  162 us (4%)
  local copies, waits for them, and re-layouts  145 us (4%)
  other arithmetic  41.4 us (1%)
  starting transfers between devices  39.8 us (1%)
    reduce_scatter x1, waiting for transfers between devices, on_device(): lax.psum_scatter(first_conv_grad, ('tm', 'space'), scatter_dimension=0, t...  689 us
    reduce_scatter x1, waiting for transfers between devices, on_device(): lax.psum_scatter(second_conv_grad, ('tm', 'space'), scatter_dimension=2,...  392 us
    reduce_scatter x1, waiting for transfers between devices, on_device(): lax.psum_scatter(cross_kv_grad, ('tm', 'space'), scatter_dimension=0, til...  261 us
    reduce_scatter x1, waiting for transfers between devices, on_device(): lax.psum_scatter(feed_out_grad, ('tm', 'space'), scatter_dimension=1, til...  183 us
    reduce_scatter x1, waiting for transfers between devices, on_device(): lax.psum_scatter(feed_in_grad, ('tm', 'space'), scatter_dimension=0, tile...  182 us
    all_gather x1, waiting for transfers between devices, on_device(): lax.all_gather(first_conv, 'space', axis=0, tiled=True)  165 us
    all_gather x1, waiting for transfers between devices, on_device(): lax.all_gather(cross_kv, 'space', axis=0, tiled=True)  147 us
    reduce_scatter x1, waiting for transfers between devices, on_device(): lax.psum_scatter(temporal_qkv_grad, ('tm', 'space'), scatter_dimension=0,...  142 us
  transfers between devices with their start and end apart: 48, of which 40 were waited for; matrix products, arithmetic and copies ran while one was open for 6% of the time, Pallas kernels for 0%

commit v1 on v0

v1 whole, which is shorter than its diff:
```python
import math

import jax
import jax.numpy as jnp
from jax import lax
from jax.sharding import PartitionSpec as P

D = 1024
HDIM = 64
TXT = 128
G = 32
R = 128
VIDS = 3
H = 16
W = 16


epsilon = 1e-05
highest = lax.Precision.HIGHEST
masked = -1e30


def mp_sum(partial_sum):
    mine = partial_sum.astype(jnp.bfloat16)
    other = lax.ppermute(mine, "mp", [(0, 1), (1, 0)])
    return mine.astype(jnp.float32) + other.astype(jnp.float32)


def part_of(source, axis_name, dim):
    size = source.shape[dim] // lax.axis_size(axis_name)
    return lax.dynamic_slice_in_dim(source, lax.axis_index(axis_name) * size, size, dim)


def space_to_all(source, split, concat):
    return lax.all_to_all(source, "space", split_axis=split, concat_axis=concat, tiled=True)


def gather_tokens(rows):
    half = part_of(rows, "mp", 1)
    line = lax.all_gather(half, "space", axis=0, tiled=True)
    return lax.all_gather(line, "mp", axis=1, tiled=True)


def scatter_tokens(partial_sum):
    half = lax.psum_scatter(
        partial_sum.astype(jnp.bfloat16), "mp", scatter_dimension=1, tiled=True
    )
    line = lax.psum_scatter(half, "space", scatter_dimension=0, tiled=True)
    return lax.all_gather(line, "mp", axis=1, tiled=True).astype(jnp.float32)


def to_clips(source):
    return lax.all_to_all(source, "tm", split_axis=2, concat_axis=1, tiled=True)


def from_clips(source):
    return lax.all_to_all(source, "tm", split_axis=1, concat_axis=2, tiled=True)


def sum_to_owner(weight_grad, dim):
    return lax.psum_scatter(
        weight_grad.astype(jnp.bfloat16), ("tm", "space"), scatter_dimension=dim, tiled=True
    ).astype(jnp.float32)


def sum_over_frames(weight_grad, dim):
    return lax.psum_scatter(
        weight_grad.astype(jnp.bfloat16), "tm", scatter_dimension=dim, tiled=True
    )


def stationary_to_owner(weight_grad, dim):
    portion = sum_over_frames(weight_grad, dim)
    frames, lines = lax.axis_size("tm"), lax.axis_size("space")
    moves = [(t * lines + s, s * frames + t) for t in range(frames) for s in range(lines)]
    return lax.ppermute(portion, ("tm", "space"), moves).astype(jnp.float32)


def padded_rims(source):
    return jnp.pad(source, ((0, 0), (0, 0), (1, 1), (1, 1), (0, 0)))


def conv_weight(weight):
    return weight.reshape(weight.shape[0], 3, 3, weight.shape[2])


def conv_frames(source, weight, spec, flipped):
    images = source.reshape((-1,) + source.shape[2:])
    kernel = conv_weight(weight)
    if flipped:
        kernel = kernel[:, ::-1, ::-1]
    result = lax.conv_general_dilated(
        images,
        kernel,
        (1, 1),
        "SAME",
        dimension_numbers=("NHWC", spec, "NHWC"),
        preferred_element_type=jnp.float32,
    )
    return result.reshape(source.shape[:4] + (result.shape[-1],))


def conv_weight_grad(source, upstream):
    padded = padded_rims(source)
    rows, cols = source.shape[2], source.shape[3]
    tap_list = []
    for tap in range(9):
        i, j = tap // 3, tap % 3
        tap_list.append(
            jnp.einsum(
                "bfhwc,bfhwk->ck",
                padded[:, :, i : i + rows, j : j + cols],
                upstream,
                preferred_element_type=jnp.float32,
            ).astype(jnp.bfloat16)
        )
    return jnp.stack(tap_list, axis=0)


def grouped_view(source):
    size = D // G
    dims_all = source.shape
    return source.reshape(
        dims_all[0], dims_all[1], dims_all[2] * dims_all[3], dims_all[4] // size, size
    )


def group_forward(source):
    grouped = grouped_view(source)
    average = jnp.mean(grouped, axis=(2, 4), keepdims=True)
    centered = grouped - average
    variance = jnp.mean(centered * centered, axis=(2, 4), keepdims=True)
    inverse = lax.rsqrt(variance + epsilon)
    return ((centered * inverse).reshape(source.shape), inverse)


def group_backward(upstream, normal, inverse):
    grouped_up = grouped_view(upstream)
    grouped_norm = grouped_view(normal)
    first_mean = jnp.mean(grouped_up, axis=(2, 4), keepdims=True)
    second_mean = jnp.mean(grouped_up * grouped_norm, axis=(2, 4), keepdims=True)
    result = inverse * (grouped_up - first_mean - grouped_norm * second_mean)
    return result.reshape(upstream.shape)


def layer_norm(source, norm_gain):
    average = jnp.mean(source, axis=-1, keepdims=True)
    centered = source - average
    variance = jnp.mean(centered * centered, axis=-1, keepdims=True)
    return centered * lax.rsqrt(variance + epsilon) * norm_gain


def layer_back(source, norm_gain, upstream):
    _, pullback = jax.vjp(layer_norm, source, norm_gain)
    return pullback(upstream)


def sinusoid(steps_int):
    counted = D // 2
    freqs = jnp.exp(-math.log(10000.0) * jnp.arange(counted, dtype=jnp.float32) / counted)
    angles = steps_int.astype(jnp.float32)[..., None] * freqs
    return jnp.concatenate([jnp.sin(angles), jnp.cos(angles)], axis=-1)


def offset_onehot(query_start, query_count, key_count):
    distance = (
        query_start
        + jnp.arange(query_count, dtype=jnp.int32)[:, None]
        - jnp.arange(key_count, dtype=jnp.int32)[None, :]
    )
    position = jnp.clip(distance, -(R // 2), R // 2 - 1) + R // 2
    return (position[:, :, None] == jnp.arange(R, dtype=jnp.int32)[None, None, :]).astype(
        jnp.float32
    )


def scores_of(queries, keys, forms, bias, valid):
    query_form, key_form, score_form = forms
    raw_scores = jnp.einsum(
        query_form + "," + key_form + "->" + score_form,
        queries,
        keys,
        preferred_element_type=jnp.float32,
    ) * (1.0 / math.sqrt(HDIM))
    if bias is not None:
        raw_scores = raw_scores + bias
    if valid is not None:
        raw_scores = jnp.where(valid, raw_scores, masked)
    return raw_scores


def attend_forward(queries, keys, values_in, forms, bias, valid):
    query_form, key_form, score_form = forms
    raw_scores = scores_of(queries, keys, forms, bias, valid)
    largest = jnp.max(raw_scores, axis=-1, keepdims=True)
    expos = jnp.exp(raw_scores - largest)
    totals = jnp.sum(expos, axis=-1, keepdims=True)
    probs = (expos / totals).astype(jnp.bfloat16)
    log_total = (largest + jnp.log(totals))[..., 0]
    result = jnp.einsum(
        score_form + "," + key_form + "->" + query_form,
        probs,
        values_in,
        preferred_element_type=jnp.float32,
    )
    return (result.astype(jnp.bfloat16), log_total)


def attend_backward(queries, keys, values_in, forms, bias, valid, log_total, upstream):
    query_form, key_form, score_form = forms
    score_scale = 1.0 / math.sqrt(HDIM)
    raw_scores = scores_of(queries, keys, forms, bias, valid)
    probs = jnp.exp(raw_scores - log_total[..., None])
    low_probs = probs.astype(jnp.bfloat16)
    prob_grad = jnp.einsum(
        query_form + "," + key_form + "->" + score_form,
        upstream,
        values_in,
        preferred_element_type=jnp.float32,
    )
    inner = jnp.sum(probs * prob_grad, axis=-1, keepdims=True)
    score_grad = (probs * (prob_grad - inner)).astype(jnp.bfloat16)
    query_grad = (
        jnp.einsum(
            score_form + "," + key_form + "->" + query_form,
            score_grad,
            keys,
            preferred_element_type=jnp.float32,
        )
        * score_scale
    )
    key_grad = (
        jnp.einsum(
            score_form + "," + query_form + "->" + key_form,
            score_grad,
            queries,
            preferred_element_type=jnp.float32,
        )
        * score_scale
    )
    value_grad = jnp.einsum(
        score_form + "," + query_form + "->" + key_form,
        low_probs,
        upstream,
        preferred_element_type=jnp.float32,
    )
    return (query_grad, key_grad, value_grad, score_grad)


def on_device(
    video,
    cotangent,
    text,
    video_ids,
    timesteps,
    text_lengths,
    group_gain,
    group_bias,
    first_conv,
    film_weight,
    second_conv,
    spatial_norm,
    spatial_qkv,
    spatial_out,
    cross_norm,
    cross_query,
    cross_kv,
    cross_out,
    temporal_norm,
    temporal_qkv,
    temporal_out,
    offset_bias,
    feed_norm,
    feed_in,
    feed_out,
):
    frames_axis, lines = lax.axis_size("tm"), lax.axis_size("space")
    slots, frame_dev, row_dev, columns, channels = video.shape
    half_width = first_conv.shape[2]
    head_local = half_width // HDIM
    pixels_dev = row_dev * columns
    frames_all = frame_dev * frames_axis
    token_rows = slots * frame_dev * pixels_dev
    text_local = text.shape[1]
    pixel_form = ("nqhe", "nkhe", "nhqk")
    frame_form = ("bfphe", "bgphe", "bphfg")
    video_lines = space_to_all(video, 4, 2)
    text_all = lax.all_gather(text, ("tm", "space"), axis=1, tiled=True)
    spatial_out = lax.all_gather(spatial_out, "space", axis=1, tiled=True)
    cross_query = lax.all_gather(cross_query, "space", axis=0, tiled=True)
    cross_out = lax.all_gather(cross_out, "space", axis=1, tiled=True)
    temporal_qkv = lax.all_gather(temporal_qkv, "space", axis=0, tiled=True)
    temporal_out = lax.all_gather(temporal_out, "space", axis=1, tiled=True)
    spatial_qkv = space_to_all(spatial_qkv, 2, 0)
    feed_in = space_to_all(feed_in, 1, 0)
    feed_out = space_to_all(feed_out, 0, 1)
    cot_rows = cotangent.reshape(token_rows, channels)
    cot_line = gather_tokens(cot_rows)

    gain_line = part_of(group_gain, "space", 0)
    bias_line = part_of(group_bias, "space", 0)
    normal_one, inverse_one = group_forward(video_lines.astype(jnp.float32))
    affine_one = normal_one * gain_line + bias_line
    first_in = jax.nn.silu(affine_one).astype(jnp.bfloat16)
    hidden_part = conv_frames(first_in, first_conv, "IHWO", False)
    hidden = lax.psum_scatter(
        hidden_part.astype(jnp.bfloat16), "space", scatter_dimension=4, tiled=True
    ).astype(jnp.float32)
    normal_two, inverse_two = group_forward(hidden)
    embed = sinusoid(timesteps).astype(jnp.bfloat16)
    film_part = jnp.einsum(
        "bvc,cjk->bvjk", part_of(embed, "space", 2), film_weight, preferred_element_type=jnp.float32
    )
    film = lax.psum_scatter(film_part, "space", scatter_dimension=3, tiled=True)
    frame_ids = part_of(video_ids, "tm", 1)
    choose = (frame_ids[:, :, None] == jnp.arange(VIDS, dtype=jnp.int32)[None, None, :]).astype(
        jnp.float32
    )
    frame_film = jnp.einsum("bfv,bvjk->bfjk", choose, film, precision=highest)
    modulated = (
        normal_two * (1.0 + frame_film[:, :, None, None, 0]) + frame_film[:, :, None, None, 1]
    )
    second_in = jax.nn.silu(modulated).astype(jnp.bfloat16)
    second_wide = lax.all_gather(second_in, "space", axis=4, tiled=True)
    conv_part = conv_frames(second_wide, second_conv, "IHWO", False)
    conv_half = lax.psum_scatter(
        conv_part.astype(jnp.bfloat16), "mp", scatter_dimension=4, tiled=True
    )
    conv_rows = space_to_all(conv_half, 2, 4).reshape(token_rows, lines, -1)
    conv_rows = lax.all_gather(conv_rows, "mp", axis=2, tiled=True).reshape(token_rows, channels)
    stream_one = video.astype(jnp.float32).reshape(token_rows, channels) + conv_rows.astype(
        jnp.float32
    )

    spatial_in = layer_norm(stream_one, spatial_norm).astype(jnp.bfloat16)
    spatial_line = gather_tokens(spatial_in)
    head_line = spatial_qkv.shape[2] // HDIM
    spatial_triple = (
        jnp.einsum("rd,djk->rjk", spatial_line, spatial_qkv, preferred_element_type=jnp.float32)
        .astype(jnp.bfloat16)
        .reshape(lines, slots * frame_dev, pixels_dev, 3, head_line, HDIM)
        .transpose(3, 1, 0, 2, 4, 5)
        .reshape(3, slots * frame_dev, H * W, head_line, HDIM)
    )
    spatial_query, spatial_key, spatial_value = spatial_triple
    spatial_mix, spatial_total = attend_forward(
        spatial_query, spatial_key, spatial_value, pixel_form, None, None
    )
    spatial_mix = space_to_all(
        spatial_mix.reshape(slots * frame_dev, H * W, head_line * HDIM), 1, 2
    ).reshape(token_rows, half_width)
    stream_two = stream_one + mp_sum(
        jnp.dot(spatial_mix, spatial_out, preferred_element_type=jnp.float32)
    )
    cross_in = layer_norm(stream_two, cross_norm).astype(jnp.bfloat16)
    cross_rows = jnp.dot(cross_in, cross_query, preferred_element_type=jnp.float32).astype(
        jnp.bfloat16
    )
    text_some = part_of(part_of(text_all, "tm", 1), "space", 2)
    text_pairs = lax.psum_scatter(
        jnp.einsum("btc,cjk->btjk", text_some, cross_kv, preferred_element_type=jnp.float32).astype(
            jnp.bfloat16
        ),
        "space",
        scatter_dimension=1,
        tiled=True,
    )
    text_pairs = lax.all_gather(text_pairs, ("tm", "space"), axis=1, tiled=True)
    cross_queries = cross_rows.reshape(slots, frame_dev * pixels_dev, head_local, HDIM)
    text_key = text_pairs[:, :, 0].reshape(slots, TXT, head_local, HDIM)
    text_value = text_pairs[:, :, 1].reshape(slots, TXT, head_local, HDIM)
    text_valid = (jnp.arange(TXT, dtype=jnp.int32)[None, :] < text_lengths[:, None])[
        :, None, None, :
    ]
    cross_mix, cross_total = attend_forward(
        cross_queries, text_key, text_value, pixel_form, None, text_valid
    )
    cross_mix = cross_mix.reshape(token_rows, half_width)
    stream_three = stream_two + mp_sum(
        jnp.dot(cross_mix, cross_out, preferred_element_type=jnp.float32)
    )
    temporal_in = layer_norm(stream_three, temporal_norm).astype(jnp.bfloat16)
    temporal_triple = (
        jnp.einsum("rd,djk->rjk", temporal_in, temporal_qkv, preferred_element_type=jnp.float32)
        .astype(jnp.bfloat16)
        .reshape(slots, frame_dev, pixels_dev, 3, half_width)
    )
    clip_triple = to_clips(temporal_triple)
    clip_pixels = clip_triple.shape[2]
    clip_query = clip_triple[:, :, :, 0].reshape(slots, frames_all, clip_pixels, head_local, HDIM)
    clip_key = clip_triple[:, :, :, 1].reshape(slots, frames_all, clip_pixels, head_local, HDIM)
    clip_value = clip_triple[:, :, :, 2].reshape(slots, frames_all, clip_pixels, head_local, HDIM)
    offset_table = offset_onehot(0, video_ids.shape[1], frames_all)
    clip_bias = jnp.einsum("qkr,rh->hqk", offset_table, offset_bias, precision=highest)[None, None]
    clip_valid = (video_ids[:, :, None] == video_ids[:, None, :])[:, None, None]
    clip_mix, clip_total = attend_forward(
        clip_query, clip_key, clip_value, frame_form, clip_bias, clip_valid
    )
    temporal_mix = from_clips(clip_mix.reshape(slots, frames_all, clip_pixels, half_width))
    temporal_mix = temporal_mix.reshape(token_rows, half_width)
    stream_four = stream_three + mp_sum(
        jnp.dot(temporal_mix, temporal_out, preferred_element_type=jnp.float32)
    )
    feed_rows = layer_norm(stream_four, feed_norm).astype(jnp.bfloat16)
    feed_line = gather_tokens(feed_rows)
    upper = jnp.dot(feed_line, feed_in, preferred_element_type=jnp.float32)
    active = jax.nn.gelu(upper).astype(jnp.bfloat16)
    final = stream_four + scatter_tokens(
        jnp.dot(active, feed_out, preferred_element_type=jnp.float32)
    )
    mixed = final.astype(jnp.bfloat16).reshape(video.shape)

    feed_out_grad = jnp.einsum("rf,rd->fd", active, cot_line, preferred_element_type=jnp.float32)
    feed_out_grad = space_to_all(sum_over_frames(feed_out_grad, 1), 1, 0).astype(jnp.float32)
    active_grad = jnp.einsum("rd,fd->rf", cot_line, feed_out, preferred_element_type=jnp.float32)
    upper_grad = jax.vjp(jax.nn.gelu, upper)[1](active_grad)[0].astype(jnp.bfloat16)
    feed_in_grad = jnp.einsum(
        "rd,rf->df", feed_line, upper_grad, preferred_element_type=jnp.float32
    )
    feed_in_grad = space_to_all(sum_over_frames(feed_in_grad, 0), 0, 1).astype(jnp.float32)
    normed_grad = scatter_tokens(
        jnp.einsum("rf,df->rd", upper_grad, feed_in, preferred_element_type=jnp.float32)
    )
    stream_grad, feed_norm_grad = layer_back(stream_four, feed_norm, normed_grad)
    upstream = cot_rows.astype(jnp.float32) + stream_grad
    branch_grad = upstream.astype(jnp.bfloat16)
    temporal_out_grad = sum_to_owner(
        jnp.einsum("rc,rd->cd", temporal_mix, branch_grad, preferred_element_type=jnp.float32), 1
    )
    mix_grad = jnp.einsum(
        "rd,cd->rc", branch_grad, temporal_out, preferred_element_type=jnp.float32
    ).astype(jnp.bfloat16)
    clip_up = to_clips(mix_grad.reshape(slots, frame_dev, pixels_dev, half_width)).reshape(
        slots, frames_all, clip_pixels, head_local, HDIM
    )
    query_grad, key_grad, value_grad, score_grad = attend_backward(
        clip_query, clip_key, clip_value, frame_form, clip_bias, clip_valid, clip_total, clip_up
    )
    score_total = jnp.sum(score_grad.astype(jnp.float32), axis=(0, 1))
    offset_bias_grad = jnp.einsum("hqk,qkr->rh", score_total, offset_table, precision=highest)
    clip_grads = (
        jnp.stack([query_grad, key_grad, value_grad], axis=3)
        .astype(jnp.bfloat16)
        .reshape(slots, frames_all, clip_pixels, 3, half_width)
    )
    triple_grad = from_clips(clip_grads)
    triple_grad = triple_grad.reshape(token_rows, 3, half_width)
    temporal_qkv_grad = sum_to_owner(
        jnp.einsum("rd,rjk->djk", temporal_in, triple_grad, preferred_element_type=jnp.float32), 0
    )
    normed_grad = mp_sum(
        jnp.einsum("rjk,djk->rd", triple_grad, temporal_qkv, preferred_element_type=jnp.float32)
    )
    stream_grad, temporal_norm_grad = layer_back(stream_three, temporal_norm, normed_grad)
    upstream = upstream + stream_grad
    branch_grad = upstream.astype(jnp.bfloat16)
    cross_out_grad = sum_to_owner(
        jnp.einsum("rc,rd->cd", cross_mix, branch_grad, preferred_element_type=jnp.float32), 1
    )
    mix_grad = (
        jnp.einsum("rd,cd->rc", branch_grad, cross_out, preferred_element_type=jnp.float32)
        .astype(jnp.bfloat16)
        .reshape(slots, frame_dev * pixels_dev, head_local, HDIM)
    )
    query_grad, key_grad, value_grad, score_grad = attend_backward(
        cross_queries, text_key, text_value, pixel_form, None, text_valid, cross_total, mix_grad
    )
    text_pair_grad = lax.psum_scatter(
        jnp.stack([key_grad, value_grad], axis=2)
        .reshape(slots, TXT, 2, half_width)
        .astype(jnp.bfloat16),
        ("tm", "space"),
        scatter_dimension=1,
        tiled=True,
    )
    text_pair_all = lax.all_gather(text_pair_grad, ("tm", "space"), axis=1, tiled=True)
    cross_kv_grad = jnp.einsum(
        "btc,btjk->cjk",
        part_of(part_of(text_all, "tm", 2), "space", 2),
        text_pair_all,
        preferred_element_type=jnp.float32,
    )
    text_part = jnp.einsum(
        "btjk,cjk->btc",
        part_of(text_pair_all, "tm", 1),
        cross_kv,
        preferred_element_type=jnp.float32,
    ).astype(jnp.bfloat16)
    text_grad = lax.psum_scatter(
        space_to_all(text_part, 1, 2), "mp", scatter_dimension=2, tiled=True
    ).astype(jnp.float32)
    query_rows_grad = query_grad.astype(jnp.bfloat16).reshape(token_rows, half_width)
    cross_query_grad = sum_to_owner(
        jnp.einsum("rd,rk->dk", cross_in, query_rows_grad, preferred_element_type=jnp.float32), 0
    )
    normed_grad = mp_sum(
        jnp.einsum("rk,dk->rd", query_rows_grad, cross_query, preferred_element_type=jnp.float32)
    )
    stream_grad, cross_norm_grad = layer_back(stream_two, cross_norm, normed_grad)
    upstream = upstream + stream_grad
    branch_grad = upstream.astype(jnp.bfloat16)
    spatial_out_grad = sum_to_owner(
        jnp.einsum("rc,rd->cd", spatial_mix, branch_grad, preferred_element_type=jnp.float32), 1
    )
    mix_grad = (
        jnp.einsum("rd,cd->rc", branch_grad, spatial_out, preferred_element_type=jnp.float32)
        .astype(jnp.bfloat16)
        .reshape(slots * frame_dev, pixels_dev, half_width)
    )
    mix_line = space_to_all(mix_grad, 2, 1).reshape(slots * frame_dev, H * W, head_line, HDIM)
    query_grad, key_grad, value_grad, score_grad = attend_backward(
        spatial_query, spatial_key, spatial_value, pixel_form, None, None, spatial_total, mix_line
    )
    triple_grad = (
        jnp.stack([query_grad, key_grad, value_grad], axis=0)
        .astype(jnp.bfloat16)
        .reshape(3, slots * frame_dev, lines, pixels_dev, head_line * HDIM)
        .transpose(2, 1, 3, 0, 4)
        .reshape(lines * token_rows, 3, head_line * HDIM)
    )
    spatial_qkv_grad = jnp.einsum(
        "rd,rjk->djk", spatial_line, triple_grad, preferred_element_type=jnp.float32
    )
    spatial_qkv_grad = space_to_all(sum_over_frames(spatial_qkv_grad, 0), 0, 2).astype(jnp.float32)
    normed_grad = scatter_tokens(
        jnp.einsum("rjk,djk->rd", triple_grad, spatial_qkv, preferred_element_type=jnp.float32)
    )
    stream_grad, spatial_norm_grad = layer_back(stream_one, spatial_norm, normed_grad)
    upstream = upstream + stream_grad
    branch_line = space_to_all(upstream.astype(jnp.bfloat16).reshape(video.shape), 4, 2)
    second_conv_grad = stationary_to_owner(conv_weight_grad(second_wide, branch_line), 2)
    second_part = conv_frames(branch_line, second_conv, "OHWI", True)
    second_in_grad = lax.psum_scatter(
        second_part.astype(jnp.bfloat16), "space", scatter_dimension=4, tiled=True
    ).astype(jnp.float32)
    modulated_grad = jax.vjp(jax.nn.silu, modulated)[1](second_in_grad)[0]
    frame_grads = jnp.stack(
        [jnp.sum(modulated_grad * normal_two, axis=(2, 3)), jnp.sum(modulated_grad, axis=(2, 3))],
        axis=2,
    )
    video_film_grad = jnp.einsum("bfv,bfjk->bvjk", choose, frame_grads, precision=highest)
    video_film_grad = lax.all_gather(
        lax.psum(video_film_grad, "tm"), "space", axis=3, tiled=True
    )
    film_weight_grad = jnp.einsum(
        "bvc,bvjk->cjk",
        part_of(part_of(embed, "tm", 2), "space", 2).astype(jnp.float32),
        video_film_grad,
        precision=highest,
    )
    hidden_grad = group_backward(
        modulated_grad * (1.0 + frame_film[:, :, None, None, 0]), normal_two, inverse_two
    ).astype(jnp.bfloat16)
    hidden_wide = lax.all_gather(hidden_grad, "space", axis=4, tiled=True)
    first_conv_grad = stationary_to_owner(conv_weight_grad(first_in, hidden_wide), 1)
    first_in_grad = mp_sum(conv_frames(hidden_wide, first_conv, "OHWI", True))
    affine_grad = jax.vjp(jax.nn.silu, affine_one)[1](first_in_grad)[0]
    group_gain_grad = jnp.sum(affine_grad * normal_one, axis=(0, 1, 2, 3))
    group_bias_grad = jnp.sum(affine_grad, axis=(0, 1, 2, 3))
    video_line_grad = group_backward(affine_grad * gain_line, normal_one, inverse_one)
    video_grad = upstream.reshape(video.shape) + space_to_all(
        video_line_grad.astype(jnp.bfloat16), 2, 4
    ).astype(jnp.float32)

    def placed(line_grad):
        whole = jnp.zeros((channels,), jnp.float32)
        return lax.dynamic_update_slice_in_dim(
            whole, line_grad, lax.axis_index("space") * line_grad.shape[0], 0
        )

    owners = frames_axis * lines
    small = jnp.concatenate(
        [
            item.reshape(owners, -1)
            for item in (
                placed(group_gain_grad),
                placed(group_bias_grad),
                spatial_norm_grad,
                cross_norm_grad,
                temporal_norm_grad,
                feed_norm_grad,
                offset_bias_grad,
            )
        ],
        axis=1,
    )
    small = lax.psum_scatter(small, ("tm", "space"), scatter_dimension=0, tiled=True)[0]
    gain_size = channels // owners
    gains = [small[i * gain_size : (i + 1) * gain_size] for i in range(6)]
    offset_bias_grad = small[6 * gain_size :].reshape(R // owners, head_local)
    return (
        mixed,
        video_grad,
        text_grad,
        gains[0],
        gains[1],
        first_conv_grad.transpose(1, 0, 2),
        film_weight_grad,
        second_conv_grad.transpose(1, 0, 2),
        gains[2],
        spatial_qkv_grad,
        spatial_out_grad,
        gains[3],
        cross_query_grad,
        cross_kv_grad,
        cross_out_grad,
        gains[4],
        temporal_qkv_grad,
        temporal_out_grad,
        offset_bias_grad,
        gains[5],
        feed_in_grad,
        feed_out_grad,
    )


def solution(mesh):
    return jax.shard_map(
        on_device,
        mesh=mesh,
        in_specs=(
            P(None, "tm", "space", None, None),
            P(None, "tm", "space", None, None),
            P(None, ("tm", "space"), None),
            P(),
            P(),
            P(),
            P(),
            P(),
            P("space", None, "mp"),
            P("space", None, "mp"),
            P("mp", None, "space"),
            P(),
            P("space", None, "mp"),
            P("mp", "space"),
            P(),
            P("space", "mp"),
            P("space", None, "mp"),
            P("mp", "space"),
            P(),
            P("space", None, "mp"),
            P("mp", "space"),
            P(None, "mp"),
            P(),
            P("space", "mp"),
            P("mp", "space"),
        ),
        out_specs=(
            P(None, "tm", "space", None, None),
            P(None, "tm", "space", None, None),
            P(None, ("tm", "space"), "mp"),
            P(("tm", "space")),
            P(("tm", "space")),
            P(("tm", "space"), None, "mp"),
            P(("tm", "space"), None, "mp"),
            P("mp", None, ("tm", "space")),
            P(("tm", "space")),
            P(("tm", "space"), None, "mp"),
            P("mp", ("tm", "space")),
            P(("tm", "space")),
            P(("tm", "space"), "mp"),
            P(("tm", "space"), None, "mp"),
            P("mp", ("tm", "space")),
            P(("tm", "space")),
            P(("tm", "space"), None, "mp"),
            P("mp", ("tm", "space")),
            P(("tm", "space"), "mp"),
            P(("tm", "space")),
            P(("tm", "space"), "mp"),
            P("mp", ("tm", "space")),
        ),
        check_vma=False,
    )
```

time: 3960 us -> 1890 us (0.48)
  waiting for transfers between devices: 3310 us -> 1020 us
  local copies, waits for them, and re-layouts: 145 us -> 305 us
  blocking collectives: 236 us -> 279 us
    reduce_scatter x24 -> x17, waiting for transfers between devices: 2410 us -> 536 us  [the longest x5 337 us: sum_to_owner(): lax.psum_scatter(weight_grad.astype(jnp.bfloat16), ('tm', 'space'), scatt...]
    all_gather x13 -> x14, waiting for transfers between devices: 756 us -> 230 us  [the longest x3 88 us: gather_tokens(): line = lax.all_gather(half, 'space', axis=0, tiled=True)]
    all_to_all x0 -> x10, waiting for transfers between devices: none -> 118 us  [space_to_all(): lax.all_to_all(source, 'space', split_axis=split, concat_axis=concat, til...]
    unnamed x369 -> x341, local copies, waits for them, and re-layouts: 51 us -> 163 us
    dot_general x17 -> x29, matrix products: 98.8 us -> 49.2 us  [the longest x18 16.4 us: conv_weight_grad(): jnp.einsum('bfhwc,bfhwk->ck', padded[:, :, i:i + rows, j:j + cols], upstr...]
    all_gather x11 -> x7, blocking collectives: 65.7 us -> 115 us  [the longest x1 47.1 us: on_device(): lax.all_gather(text_pair_grad, ('tm', 'space'), axis=1, tiled=True)]
    psum x6 -> x1, blocking collectives: 66.6 us -> 18.1 us  [on_device(): lax.psum(video_film_grad, 'tm')]
    all_to_all x0 -> x10, starting transfers between devices: none -> 41.7 us  [space_to_all(): lax.all_to_all(source, 'space', split_axis=split, concat_axis=concat, til...]
  transfers between devices with their start and end apart: 48 -> 57, of which waited for: 40 -> 39; matrix products, arithmetic and copies ran while one was open for 6% -> 13% of each run, Pallas kernels for 0% -> 0%
where the time goes in v1:
time: 1890 us; the launch traced here: 1880 us
  waiting for transfers between devices  1020 us (54%)
  local copies, waits for them, and re-layouts  305 us (16%)
  blocking collectives  279 us (15%)
  matrix products  127 us (7%)
  starting transfers between devices  69.8 us (4%)
  other arithmetic  57.7 us (3%)
    reduce_scatter x5, waiting for transfers between devices, sum_to_owner(): lax.psum_scatter(weight_grad.astype(jnp.bfloat16), ('tm', 'space'), scatt...  337 us
    unnamed x341, local copies, waits for them, and re-layouts  163 us
    all_to_all x10, waiting for transfers between devices, space_to_all(): lax.all_to_all(source, 'space', split_axis=split, concat_axis=concat, til...  118 us
    unnamed x43, waiting for transfers between devices  109 us
    reduce_scatter x5, waiting for transfers between devices, sum_over_frames(): lax.psum_scatter(weight_grad.astype(jnp.bfloat16), 'tm', scatter_dimensio...  89.4 us
    all_gather x3, waiting for transfers between devices, gather_tokens(): line = lax.all_gather(half, 'space', axis=0, tiled=True)  88 us
    unnamed x1, blocking collectives  84.3 us
    reduce_scatter x3, waiting for transfers between devices, scatter_tokens(): line = lax.psum_scatter(half, 'space', scatter_dimension=0, tiled=True)  83.4 us
  transfers between devices with their start and end apart: 57, of which 39 were waited for; matrix products, arithmetic and copies ran while one was open for 13% of the time, Pallas kernels for 0%

profile of v1, /device:TPU:2, one launch (start us, length us, event | category | flops | bytes accessed | tf_op | source)
XLA Modules:
  0.0 1876.4 jit_solution(17224866909273308164)
XLA Ops:
  30.6 10.6 all-to-all-done
  60.8 12.1 copy.873
  72.9 15.8 reshape.686
  90.3 25.2 %reduce-scatter.70.cloned.1.call-done = bf16[128,1024]{1,0:T(8,128)(2,1)} async-done(((bf16[512,1024]{1,0:T(8,128)(2,1)}), bf16[128,1024]{1,0:T(8,128)(2,1)}) %reduce-scatter.70.cloned.1.call-update) | async-done | bytes 262160
  124.3 27.5 %all-gather.15.cloned.1.call-done = bf16[2,2,16,16,512]{4,3,2,1,0:T(8,128)(2,1)} async-done(((bf16[2,2,16,16,128]{4,3,2,1,0:T(8,128)(2,1)}), bf16[2,2,16,16,512]{4,3,2,1,0:T(8,128)(2,1)}) %all-gather.15.cloned.1.call-update) | async-done | bytes 1048592 | tf_op jit(solution)/shard_map/all_gather | solution.py:324
  166.7 8.8 reshape.690
  175.5 7.6 reduce-scatter.74.cloned.1.call-done
  195.0 9.3 all-to-all-done.1
  219.1 26.5 %all-gather.17.cloned.1.call-done = bf16[1024,512]{1,0:T(8,128)(2,1)} async-done(((bf16[256,512]{1,0:T(8,128)(2,1)}), bf16[1024,512]{1,0:T(8,128)(2,1)}) %all-gather.17.cloned.1.call-update) | async-done | bytes 1048592 | tf_op jit(solution)/shard_map/all_gather | solution.py:40
  246.5 62.3 %all-gather.23.cloned.1.call-done = bf16[2,128,4096]{2,1,0:T(8,128)(2,1)} async-done(((bf16[2,8,4096]{2,1,0:T(8,128)(2,1)}), bf16[2,128,4096]{2,1,0:T(8,128)(2,1)}) %all-gather.23.cloned.1.call-update) | async-done | bytes 2097168 | tf_op jit(solution)/shard_map/all_gather | solution.py:288
  318.9 38.6 %all-to-all-done.2 = bf16[256,3,512]{0,1,2:T(4,128)(2,1)S(1)} async-done(((bf16[256,3,512]{0,1,2:T(4,128)(2,1)}), bf16[256,3,512]{0,1,2:T(4,128)(2,1)S(1)}, u32[]{:S(2)}, u32[]{:S(2)}) %all-to-all-start.2) | async-done | bytes 786464 | tf_op jit(solution)/shard_map/all_to_all | solution.py:35
  378.1 9.5 all_to_all.253
  390.7 45.0 %all_gather.69 = bf16[2,128,2,512]{3,2,0,1:T(2,128)(2,1)S(1)} all-gather(bf16[2,8,2,512]{3,2,0,1:T(2,128)(2,1)S(1)} %bitcast.849), channel_id=1, replica_groups=mesh['tm'=4,'space'=4,'mp'=2] {'tm','space'}, dimensions={1}, use_global_device_ids=true | all-gather | bytes 557056 | tf_op jit(solution)/shard_map/all_gather | solution.py:368
  461.1 52.0 %all-gather.29.cloned.1.call-done = bf16[1024,3,512]{2,0,1:T(8,128)(2,1)} async-done(((bf16[256,3,512]{2,0,1:T(8,128)(2,1)}), bf16[1024,3,512]{2,0,1:T(8,128)(2,1)}) %all-gather.29.cloned.1.call-update) | async-done | bytes 3145744 | tf_op jit(solution)/shard_map/all_gather | solution.py:292
  523.2 10.2 all-to-all-done.4
  548.2 8.6 all_to_all.254
  566.1 21.7 %all-gather.37.cloned.1.call-done = bf16[1024,512]{1,0:T(8,128)(2,1)} async-done(((bf16[256,512]{1,0:T(8,128)(2,1)}), bf16[1024,512]{1,0:T(8,128)(2,1)}) %all-gather.37.cloned.1.call-update) | async-done | bytes 1048592 | tf_op jit(solution)/shard_map/all_gather | solution.py:40
  592.1 39.8 %all-gather.33.cloned.1.call-done = bf16[1024,512]{1,0:T(8,128)(2,1)} async-done(((bf16[256,512]{1,0:T(8,128)(2,1)}), bf16[1024,512]{1,0:T(8,128)(2,1)}) %all-gather.33.cloned.1.call-update) | async-done | bytes 1048592 | tf_op jit(solution)/shard_map/all_gather | solution.py:40
  642.8 23.4 %all-to-all-done.6 = bf16[256,4,512]{0,2,1:T(8,128)(2,1)} async-done(((bf16[256,4,512]{0,2,1:T(8,128)(2,1)}), bf16[256,4,512]{0,2,1:T(8,128)(2,1)}, u32[]{:S(2)}, u32[]{:S(2)}) %all-to-all-start.6) | async-done | bytes 1048608 | tf_op jit(solution)/shard_map/all_to_all | solution.py:35
  692.0 13.1 reduce-scatter.36.cloned.1.call-done
  705.1 30.2 %reduce-scatter.42.cloned.1.call-done = bf16[256,512]{1,0:T(8,128)(2,1)} async-done(((bf16[1024,512]{1,0:T(8,128)(2,1)}), bf16[256,512]{1,0:T(8,128)(2,1)}) %reduce-scatter.42.cloned.1.call-update) | async-done | bytes 262160 | tf_op jit(solution)/shard_map/reduce_scatter | solution.py:48
  740.7 22.8 %reduce-scatter.38.cloned.1.call-done = bf16[256,512]{1,0:T(8,128)(2,1)} async-done(((bf16[1024,512]{1,0:T(8,128)(2,1)}), bf16[256,512]{1,0:T(8,128)(2,1)}) %reduce-scatter.38.cloned.1.call-update) | async-done | bytes 262160 | tf_op jit(solution)/shard_map/reduce_scatter | solution.py:48
  805.0 13.2 all_to_all.255
  849.0 9.2 all-to-all-done.10
  888.4 8.1 reduce-scatter.44.cloned.1.call-done
  896.6 30.4 %reduce-scatter.46.cloned.1.call-done = bf16[256,512]{1,0:T(8,128)(2,1)} async-done(((bf16[1024,512]{1,0:T(8,128)(2,1)}), bf16[256,512]{1,0:T(8,128)(2,1)}) %reduce-scatter.46.cloned.1.call-update) | async-done | bytes 262160 | tf_op jit(solution)/shard_map/reduce_scatter | solution.py:48
  947.4 19.7 %all_to_all.256 = bf16[4,2,32768]{2,1,0:T(2,128)(2,1)} all-to-all(bf16[4,2,32768]{2,1,0:T(2,128)(2,1)} %reshape.713), channel_id=1, replica_groups=mesh['tm'=4,'space'=4,'mp'=2] {'space'}, dimensions={0} | all-to-all | bytes 1048576 | tf_op jit(solution)/shard_map/all_to_all | solution.py:35
  986.5 15.0 copy.881
  1001.5 15.9 reshape.694
  1021.2 22.6 %reduce-scatter.78.cloned.1.call-done = bf16[128,1024]{1,0:T(8,128)(2,1)} async-done(((bf16[512,1024]{1,0:T(8,128)(2,1)}), bf16[128,1024]{1,0:T(8,128)(2,1)}) %reduce-scatter.78.cloned.1.call-update) | async-done | bytes 262160
  1066.3 49.9 %reduce-scatter.80.cloned.1.call-done = bf16[8,2048]{1,0:T(8,128)(2,1)} async-done(((bf16[128,2048]{1,0:T(8,128)(2,1)}), bf16[8,2048]{1,0:T(8,128)(2,1)}) %reduce-scatter.80.cloned.1.call-update) | async-done | bytes 32784
  1117.0 47.1 %all_gather.82 = bf16[2,128,2,512]{3,1,2,0:T(8,128)(2,1)S(1)} all-gather(bf16[2,8,2,512]{3,1,2,0:T(8,128)(2,1)S(1)} %copy.884), channel_id=1, replica_groups=mesh['tm'=4,'space'=4,'mp'=2] {'tm','space'}, dimensions={1}, use_global_device_ids=true | all-gather | bytes 557056 | tf_op jit(solution)/shard_map/all_gather | solution.py:476
  1166.8 10.4 all_to_all.257
  1230.4 9.3 all-to-all-done.15
  1244.9 9.6 all-to-all-done.16
  1256.3 35.7 %reduce-scatter.64.cloned.1.call-done = bf16[512,64]{0,1:T(8,128)(2,1)} async-done(((bf16[512,1024]{0,1:T(8,128)(2,1)}), bf16[512,64]{0,1:T(8,128)(2,1)}) %reduce-scatter.64.cloned.1.call-update) | async-done | bytes 65552 | tf_op jit(solution)/shard_map/reduce_scatter | solution.py:61
  1293.5 31.0 %reduce-scatter.54.cloned.1.call-done = bf16[256,3,128]{2,0,1:T(8,128)(2,1)} async-done(((bf16[1024,3,128]{2,0,1:T(8,128)(2,1)}), bf16[256,3,128]{2,0,1:T(8,128)(2,1)}) %reduce-scatter.54.cloned.1.call-update) | async-done | bytes 196624 | tf_op jit(solution)/shard_map/reduce_scatter | solution.py:67
  1332.7 7.1 all-to-all-done.14
  1347.9 64.2 %reduce-scatter.58.cloned.1.call-done = bf16[64,512]{1,0:T(8,128)(2,1)} async-done(((bf16[1024,512]{1,0:T(8,128)(2,1)}), bf16[64,512]{1,0:T(8,128)(2,1)}) %reduce-scatter.58.cloned.1.call-update) | async-done | bytes 65552 | tf_op jit(solution)/shard_map/reduce_scatter | solution.py:61
  1413.6 76.3 %reduce-scatter.60.cloned.1.call-done = bf16[512,64]{0,1:T(8,128)(2,1)} async-done(((bf16[512,1024]{0,1:T(8,128)(2,1)}), bf16[512,64]{0,1:T(8,128)(2,1)}) %reduce-scatter.60.cloned.1.call-update) | async-done | bytes 65552 | tf_op jit(solution)/shard_map/reduce_scatter | solution.py:61
  1491.4 76.7 %reduce-scatter.56.cloned.1.call-done = bf16[512,64]{0,1:T(8,128)(2,1)} async-done(((bf16[512,1024]{0,1:T(8,128)(2,1)}), bf16[512,64]{0,1:T(8,128)(2,1)}) %reduce-scatter.56.cloned.1.call-update) | async-done | bytes 65552 | tf_op jit(solution)/shard_map/reduce_scatter | solution.py:61
  1570.8 84.6 %reduce-scatter.62.cloned.1.call-done = bf16[64,3,512]{2,0,1:T(8,128)(2,1)} async-done(((bf16[1024,3,512]{2,0,1:T(8,128)(2,1)}), bf16[64,3,512]{2,0,1:T(8,128)(2,1)}) %reduce-scatter.62.cloned.1.call-update) | async-done | bytes 196624 | tf_op jit(solution)/shard_map/reduce_scatter | solution.py:61
  1657.2 58.4 %reduce-scatter.52.cloned.1.call-done = bf16[9,512,64]{1,0,2:T(8,128)(2,1)} async-done(((bf16[9,512,256]{1,0,2:T(8,128)(2,1)}), bf16[9,512,64]{1,0,2:T(8,128)(2,1)}) %reduce-scatter.52.cloned.1.call-update) | async-done | bytes 589840 | tf_op jit(solution)/shard_map/reduce_scatter | solution.py:67
  1721.7 18.1 psum.7
  1739.8 13.3 all_gather.83
  1755.0 84.3 %all-reduce.2 = f32[16,448]{1,0:T(8,128)S(1)} all-reduce(f32[16,448]{1,0:T(8,128)S(1)} %concatenate.14), channel_id=15, replica_groups=mesh['tm'=4,'space'=4,'mp'=2] {'tm','space'}, use_global_device_ids=true, to_apply=%region_61.62.clone | all-reduce | flops 7168 | bytes 57344
  1839.4 11.6 collective-permute-start.6
  1859.0 7.8 collective-permute-done.6
  (781 shorter events, 508.7 us)
Async XLA Ops:
  20.6 20.6 %all-to-all-start = ((bf16[4,2,32768]{2,1,0:T(2,128)(2,1)}), bf16[4,2,32768]{2,1,0:T(2,128)(2,1)}, u32[]{:S(2)}, u32[]{:S(2)}) async-start(bf16[4,2,32768]{2,1,0:T(2,128)(2,1)} %reshape.709), calls=%async_computation | async-start | bytes 1048576 | tf_op jit(solution)/shard_map/all_to_all | solution.py:35
  25.5 63.4 %reduce-scatter.72.cloned.1.call-start = ((), (), s32[]{:S(2)}) async-start(), calls=%async_computation.72 | async-start | bytes 327680
  28.8 86.6 %reduce-scatter.70.cloned.1.call-start = ((), (), s32[]{:S(2)}) async-start(), calls=%async_computation.71 | async-start | bytes 1310720
  88.8 63.1 %all-gather.15.cloned.1.call-start = ((), (), s32[]{:S(2)}) async-start(), calls=%async_computation.40 | async-start | bytes 1310720 | tf_op jit(solution)/shard_map/all_gather | solution.py:324
  123.8 59.3 %reduce-scatter.74.cloned.1.call-start = ((), (), s32[]{:S(2)}) async-start(), calls=%async_computation.73 | async-start | bytes 786432
  194.9 50.7 %all-gather.17.cloned.1.call-start = ((), (), s32[]{:S(2)}) async-start(), calls=%async_computation.41 | async-start | bytes 1310720 | tf_op jit(solution)/shard_map/all_gather | solution.py:40
  218.5 90.3 %all-gather.23.cloned.1.call-start = ((), (), s32[]{:S(2)}) async-start(), calls=%async_computation.44 | async-start | bytes 2228224 | tf_op jit(solution)/shard_map/all_gather | solution.py:288
  219.1 139.7 %all-gather.19.cloned.1.call-start = ((), (), s32[]{:S(2)}) async-start(), calls=%async_computation.42 | async-start | bytes 3145728 | tf_op jit(solution)/shard_map/all_gather | solution.py:41
  245.7 142.2 %all-gather.21.cloned.1.call-start = ((), (), s32[]{:S(2)}) async-start(), calls=%async_computation.43 | async-start | bytes 1310720 | tf_op jit(solution)/shard_map/all_gather | solution.py:289
  246.4 143.4 %reduce-scatter.76.cloned.1.call-start = ((), (), s32[]{:S(2)}) async-start(), calls=%async_computation.74 | async-start | bytes 163840
  312.0 131.5 %all-gather.25.cloned.1.call-start = ((), (), s32[]{:S(2)}) async-start(), calls=%async_computation.45 | async-start | bytes 1310720 | tf_op jit(solution)/shard_map/all_gather | solution.py:290
  312.6 140.9 %all-gather.27.cloned.1.call-start = ((), (), s32[]{:S(2)}) async-start(), calls=%async_computation.46 | async-start | bytes 1310720 | tf_op jit(solution)/shard_map/all_gather | solution.py:291
  314.7 42.7 %all-to-all-start.2 = ((bf16[256,3,512]{0,1,2:T(4,128)(2,1)}), bf16[256,3,512]{0,1,2:T(4,128)(2,1)S(1)}, u32[]{:S(2)}, u32[]{:S(2)}) async-start(bf16[256,3,512]{0,1,2:T(4,128)(2,1)} %copy.720), calls=%async_computation.2 | async-start | bytes 2097152 | tf_op jit(solution)/shard_map/all_to_all | solution.py:35
  318.3 194.8 %all-gather.29.cloned.1.call-start = ((), (), s32[]{:S(2)}) async-start(), calls=%async_computation.47 | async-start | bytes 3932160 | tf_op jit(solution)/shard_map/all_gather | solution.py:292
  318.8 238.7 %all-gather.31.cloned.1.call-start = ((), (), s32[]{:S(2)}) async-start(), calls=%async_computation.48 | async-start | bytes 1310720 | tf_op jit(solution)/shard_map/all_gather | solution.py:293
  389.7 51.5 %collective-permute-start = (bf16[256,1024]{1,0:T(8,128)(2,1)S(1)}, bf16[256,1024]{1,0:T(8,128)(2,1)}, u32[]{:S(2)}, u32[]{:S(2)}) collective-permute-start(bf16[256,1024]{1,0:T(8,128)(2,1)S(1)} %convolution_convert_fusion.15), channel_id=1, source_target_pairs={{0,1},{1,0},{2,3},{3,2},{4,5},{5,4},{6,7},{7,6},{8,9},{9,8},{10,11... | collective-permute-start | bytes 1572872 | tf_op jit(solution)/shard_map/ppermute | solution.py:25
  518.1 15.3 all-to-all-start.4
  522.8 64.9 %all-gather.37.cloned.1.call-start = ((), (), s32[]{:S(2)}) async-start(), calls=%async_computation.53 | async-start | bytes 1310720 | tf_op jit(solution)/shard_map/all_gather | solution.py:40
  561.7 70.2 %all-gather.33.cloned.1.call-start = ((), (), s32[]{:S(2)}) async-start(), calls=%async_computation.49 | async-start | bytes 1310720 | tf_op jit(solution)/shard_map/all_gather | solution.py:40
  566.0 102.5 %all-gather.39.cloned.1.call-start = ((), (), s32[]{:S(2)}) async-start(), calls=%async_computation.54 | async-start | bytes 3145728 | tf_op jit(solution)/shard_map/all_gather | solution.py:41
  587.8 47.1 %all-to-all-start.7 = ((bf16[4,512,256]{2,1,0:T(8,128)(2,1)}), bf16[4,512,256]{2,1,0:T(8,128)(2,1)}, u32[]{:S(2)}, u32[]{:S(2)}) async-start(bf16[4,512,256]{2,1,0:T(8,128)(2,1)} %bitcast.820), calls=%async_computation.7 | async-start | bytes 2097152 | tf_op jit(solution)/shard_map/all_to_all | solution.py:35
  592.1 80.8 %all-gather.35.cloned.1.call-start = ((), (), s32[]{:S(2)}) async-start(), calls=%async_computation.50 | async-start | bytes 3145728 | tf_op jit(solution)/shard_map/all_gather | solution.py:41
  634.9 31.4 %all-to-all-start.6 = ((bf16[256,4,512]{0,2,1:T(8,128)(2,1)}), bf16[256,4,512]{0,2,1:T(8,128)(2,1)}, u32[]{:S(2)}, u32[]{:S(2)}) async-start(bf16[256,4,512]{0,2,1:T(8,128)(2,1)} %bitcast.773), calls=%async_computation.6 | async-start | bytes 2097152 | tf_op jit(solution)/shard_map/all_to_all | solution.py:35
  640.1 51.8 %reduce-scatter.40.cloned.1.call-start = ((), (), s32[]{:S(2)}) async-start(), calls=%async_computation.55 | async-start | bytes 3145728 | tf_op jit(solution)/shard_map/reduce_scatter | solution.py:45
  682.8 22.2 %reduce-scatter.36.cloned.1.call-start = ((), (), s32[]{:S(2)}) async-start(), calls=%async_computation.51 | async-start | bytes 3145728 | tf_op jit(solution)/shard_map/reduce_scatter | solution.py:45
  687.6 47.8 %reduce-scatter.42.cloned.1.call-start = ((), (), s32[]{:S(2)}) async-start(), calls=%async_computation.56 | async-start | bytes 1310720 | tf_op jit(solution)/shard_map/reduce_scatter | solution.py:48
  691.9 71.6 %reduce-scatter.38.cloned.1.call-start = ((), (), s32[]{:S(2)}) async-start(), calls=%async_computation.52 | async-start | bytes 1310720 | tf_op jit(solution)/shard_map/reduce_scatter | solution.py:48
  848.7 47.8 %reduce-scatter.44.cloned.1.call-start = ((), (), s32[]{:S(2)}) async-start(), calls=%async_computation.57 | async-start | bytes 3145728 | tf_op jit(solution)/shard_map/reduce_scatter | solution.py:45
  888.3 38.6 %reduce-scatter.46.cloned.1.call-start = ((), (), s32[]{:S(2)}) async-start(), calls=%async_computation.58 | async-start | bytes 1310720 | tf_op jit(solution)/shard_map/reduce_scatter | solution.py:48
  896.5 147.3 %reduce-scatter.78.cloned.1.call-start = ((), (), s32[]{:S(2)}) async-start(), calls=%async_computation.75 | async-start | bytes 1310720
  1017.5 98.7 %reduce-scatter.80.cloned.1.call-start = ((), (), s32[]{:S(2)}) async-start(), calls=%async_computation.76 | async-start | bytes 557056
  1021.0 171.5 %all-gather.41.cloned.1.call-start = ((), (), s32[]{:S(2)}) async-start(), calls=%async_computation.59 | async-start | bytes 1310720 | tf_op jit(solution)/shard_map/all_gather | solution.py:554
  1052.1 173.0 %reduce-scatter.66.cloned.1.call-start = ((), (), s32[]{:S(2)}) async-start(), calls=%async_computation.69 | async-start | bytes 1310720 | tf_op jit(solution)/shard_map/reduce_scatter | solution.py:67
  1056.1 172.5 %reduce-scatter.68.cloned.1.call-start = ((), (), s32[]{:S(2)}) async-start(), calls=%async_computation.70 | async-start | bytes 1310720 | tf_op jit(solution)/shard_map/reduce_scatter | solution.py:67
  1060.9 231.2 %reduce-scatter.64.cloned.1.call-start = ((), (), s32[]{:S(2)}) async-start(), calls=%async_computation.68 | async-start | bytes 1114112 | tf_op jit(solution)/shard_map/reduce_scatter | solution.py:61
  1062.4 262.1 %reduce-scatter.54.cloned.1.call-start = ((), (), s32[]{:S(2)}) async-start(), calls=%async_computation.63 | async-start | bytes 983040 | tf_op jit(solution)/shard_map/reduce_scatter | solution.py:67
  1066.3 280.1 %reduce-scatter.48.cloned.1.call-start = ((), (), s32[]{:S(2)}) async-start(), calls=%async_computation.60 | async-start | bytes 196608 | tf_op jit(solution)/shard_map/reduce_scatter | solution.py:489
  1178.0 234.1 %reduce-scatter.58.cloned.1.call-start = ((), (), s32[]{:S(2)}) async-start(), calls=%async_computation.65 | async-start | bytes 1114112 | tf_op jit(solution)/shard_map/reduce_scatter | solution.py:61
  1179.7 310.2 %reduce-scatter.60.cloned.1.call-start = ((), (), s32[]{:S(2)}) async-start(), calls=%async_computation.66 | async-start | bytes 1114112 | tf_op jit(solution)/shard_map/reduce_scatter | solution.py:61
  1182.3 385.8 %reduce-scatter.56.cloned.1.call-start = ((), (), s32[]{:S(2)}) async-start(), calls=%async_computation.64 | async-start | bytes 1114112 | tf_op jit(solution)/shard_map/reduce_scatter | solution.py:61
  1183.8 471.6 %reduce-scatter.62.cloned.1.call-start = ((), (), s32[]{:S(2)}) async-start(), calls=%async_computation.67 | async-start | bytes 3342336 | tf_op jit(solution)/shard_map/reduce_scatter | solution.py:61
  1186.7 528.8 %reduce-scatter.52.cloned.1.call-start = ((), (), s32[]{:S(2)}) async-start(), calls=%async_computation.62 | async-start | bytes 5242880 | tf_op jit(solution)/shard_map/reduce_scatter | solution.py:67
  1211.2 628.2 %reduce-scatter.50.cloned.1.call-start = ((), (), s32[]{:S(2)}) async-start(), calls=%async_computation.61 | async-start | bytes 2949120 | tf_op jit(solution)/shard_map/reduce_scatter | solution.py:67
  1225.1 14.6 all-to-all-start.15
  1239.7 14.8 all-to-all-start.16
  1339.8 513.1 %all-to-all-start.12 = ((bf16[2,2,16,16,256]{4,3,1,0,2:T(8,128)(2,1)}), bf16[2,2,16,16,256]{4,3,1,0,2:T(8,128)(2,1)S(1)}, u32[]{:S(2)}, u32[]{:S(2)}) async-start(bf16[2,2,16,16,256]{4,3,1,0,2:T(8,128)(2,1)} %copy.794), calls=%async_computation.18 | async-start | bytes 1048576 | tf_op jit(solution)/shard_map/all_to_all | solution.py:35
  1718.0 138.9 %collective-permute-start.7 = (bf16[9,512,64]{1,2,0:T(8,128)(2,1)}, bf16[9,512,64]{1,2,0:T(8,128)(2,1)}, u32[]{:S(2)}, u32[]{:S(2)}) collective-permute-start(bf16[9,512,64]{1,2,0:T(8,128)(2,1)} %copy.808), channel_id=1, source_target_pairs={{0,0},{2,8},{4,16},{6,24},{8,2},{10,10},{12,18},{14,26},{16,4},{18... | collective-permute-start | bytes 1769480 | tf_op jit(solution)/shard_map/ppermute | solution.py:76
  1839.4 27.5 %collective-permute-start.6 = (bf16[9,64,512]{2,1,0:T(8,128)(2,1)}, bf16[9,64,512]{2,1,0:T(8,128)(2,1)}, u32[]{:S(2)}, u32[]{:S(2)}) collective-permute-start(bf16[9,64,512]{2,1,0:T(8,128)(2,1)} %reduce-scatter.50.cloned.1.call-done), channel_id=1, source_target_pairs={{0,0},{2,8},{4,16},{6,24},{8,2},{10,10},{12,18},{14,26},{16,4},{18... | collective-permute-start | bytes 1769480 | tf_op jit(solution)/shard_map/ppermute | solution.py:76
  (162 other events, 2438.2 us)
Sparse Core Ops, SparseCore 0:
  29.2 21.0 reduce-scatter.71
  88.9 26.5 reduce-scatter.69
  124.0 27.8 all-gather.14
  175.6 7.4 reduce-scatter.73
  218.6 26.9 all-gather.16
  248.7 60.1 all-gather.22
  310.5 9.4 all-gather.18
  321.6 39.3 all-gather.20
  363.8 19.0 reduce-scatter.75
  384.4 32.0 all-gather.24
  418.0 31.8 all-gather.26
  451.3 61.7 all-gather.28
  514.7 27.8 all-gather.30
  561.9 25.8 all-gather.36
  589.7 42.1 all-gather.32
  633.3 13.0 all-gather.38
  647.8 11.7 all-gather.34
  683.0 8.9 reduce-scatter.39
  694.2 10.7 reduce-scatter.35
  707.2 28.0 reduce-scatter.41
  737.7 25.7 reduce-scatter.37
  888.5 7.9 reduce-scatter.43
  898.9 28.0 reduce-scatter.45
  1017.6 26.1 reduce-scatter.77
  1046.7 69.4 reduce-scatter.79
  1118.2 36.7 all-gather.40
  1157.7 27.4 reduce-scatter.65
  1188.4 27.7 reduce-scatter.67
  1218.4 73.5 reduce-scatter.63
  1295.0 29.4 reduce-scatter.53
  1327.4 7.7 reduce-scatter.47
  1337.6 74.5 reduce-scatter.57
  1414.2 75.6 reduce-scatter.59
  1492.8 75.1 reduce-scatter.55
  1570.4 84.9 reduce-scatter.61
  1658.2 57.2 reduce-scatter.51
  1718.7 60.2 reduce-scatter.49

commit v2 on v1

--- a/solution.py
+++ b/solution.py
@@ -3,6 +3,8 @@
 import jax
 import jax.numpy as jnp
 from jax import lax
+from jax.experimental import pallas as pl
+from jax.experimental.pallas import tpu as pltpu
 from jax.sharding import PartitionSpec as P
 
 D = 1024
@@ -35,45 +37,533 @@
     return lax.all_to_all(source, "space", split_axis=split, concat_axis=concat, tiled=True)
 
 
-def gather_tokens(rows):
-    half = part_of(rows, "mp", 1)
-    line = lax.all_gather(half, "space", axis=0, tiled=True)
-    return lax.all_gather(line, "mp", axis=1, tiled=True)
-
-
-def scatter_tokens(partial_sum):
-    half = lax.psum_scatter(
-        partial_sum.astype(jnp.bfloat16), "mp", scatter_dimension=1, tiled=True
-    )
-    line = lax.psum_scatter(half, "space", scatter_dimension=0, tiled=True)
-    return lax.all_gather(line, "mp", axis=1, tiled=True).astype(jnp.float32)
-
-
-def to_clips(source):
-    return lax.all_to_all(source, "tm", split_axis=2, concat_axis=1, tiled=True)
-
-
-def from_clips(source):
-    return lax.all_to_all(source, "tm", split_axis=1, concat_axis=2, tiled=True)
-
-
-def sum_to_owner(weight_grad, dim):
-    return lax.psum_scatter(
-        weight_grad.astype(jnp.bfloat16), ("tm", "space"), scatter_dimension=dim, tiled=True
-    ).astype(jnp.float32)
-
-
-def sum_over_frames(weight_grad, dim):
-    return lax.psum_scatter(
-        weight_grad.astype(jnp.bfloat16), "tm", scatter_dimension=dim, tiled=True
-    )
-
-
-def stationary_to_owner(weight_grad, dim):
-    portion = sum_over_frames(weight_grad, dim)
+MESH = pl.DeviceIdType.MESH
+lane = 128
+ANY = pl.BlockSpec(memory_space=pl.ANY)
+VMEM = pl.BlockSpec(memory_space=pltpu.VMEM)
+
+
+def meet(peers):
+    gate = pltpu.get_barrier_semaphore()
+    for peer in peers:
+        pl.semaphore_signal(gate, inc=1, device_id=peer, device_id_type=MESH)
+    pl.semaphore_wait(gate, len(peers))
+
+
+def others(axis_name):
+    count = lax.axis_size(axis_name)
+    me = lax.axis_index(axis_name)
+    return [(step, lax.rem(me + step, count)) for step in range(1, count)]
+
+
+def send(source, target, send_sem, recv_sem, peer):
+    copy = pltpu.make_async_remote_copy(
+        src_ref=source,
+        dst_ref=target,
+        send_sem=send_sem,
+        recv_sem=recv_sem,
+        device_id=peer,
+        device_id_type=MESH,
+    )
+    copy.start()
+    return copy
+
+
+def keep(source, target, sem):
+    copy = pltpu.make_async_copy(source, target, sem)
+    copy.start()
+    return copy
+
+
+def cols_of(ref, index, width):
+    return ref.at[:, :, pl.ds(pl.multiple_of(index * width, width), width)]
+
+
+def rows_of(ref, index, width):
+    return ref.at[:, pl.ds(pl.multiple_of(index * width, width), width), :]
+
+
+def talk(kernel, result, operands, scratch, number, specs=None, out_spec=ANY):
+    return pl.pallas_call(
+        kernel,
+        out_shape=result,
+        in_specs=[ANY] * len(operands) if specs is None else specs,
+        out_specs=out_spec,
+        scratch_shapes=scratch,
+        compiler_params=pltpu.CompilerParams(
+            collective_id=number, has_side_effects=True, vmem_limit_bytes=48 * 1024 * 1024
+        ),
+    )(*operands)
+
+
+def dma_sems(*counts):
+    return [pltpu.SemaphoreType.DMA((max(count, 1),)) for count in counts]
+
+
+def flat_index(axes):
+    index = 0
+    for name in axes:
+        index = index * lax.axis_size(name) + lax.axis_index(name)
+    return index
+
+
+def flat_peers(axes):
+    count = math.prod(lax.axis_size(name) for name in axes)
+    me = flat_index(axes)
+    peers = []
+    for step in range(1, count):
+        peer = lax.rem(me + step, count)
+        place, rest = {}, peer
+        for name in reversed(axes):
+            place[name] = lax.rem(rest, lax.axis_size(name))
+            rest = rest // lax.axis_size(name)
+        peers.append((step, peer, place))
+    return peers
+
+
+def exchange(source, axes, number):
+    count = source.shape[0]
+
+    def kernel(x_ref, out_ref, send_sem, recv_sem, own_sem):
+        me = flat_index(axes)
+        peers = flat_peers(axes)
+        meet([place for _, _, place in peers])
+        copies = [
+            send(x_ref.at[peer], out_ref.at[me], send_sem.at[i - 1], recv_sem.at[i - 1], place)
+            for i, peer, place in peers
+        ]
+        copies.append(keep(x_ref.at[me], out_ref.at[me], own_sem.at[0]))
+        for copy in copies:
+            copy.wait()
+
+    result = jax.ShapeDtypeStruct(source.shape, source.dtype)
+    return talk(kernel, result, [source], dma_sems(count - 1, count - 1, 1), number)
+
+
+def share(source, axes, number):
+    count = math.prod(lax.axis_size(name) for name in axes)
+
+    def kernel(x_ref, out_ref, send_sem, recv_sem, own_sem):
+        me = flat_index(axes)
+        peers = flat_peers(axes)
+        meet([place for _, _, place in peers])
+        copies = [
+            send(x_ref, out_ref.at[me], send_sem.at[i - 1], recv_sem.at[i - 1], place)
+            for i, _, place in peers
+        ]
+        copies.append(keep(x_ref, out_ref.at[me], own_sem.at[0]))
+        for copy in copies:
+            copy.wait()
+
+    result = jax.ShapeDtypeStruct((count,) + source.shape, source.dtype)
+    return talk(kernel, result, [source], dma_sems(count - 1, count - 1, 1), number)
+
+
+class FrameSum:
+    def __init__(self, source):
+        self.count, self.rows, self.width = source.shape
+        self.source = source
+        self.result = jax.ShapeDtypeStruct((self.rows, self.width), jnp.bfloat16)
+        self.scratch = [
+            pltpu.VMEM((max(self.count - 1, 1), self.rows, self.width), jnp.bfloat16),
+            pltpu.VMEM((self.rows, self.width), jnp.bfloat16),
+        ] + dma_sems(self.count - 1, self.count - 1, 1)
+
+    def peers(self):
+        return [{"tm": peer} for _, peer in others("tm")]
+
+    def start(self, w_ref, got_ref, own_ref, send_sem, recv_sem, own_sem):
+        me = lax.axis_index("tm")
+        self.copies = [
+            send(w_ref.at[peer], got_ref.at[i - 1], send_sem.at[i - 1], recv_sem.at[i - 1], {"tm": peer})
+            for i, peer in others("tm")
+        ]
+        self.copies.append(keep(w_ref.at[me], own_ref, own_sem.at[0]))
+
+    def finish(self, out_ref, got_ref, own_ref):
+        for copy in self.copies:
+            copy.wait()
+        block = min(16, self.rows)
+
+        def some(index, carry):
+            rows = pl.ds(pl.multiple_of(index * block, block), block)
+            total = own_ref[rows, :].astype(jnp.float32)
+            for step in range(self.count - 1):
+                total = total + got_ref[step, rows, :].astype(jnp.float32)
+            out_ref[rows, :] = total.astype(jnp.bfloat16)
+            return carry
+
+        lax.fori_loop(0, self.rows // block, some, 0)
+
+
+def talk_with(kernel, peers, result, operands, scratch, number, extra, specs=None, out_spec=ANY):
+    specs = [ANY] * len(operands) if specs is None else specs
+    if extra is None:
+
+        def alone(*refs):
+            meet(peers())
+            kernel(*refs)
+
+        return talk(alone, result, operands, scratch, number, specs, out_spec), None
+    inputs, own_scratch = len(operands), len(scratch)
+
+    def both(*refs):
+        ins, w_ref = refs[:inputs], refs[inputs]
+        out_ref, sum_ref = refs[inputs + 1 : inputs + 3]
+        rest = refs[inputs + 3 :]
+        mine, theirs = rest[:own_scratch], rest[own_scratch:]
+        meet(peers() + extra.peers())
+        extra.start(w_ref, *theirs)
+        kernel(*ins, out_ref, *mine)
+        extra.finish(sum_ref, theirs[0], theirs[1])
+
+    return talk(
+        both,
+        (result, extra.result),
+        operands + [extra.source],
+        scratch + extra.scratch,
+        number,
+        specs + [ANY],
+        (out_spec, VMEM),
+    )
+
+
+def line_peers():
+    return [{"space": peer} for _, peer in others("space")]
+
+
+def to_lines(source, per_core, number):
+    images, pixels, channels = source.shape
+    lines, cores = lax.axis_size("space"), lax.axis_size("mp")
+    pieces = lines * cores if per_core else lines
+    width = channels // pieces
+    if width % lane != 0 or pixels % 16 != 0:
+        if per_core:
+            parts = source.reshape(images, pixels, lines, cores, width)
+            parts = lax.dynamic_index_in_dim(parts, lax.axis_index("mp"), 3, keepdims=False)
+            source = parts.reshape(images, pixels, lines * width)
+        return lax.all_to_all(source, "space", split_axis=2, concat_axis=1, tiled=True)
+
+    def kernel(x_ref, out_ref, send_sem, recv_sem, own_sem):
+        me, core = lax.axis_index("space"), lax.axis_index("mp")
+        place = (lambda s: s * cores + core) if per_core else (lambda s: s)
+        meet([{"space": peer} for _, peer in others("space")])
+        target = rows_of(out_ref, me, pixels)
+        copies = [
+            send(cols_of(x_ref, place(peer), width), target, send_sem.at[i - 1], recv_sem.at[i - 1], {"space": peer})
+            for i, peer in others("space")
+        ]
+        copies.append(keep(cols_of(x_ref, place(me), width), target, own_sem.at[0]))
+        for copy in copies:
+            copy.wait()
+
+    result = jax.ShapeDtypeStruct((images, lines * pixels, width), source.dtype)
+    return talk(kernel, result, [source], dma_sems(lines - 1, lines - 1, 1), number)
+
+
+def plain_sum(extra):
+    if extra is None:
+        return None
+    return lax.psum_scatter(extra.source, "tm", scatter_dimension=0, tiled=True)[0]
+
+
+def from_lines(source, per_core, number, extra=None):
+    images, line_pixels, width = source.shape
+    lines, cores = lax.axis_size("space"), lax.axis_size("mp")
+    pixels = line_pixels // lines
+    pieces = lines * cores if per_core else lines
+    if width % lane != 0 or pixels % 16 != 0:
+        part = lax.all_to_all(source, "space", split_axis=1, concat_axis=2, tiled=True)
+        if per_core:
+            part = part.reshape(images, pixels, lines, 1, width)
+            part = lax.all_gather(part, "mp", axis=3, tiled=True)
+        return part.reshape(images, pixels, pieces * width), plain_sum(extra)
+
+    def kernel(x_ref, out_ref, send_sem, recv_sem, pass_sem, gain_sem, own_sem):
+        me, core = lax.axis_index("space"), lax.axis_index("mp")
+        place = (lambda s: s * cores + core) if per_core else (lambda s: s)
+        twin = {"mp": 1 - core}
+        target = cols_of(out_ref, place(me), width)
+        copies = [
+            send(rows_of(x_ref, peer, pixels), target, send_sem.at[i - 1], recv_sem.at[i - 1], {"space": peer})
+            for i, peer in others("space")
+        ]
+        own = keep(rows_of(x_ref, me, pixels), target, own_sem.at[0])
+        passed = []
+        if per_core:
+            passed.append(send(rows_of(x_ref, me, pixels), target, pass_sem.at[0], gain_sem.at[0], twin))
+        for step in range(1, lines):
+            copies[step - 1].wait_recv()
+            if per_core:
+                origin = lax.rem(me - step + lines, lines)
+                got = cols_of(out_ref, place(origin), width)
+                passed.append(send(got, got, pass_sem.at[step], gain_sem.at[step], twin))
+        for copy in copies:
+            copy.wait_send()
+        own.wait()
+        for copy in passed:
+            copy.wait()
+
+    def peers():
+        return line_peers() + ([{"mp": 1 - lax.axis_index("mp")}] if per_core else [])
+
+    result = jax.ShapeDtypeStruct((images, pixels, pieces * width), source.dtype)
+    sems = dma_sems(lines - 1, lines - 1, lines, lines, 1)
+    return talk_with(kernel, peers, result, [source], sems, number, extra)
+
+
+def gather_lines(source, number, extra=None):
+    images, line_pixels, width = source.shape
+    lines = lax.axis_size("space")
+    if width % lane != 0:
+        return lax.all_gather(source, "space", axis=2, tiled=True), plain_sum(extra)
+
+    def kernel(x_ref, out_ref, send_sem, recv_sem, own_sem):
+        me = lax.axis_index("space")
+        target = cols_of(out_ref, me, width)
+        copies = [
+            send(x_ref, target, send_sem.at[i - 1], recv_sem.at[i - 1], {"space": peer})
+            for i, peer in others("space")
+        ]
+        copies.append(keep(x_ref, target, own_sem.at[0]))
+        for copy in copies:
+            copy.wait()
+
+    result = jax.ShapeDtypeStruct((images, line_pixels, lines * width), source.dtype)
+    sems = dma_sems(lines - 1, lines - 1, 1)
+    return talk_with(kernel, line_peers, result, [source], sems, number, extra)
+
+
+def gather_cores(source, number):
+    images, line_pixels, width = source.shape
+    cores = lax.axis_size("mp")
+    if width % lane != 0:
+        return lax.all_gather(source, "mp", axis=2, tiled=True)
+
+    def kernel(x_ref, out_ref, send_sem, recv_sem, own_sem):
+        core = lax.axis_index("mp")
+        twin = {"mp": 1 - core}
+        meet([twin])
+        target = cols_of(out_ref, core, width)
+        copy = send(x_ref, target, send_sem.at[0], recv_sem.at[0], twin)
+        own = keep(x_ref, target, own_sem.at[0])
+        copy.wait()
+        own.wait()
+
+    result = jax.ShapeDtypeStruct((images, line_pixels, cores * width), source.dtype)
+    return talk(kernel, result, [source], dma_sems(1, 1, 1), number)
+
+
+def sum_lines(source, number, extra=None):
+    images, line_pixels, channels = source.shape
+    lines = lax.axis_size("space")
+    width = channels // lines
+    if width % lane != 0:
+        total = lax.psum_scatter(source, "space", scatter_dimension=2, tiled=True)
+        return total.astype(jnp.float32), plain_sum(extra)
+
+    def kernel(x_ref, out_ref, got_ref, send_sem, recv_sem):
+        me = lax.axis_index("space")
+        copies = [
+            send(cols_of(x_ref, peer, width), got_ref.at[i - 1], send_sem.at[i - 1], recv_sem.at[i - 1], {"space": peer})
+            for i, peer in others("space")
+        ]
+        mine = pl.ds(pl.multiple_of(me * width, width), width)
+        for copy in copies:
+            copy.wait()
+        for image in range(images):
+            total = x_ref[image, :, mine].astype(jnp.float32)
+            for step in range(lines - 1):
+                total = total + got_ref[step, image].astype(jnp.float32)
+            out_ref[image] = total
+
+    result = jax.ShapeDtypeStruct((images, line_pixels, width), jnp.float32)
+    scratch = [pltpu.VMEM((lines - 1, images, line_pixels, width), source.dtype)]
+    scratch = scratch + dma_sems(lines - 1, lines - 1)
+    return talk_with(
+        kernel, line_peers, result, [source], scratch, number, extra, [VMEM], VMEM
+    )
+
+
+def sum_cores(source, number):
+    images, line_pixels, channels = source.shape
+    cores = lax.axis_size("mp")
+    width = channels // cores
+    if width % lane != 0:
+        return lax.psum_scatter(source, "mp", scatter_dimension=2, tiled=True).astype(jnp.float32)
+
+    def kernel(x_ref, out_ref, got_ref, send_sem, recv_sem):
+        core = lax.axis_index("mp")
+        twin = {"mp": 1 - core}
+        meet([twin])
+        copy = send(cols_of(x_ref, 1 - core, width), got_ref, send_sem.at[0], recv_sem.at[0], twin)
+        mine = pl.ds(pl.multiple_of(core * width, width), width)
+        copy.wait()
+        for image in range(images):
+            out_ref[image] = x_ref[image, :, mine].astype(jnp.float32) + got_ref[image].astype(
+                jnp.float32
+            )
+
+    result = jax.ShapeDtypeStruct((images, line_pixels, width), jnp.float32)
+    scratch = [pltpu.VMEM((images, line_pixels, width), source.dtype)]
+    return talk(kernel, result, [source], scratch + dma_sems(1, 1), number, [VMEM], VMEM)
+
+
+def gather_tokens(rows, number):
+    count, channels = rows.shape
+    lines, cores = lax.axis_size("space"), lax.axis_size("mp")
+    width = channels // cores
+    source = rows.reshape(1, count, channels)
+
+    def kernel(x_ref, out_ref, send_sem, recv_sem, pass_sem, gain_sem, own_sem):
+        me, core = lax.axis_index("space"), lax.axis_index("mp")
+        twin = {"mp": 1 - core}
+        meet([{"space": peer} for _, peer in others("space")] + [twin])
+
+        def spot(origin):
+            return cols_of(rows_of(out_ref, origin, count), core, width)
+
+        copies = [
+            send(cols_of(x_ref, core, width), spot(me), send_sem.at[i - 1], recv_sem.at[i - 1], {"space": peer})
+            for i, peer in others("space")
+        ]
+        own = keep(x_ref, rows_of(out_ref, me, count), own_sem.at[0])
+        passed = []
+        for step in range(1, lines):
+            copies[step - 1].wait_recv()
+            got = spot(lax.rem(me - step + lines, lines))
+            passed.append(send(got, got, pass_sem.at[step - 1], gain_sem.at[step - 1], twin))
+        for copy in copies:
+            copy.wait_send()
+        own.wait()
+        for copy in passed:
+            copy.wait()
+
+    result = jax.ShapeDtypeStruct((1, lines * count, channels), rows.dtype)
+    sems = dma_sems(lines - 1, lines - 1, lines - 1, lines - 1, 1)
+    return talk(kernel, result, [source], sems, number).reshape(lines * count, channels)
+
+
+def scatter_tokens(partial_sum, number, extra=None):
+    all_rows, channels = partial_sum.shape
+    lines, cores = lax.axis_size("space"), lax.axis_size("mp")
+    count, width = all_rows // lines, channels // cores
+    source = partial_sum.astype(jnp.bfloat16).reshape(lines, count, channels)
+
+    def kernel(x_ref, out_ref, twin_ref, sum_ref, got_ref, s_sem, r_sem, s2_sem, r2_sem, s3_sem, r3_sem):
+        me, core = lax.axis_index("space"), lax.axis_index("mp")
+        twin = {"mp": 1 - core}
+        theirs = pl.ds(pl.multiple_of((1 - core) * width, width), width)
+        mine = pl.ds(pl.multiple_of(core * width, width), width)
+        order = [(i, peer) for i, peer in others("space")] + [(0, me)]
+        first = [
+            send(x_ref.at[target, :, theirs], twin_ref.at[i], s_sem.at[i], r_sem.at[i], twin)
+            for i, target in order
+        ]
+        second = []
+        for (i, target), copy in zip(order, first):
+            copy.wait_recv()
+            total = x_ref[target, :, mine].astype(jnp.float32) + twin_ref[i].astype(jnp.float32)
+            if i == 0:
+                own = total
+            else:
+                sum_ref[i - 1] = total.astype(jnp.bfloat16)
+                second.append(
+                    send(sum_ref.at[i - 1], got_ref.at[i - 1], s2_sem.at[i - 1], r2_sem.at[i - 1], {"space": target})
+                )
+        for copy in second:
+            copy.wait_recv()
+        for i in range(lines - 1):
+            own = own + got_ref[i].astype(jnp.float32)
+        out_ref[:, mine] = own.astype(jnp.bfloat16)
+        third = send(out_ref.at[:, mine], out_ref.at[:, mine], s3_sem.at[0], r3_sem.at[0], twin)
+        for copy in first + second:
+            copy.wait_send()
+        third.wait()
+
+    result = jax.ShapeDtypeStruct((count, channels), jnp.bfloat16)
+    scratch = [
+        pltpu.VMEM((lines, count, width), jnp.bfloat16),
+        pltpu.VMEM((max(lines - 1, 1), count, width), jnp.bfloat16),
+        pltpu.VMEM((max(lines - 1, 1), count, width), jnp.bfloat16),
+    ]
+    sems = dma_sems(lines, lines, lines - 1, lines - 1, 1, 1)
+
+    def peers():
+        return line_peers() + [{"mp": 1 - lax.axis_index("mp")}]
+
+    total, other = talk_with(
+        kernel, peers, result, [source], scratch + sems, number, extra, [VMEM], VMEM
+    )
+    return total.astype(jnp.float32), other
+
+
+def to_clips(source, number):
+    slots, frames, pixels, channels = source.shape
+    count = lax.axis_size("tm")
+    few = pixels // count
+    if few % 16 != 0:
+        return lax.all_to_all(source, "tm", split_axis=2, concat_axis=1, tiled=True)
+
+    def kernel(x_ref, out_ref, send_sem, recv_sem, own_sem):
+        me = lax.axis_index("tm")
+        meet([{"tm": peer} for _, peer in others("tm")])
+        target = out_ref.at[:, pl.ds(me * frames, frames)]
+
+        def part(index):
+            return x_ref.at[:, :, pl.ds(pl.multiple_of(index * few, few), few)]
+
+        copies = [
+            send(part(peer), target, send_sem.at[i - 1], recv_sem.at[i - 1], {"tm": peer})
+            for i, peer in others("tm")
+        ]
+        copies.append(keep(part(me), target, own_sem.at[0]))
+        for copy in copies:
+            copy.wait()
+
+    result = jax.ShapeDtypeStruct((slots, count * frames, few, channels), source.dtype)
+    return talk(kernel, result, [source], dma_sems(count - 1, count - 1, 1), number)
+
+
+def from_clips(source, number):
+    slots, all_frames, few, channels = source.shape
+    count = lax.axis_size("tm")
+    frames = all_frames // count
+    if few % 16 != 0:
+        return lax.all_to_all(source, "tm", split_axis=1, concat_axis=2, tiled=True)
+
+    def kernel(x_ref, out_ref, send_sem, recv_sem, own_sem):
+        me = lax.axis_index("tm")
+        meet([{"tm": peer} for _, peer in others("tm")])
+        target = out_ref.at[:, :, pl.ds(pl.multiple_of(me * few, few), few)]
+
+        def part(index):
+            return x_ref.at[:, pl.ds(index * frames, frames)]
+
+        copies = [
+            send(part(peer), target, send_sem.at[i - 1], recv_sem.at[i - 1], {"tm": peer})
+            for i, peer in others("tm")
+        ]
+        copies.append(keep(part(me), target, own_sem.at[0]))
+        for copy in copies:
+            copy.wait()
+
+    result = jax.ShapeDtypeStruct((slots, frames, count * few, channels), source.dtype)
+    return talk(kernel, result, [source], dma_sems(count - 1, count - 1, 1), number)
+
+
+def sum_to_owner(weight_grad):
+    return lax.psum_scatter(weight_grad, ("tm", "space"), scatter_dimension=0, tiled=True)
+
+
+def by_frames(weight_grad):
+    return FrameSum(weight_grad.reshape(lax.axis_size("tm"), -1, weight_grad.shape[1]))
+
+
+def to_owner(portion):
     frames, lines = lax.axis_size("tm"), lax.axis_size("space")
     moves = [(t * lines + s, s * frames + t) for t in range(frames) for s in range(lines)]
-    return lax.ppermute(portion, ("tm", "space"), moves).astype(jnp.float32)
+    return lax.ppermute(portion, ("tm", "space"), moves)
 
 
 def padded_rims(source):
@@ -100,7 +590,7 @@
     return result.reshape(source.shape[:4] + (result.shape[-1],))
 
 
-def conv_weight_grad(source, upstream):
+def conv_weight_grad(source, upstream, form):
     padded = padded_rims(source)
     rows, cols = source.shape[2], source.shape[3]
     tap_list = []
@@ -108,13 +598,13 @@
         i, j = tap // 3, tap % 3
         tap_list.append(
             jnp.einsum(
-                "bfhwc,bfhwk->ck",
+                "bfhwc,bfhwk->" + form,
                 padded[:, :, i : i + rows, j : j + cols],
                 upstream,
                 preferred_element_type=jnp.float32,
             ).astype(jnp.bfloat16)
         )
-    return jnp.stack(tap_list, axis=0)
+    return jnp.concatenate(tap_list, axis=1)
 
 
 def grouped_view(source):
@@ -284,28 +774,42 @@
     text_local = text.shape[1]
     pixel_form = ("nqhe", "nkhe", "nhqk")
     frame_form = ("bfphe", "bgphe", "bphfg")
-    video_lines = space_to_all(video, 4, 2)
-    text_all = lax.all_gather(text, ("tm", "space"), axis=1, tiled=True)
-    spatial_out = lax.all_gather(spatial_out, "space", axis=1, tiled=True)
-    cross_query = lax.all_gather(cross_query, "space", axis=0, tiled=True)
-    cross_out = lax.all_gather(cross_out, "space", axis=1, tiled=True)
-    temporal_qkv = lax.all_gather(temporal_qkv, "space", axis=0, tiled=True)
-    temporal_out = lax.all_gather(temporal_out, "space", axis=1, tiled=True)
+    images = slots * frame_dev
+    core_shape = (slots, frame_dev, H, W, -1)
+    video_lines = to_lines(video.reshape(images, pixels_dev, channels), True, 1).reshape(core_shape)
+    everyone = ("tm", "space")
+    owners = frames_axis * lines
+    out_piece = part_of(jnp.concatenate([spatial_out, cross_out, temporal_out], axis=1), "tm", 0)
+    out_all = lax.all_gather(out_piece, everyone, axis=0, tiled=False)
+    out_all = out_all.reshape(frames_axis, lines, -1, 3, channels // lines)
+    out_all = out_all.transpose(3, 0, 2, 1, 4).reshape(3, half_width, channels)
+    spatial_out, cross_out, temporal_out = out_all[0], out_all[1], out_all[2]
+    in_piece = jnp.concatenate([cross_query, temporal_qkv.reshape(-1, 3 * half_width)], axis=1)
+    in_all = lax.all_gather(part_of(in_piece, "tm", 1), everyone, axis=0, tiled=False)
+    in_all = in_all.reshape(frames_axis, channels, -1)
+    if in_all.shape[2] == half_width:
+        cross_query, temporal_qkv = in_all[0], in_all[1:]
+    else:
+        in_all = in_all.transpose(1, 0, 2).reshape(channels, 4, half_width).transpose(1, 0, 2)
+        cross_query, temporal_qkv = in_all[0], in_all[1:]
+    text_rows = slots * text_local
+    text_flat = text.reshape(text_rows, -1)
+    text_width = text_flat.shape[1]
     spatial_qkv = space_to_all(spatial_qkv, 2, 0)
     feed_in = space_to_all(feed_in, 1, 0)
     feed_out = space_to_all(feed_out, 0, 1)
     cot_rows = cotangent.reshape(token_rows, channels)
-    cot_line = gather_tokens(cot_rows)
-
-    gain_line = part_of(group_gain, "space", 0)
-    bias_line = part_of(group_bias, "space", 0)
+    cot_line = gather_tokens(cot_rows, 2)
+
+    gain_line = part_of(part_of(group_gain, "space", 0), "mp", 0)
+    bias_line = part_of(part_of(group_bias, "space", 0), "mp", 0)
     normal_one, inverse_one = group_forward(video_lines.astype(jnp.float32))
     affine_one = normal_one * gain_line + bias_line
     first_in = jax.nn.silu(affine_one).astype(jnp.bfloat16)
+    first_in = gather_cores(first_in.reshape(images, H * W, -1), 3).reshape(core_shape)
     hidden_part = conv_frames(first_in, first_conv, "IHWO", False)
-    hidden = lax.psum_scatter(
-        hidden_part.astype(jnp.bfloat16), "space", scatter_dimension=4, tiled=True
-    ).astype(jnp.float32)
+    hidden = sum_lines(hidden_part.astype(jnp.bfloat16).reshape(images, H * W, half_width), 4)
+    hidden = hidden[0].reshape(core_shape)
     normal_two, inverse_two = group_forward(hidden)
     embed = sinusoid(timesteps).astype(jnp.bfloat16)
     film_part = jnp.einsum(
@@ -321,19 +825,17 @@
         normal_two * (1.0 + frame_film[:, :, None, None, 0]) + frame_film[:, :, None, None, 1]
     )
     second_in = jax.nn.silu(modulated).astype(jnp.bfloat16)
-    second_wide = lax.all_gather(second_in, "space", axis=4, tiled=True)
+    second_wide = gather_lines(second_in.reshape(images, H * W, -1), 5)[0].reshape(core_shape)
     conv_part = conv_frames(second_wide, second_conv, "IHWO", False)
-    conv_half = lax.psum_scatter(
-        conv_part.astype(jnp.bfloat16), "mp", scatter_dimension=4, tiled=True
-    )
-    conv_rows = space_to_all(conv_half, 2, 4).reshape(token_rows, lines, -1)
-    conv_rows = lax.all_gather(conv_rows, "mp", axis=2, tiled=True).reshape(token_rows, channels)
+    conv_half = sum_cores(conv_part.astype(jnp.bfloat16).reshape(images, H * W, -1), 6)
+    conv_rows = from_lines(conv_half.astype(jnp.bfloat16), True, 7)[0]
+    conv_rows = conv_rows.reshape(token_rows, channels)
     stream_one = video.astype(jnp.float32).reshape(token_rows, channels) + conv_rows.astype(
         jnp.float32
     )
 
     spatial_in = layer_norm(stream_one, spatial_norm).astype(jnp.bfloat16)
-    spatial_line = gather_tokens(spatial_in)
+    spatial_line = gather_tokens(spatial_in, 8)
     head_line = spatial_qkv.shape[2] // HDIM
     spatial_triple = (
         jnp.einsum("rd,djk->rjk", spatial_line, spatial_qkv, preferred_element_type=jnp.float32)
@@ -346,9 +848,9 @@
     spatial_mix, spatial_total = attend_forward(
         spatial_query, spatial_key, spatial_value, pixel_form, None, None
     )
-    spatial_mix = space_to_all(
-        spatial_mix.reshape(slots * frame_dev, H * W, head_line * HDIM), 1, 2
-    ).reshape(token_rows, half_width)
+    spatial_mix = from_lines(
+        spatial_mix.reshape(slots * frame_dev, H * W, head_line * HDIM), False, 9
+    )[0].reshape(token_rows, half_width)
     stream_two = stream_one + mp_sum(
         jnp.dot(spatial_mix, spatial_out, preferred_element_type=jnp.float32)
     )
@@ -356,16 +858,20 @@
     cross_rows = jnp.dot(cross_in, cross_query, preferred_element_type=jnp.float32).astype(
         jnp.bfloat16
     )
-    text_some = part_of(part_of(text_all, "tm", 1), "space", 2)
-    text_pairs = lax.psum_scatter(
-        jnp.einsum("btc,cjk->btjk", text_some, cross_kv, preferred_element_type=jnp.float32).astype(
-            jnp.bfloat16
-        ),
-        "space",
-        scatter_dimension=1,
-        tiled=True,
-    )
-    text_pairs = lax.all_gather(text_pairs, ("tm", "space"), axis=1, tiled=True)
+    text_line = to_lines(text_flat[None], False, 24)[0]
+    text_part = jnp.dot(
+        text_line, cross_kv.reshape(cross_kv.shape[0], -1), preferred_element_type=jnp.float32
+    )
+    text_part = exchange(
+        text_part.astype(jnp.bfloat16).reshape(lines, text_rows, -1), ("space",), 25
+    )
+    text_part = jnp.sum(text_part.astype(jnp.float32), axis=0).astype(jnp.bfloat16)
+    text_pairs = (
+        share(text_part, everyone, 26)
+        .reshape(owners, slots, text_local, 2, half_width)
+        .transpose(1, 0, 2, 3, 4)
+        .reshape(slots, TXT, 2, half_width)
+    )
     cross_queries = cross_rows.reshape(slots, frame_dev * pixels_dev, head_local, HDIM)
     text_key = text_pairs[:, :, 0].reshape(slots, TXT, head_local, HDIM)
     text_value = text_pairs[:, :, 1].reshape(slots, TXT, head_local, HDIM)
@@ -381,12 +887,13 @@
     )
     temporal_in = layer_norm(stream_three, temporal_norm).astype(jnp.bfloat16)
     temporal_triple = (
-        jnp.einsum("rd,djk->rjk", temporal_in, temporal_qkv, preferred_element_type=jnp.float32)
+        jnp.einsum("rd,jdk->rjk", temporal_in, temporal_qkv, preferred_element_type=jnp.float32)
         .astype(jnp.bfloat16)
         .reshape(slots, frame_dev, pixels_dev, 3, half_width)
     )
-    clip_triple = to_clips(temporal_triple)
+    clip_triple = to_clips(temporal_triple.reshape(slots, frame_dev, pixels_dev, 3 * half_width), 10)
     clip_pixels = clip_triple.shape[2]
+    clip_triple = clip_triple.reshape(slots, frames_all, clip_pixels, 3, half_width)
     clip_query = clip_triple[:, :, :, 0].reshape(slots, frames_all, clip_pixels, head_local, HDIM)
     clip_key = clip_triple[:, :, :, 1].reshape(slots, frames_all, clip_pixels, head_local, HDIM)
     clip_value = clip_triple[:, :, :, 2].reshape(slots, frames_all, clip_pixels, head_local, HDIM)
@@ -396,41 +903,44 @@
     clip_mix, clip_total = attend_forward(
         clip_query, clip_key, clip_value, frame_form, clip_bias, clip_valid
     )
-    temporal_mix = from_clips(clip_mix.reshape(slots, frames_all, clip_pixels, half_width))
+    temporal_mix = from_clips(clip_mix.reshape(slots, frames_all, clip_pixels, half_width), 11)
     temporal_mix = temporal_mix.reshape(token_rows, half_width)
     stream_four = stream_three + mp_sum(
         jnp.dot(temporal_mix, temporal_out, preferred_element_type=jnp.float32)
     )
     feed_rows = layer_norm(stream_four, feed_norm).astype(jnp.bfloat16)
-    feed_line = gather_tokens(feed_rows)
+    feed_line = gather_tokens(feed_rows, 12)
     upper = jnp.dot(feed_line, feed_in, preferred_element_type=jnp.float32)
     active = jax.nn.gelu(upper).astype(jnp.bfloat16)
     final = stream_four + scatter_tokens(
-        jnp.dot(active, feed_out, preferred_element_type=jnp.float32)
-    )
+        jnp.dot(active, feed_out, preferred_element_type=jnp.float32), 13
+    )[0]
     mixed = final.astype(jnp.bfloat16).reshape(video.shape)
 
-    feed_out_grad = jnp.einsum("rf,rd->fd", active, cot_line, preferred_element_type=jnp.float32)
-    feed_out_grad = space_to_all(sum_over_frames(feed_out_grad, 1), 1, 0).astype(jnp.float32)
+    feed_out_grad = jnp.einsum("rf,rd->df", active, cot_line, preferred_element_type=jnp.float32)
     active_grad = jnp.einsum("rd,fd->rf", cot_line, feed_out, preferred_element_type=jnp.float32)
     upper_grad = jax.vjp(jax.nn.gelu, upper)[1](active_grad)[0].astype(jnp.bfloat16)
     feed_in_grad = jnp.einsum(
         "rd,rf->df", feed_line, upper_grad, preferred_element_type=jnp.float32
     )
-    feed_in_grad = space_to_all(sum_over_frames(feed_in_grad, 0), 0, 1).astype(jnp.float32)
-    normed_grad = scatter_tokens(
-        jnp.einsum("rf,df->rd", upper_grad, feed_in, preferred_element_type=jnp.float32)
+    feed_grads = jnp.concatenate(
+        [feed_in_grad.astype(jnp.bfloat16), feed_out_grad.astype(jnp.bfloat16)], axis=1
+    )
+    normed_grad, feed_grads = scatter_tokens(
+        jnp.einsum("rf,df->rd", upper_grad, feed_in, preferred_element_type=jnp.float32),
+        14,
+        by_frames(feed_grads),
     )
     stream_grad, feed_norm_grad = layer_back(stream_four, feed_norm, normed_grad)
     upstream = cot_rows.astype(jnp.float32) + stream_grad
     branch_grad = upstream.astype(jnp.bfloat16)
-    temporal_out_grad = sum_to_owner(
-        jnp.einsum("rc,rd->cd", temporal_mix, branch_grad, preferred_element_type=jnp.float32), 1
-    )
+    temporal_out_grad = jnp.einsum(
+        "rc,rd->dc", temporal_mix, branch_grad, preferred_element_type=jnp.float32
+    ).astype(jnp.bfloat16)
     mix_grad = jnp.einsum(
         "rd,cd->rc", branch_grad, temporal_out, preferred_element_type=jnp.float32
     ).astype(jnp.bfloat16)
-    clip_up = to_clips(mix_grad.reshape(slots, frame_dev, pixels_dev, half_width)).reshape(
+    clip_up = to_clips(mix_grad.reshape(slots, frame_dev, pixels_dev, half_width), 15).reshape(
         slots, frames_all, clip_pixels, head_local, HDIM
     )
     query_grad, key_grad, value_grad, score_grad = attend_backward(
@@ -441,22 +951,27 @@
     clip_grads = (
         jnp.stack([query_grad, key_grad, value_grad], axis=3)
         .astype(jnp.bfloat16)
-        .reshape(slots, frames_all, clip_pixels, 3, half_width)
-    )
-    triple_grad = from_clips(clip_grads)
+        .reshape(slots, frames_all, clip_pixels, 3 * half_width)
+    )
+    triple_grad = from_clips(clip_grads, 16)
     triple_grad = triple_grad.reshape(token_rows, 3, half_width)
-    temporal_qkv_grad = sum_to_owner(
-        jnp.einsum("rd,rjk->djk", temporal_in, triple_grad, preferred_element_type=jnp.float32), 0
+    temporal_qkv_grad = jnp.dot(
+        temporal_in.T,
+        triple_grad.reshape(token_rows, 3 * half_width),
+        preferred_element_type=jnp.float32,
+    ).astype(jnp.bfloat16)
+    temporal_grads = sum_to_owner(
+        jnp.concatenate([temporal_qkv_grad, temporal_out_grad], axis=1)
     )
     normed_grad = mp_sum(
-        jnp.einsum("rjk,djk->rd", triple_grad, temporal_qkv, preferred_element_type=jnp.float32)
+        jnp.einsum("rjk,jdk->rd", triple_grad, temporal_qkv, preferred_element_type=jnp.float32)
     )
     stream_grad, temporal_norm_grad = layer_back(stream_three, temporal_norm, normed_grad)
     upstream = upstream + stream_grad
     branch_grad = upstream.astype(jnp.bfloat16)
-    cross_out_grad = sum_to_owner(
-        jnp.einsum("rc,rd->cd", cross_mix, branch_grad, preferred_element_type=jnp.float32), 1
-    )
+    cross_out_grad = jnp.einsum(
+        "rc,rd->dc", cross_mix, branch_grad, preferred_element_type=jnp.float32
+    ).astype(jnp.bfloat16)
     mix_grad = (
         jnp.einsum("rd,cd->rc", branch_grad, cross_out, preferred_element_type=jnp.float32)
         .astype(jnp.bfloat16)
@@ -465,49 +980,52 @@
     query_grad, key_grad, value_grad, score_grad = attend_backward(
         cross_queries, text_key, text_value, pixel_form, None, text_valid, cross_total, mix_grad
     )
-    text_pair_grad = lax.psum_scatter(
+    pair_grad = (
         jnp.stack([key_grad, value_grad], axis=2)
-        .reshape(slots, TXT, 2, half_width)
-        .astype(jnp.bfloat16),
-        ("tm", "space"),
-        scatter_dimension=1,
-        tiled=True,
-    )
-    text_pair_all = lax.all_gather(text_pair_grad, ("tm", "space"), axis=1, tiled=True)
+        .astype(jnp.bfloat16)
+        .reshape(slots, owners, text_local, 2 * half_width)
+        .transpose(1, 0, 2, 3)
+        .reshape(owners, text_rows, 2 * half_width)
+    )
+    pair_grad = exchange(pair_grad, everyone, 27)
+    pair_grad = jnp.sum(pair_grad.astype(jnp.float32), axis=0).astype(jnp.bfloat16)
+    pair_all = share(pair_grad, everyone, 28)
+    text_cols = text_flat.reshape(text_rows, owners, -1).transpose(1, 0, 2)
+    text_cols = exchange(text_cols, everyone, 29)
     cross_kv_grad = jnp.einsum(
-        "btc,btjk->cjk",
-        part_of(part_of(text_all, "tm", 2), "space", 2),
-        text_pair_all,
-        preferred_element_type=jnp.float32,
-    )
+        "prc,prk->ck", text_cols, pair_all, preferred_element_type=jnp.float32
+    ).reshape(-1, 2, half_width)
     text_part = jnp.einsum(
-        "btjk,cjk->btc",
-        part_of(text_pair_all, "tm", 1),
-        cross_kv,
+        "srk,ck->src",
+        part_of(pair_all, "tm", 0),
+        cross_kv.reshape(cross_kv.shape[0], -1),
         preferred_element_type=jnp.float32,
     ).astype(jnp.bfloat16)
-    text_grad = lax.psum_scatter(
-        space_to_all(text_part, 1, 2), "mp", scatter_dimension=2, tiled=True
-    ).astype(jnp.float32)
+    text_part = exchange(text_part, ("space",), 30).transpose(1, 0, 2).reshape(text_rows, -1)
+    text_half = part_of(mp_sum(text_part), "mp", 1)
+    text_grad = text_half.reshape(slots, text_local, -1)
     query_rows_grad = query_grad.astype(jnp.bfloat16).reshape(token_rows, half_width)
-    cross_query_grad = sum_to_owner(
-        jnp.einsum("rd,rk->dk", cross_in, query_rows_grad, preferred_element_type=jnp.float32), 0
-    )
+    cross_query_grad = jnp.einsum(
+        "rd,rk->dk", cross_in, query_rows_grad, preferred_element_type=jnp.float32
+    ).astype(jnp.bfloat16)
     normed_grad = mp_sum(
         jnp.einsum("rk,dk->rd", query_rows_grad, cross_query, preferred_element_type=jnp.float32)
     )
     stream_grad, cross_norm_grad = layer_back(stream_two, cross_norm, normed_grad)
     upstream = upstream + stream_grad
     branch_grad = upstream.astype(jnp.bfloat16)
-    spatial_out_grad = sum_to_owner(
-        jnp.einsum("rc,rd->cd", spatial_mix, branch_grad, preferred_element_type=jnp.float32), 1
+    spatial_out_grad = jnp.einsum(
+        "rc,rd->dc", spatial_mix, branch_grad, preferred_element_type=jnp.float32
+    ).astype(jnp.bfloat16)
+    cross_grads = sum_to_owner(
+        jnp.concatenate([cross_query_grad, cross_out_grad, spatial_out_grad], axis=1)
     )
     mix_grad = (
         jnp.einsum("rd,cd->rc", branch_grad, spatial_out, preferred_element_type=jnp.float32)
         .astype(jnp.bfloat16)
         .reshape(slots * frame_dev, pixels_dev, half_width)
     )
-    mix_line = space_to_all(mix_grad, 2, 1).reshape(slots * frame_dev, H * W, head_line, HDIM)
+    mix_line = to_lines(mix_grad, False, 17).reshape(slots * frame_dev, H * W, head_line, HDIM)
     query_grad, key_grad, value_grad, score_grad = attend_backward(
         spatial_query, spatial_key, spatial_value, pixel_form, None, None, spatial_total, mix_line
     )
@@ -518,29 +1036,39 @@
         .transpose(2, 1, 3, 0, 4)
         .reshape(lines * token_rows, 3, head_line * HDIM)
     )
-    spatial_qkv_grad = jnp.einsum(
-        "rd,rjk->djk", spatial_line, triple_grad, preferred_element_type=jnp.float32
-    )
-    spatial_qkv_grad = space_to_all(sum_over_frames(spatial_qkv_grad, 0), 0, 2).astype(jnp.float32)
+    spatial_qkv_grad = jnp.dot(
+        spatial_line.T,
+        triple_grad.reshape(lines * token_rows, -1),
+        preferred_element_type=jnp.float32,
+    ).astype(jnp.bfloat16)
     normed_grad = scatter_tokens(
-        jnp.einsum("rjk,djk->rd", triple_grad, spatial_qkv, preferred_element_type=jnp.float32)
-    )
+        jnp.einsum("rjk,djk->rd", triple_grad, spatial_qkv, preferred_element_type=jnp.float32), 18
+    )[0]
     stream_grad, spatial_norm_grad = layer_back(stream_one, spatial_norm, normed_grad)
     upstream = upstream + stream_grad
-    branch_line = space_to_all(upstream.astype(jnp.bfloat16).reshape(video.shape), 4, 2)
-    second_conv_grad = stationary_to_owner(conv_weight_grad(second_wide, branch_line), 2)
+    branch_line = upstream.astype(jnp.bfloat16).reshape(images, pixels_dev, channels)
+    branch_line = to_lines(branch_line, False, 19).reshape(core_shape)
+    second_conv_grad = conv_weight_grad(second_wide, branch_line, "kc")
     second_part = conv_frames(branch_line, second_conv, "OHWI", True)
-    second_in_grad = lax.psum_scatter(
-        second_part.astype(jnp.bfloat16), "space", scatter_dimension=4, tiled=True
-    ).astype(jnp.float32)
+    second_in_grad, spatial_qkv_grad = sum_lines(
+        second_part.astype(jnp.bfloat16).reshape(images, H * W, half_width),
+        20,
+        by_frames(spatial_qkv_grad),
+    )
+    second_in_grad = second_in_grad.reshape(core_shape)
     modulated_grad = jax.vjp(jax.nn.silu, modulated)[1](second_in_grad)[0]
     frame_grads = jnp.stack(
         [jnp.sum(modulated_grad * normal_two, axis=(2, 3)), jnp.sum(modulated_grad, axis=(2, 3))],
         axis=2,
     )
     video_film_grad = jnp.einsum("bfv,bfjk->bvjk", choose, frame_grads, precision=highest)
-    video_film_grad = lax.all_gather(
-        lax.psum(video_film_grad, "tm"), "space", axis=3, tiled=True
+    film_shares = share(
+        video_film_grad.reshape(slots * VIDS * 2, -1), everyone, 31
+    ).reshape(frames_axis, lines, slots, VIDS, 2, -1)
+    video_film_grad = (
+        jnp.sum(film_shares, axis=0)
+        .transpose(1, 2, 3, 0, 4)
+        .reshape(slots, VIDS, 2, half_width)
     )
     film_weight_grad = jnp.einsum(
         "bvc,bvjk->cjk",
@@ -551,24 +1079,37 @@
     hidden_grad = group_backward(
         modulated_grad * (1.0 + frame_film[:, :, None, None, 0]), normal_two, inverse_two
     ).astype(jnp.bfloat16)
-    hidden_wide = lax.all_gather(hidden_grad, "space", axis=4, tiled=True)
-    first_conv_grad = stationary_to_owner(conv_weight_grad(first_in, hidden_wide), 1)
-    first_in_grad = mp_sum(conv_frames(hidden_wide, first_conv, "OHWI", True))
+    hidden_wide, second_conv_grad = gather_lines(
+        hidden_grad.reshape(images, H * W, -1), 21, by_frames(second_conv_grad)
+    )
+    hidden_wide = hidden_wide.reshape(core_shape)
+    first_conv_grad = conv_weight_grad(first_in, hidden_wide, "ck")
+    first_in_grad = conv_frames(hidden_wide, first_conv, "OHWI", True).astype(jnp.bfloat16)
+    first_in_grad = sum_cores(first_in_grad.reshape(images, H * W, -1), 22).reshape(core_shape)
     affine_grad = jax.vjp(jax.nn.silu, affine_one)[1](first_in_grad)[0]
     group_gain_grad = jnp.sum(affine_grad * normal_one, axis=(0, 1, 2, 3))
     group_bias_grad = jnp.sum(affine_grad, axis=(0, 1, 2, 3))
     video_line_grad = group_backward(affine_grad * gain_line, normal_one, inverse_one)
-    video_grad = upstream.reshape(video.shape) + space_to_all(
-        video_line_grad.astype(jnp.bfloat16), 2, 4
-    ).astype(jnp.float32)
+    video_rows_grad, first_conv_grad = from_lines(
+        video_line_grad.astype(jnp.bfloat16).reshape(images, H * W, -1),
+        True,
+        23,
+        by_frames(first_conv_grad),
+    )
+    video_grad = upstream.reshape(video.shape) + video_rows_grad.reshape(video.shape).astype(
+        jnp.float32
+    )
 
     def placed(line_grad):
         whole = jnp.zeros((channels,), jnp.float32)
         return lax.dynamic_update_slice_in_dim(
-            whole, line_grad, lax.axis_index("space") * line_grad.shape[0], 0
+            whole,
+            line_grad,
+            (lax.axis_index("space") * cores + lax.axis_index("mp")) * line_grad.shape[0],
+            0,
         )
 
-    owners = frames_axis * lines
+    cores = lax.axis_size("mp")
     small = jnp.concatenate(
         [
             item.reshape(owners, -1)
@@ -584,9 +1125,34 @@
         ],
         axis=1,
     )
-    small = lax.psum_scatter(small, ("tm", "space"), scatter_dimension=0, tiled=True)[0]
+    small = jnp.sum(exchange(small[:, None], everyone, 32), axis=(0, 1))
+    small_twin = lax.ppermute(small, "mp", [(0, 1), (1, 0)])
     gain_size = channels // owners
     gains = [small[i * gain_size : (i + 1) * gain_size] for i in range(6)]
+    for i in range(2):
+        gains[i] = gains[i] + small_twin[i * gain_size : (i + 1) * gain_size]
+    local = jnp.concatenate([feed_grads, spatial_qkv_grad], axis=1)
+    local = exchange(local.reshape(lines, -1, local.shape[1]), ("space",), 33).astype(jnp.float32)
+    feed_width = feed_in.shape[1]
+    local_rows = local.shape[1]
+    feed_in_grad = local[:, :, :feed_width].transpose(1, 0, 2).reshape(local_rows, -1)
+    feed_out_grad = local[:, :, feed_width : 2 * feed_width].transpose(0, 2, 1)
+    feed_out_grad = feed_out_grad.reshape(-1, local_rows)
+    spatial_qkv_grad = (
+        local[:, :, 2 * feed_width :]
+        .reshape(lines, local_rows, 3, -1)
+        .transpose(1, 2, 0, 3)
+        .reshape(local_rows, 3, half_width)
+    )
+    first_conv_grad = to_owner(first_conv_grad).astype(jnp.float32)
+    second_conv_grad = to_owner(second_conv_grad).astype(jnp.float32)
+    temporal_grads = temporal_grads.astype(jnp.float32)
+    cross_grads = cross_grads.astype(jnp.float32)
+    temporal_qkv_grad = temporal_grads[:, : 3 * half_width].reshape(-1, 3, half_width)
+    temporal_out_grad = temporal_grads[:, 3 * half_width :].T
+    cross_query_grad = cross_grads[:, :half_width]
+    cross_out_grad = cross_grads[:, half_width : 2 * half_width].T
+    spatial_out_grad = cross_grads[:, 2 * half_width :].T
     offset_bias_grad = small[6 * gain_size :].reshape(R // owners, head_local)
     return (
         mixed,
@@ -594,9 +1160,9 @@
         text_grad,
         gains[0],
         gains[1],
-        first_conv_grad.transpose(1, 0, 2),
+        first_conv_grad.reshape(-1, 9, half_width),
         film_weight_grad,
-        second_conv_grad.transpose(1, 0, 2),
+        second_conv_grad.reshape(-1, 9, half_width).transpose(2, 1, 0),
         gains[2],
         spatial_qkv_grad,
         spatial_out_grad,

time: 1890 us -> 1150 us (0.61)
  waiting for transfers between devices: 1020 us -> 67.7 us
  Pallas kernels: 0 us -> 646 us
  blocking collectives: 279 us -> 0 us
  local copies, waits for them, and re-layouts: 305 us -> 226 us
  starting transfers between devices: 69.8 us -> 28.3 us
  matrix products: 127 us -> 101 us
    pallas_call x0 -> x33, Pallas kernels: none -> 646 us  [talk(): pl.pallas_call(kernel, out_shape=result, in_specs=[ANY] * len(operands) i...]
    reduce_scatter x17 -> x1, waiting for transfers between devices: 536 us -> 0.01 us  [sum_to_owner(): lax.psum_scatter(weight_grad, ('tm', 'space'), scatter_dimension=0, tiled...]
    all_gather x14 -> x2, waiting for transfers between devices: 230 us -> 0.03 us  [the longest x1 0.03 us: on_device(): lax.all_gather(part_of(in_piece, 'tm', 1), everyone, axis=0, tiled=False)]
    all_to_all x10 -> x3, waiting for transfers between devices: 118 us -> 0.01 us  [space_to_all(): lax.all_to_all(source, 'space', split_axis=split, concat_axis=concat, til...]
    all_gather x7 -> x0, blocking collectives: 115 us -> none  [the longest x1 47.1 us: on_device(): lax.all_gather(text_pair_grad, ('tm', 'space'), axis=1, tiled=True)]
    unnamed x43 -> x7, waiting for transfers between devices: 109 us -> 0.09 us
    unnamed x341 -> x356, local copies, waits for them, and re-layouts: 163 us -> 65.1 us
    unnamed x1 -> x0, blocking collectives: 84.3 us -> none
  transfers between devices with their start and end apart: 57 -> 17, of which waited for: 39 -> 4; matrix products, arithmetic and copies ran while one was open for 13% -> 24% of each run, Pallas kernels for 0% -> 47%
where the time goes in v2:
time: 1150 us; the launch traced here: 1140 us
  Pallas kernels  646 us (56%)
  local copies, waits for them, and re-layouts  226 us (20%)
  matrix products  101 us (9%)
  waiting for transfers between devices  67.7 us (6%)
  other arithmetic  49.2 us (4%)
  starting transfers between devices  28.3 us (2%)
  between operations  19.2 us (2%)
    pallas_call x33, Pallas kernels, talk(): pl.pallas_call(kernel, out_shape=result, in_specs=[ANY] * len(operands) i...  646 us
    unnamed x356, local copies, waits for them, and re-layouts  65.1 us
    ppermute x2, waiting for transfers between devices, to_owner(): return lax.ppermute(portion, ('tm', 'space'), moves)  65 us
  transfers between devices with their start and end apart: 17, of which 4 were waited for; matrix products, arithmetic and copies ran while one was open for 24% of the time, Pallas kernels for 47%

profile of v2, /device:TPU:2, one launch (start us, length us, event | category | flops | bytes accessed | tf_op | source)
XLA Modules:
  0.0 1138.3 jit_solution(9652856327391549348)
XLA Ops:
  17.3 5.0 all-to-all-start
  26.8 33.2 %shard_map.408 = bf16[4,256,128]{2,1,0:T(8,128)(2,1)S(1)} custom-call(bf16[4,64,1024]{2,1,0:T(8,128)(2,1)S(1)} %bitcast.572), custom_call_target="tpu_custom_call" | custom-call | tf_op jit(solution)/shard_map/pallas_call | solution.py:87
  65.0 5.8 convolution_convert_fusion.8
  71.1 32.6 %shard_map.410 = f32[4,256,128]{2,1,0:T(8,128)S(1)} custom-call(bf16[4,256,512]{2,1,0:T(8,128)(2,1)S(1)} %bitcast.578), custom_call_target="tpu_custom_call" | custom-call | tf_op jit(solution)/shard_map/pallas_call | solution.py:87
  106.8 14.9 %shard_map.416 = bf16[1,64,1024]{2,1,0:T(8,128)(2,1)S(1)} custom-call(bf16[1,16,4096]{2,1,0:T(8,128)(2,1)S(1)} %bitcast.626), custom_call_target="tpu_custom_call" | custom-call | tf_op jit(solution)/shard_map/pallas_call | solution.py:87
  122.2 5.8 shard_map.417
  129.4 16.2 %shard_map.418 = bf16[16,16,1024]{2,1,0:T(8,128)(2,1)S(1)} custom-call(bf16[16,1024]{1,0:T(8,128)(2,1)S(1)} %copy-done.44), custom_call_target="tpu_custom_call" | custom-call | tf_op jit(solution)/shard_map/pallas_call | solution.py:87
  152.1 25.4 %shard_map.411 = bf16[4,256,512]{2,1,0:T(8,128)(2,1)S(1)} custom-call(bf16[4,256,128]{2,1,0:T(8,128)(2,1)S(1)} %multiply_convert_fusion.8.refs_0_), custom_call_target="tpu_custom_call" | custom-call | tf_op jit(solution)/shard_map/pallas_call | solution.py:87
  184.2 16.4 %shard_map.413 = bf16[4,64,1024]{2,1,0:T(8,128)(2,1)S(1)} custom-call(bf16[4,256,128]{2,1,0:T(8,128)(2,1)S(1)} %convert_element_type.420.refs_0_), custom_call_target="tpu_custom_call" | custom-call | tf_op jit(solution)/shard_map/pallas_call | solution.py:87
  205.9 36.1 %shard_map.414 = bf16[1,1024,1024]{2,1,0:T(8,128)(2,1)S(1)} custom-call(bf16[1,256,1024]{2,1,0:T(8,128)(2,1)S(1)} %fusion.107.x_ref), custom_call_target="tpu_custom_call" | custom-call | tf_op jit(solution)/shard_map/pallas_call | solution.py:87
  243.5 10.4 all-to-all-start.1
  264.0 4.0 fusion.248
  286.9 10.3 shard_map.415
  297.9 4.7 copy.373
  302.6 6.1 reshape.894
  308.7 4.2 fusion.247
  324.1 4.2 copy.384
  355.8 4.7 copy.385
  370.4 15.0 %shard_map.419 = bf16[2,8,16,1536]{3,2,1,0:T(8,128)(2,1)S(1)} custom-call(bf16[2,2,64,1536]{3,2,1,0:T(8,128)(2,1)S(1)} %copy-done.16), custom_call_target="tpu_custom_call" | custom-call | tf_op jit(solution)/shard_map/pallas_call | solution.py:87
  389.8 4.9 all-to-all-start.2
  394.9 6.4 slice_reduce_fusion.2
  414.8 5.9 shard_map.420
  423.9 24.0 %shard_map.423 = bf16[1,1024,1024]{2,1,0:T(8,128)(2,1)S(1)} custom-call(bf16[1,256,1024]{2,1,0:T(8,128)(2,1)S(1)} %bitcast.576), custom_call_target="tpu_custom_call" | custom-call | tf_op jit(solution)/shard_map/pallas_call | solution.py:87
  458.4 27.9 %shard_map.421 = bf16[1,1024,1024]{2,1,0:T(8,128)(2,1)S(1)} custom-call(bf16[1,256,1024]{2,1,0:T(8,128)(2,1)S(1)} %fusion.150.x_ref), custom_call_target="tpu_custom_call" | custom-call | tf_op jit(solution)/shard_map/pallas_call | solution.py:87
  500.0 3.9 copy.398
  507.1 33.7 %shard_map.424 = (bf16[256,1024]{1,0:T(8,128)(2,1)S(1)}, bf16[256,1024]{1,0:T(8,128)(2,1)S(1)}) custom-call(bf16[4,256,1024]{2,1,0:T(8,128)(2,1)S(1)} %bitcast.588, bf16[4,256,1024]{2,1,0:T(8,128)(2,1)S(1)} %bitcast.574), custom_call_target="tpu_custom_call" | custom-call | tf_op jit(solution)/shard_map/pallas_call | solution.py:87
  541.9 26.2 %shard_map.422 = bf16[256,1024]{1,0:T(8,128)(2,1)S(1)} custom-call(bf16[4,256,1024]{2,1,0:T(8,128)(2,1)S(1)} %bitcast.586), custom_call_target="tpu_custom_call" | custom-call | tf_op jit(solution)/shard_map/pallas_call | solution.py:87
  570.5 6.7 shard_map.425
  591.8 11.5 %shard_map.426 = bf16[2,2,64,1536]{3,2,1,0:T(8,128)(2,1)S(1)} custom-call(bf16[2,8,16,1536]{3,2,1,0:T(8,128)(2,1)S(1)} %copy-done.18), custom_call_target="tpu_custom_call" | custom-call | tf_op jit(solution)/shard_map/pallas_call | solution.py:87
  604.2 4.0 reshape.914
  634.1 4.7 copy.491
  638.9 4.7 reshape.995
  643.7 15.0 %shard_map.440 = bf16[16,16,256]{2,1,0:T(8,128)(2,1)S(1)} custom-call(bf16[16,16,256]{2,1,0:T(8,128)(2,1)S(1)} %bitcast.628), custom_call_target="tpu_custom_call" | custom-call | tf_op jit(solution)/shard_map/pallas_call | solution.py:87
  680.3 19.7 %shard_map.434 = bf16[16,16,1024]{2,1,0:T(8,128)(2,1)S(1)} custom-call(bf16[16,16,1024]{2,1,0:T(8,128)(2,1)S(1)} %copy_bitcast_fusion.1.x_ref), custom_call_target="tpu_custom_call" | custom-call | tf_op jit(solution)/shard_map/pallas_call | solution.py:87
  701.9 15.9 %shard_map.435 = bf16[16,16,1024]{2,1,0:T(8,128)(2,1)S(1)} custom-call(bf16[16,1024]{1,0:T(8,128)(2,1)S(1)} %reduce_sum.576.x_ref), custom_call_target="tpu_custom_call" | custom-call | tf_op jit(solution)/shard_map/pallas_call | solution.py:87
  720.2 6.5 shard_map.436
  734.8 9.3 shard_map.427
  770.8 34.3 %shard_map.428 = bf16[256,1024]{1,0:T(8,128)(2,1)S(1)} custom-call(bf16[4,256,1024]{2,1,0:T(8,128)(2,1)S(1)} %bitcast.587), custom_call_target="tpu_custom_call" | custom-call | tf_op jit(solution)/shard_map/pallas_call | solution.py:87
  807.8 30.5 %shard_map.429 = bf16[4,256,256]{2,1,0:T(8,128)(2,1)S(1)} custom-call(bf16[4,64,1024]{2,1,0:T(8,128)(2,1)S(1)} %bitcast.592), custom_call_target="tpu_custom_call" | custom-call | tf_op jit(solution)/shard_map/pallas_call | solution.py:87
  842.2 42.5 %shard_map.430 = (f32[4,256,128]{2,1,0:T(8,128)S(1)}, bf16[256,384]{1,0:T(8,128)(2,1)S(1)}) custom-call(bf16[4,256,512]{2,1,0:T(8,128)(2,1)S(1)} %bitcast.577, bf16[4,256,384]{2,1,0:T(8,128)(2,1)S(1)} %bitcast.604), custom_call_target="tpu_custom_call" | custom-call | tf_op jit(solution)/shard_map/pallas_call | solution.py:87
  884.8 44.5 %shard_map.439 = bf16[4,64,1408]{2,1,0:T(8,128)(2,1)S(1)} custom-call(bf16[4,64,1408]{2,1,0:T(8,128)(2,1)S(1)} %bitcast.579), custom_call_target="tpu_custom_call" | custom-call | tf_op jit(solution)/shard_map/pallas_call | solution.py:87
  932.2 13.7 %shard_map.438 = f32[16,12,128]{2,1,0:T(8,128)S(1)} custom-call(f32[12,128]{1,0:T(8,128)S(1)} %reshape.942.x_ref), custom_call_target="tpu_custom_call" | custom-call | tf_op jit(solution)/shard_map/pallas_call | solution.py:87
  954.8 29.8 %shard_map.431 = (bf16[4,256,512]{2,1,0:T(8,128)(2,1)S(1)}, bf16[64,4608]{1,0:T(8,128)(2,1)}) custom-call(bf16[4,256,128]{2,1,0:T(8,128)(2,1)S(1)} %multiply_convert_fusion.7.refs_0_, bf16[4,64,4608]{2,1,0:T(8,128)(2,1)S(1)} %bitcast.584), custom_call_target="tpu_custom_call" | custom-call | tf_op jit(solution)/shard_map/pallas_call | solution.py:87
  984.7 3.9 convolution_convert_fusion.16
  992.0 7.8 shard_map.437
  1006.5 29.8 %shard_map.433 = (bf16[4,64,1024]{2,1,0:T(8,128)(2,1)S(1)}, bf16[64,4608]{1,0:T(8,128)(2,1)S(1)}) custom-call(bf16[4,256,128]{2,1,0:T(8,128)(2,1)S(1)} %fusion.143.refs_0_, bf16[4,64,4608]{2,1,0:T(8,128)(2,1)S(1)} %bitcast.585), custom_call_target="tpu_custom_call" | custom-call | tf_op jit(solution)/shard_map/pallas_call | solution.py:87
  1050.1 55.6 %collective-permute-done.7 = bf16[64,4608]{1,0:T(8,128)(2,1)} collective-permute-done((bf16[64,4608]{1,0:T(8,128)(2,1)S(1)}, bf16[64,4608]{1,0:T(8,128)(2,1)}, u32[]{:S(2)}, u32[]{:S(2)}) %collective-permute-start.7) | collective-permute-done | bytes 589856 | tf_op jit(solution)/shard_map/ppermute | solution.py:566
  1107.9 9.4 collective-permute-done.8
  (680 shorter events, 331.2 us)
Async XLA Ops:
  8.0 169.5 %copy-start = (bf16[512,9,256]{2,0,1:T(8,128)(2,1)S(1)}, bf16[512,9,256]{2,0,1:T(8,128)(2,1)}, u32[]{:S(2)}) copy-start(bf16[512,9,256]{2,0,1:T(8,128)(2,1)} %param.35) | copy-start | bytes 7077892
  8.0 140.8 %reduce-scatter.10.cloned.1.call-start = ((), (), s32[]{:S(2)}) async-start(), calls=%async_computation.9 | async-start | bytes 327680
  13.3 284.6 %all-gather.5.cloned.1.call-start = ((), (), s32[]{:S(2)}) async-start(), calls=%async_computation.7 | async-start | bytes 3342336 | tf_op jit(solution)/shard_map/all_gather | solution.py:783
  17.3 226.2 %all-to-all-start = ((bf16[256,3,512]{0,1,2:T(4,128)(2,1)}), bf16[256,3,512]{0,1,2:T(4,128)(2,1)}, u32[]{:S(2)}, u32[]{:S(2)}) async-start(bf16[256,3,512]{0,1,2:T(4,128)(2,1)} %copy.366), calls=%async_computation | async-start | bytes 2097152 | tf_op jit(solution)/shard_map/all_to_all | solution.py:37
  22.3 311.4 %all-gather.7.cloned.1.call-start = ((), (), s32[]{:S(2)}) async-start(), calls=%async_computation.8 | async-start | bytes 4456448 | tf_op jit(solution)/shard_map/all_gather | solution.py:788
  104.1 47.7 %copy-start.109 = (f32[4,128]{1,0:T(4,128)}, f32[4,128]{1,0:T(4,128)S(1)}, u32[]{:S(2)}) copy-start(f32[4,128]{1,0:T(4,128)S(1)} %sub.276) | copy-start | bytes 6148
  104.5 47.3 %copy-start.119 = (f32[4,128]{1,0:T(4,128)}, f32[4,128]{1,0:T(4,128)S(1)}, u32[]{:S(2)}) copy-start(f32[4,128]{1,0:T(4,128)S(1)} %mul.693) | copy-start | bytes 6148
  122.2 26.6 %copy-start.151 = (s32[2,8]{1,0:T(2,128)S(1)}, s32[2,8]{1,0:T(2,128)}, u32[]{:S(2)}) copy-start(s32[2,8]{1,0:T(2,128)} %param.28) | copy-start | bytes 196
  148.8 33.6 %copy-start.160 = (s32[2,2]{1,0:T(2,128)}, s32[2,2]{1,0:T(2,128)S(1)}, u32[]{:S(2)}) copy-start(s32[2,2]{1,0:T(2,128)S(1)} %constant_dynamic-slice_fusion) | copy-start | bytes 52
  151.8 30.6 %copy-start.121 = (f32[2,2,1,128]{3,1,2,0:T(2,128)}, f32[2,2,1,128]{3,1,2,0:T(2,128)S(1)}, u32[]{:S(2)}) copy-start(f32[2,2,1,128]{3,1,2,0:T(2,128)S(1)} %get-tuple-element.200) | copy-start | bytes 6148
  151.8 30.6 %copy-start.136 = (f32[2,2,1,128]{3,1,2,0:T(2,128)}, f32[2,2,1,128]{3,1,2,0:T(2,128)S(1)}, u32[]{:S(2)}) copy-start(f32[2,2,1,128]{3,1,2,0:T(2,128)S(1)} %get-tuple-element.201) | copy-start | bytes 6148
  202.8 39.2 %copy-start.134 = (f32[256]{0:T(256)}, f32[256]{0:T(256)S(1)}, u32[]{:S(2)}) copy-start(f32[256]{0:T(256)S(1)} %div.171) | copy-start | bytes 3076
  204.4 37.6 %copy-start.149 = (f32[256]{0:T(256)}, f32[256]{0:T(256)S(1)}, u32[]{:S(2)}) copy-start(f32[256]{0:T(256)S(1)} %add.330) | copy-start | bytes 3076
  204.5 37.6 %copy-start.145 = (f32[256]{0:T(256)}, f32[256]{0:T(256)S(1)}, u32[]{:S(2)}) copy-start(f32[256]{0:T(256)S(1)} %rsqrt.62) | copy-start | bytes 3076
  243.5 146.3 %all-to-all-start.1 = ((bf16[256,4,512]{0,2,1:T(8,128)(2,1)}), bf16[256,4,512]{0,2,1:T(8,128)(2,1)}, u32[]{:S(2)}, u32[]{:S(2)}) async-start(bf16[256,4,512]{0,2,1:T(8,128)(2,1)} %bitcast.655), calls=%async_computation.1 | async-start | bytes 2097152 | tf_op jit(solution)/shard_map/all_to_all | solution.py:37
  319.5 11.3 collective-permute-start
  344.8 15.7 %collective-permute-start.1 = (bf16[256,1024]{1,0:T(8,128)(2,1)}, bf16[256,1024]{1,0:T(8,128)(2,1)}, u32[]{:S(2)}, u32[]{:S(2)}) collective-permute-start(bf16[256,1024]{1,0:T(8,128)(2,1)} %convolution_convert_fusion.14), channel_id=1, source_target_pairs={{0,1},{1,0},{2,3},{3,2},{4,5},{5,4},{6,7},{7,6},{8,9},{9,8},{10,11... | collective-permute-start | bytes 1572872 | tf_op jit(solution)/shard_map/ppermute | solution.py:27
  389.8 61.8 %all-to-all-start.2 = ((bf16[4,512,256]{2,1,0:T(8,128)(2,1)}), bf16[4,512,256]{2,1,0:T(8,128)(2,1)}, u32[]{:S(2)}, u32[]{:S(2)}) async-start(bf16[4,512,256]{2,1,0:T(8,128)(2,1)} %bitcast.677), calls=%async_computation.2 | async-start | bytes 2097152 | tf_op jit(solution)/shard_map/all_to_all | solution.py:37
  394.8 725.6 %reduce-scatter.12.cloned.1.call-start = ((), (), s32[]{:S(2)}) async-start(), calls=%async_computation.10 | async-start | bytes 3342336
  423.9 31.0 %collective-permute-start.2 = (bf16[256,1024]{1,0:T(8,128)(2,1)}, bf16[256,1024]{1,0:T(8,128)(2,1)}, u32[]{:S(2)}, u32[]{:S(2)}) collective-permute-start(bf16[256,1024]{1,0:T(8,128)(2,1)} %convolution_convert_fusion.12), channel_id=1, source_target_pairs={{0,1},{1,0},{2,3},{3,2},{4,5},{5,4},{6,7},{7,6},{8,9},{9,8},{10,11... | collective-permute-start | bytes 1572872 | tf_op jit(solution)/shard_map/ppermute | solution.py:27
  458.2 28.2 %copy-start.91 = (bf16[4,256,512]{2,1,0:T(8,128)(2,1)S(1)}, bf16[4,256,512]{2,1,0:T(8,128)(2,1)}, u32[]{:S(2)}) copy-start(bf16[4,256,512]{2,1,0:T(8,128)(2,1)} %copy.396) | copy-start | bytes 3145732
  507.1 33.8 %copy-start.59 = (f32[256,1024]{1,0:T(8,128)S(1)}, f32[256,1024]{1,0:T(8,128)}, u32[]{:S(2)}) copy-start(f32[256,1024]{1,0:T(8,128)} %copy-done.58) | copy-start | bytes 3145732
  507.1 33.8 %copy-start.144 = (f32[256]{0:T(256)S(1)}, f32[256]{0:T(256)}, u32[]{:S(2)}) copy-start(f32[256]{0:T(256)} %copy-done.143) | copy-start | bytes 3076
  507.1 34.8 %copy-start.157 = (f32[256]{0:T(256)S(1)}, f32[256]{0:T(256)}, u32[]{:S(2)}) copy-start(f32[256]{0:T(256)} %copy-done.156) | copy-start | bytes 3076
  507.1 34.8 %copy-start.27 = (bf16[1024,1024]{1,0:T(8,128)(2,1)S(1)}, bf16[1024,1024]{1,0:T(8,128)(2,1)}, u32[]{:S(2)}) copy-start(bf16[1024,1024]{1,0:T(8,128)(2,1)} %convolution_convert_fusion.2) | copy-start | bytes 6291460
  540.8 27.3 %copy-start.42 = (bf16[256,1024]{1,0:T(8,128)(2,1)}, bf16[256,1024]{1,0:T(8,128)(2,1)S(1)}, u32[]{:S(2)}) copy-start(bf16[256,1024]{1,0:T(8,128)(2,1)S(1)} %get-tuple-element.36) | copy-start | bytes 1572868
  611.6 2.0 collective-permute-start.3
  627.1 2.0 collective-permute-start.4
  638.8 487.9 %reduce-scatter.8.cloned.1.call-start = ((), (), s32[]{:S(2)}) async-start(), calls=%async_computation.6 | async-start | bytes 4456448 | tf_op jit(solution)/shard_map/reduce_scatter | solution.py:556
  643.6 22.2 %copy-start.116 = (f32[256]{0:T(256)S(1)}, f32[256]{0:T(256)}, u32[]{:S(2)}) copy-start(f32[256]{0:T(256)} %copy-done.114) | copy-start | bytes 3076
  643.6 22.2 %copy-start.131 = (f32[256]{0:T(256)S(1)}, f32[256]{0:T(256)}, u32[]{:S(2)}) copy-start(f32[256]{0:T(256)} %copy-done.129) | copy-start | bytes 3076
  701.9 24.9 %copy-start.46 = (bf16[16,16,256]{2,1,0:T(8,128)(2,1)S(1)}, bf16[16,16,256]{2,1,0:T(8,128)(2,1)}, u32[]{:S(2)}) copy-start(bf16[16,16,256]{2,1,0:T(8,128)(2,1)} %copy-done.45) | copy-start | bytes 393220
  726.7 4.6 collective-permute-start.5
  770.8 34.4 %copy-start.5 = (bf16[4,64,1024]{2,1,0:T(8,128)(2,1)S(1)}, bf16[4,64,1024]{2,1,0:T(8,128)(2,1)}, u32[]{:S(2)}) copy-start(bf16[4,64,1024]{2,1,0:T(8,128)(2,1)} %copy-done.3) | copy-start | bytes 1572868
  770.8 34.4 %copy-start.135 = (f32[256]{0:T(256)S(1)}, f32[256]{0:T(256)}, u32[]{:S(2)}) copy-start(f32[256]{0:T(256)} %copy-done.134) | copy-start | bytes 3076
  770.8 34.8 %copy-start.150 = (f32[256]{0:T(256)S(1)}, f32[256]{0:T(256)}, u32[]{:S(2)}) copy-start(f32[256]{0:T(256)} %copy-done.149) | copy-start | bytes 3076
  770.8 34.8 %copy-start.146 = (f32[256]{0:T(256)S(1)}, f32[256]{0:T(256)}, u32[]{:S(2)}) copy-start(f32[256]{0:T(256)} %copy-done.145) | copy-start | bytes 3076
  842.0 42.7 %copy-start.43 = (bf16[256,1024]{1,0:T(8,128)(2,1)S(1)}, bf16[256,1024]{1,0:T(8,128)(2,1)}, u32[]{:S(2)}) copy-start(bf16[256,1024]{1,0:T(8,128)(2,1)} %copy-done.42) | copy-start | bytes 1572868
  884.8 45.9 %copy-start.110 = (f32[4,128]{1,0:T(4,128)S(1)}, f32[4,128]{1,0:T(4,128)}, u32[]{:S(2)}) copy-start(f32[4,128]{1,0:T(4,128)} %copy-done.109) | copy-start | bytes 6148
  884.8 45.9 %copy-start.120 = (f32[4,128]{1,0:T(4,128)S(1)}, f32[4,128]{1,0:T(4,128)}, u32[]{:S(2)}) copy-start(f32[4,128]{1,0:T(4,128)} %copy-done.119) | copy-start | bytes 6148
  884.8 45.9 %copy-start.122 = (f32[2,2,1,128]{3,1,2,0:T(2,128)S(1)}, f32[2,2,1,128]{3,1,2,0:T(2,128)}, u32[]{:S(2)}) copy-start(f32[2,2,1,128]{3,1,2,0:T(2,128)} %copy-done.121) | copy-start | bytes 6148
  884.8 45.9 %copy-start.137 = (f32[2,2,1,128]{3,1,2,0:T(2,128)S(1)}, f32[2,2,1,128]{3,1,2,0:T(2,128)}, u32[]{:S(2)}) copy-start(f32[2,2,1,128]{3,1,2,0:T(2,128)} %copy-done.136) | copy-start | bytes 6148
  954.8 29.9 %copy-start.165 = (bf16[256,9,512]{2,0,1:T(8,128)(2,1)S(1)}, bf16[256,9,512]{2,0,1:T(8,128)(2,1)}, u32[]{:S(2)}) copy-start(bf16[256,9,512]{2,0,1:T(8,128)(2,1)} %param.33) | copy-start | bytes 7077892
  999.9 48.9 %collective-permute-start.6 = (f32[448]{0:T(512)S(1)}, f32[448]{0:T(512)S(1)}, u32[]{:S(2)}, u32[]{:S(2)}) collective-permute-start(f32[448]{0:T(512)S(1)} %reduce_sum.584), channel_id=1, source_target_pairs={{0,1},{1,0},{2,3},{3,2},{4,5},{5,4},{6,7},{7,6},{8,9},{9,8},{10,11... | collective-permute-start | bytes 5384 | tf_op jit(solution)/shard_map/ppermute | solution.py:1129
  1006.4 36.6 %copy-start.77 = (f32[256,1024]{1,0:T(8,128)S(1)}, f32[256,1024]{1,0:T(8,128)}, u32[]{:S(2)}) copy-start(f32[256,1024]{1,0:T(8,128)} %get-tuple-element.172) | copy-start | bytes 3145732
  1006.4 37.8 %copy-start.76 = (f32[4,64,1408]{2,1,0:T(8,128)S(1)}, f32[4,64,1408]{2,1,0:T(8,128)}, u32[]{:S(2)}) copy-start(f32[4,64,1408]{2,1,0:T(8,128)} %convert_element_type.521) | copy-start | bytes 4325380
  1036.3 69.3 %collective-permute-start.7 = (bf16[64,4608]{1,0:T(8,128)(2,1)S(1)}, bf16[64,4608]{1,0:T(8,128)(2,1)}, u32[]{:S(2)}, u32[]{:S(2)}) collective-permute-start(bf16[64,4608]{1,0:T(8,128)(2,1)S(1)} %get-tuple-element.34), channel_id=1, source_target_pairs={{0,0},{2,8},{4,16},{6,24},{8,2},{10,10},{12,18},{14,26},{16,4},{18... | collective-permute-start | bytes 1769480 | tf_op jit(solution)/shard_map/ppermute | solution.py:566
  1039.3 78.1 %collective-permute-start.8 = (bf16[64,4608]{1,0:T(8,128)(2,1)}, bf16[64,4608]{1,0:T(8,128)(2,1)}, u32[]{:S(2)}, u32[]{:S(2)}) collective-permute-start(bf16[64,4608]{1,0:T(8,128)(2,1)} %get-tuple-element.35), channel_id=1, source_target_pairs={{0,0},{2,8},{4,16},{6,24},{8,2},{10,10},{12,18},{14,26},{16,4},{18... | collective-permute-start | bytes 1769480 | tf_op jit(solution)/shard_map/ppermute | solution.py:566
  (136 other events, 393.0 us)
Sparse Core Ops, SparseCore 0:
  13.4 26.0 reduce-scatter.9
Sparse Core Ops, SparseCore 1:
  17.6 94.0 all-gather.4
  114.6 132.9 all-gather.6
  638.9 139.0 reduce-scatter.11
  780.4 152.8 reduce-scatter.7

commit v3 on v2

v3 whole, which is shorter than its diff:
```python
import math

import jax
import jax.numpy as jnp
from jax import lax
from jax.experimental import pallas as pl
from jax.experimental.pallas import tpu as pltpu
from jax.sharding import PartitionSpec as P

D = 1024
HDIM = 64
TXT = 128
G = 32
R = 128
VIDS = 3
H = 16
W = 16


epsilon = 1e-05
highest = lax.Precision.HIGHEST
masked = -1e30


def twin_add(partial_sum):
    mine = partial_sum.astype(jnp.bfloat16)
    other = lax.ppermute(mine, "mp", [(0, 1), (1, 0)])
    return mine.astype(jnp.float32) + other.astype(jnp.float32)


def part_of(source, axis_name, dim):
    size = source.shape[dim] // lax.axis_size(axis_name)
    return lax.dynamic_slice_in_dim(source, lax.axis_index(axis_name) * size, size, dim)


MESH = pl.DeviceIdType.MESH
lane = 128
ANY = pl.BlockSpec(memory_space=pl.ANY)
VMEM = pl.BlockSpec(memory_space=pltpu.VMEM)


def meet(peers):
    gate = pltpu.get_barrier_semaphore()
    for peer in peers:
        pl.semaphore_signal(gate, inc=1, device_id=peer, device_id_type=MESH)
    pl.semaphore_wait(gate, len(peers))


def others(axis_name):
    count = lax.axis_size(axis_name)
    me = lax.axis_index(axis_name)
    return [(step, lax.rem(me + step, count)) for step in range(1, count)]


def send(source, target, send_sem, recv_sem, peer):
    copy = pltpu.make_async_remote_copy(
        src_ref=source,
        dst_ref=target,
        send_sem=send_sem,
        recv_sem=recv_sem,
        device_id=peer,
        device_id_type=MESH,
    )
    copy.start()
    return copy


def keep(source, target, sem):
    copy = pltpu.make_async_copy(source, target, sem)
    copy.start()
    return copy


def cols_of(ref, index, width):
    return ref.at[:, :, pl.ds(pl.multiple_of(index * width, width), width)]


def rows_of(ref, index, width):
    return ref.at[:, pl.ds(pl.multiple_of(index * width, width), width), :]


def talk(kernel, result, operands, scratch, number, specs=None, out_spec=ANY):
    return pl.pallas_call(
        kernel,
        out_shape=result,
        in_specs=[ANY] * len(operands) if specs is None else specs,
        out_specs=out_spec,
        scratch_shapes=scratch,
        compiler_params=pltpu.CompilerParams(
            collective_id=number, has_side_effects=True, vmem_limit_bytes=48 * 1024 * 1024
        ),
    )(*operands)


def dma_sems(*counts):
    return [pltpu.SemaphoreType.DMA((max(count, 1),)) for count in counts]


def flat_index(axes):
    index = 0
    for name in axes:
        index = index * lax.axis_size(name) + lax.axis_index(name)
    return index


def flat_peers(axes):
    count = math.prod(lax.axis_size(name) for name in axes)
    me = flat_index(axes)
    peers = []
    for step in range(1, count):
        peer = lax.rem(me + step, count)
        place, rest = {}, peer
        for name in reversed(axes):
            place[name] = lax.rem(rest, lax.axis_size(name))
            rest = rest // lax.axis_size(name)
        peers.append((step, peer, place))
    return peers


class Rider:
    scratch = ()
    result_spec = ANY

    def peers(self):
        return [place for _, _, place in flat_peers(self.axes)]


class Exchange(Rider):
    def __init__(self, source, axes):
        self.source, self.axes = source, axes
        count = source.shape[0]
        self.result = jax.ShapeDtypeStruct(source.shape, source.dtype)
        self.scratch = dma_sems(count - 1, count - 1, 1)

    def plain(self):
        return lax.all_to_all(self.source, self.axes, split_axis=0, concat_axis=0, tiled=True)

    def start(self, x_ref, out_ref, send_sem, recv_sem, own_sem):
        me = flat_index(self.axes)
        self.copies = [
            send(x_ref.at[peer], out_ref.at[me], send_sem.at[i - 1], recv_sem.at[i - 1], place)
            for i, peer, place in flat_peers(self.axes)
        ]
        self.copies.append(keep(x_ref.at[me], out_ref.at[me], own_sem.at[0]))

    def finish(self, *refs):
        for copy in self.copies:
            copy.wait()


class Share(Rider):
    def __init__(self, source, axes, first=0, size=None):
        self.source, self.axes = source, axes
        self.first, self.size = first, size
        count = math.prod(lax.axis_size(name) for name in axes)
        shape = source.shape if size is None else (size,) + source.shape[1:]
        self.result = jax.ShapeDtypeStruct((count,) + shape, source.dtype)
        self.scratch = dma_sems(count - 1, count - 1, 1)

    def plain(self):
        source = self.source
        if self.size is not None:
            source = source[self.first : self.first + self.size]
        return lax.all_gather(source, self.axes, axis=0, tiled=False)

    def start(self, x_ref, out_ref, send_sem, recv_sem, own_sem):
        me = flat_index(self.axes)
        part = x_ref if self.size is None else x_ref.at[pl.ds(self.first, self.size)]
        self.copies = [
            send(part, out_ref.at[me], send_sem.at[i - 1], recv_sem.at[i - 1], place)
            for i, _, place in flat_peers(self.axes)
        ]
        self.copies.append(keep(part, out_ref.at[me], own_sem.at[0]))

    def finish(self, *refs):
        for copy in self.copies:
            copy.wait()


class JoinCores(Rider):
    def __init__(self, source):
        self.source = source
        self.rows, self.width = source.shape
        shape = (self.rows, self.width * lax.axis_size("mp"))
        self.result = jax.ShapeDtypeStruct(shape, source.dtype)
        self.scratch = dma_sems(1, 1, 1)

    def peers(self):
        return twin_peers()

    def plain(self):
        return lax.all_gather(self.source, "mp", axis=1, tiled=True)

    def start(self, x_ref, out_ref, send_sem, recv_sem, own_sem):
        core = lax.axis_index("mp")
        mine = out_ref.at[:, pl.ds(pl.multiple_of(core * self.width, self.width), self.width)]
        self.copies = [
            send(x_ref, mine, send_sem.at[0], recv_sem.at[0], {"mp": 1 - core}),
            keep(x_ref, mine, own_sem.at[0]),
        ]

    def finish(self, *refs):
        for copy in self.copies:
            copy.wait()


class LineColumns(Rider):
    axes = ("space",)

    def __init__(self, source):
        self.source = source
        lines = lax.axis_size("space")
        self.width = source.shape[1] // lines
        shape = (lines, source.shape[0], self.width)
        self.result = jax.ShapeDtypeStruct(shape, source.dtype)
        self.scratch = dma_sems(lines - 1, lines - 1, 1)

    def plain(self):
        return lax.all_to_all(
            self.source[None], "space", split_axis=2, concat_axis=0, tiled=True
        )

    def start(self, x_ref, out_ref, send_sem, recv_sem, own_sem):
        me = lax.axis_index("space")

        def part(index):
            return x_ref.at[:, pl.ds(pl.multiple_of(index * self.width, self.width), self.width)]

        self.copies = [
            send(part(peer), out_ref.at[me], send_sem.at[i - 1], recv_sem.at[i - 1], {"space": peer})
            for i, peer in others("space")
        ]
        self.copies.append(keep(part(me), out_ref.at[me], own_sem.at[0]))

    def finish(self, *refs):
        for copy in self.copies:
            copy.wait()


class FrameSum(Rider):
    axes = ("tm",)
    result_spec = VMEM

    def __init__(self, source):
        self.count, self.rows, self.width = source.shape
        self.source = source
        self.result = jax.ShapeDtypeStruct((self.rows, self.width), jnp.bfloat16)
        self.scratch = [
            pltpu.VMEM((max(self.count - 1, 1), self.rows, self.width), jnp.bfloat16),
            pltpu.VMEM((self.rows, self.width), jnp.bfloat16),
        ] + dma_sems(self.count - 1, self.count - 1, 1)

    def plain(self):
        return lax.psum_scatter(self.source, "tm", scatter_dimension=0, tiled=True)[0]

    def start(self, w_ref, out_ref, got_ref, own_ref, send_sem, recv_sem, own_sem):
        me = lax.axis_index("tm")
        self.copies = [
            send(w_ref.at[peer], got_ref.at[i - 1], send_sem.at[i - 1], recv_sem.at[i - 1], {"tm": peer})
            for i, peer in others("tm")
        ]
        self.copies.append(keep(w_ref.at[me], own_ref, own_sem.at[0]))

    def finish(self, w_ref, out_ref, got_ref, own_ref, *sems):
        for copy in self.copies:
            copy.wait()
        block = min(16, self.rows)

        def some(index, carry):
            rows = pl.ds(pl.multiple_of(index * block, block), block)
            total = own_ref[rows, :].astype(jnp.float32)
            for step in range(self.count - 1):
                total = total + got_ref[step, rows, :].astype(jnp.float32)
            out_ref[rows, :] = total.astype(jnp.bfloat16)
            return carry

        lax.fori_loop(0, self.rows // block, some, 0)


class Keep(Rider):
    def __init__(self, source):
        self.source = source
        self.result = jax.ShapeDtypeStruct(source.shape, source.dtype)
        self.scratch = dma_sems(1)

    def peers(self):
        return []

    def plain(self):
        return self.source

    def start(self, x_ref, out_ref, own_sem):
        self.copy = keep(x_ref, out_ref, own_sem.at[0])

    def finish(self, *refs):
        self.copy.wait()


class TapSum(Rider):
    axes = ("tm",)
    result_spec = VMEM

    def __init__(self, source):
        self.taps, all_rows, self.width = source.shape
        self.count = lax.axis_size("tm")
        self.rows = all_rows // self.count
        self.source = source
        shape = (self.taps, self.rows, self.width)
        self.result = jax.ShapeDtypeStruct(shape, jnp.bfloat16)
        self.scratch = [
            pltpu.VMEM((max(self.count - 1, 1),) + shape, jnp.bfloat16),
            pltpu.VMEM(shape, jnp.bfloat16),
        ] + dma_sems(self.count - 1, self.count - 1, 1)

    def plain(self):
        return lax.psum_scatter(self.source, "tm", scatter_dimension=1, tiled=True)

    def start(self, w_ref, out_ref, got_ref, own_ref, send_sem, recv_sem, own_sem):
        me = lax.axis_index("tm")
        self.copies = [
            send(rows_of(w_ref, peer, self.rows), got_ref.at[i - 1], send_sem.at[i - 1], recv_sem.at[i - 1], {"tm": peer})
            for i, peer in others("tm")
        ]
        self.copies.append(keep(rows_of(w_ref, me, self.rows), own_ref, own_sem.at[0]))

    def finish(self, w_ref, out_ref, got_ref, own_ref, *sems):
        for copy in self.copies:
            copy.wait()

        def some(tap, carry):
            total = own_ref[tap].astype(jnp.float32)
            for step in range(self.count - 1):
                total = total + got_ref[step, tap].astype(jnp.float32)
            out_ref[tap] = total.astype(jnp.bfloat16)
            return carry

        lax.fori_loop(0, self.taps, some, 0)


def plain_all(riders):
    return [rider.plain() for rider in riders]


def talk_with(kernel, peers, result, operands, scratch, number, riders, specs=None, out_spec=ANY):
    specs = [ANY] * len(operands) if specs is None else specs
    inputs, own_scratch, count = len(operands), len(scratch), len(riders)

    def whole(*refs):
        ins, rider_ins = refs[:inputs], refs[inputs : inputs + count]
        out_ref = refs[inputs + count]
        rider_outs = refs[inputs + count + 1 : inputs + 2 * count + 1]
        rest = refs[inputs + 2 * count + 1 :]
        mine, rest = rest[:own_scratch], rest[own_scratch:]
        packs = []
        for rider, x_ref, y_ref in zip(riders, rider_ins, rider_outs):
            packs.append((x_ref, y_ref) + tuple(rest[: len(rider.scratch)]))
            rest = rest[len(rider.scratch) :]
        meet(peers() + [peer for rider in riders for peer in rider.peers()])
        for rider, pack in zip(riders, packs):
            rider.start(*pack)
        kernel(*ins, out_ref, *mine)
        for rider, pack in zip(riders, packs):
            rider.finish(*pack)

    results = talk(
        whole,
        (result,) + tuple(rider.result for rider in riders),
        operands + [rider.source for rider in riders],
        scratch + [item for rider in riders for item in rider.scratch],
        number,
        specs + [ANY] * count,
        (out_spec,) + tuple(rider.result_spec for rider in riders),
    )
    return results[0], list(results[1:])


def line_peers():
    return [{"space": peer} for _, peer in others("space")]


def frame_peers():
    return [{"tm": peer} for _, peer in others("tm")]


def twin_peers():
    return [{"mp": 1 - lax.axis_index("mp")}]


def to_lines(source, per_core, number, riders=(), join=False):
    images, pixels, channels = source.shape
    lines, cores = lax.axis_size("space"), lax.axis_size("mp")
    pieces = lines * cores if per_core or join else lines
    width = channels // pieces
    if width % lane != 0 or pixels % 16 != 0:
        if per_core:
            parts = source.reshape(images, pixels, lines, cores, width)
            parts = lax.dynamic_index_in_dim(parts, lax.axis_index("mp"), 3, keepdims=False)
            source = parts.reshape(images, pixels, lines * width)
        moved = lax.all_to_all(source, "space", split_axis=2, concat_axis=1, tiled=True)
        return moved, plain_all(riders)

    def kernel(x_ref, out_ref, send_sem, recv_sem, pass_sem, gain_sem, own_sem):
        me, core = lax.axis_index("space"), lax.axis_index("mp")
        twin = {"mp": 1 - core}
        place = (lambda s: s * cores + core) if per_core or join else (lambda s: s)

        def spot(origin):
            rows = rows_of(out_ref, origin, pixels)
            return cols_of(rows, core, width) if join else rows

        copies = [
            send(cols_of(x_ref, place(peer), width), spot(me), send_sem.at[i - 1], recv_sem.at[i - 1], {"space": peer})
            for i, peer in others("space")
        ]
        if join:
            own_width = cores * width
            own = keep(cols_of(x_ref, me, own_width), rows_of(out_ref, me, pixels), own_sem.at[0])
        else:
            own = keep(cols_of(x_ref, place(me), width), spot(me), own_sem.at[0])
        passed = []
        for step in range(1, lines):
            copies[step - 1].wait_recv()
            if join:
                got = spot(lax.rem(me - step + lines, lines))
                passed.append(send(got, got, pass_sem.at[step - 1], gain_sem.at[step - 1], twin))
        for copy in copies:
            copy.wait_send()
        own.wait()
        for copy in passed:
            copy.wait()

    def peers():
        return line_peers() + (twin_peers() if join else [])

    held = cores * width if join else width
    result = jax.ShapeDtypeStruct((images, lines * pixels, held), source.dtype)
    sems = dma_sems(lines - 1, lines - 1, lines - 1, lines - 1, 1)
    return talk_with(kernel, peers, result, [source], sems, number, riders)


def from_lines(source, per_core, number, riders=()):
    images, line_pixels, width = source.shape
    lines, cores = lax.axis_size("space"), lax.axis_size("mp")
    pixels = line_pixels // lines
    pieces = lines * cores if per_core else lines
    if width % lane != 0 or pixels % 16 != 0:
        part = lax.all_to_all(source, "space", split_axis=1, concat_axis=2, tiled=True)
        if per_core:
            part = part.reshape(images, pixels, lines, 1, width)
            part = lax.all_gather(part, "mp", axis=3, tiled=True)
        return part.reshape(images, pixels, pieces * width), plain_all(riders)

    def kernel(x_ref, out_ref, send_sem, recv_sem, pass_sem, gain_sem, own_sem):
        me, core = lax.axis_index("space"), lax.axis_index("mp")
        place = (lambda s: s * cores + core) if per_core else (lambda s: s)
        twin = {"mp": 1 - core}
        target = cols_of(out_ref, place(me), width)
        copies = [
            send(rows_of(x_ref, peer, pixels), target, send_sem.at[i - 1], recv_sem.at[i - 1], {"space": peer})
            for i, peer in others("space")
        ]
        own = keep(rows_of(x_ref, me, pixels), target, own_sem.at[0])
        passed = []
        if per_core:
            passed.append(send(rows_of(x_ref, me, pixels), target, pass_sem.at[0], gain_sem.at[0], twin))
        for step in range(1, lines):
            copies[step - 1].wait_recv()
            if per_core:
                origin = lax.rem(me - step + lines, lines)
                got = cols_of(out_ref, place(origin), width)
                passed.append(send(got, got, pass_sem.at[step], gain_sem.at[step], twin))
        for copy in copies:
            copy.wait_send()
        own.wait()
        for copy in passed:
            copy.wait()

    def peers():
        return line_peers() + ([{"mp": 1 - lax.axis_index("mp")}] if per_core else [])

    result = jax.ShapeDtypeStruct((images, pixels, pieces * width), source.dtype)
    sems = dma_sems(lines - 1, lines - 1, lines, lines, 1)
    return talk_with(kernel, peers, result, [source], sems, number, riders)


def gather_lines(source, number, riders=()):
    images, line_pixels, width = source.shape
    lines = lax.axis_size("space")
    if width % lane != 0:
        return lax.all_gather(source, "space", axis=2, tiled=True), plain_all(riders)

    def kernel(x_ref, out_ref, send_sem, recv_sem, own_sem):
        me = lax.axis_index("space")
        target = cols_of(out_ref, me, width)
        copies = [
            send(x_ref, target, send_sem.at[i - 1], recv_sem.at[i - 1], {"space": peer})
            for i, peer in others("space")
        ]
        copies.append(keep(x_ref, target, own_sem.at[0]))
        for copy in copies:
            copy.wait()

    result = jax.ShapeDtypeStruct((images, line_pixels, lines * width), source.dtype)
    sems = dma_sems(lines - 1, lines - 1, 1)
    return talk_with(kernel, line_peers, result, [source], sems, number, riders)


def gather_cores(source, number, riders=()):
    images, line_pixels, width = source.shape
    cores = lax.axis_size("mp")
    if width % lane != 0:
        return lax.all_gather(source, "mp", axis=2, tiled=True), plain_all(riders)

    def kernel(x_ref, out_ref, send_sem, recv_sem, own_sem):
        core = lax.axis_index("mp")
        twin = {"mp": 1 - core}
        target = cols_of(out_ref, core, width)
        copy = send(x_ref, target, send_sem.at[0], recv_sem.at[0], twin)
        own = keep(x_ref, target, own_sem.at[0])
        copy.wait()
        own.wait()

    result = jax.ShapeDtypeStruct((images, line_pixels, cores * width), source.dtype)
    return talk_with(kernel, twin_peers, result, [source], dma_sems(1, 1, 1), number, riders)


def sum_lines(source, number, riders=()):
    images, line_pixels, channels = source.shape
    lines = lax.axis_size("space")
    width = channels // lines
    if width % lane != 0:
        total = lax.psum_scatter(source, "space", scatter_dimension=2, tiled=True)
        return total.astype(jnp.float32), plain_all(riders)

    def kernel(x_ref, out_ref, got_ref, send_sem, recv_sem):
        me = lax.axis_index("space")
        copies = [
            send(cols_of(x_ref, peer, width), got_ref.at[i - 1], send_sem.at[i - 1], recv_sem.at[i - 1], {"space": peer})
            for i, peer in others("space")
        ]
        mine = pl.ds(pl.multiple_of(me * width, width), width)
        for copy in copies:
            copy.wait()
        for image in range(images):
            total = x_ref[image, :, mine].astype(jnp.float32)
            for step in range(lines - 1):
                total = total + got_ref[step, image].astype(jnp.float32)
            out_ref[image] = total

    result = jax.ShapeDtypeStruct((images, line_pixels, width), jnp.float32)
    scratch = [pltpu.VMEM((lines - 1, images, line_pixels, width), source.dtype)]
    scratch = scratch + dma_sems(lines - 1, lines - 1)
    return talk_with(
        kernel, line_peers, result, [source], scratch, number, riders, [VMEM], VMEM
    )


def sum_cores(source, number, riders=()):
    images, line_pixels, channels = source.shape
    cores = lax.axis_size("mp")
    width = channels // cores
    if width % lane != 0:
        total = lax.psum_scatter(source, "mp", scatter_dimension=2, tiled=True)
        return total.astype(jnp.float32), plain_all(riders)

    def kernel(x_ref, out_ref, got_ref, send_sem, recv_sem):
        core = lax.axis_index("mp")
        twin = {"mp": 1 - core}
        copy = send(cols_of(x_ref, 1 - core, width), got_ref, send_sem.at[0], recv_sem.at[0], twin)
        mine = pl.ds(pl.multiple_of(core * width, width), width)
        copy.wait()
        for image in range(images):
            out_ref[image] = x_ref[image, :, mine].astype(jnp.float32) + got_ref[image].astype(
                jnp.float32
            )

    result = jax.ShapeDtypeStruct((images, line_pixels, width), jnp.float32)
    scratch = [pltpu.VMEM((images, line_pixels, width), source.dtype)]
    scratch = scratch + dma_sems(1, 1)
    return talk_with(
        kernel, twin_peers, result, [source], scratch, number, riders, [VMEM], VMEM
    )


def gather_tokens(rows, number, riders=()):
    count, channels = rows.shape
    lines, cores = lax.axis_size("space"), lax.axis_size("mp")
    width = channels // cores
    source = rows.reshape(1, count, channels)

    def kernel(x_ref, out_ref, send_sem, recv_sem, pass_sem, gain_sem, own_sem):
        me, core = lax.axis_index("space"), lax.axis_index("mp")
        twin = {"mp": 1 - core}

        def spot(origin):
            return cols_of(rows_of(out_ref, origin, count), core, width)

        copies = [
            send(cols_of(x_ref, core, width), spot(me), send_sem.at[i - 1], recv_sem.at[i - 1], {"space": peer})
            for i, peer in others("space")
        ]
        own = keep(x_ref, rows_of(out_ref, me, count), own_sem.at[0])
        passed = []
        for step in range(1, lines):
            copies[step - 1].wait_recv()
            got = spot(lax.rem(me - step + lines, lines))
            passed.append(send(got, got, pass_sem.at[step - 1], gain_sem.at[step - 1], twin))
        for copy in copies:
            copy.wait_send()
        own.wait()
        for copy in passed:
            copy.wait()

    result = jax.ShapeDtypeStruct((1, lines * count, channels), rows.dtype)
    sems = dma_sems(lines - 1, lines - 1, lines - 1, lines - 1, 1)

    def peers():
        return line_peers() + twin_peers()

    line, others_done = talk_with(kernel, peers, result, [source], sems, number, riders)
    return line.reshape(lines * count, channels), others_done


def scatter_tokens(partial_sum, number, riders=()):
    all_rows, channels = partial_sum.shape
    lines, cores = lax.axis_size("space"), lax.axis_size("mp")
    count, width = all_rows // lines, channels // cores
    source = partial_sum.astype(jnp.bfloat16).reshape(lines, count, channels)

    def kernel(x_ref, out_ref, twin_ref, sum_ref, got_ref, s_sem, r_sem, s2_sem, r2_sem, s3_sem, r3_sem):
        me, core = lax.axis_index("space"), lax.axis_index("mp")
        twin = {"mp": 1 - core}
        theirs = pl.ds(pl.multiple_of((1 - core) * width, width), width)
        mine = pl.ds(pl.multiple_of(core * width, width), width)
        order = [(i, peer) for i, peer in others("space")] + [(0, me)]
        first = [
            send(x_ref.at[target, :, theirs], twin_ref.at[i], s_sem.at[i], r_sem.at[i], twin)
            for i, target in order
        ]
        second = []
        for (i, target), copy in zip(order, first):
            copy.wait_recv()
            total = x_ref[target, :, mine].astype(jnp.float32) + twin_ref[i].astype(jnp.float32)
            if i == 0:
                own = total
            else:
                sum_ref[i - 1] = total.astype(jnp.bfloat16)
                second.append(
                    send(sum_ref.at[i - 1], got_ref.at[i - 1], s2_sem.at[i - 1], r2_sem.at[i - 1], {"space": target})
                )
        for copy in second:
            copy.wait_recv()
        for i in range(lines - 1):
            own = own + got_ref[i].astype(jnp.float32)
        out_ref[:, mine] = own.astype(jnp.bfloat16)
        third = send(out_ref.at[:, mine], out_ref.at[:, mine], s3_sem.at[0], r3_sem.at[0], twin)
        for copy in first + second:
            copy.wait_send()
        third.wait()

    result = jax.ShapeDtypeStruct((count, channels), jnp.bfloat16)
    scratch = [
        pltpu.VMEM((lines, count, width), jnp.bfloat16),
        pltpu.VMEM((max(lines - 1, 1), count, width), jnp.bfloat16),
        pltpu.VMEM((max(lines - 1, 1), count, width), jnp.bfloat16),
    ]
    sems = dma_sems(lines, lines, lines - 1, lines - 1, 1, 1)

    def peers():
        return line_peers() + [{"mp": 1 - lax.axis_index("mp")}]

    total, other = talk_with(
        kernel, peers, result, [source], scratch + sems, number, riders, [VMEM], VMEM
    )
    return total, other


def to_clips(source, number, riders=()):
    slots, frames, pixels, channels = source.shape
    count = lax.axis_size("tm")
    few = pixels // count
    if few % 16 != 0:
        return lax.all_to_all(source, "tm", split_axis=2, concat_axis=1, tiled=True), plain_all(riders)

    def kernel(x_ref, out_ref, send_sem, recv_sem, own_sem):
        me = lax.axis_index("tm")
        target = out_ref.at[:, pl.ds(me * frames, frames)]

        def part(index):
            return x_ref.at[:, :, pl.ds(pl.multiple_of(index * few, few), few)]

        copies = [
            send(part(peer), target, send_sem.at[i - 1], recv_sem.at[i - 1], {"tm": peer})
            for i, peer in others("tm")
        ]
        copies.append(keep(part(me), target, own_sem.at[0]))
        for copy in copies:
            copy.wait()

    result = jax.ShapeDtypeStruct((slots, count * frames, few, channels), source.dtype)
    sems = dma_sems(count - 1, count - 1, 1)
    return talk_with(kernel, frame_peers, result, [source], sems, number, riders)


def from_clips(source, number, riders=()):
    slots, all_frames, few, channels = source.shape
    count = lax.axis_size("tm")
    frames = all_frames // count
    if few % 16 != 0:
        return lax.all_to_all(source, "tm", split_axis=1, concat_axis=2, tiled=True), plain_all(riders)

    def kernel(x_ref, out_ref, send_sem, recv_sem, own_sem):
        me = lax.axis_index("tm")
        target = out_ref.at[:, :, pl.ds(pl.multiple_of(me * few, few), few)]

        def part(index):
            return x_ref.at[:, pl.ds(index * frames, frames)]

        copies = [
            send(part(peer), target, send_sem.at[i - 1], recv_sem.at[i - 1], {"tm": peer})
            for i, peer in others("tm")
        ]
        copies.append(keep(part(me), target, own_sem.at[0]))
        for copy in copies:
            copy.wait()

    result = jax.ShapeDtypeStruct((slots, frames, count * few, channels), source.dtype)
    sems = dma_sems(count - 1, count - 1, 1)
    return talk_with(kernel, frame_peers, result, [source], sems, number, riders)


def by_owner_line(source, owners, lines):
    parts = source.reshape(source.shape[:-1] + (owners // lines, lines, -1))
    return parts.swapaxes(-3, -2).reshape(source.shape)


def by_frames(weight_grad):
    return FrameSum(weight_grad.reshape(lax.axis_size("tm"), -1, weight_grad.shape[1]))


def padded_rims(source):
    return jnp.pad(source, ((0, 0), (0, 0), (1, 1), (1, 1), (0, 0)))


def conv_weight(weight):
    return weight.reshape(weight.shape[0], 3, 3, weight.shape[2])


def conv_frames(source, weight, spec, flipped):
    images = source.reshape((-1,) + source.shape[2:])
    kernel = conv_weight(weight)
    if flipped:
        kernel = kernel[:, ::-1, ::-1]
    result = lax.conv_general_dilated(
        images,
        kernel,
        (1, 1),
        "SAME",
        dimension_numbers=("NHWC", spec, "NHWC"),
        preferred_element_type=jnp.float32,
    )
    return result.reshape(source.shape[:4] + (result.shape[-1],))


def conv_weight_grad(source, upstream, form):
    padded = padded_rims(source)
    rows, cols = source.shape[2], source.shape[3]
    tap_list = []
    for tap in range(9):
        i, j = tap // 3, tap % 3
        tap_list.append(
            jnp.einsum(
                "bfhwc,bfhwk->" + form,
                padded[:, :, i : i + rows, j : j + cols],
                upstream,
                preferred_element_type=jnp.float32,
            ).astype(jnp.bfloat16)
        )
    return jnp.stack(tap_list)


def sinusoid(steps_int):
    counted = D // 2
    freqs = jnp.exp(-math.log(10000.0) * jnp.arange(counted, dtype=jnp.float32) / counted)
    angles = steps_int.astype(jnp.float32)[..., None] * freqs
    return jnp.concatenate([jnp.sin(angles), jnp.cos(angles)], axis=-1)


def offset_onehot(query_start, query_count, key_count):
    distance = (
        query_start
        + jnp.arange(query_count, dtype=jnp.int32)[:, None]
        - jnp.arange(key_count, dtype=jnp.int32)[None, :]
    )
    position = jnp.clip(distance, -(R // 2), R // 2 - 1) + R // 2
    return (position[:, :, None] == jnp.arange(R, dtype=jnp.int32)[None, None, :]).astype(
        jnp.float32
    )


def local(kernel, results, operands, grid, in_specs, out_specs, scratch=()):
    return pl.pallas_call(
        kernel,
        out_shape=results,
        grid=grid,
        in_specs=in_specs,
        out_specs=out_specs,
        scratch_shapes=list(scratch),
        compiler_params=pltpu.CompilerParams(vmem_limit_bytes=48 * 1024 * 1024),
    )(*operands)


def dot(a, b):
    return jnp.dot(a, b, preferred_element_type=jnp.float32)


def dot_nt(a, b):
    return lax.dot_general(a, b, (((1,), (1,)), ((), ())), preferred_element_type=jnp.float32)


def dot_tn(a, b):
    return lax.dot_general(a, b, (((0,), (0,)), ((), ())), preferred_element_type=jnp.float32)


def low(value):
    return value.astype(jnp.bfloat16)


def head_probs(query, key, bias, valid):
    scores = dot_nt(query, key) * (1.0 / math.sqrt(HDIM))
    if bias is not None:
        scores = scores + bias
    if valid is not None:
        scores = jnp.where(valid, scores, masked)
    expos = jnp.exp(scores - jnp.max(scores, axis=-1, keepdims=True))
    return expos / jnp.sum(expos, axis=-1, keepdims=True)


def head_forward(query, key, value, bias, valid):
    return dot(low(head_probs(query, key, bias, valid)), value)


def head_backward(query, key, value, bias, valid, upstream):
    probs = head_probs(query, key, bias, valid)
    prob_grad = dot_nt(upstream, value)
    inner = jnp.sum(probs * prob_grad, axis=-1, keepdims=True)
    score_grad = low(probs * (prob_grad - inner))
    scale = 1.0 / math.sqrt(HDIM)
    return (
        dot(score_grad, key) * scale,
        dot_tn(score_grad, query) * scale,
        dot_tn(low(probs), upstream),
        score_grad,
    )


def norm_forward(source, gain):
    centered = source - jnp.mean(source, axis=-1, keepdims=True)
    variance = jnp.mean(centered * centered, axis=-1, keepdims=True)
    return centered * lax.rsqrt(variance + epsilon) * gain


def norm_backward(source, gain, upstream):
    centered = source - jnp.mean(source, axis=-1, keepdims=True)
    variance = jnp.mean(centered * centered, axis=-1, keepdims=True)
    inverse = lax.rsqrt(variance + epsilon)
    normal = centered * inverse
    gain_grad = jnp.sum(upstream * normal, axis=0, keepdims=True)
    scaled = upstream * gain
    first = jnp.mean(scaled, axis=-1, keepdims=True)
    second = jnp.mean(scaled * normal, axis=-1, keepdims=True)
    return inverse * (scaled - first - normal * second), gain_grad


def in_weight(halves, index):
    per = halves[0].shape[0] // 4
    return jnp.concatenate(
        [
            jnp.concatenate([half[t, s] for half in halves for s in range(half.shape[1])], axis=0)
            for t in range(index * per, (index + 1) * per)
        ],
        axis=1,
    )


def out_weight(halves, index):
    frames, width = halves[0].shape[0], halves[0].shape[3] // 3
    cols = slice(index * width, (index + 1) * width)
    return jnp.concatenate(
        [
            jnp.concatenate([half[t, s, :, cols] for t in range(frames)], axis=0)
            for half in halves
            for s in range(half.shape[1])
        ],
        axis=1,
    )


def spatial_forward(rows, weight):
    lines, images, pixels, channels = rows.shape
    width = weight.shape[2]
    count = lines * pixels

    def kernel(x_ref, w_ref, triple_ref, mix_ref):
        x = x_ref[...].reshape(count, channels)
        for j in range(3):
            triple_ref[0, j] = low(dot(x, w_ref[j]))
        for head in range(width // HDIM):
            cols = slice(head * HDIM, (head + 1) * HDIM)
            query, key, value = (triple_ref[0, j, :, cols] for j in range(3))
            mix_ref[0, :, cols] = low(head_forward(query, key, value, None, None))

    return local(
        kernel,
        (
            jax.ShapeDtypeStruct((images, 3, count, width), jnp.bfloat16),
            jax.ShapeDtypeStruct((images, count, width), jnp.bfloat16),
        ),
        (rows, weight),
        (images,),
        [
            pl.BlockSpec((lines, 1, pixels, channels), lambda i: (0, i, 0, 0)),
            pl.BlockSpec(weight.shape, lambda i: (0, 0, 0)),
        ],
        (
            pl.BlockSpec((1, 3, count, width), lambda i: (i, 0, 0, 0)),
            pl.BlockSpec((1, count, width), lambda i: (i, 0, 0)),
        ),
    )


def spatial_backward(rows, weight, triple, upstream):
    lines, images, pixels, channels = rows.shape
    width = weight.shape[2]
    count = lines * pixels

    def kernel(x_ref, w_ref, triple_ref, up_ref, grad_ref, dw_ref, grads_ref, total_ref):
        step = pl.program_id(0)
        x = x_ref[...].reshape(count, channels)
        for head in range(width // HDIM):
            cols = slice(head * HDIM, (head + 1) * HDIM)
            query, key, value = (triple_ref[0, j, :, cols] for j in range(3))
            grads = head_backward(query, key, value, None, None, up_ref[0, :, cols])
            for j in range(3):
                grads_ref[j, :, cols] = low(grads[j])
        part = dot_nt(grads_ref[0], w_ref[0])
        part = part + dot_nt(grads_ref[1], w_ref[1])
        part = part + dot_nt(grads_ref[2], w_ref[2])
        grad_ref[...] = low(part).reshape(lines, 1, pixels, channels)

        @pl.when(step == 0)
        def _():
            total_ref[...] = jnp.zeros_like(total_ref)

        for j in range(3):
            total_ref[j] += dot_tn(x, grads_ref[j])

        @pl.when(step == images - 1)
        def _():
            for j in range(3):
                dw_ref[:, j * width : (j + 1) * width] = low(total_ref[j])

    return local(
        kernel,
        (
            jax.ShapeDtypeStruct((lines, images, pixels, channels), jnp.bfloat16),
            jax.ShapeDtypeStruct((channels, 3 * width), jnp.bfloat16),
        ),
        (rows, weight, triple, upstream),
        (images,),
        [
            pl.BlockSpec((lines, 1, pixels, channels), lambda i: (0, i, 0, 0)),
            pl.BlockSpec(weight.shape, lambda i: (0, 0, 0)),
            pl.BlockSpec((1, 3, count, width), lambda i: (i, 0, 0, 0)),
            pl.BlockSpec((1, count, width), lambda i: (i, 0, 0)),
        ],
        (
            pl.BlockSpec((lines, 1, pixels, channels), lambda i: (0, i, 0, 0)),
            pl.BlockSpec((channels, 3 * width), lambda i: (0, 0)),
        ),
        [
            pltpu.VMEM((3, count, width), jnp.bfloat16),
            pltpu.VMEM((3, channels, width), jnp.float32),
        ],
    )


def dot_exact(a, b):
    return jnp.dot(a, b, preferred_element_type=jnp.float32, precision=highest)


def clip_masks(rows, few, ids_ref, turned_ref):
    across = lax.broadcasted_iota(jnp.int32, (rows, rows), 1)
    down = lax.broadcasted_iota(jnp.int32, (rows, rows), 0)
    return (lax.rem(across, few) == lax.rem(down, few)) & (ids_ref[0] == turned_ref[0])


def temporal_forward(clip, bias, ids, few):
    slots, rows, triple = clip.shape
    width = triple // 3

    def kernel(x_ref, bias_ref, ids_ref, turned_ref, mix_ref):
        valid = clip_masks(rows, few, ids_ref, turned_ref)
        for head in range(width // HDIM):
            at = head * HDIM
            query, key, value = (
                x_ref[0, :, j * width + at : j * width + at + HDIM] for j in range(3)
            )
            mix = head_forward(query, key, value, bias_ref[head], valid)
            mix_ref[0, :, at : at + HDIM] = low(mix)

    return local(
        kernel,
        jax.ShapeDtypeStruct((slots, rows, width), jnp.bfloat16),
        (clip, bias, ids[:, :, None], ids[:, None, :]),
        (slots,),
        [
            pl.BlockSpec((1, rows, triple), lambda i: (i, 0, 0)),
            pl.BlockSpec(bias.shape, lambda i: (0, 0, 0)),
            pl.BlockSpec((1, rows, 1), lambda i: (i, 0, 0)),
            pl.BlockSpec((1, 1, rows), lambda i: (i, 0, 0)),
        ],
        pl.BlockSpec((1, rows, width), lambda i: (i, 0, 0)),
    )


def temporal_backward(clip, bias, ids, few, upstream):
    slots, rows, triple = clip.shape
    width = triple // 3
    frames = rows // few

    def kernel(x_ref, bias_ref, ids_ref, turned_ref, up_ref, grad_ref, score_ref):
        step = pl.program_id(0)
        valid = clip_masks(rows, few, ids_ref, turned_ref)
        frame = lax.broadcasted_iota(jnp.int32, (frames, rows), 0)
        row = lax.broadcasted_iota(jnp.int32, (frames, rows), 1)
        gather = low((row // few == frame).astype(jnp.float32))

        @pl.when(step == 0)
        def _():
            score_ref[...] = jnp.zeros_like(score_ref)

        for head in range(width // HDIM):
            at = head * HDIM
            query, key, value = (
                x_ref[0, :, j * width + at : j * width + at + HDIM] for j in range(3)
            )
            grads = head_backward(
                query, key, value, bias_ref[head], valid, up_ref[0, :, at : at + HDIM]
            )
            for j in range(3):
                grad_ref[0, :, j * width + at : j * width + at + HDIM] = low(grads[j])
            score_ref[head] += dot(gather, grads[3])

    return local(
        kernel,
        (
            jax.ShapeDtypeStruct((slots, rows, triple), jnp.bfloat16),
            jax.ShapeDtypeStruct((bias.shape[0], frames, rows), jnp.float32),
        ),
        (clip, bias, ids[:, :, None], ids[:, None, :], upstream),
        (slots,),
        [
            pl.BlockSpec((1, rows, triple), lambda i: (i, 0, 0)),
            pl.BlockSpec(bias.shape, lambda i: (0, 0, 0)),
            pl.BlockSpec((1, rows, 1), lambda i: (i, 0, 0)),
            pl.BlockSpec((1, 1, rows), lambda i: (i, 0, 0)),
            pl.BlockSpec((1, rows, width), lambda i: (i, 0, 0)),
        ],
        (
            pl.BlockSpec((1, rows, triple), lambda i: (i, 0, 0)),
            pl.BlockSpec((bias.shape[0], frames, rows), lambda i: (0, 0, 0)),
        ),
    )


def gelu_pair(upper):
    rate = math.sqrt(2.0 / math.pi)
    square = upper * upper
    bend = jnp.tanh(rate * (upper + 0.044715 * square * upper))
    half = 0.5 * (1.0 + bend)
    slope = half + 0.5 * upper * (1.0 - bend * bend) * rate * (1.0 + 3.0 * 0.044715 * square)
    return upper * half, slope


def feed_both(rows, cot, w_in, w_out):
    lines, count, channels = rows.shape
    hidden = w_in.shape[1]

    def kernel(x_ref, cot_ref, in_ref, out_ref, y_ref, grad_ref, dw_ref, first_ref, second_ref):
        step = pl.program_id(0)
        x, up = x_ref[0], cot_ref[0]
        active, slope = gelu_pair(dot(x, in_ref[...]))
        active = low(active)
        upper_grad = low(dot_nt(up, out_ref[...]) * slope)
        y_ref[0] = low(dot(active, out_ref[...]))
        grad_ref[0] = low(dot_nt(upper_grad, in_ref[...]))

        @pl.when(step == 0)
        def _():
            first_ref[...] = dot_tn(x, upper_grad)
            second_ref[...] = dot_tn(up, active)

        @pl.when(step > 0)
        def _():
            first_ref[...] += dot_tn(x, upper_grad)
            second_ref[...] += dot_tn(up, active)

        @pl.when(step == lines - 1)
        def _():
            dw_ref[:, :hidden] = low(first_ref[...])
            dw_ref[:, hidden:] = low(second_ref[...])

    block = pl.BlockSpec((1, count, channels), lambda i: (i, 0, 0))
    return local(
        kernel,
        (
            jax.ShapeDtypeStruct(rows.shape, jnp.bfloat16),
            jax.ShapeDtypeStruct(rows.shape, jnp.bfloat16),
            jax.ShapeDtypeStruct((channels, 2 * hidden), jnp.bfloat16),
        ),
        (rows, cot, w_in, w_out),
        (lines,),
        [
            block,
            block,
            pl.BlockSpec(w_in.shape, lambda i: (0, 0)),
            pl.BlockSpec(w_out.shape, lambda i: (0, 0)),
        ],
        (block, block, pl.BlockSpec((channels, 2 * hidden), lambda i: (0, 0))),
        [
            pltpu.VMEM((channels, hidden), jnp.float32),
            pltpu.VMEM((channels, hidden), jnp.float32),
        ],
    )


def twin_sum(partial_sum, mine_ref, theirs_ref, send_sem, recv_sem, work=None):
    mine_ref[...] = low(partial_sum)
    copy = send(mine_ref, theirs_ref, send_sem, recv_sem, {"mp": 1 - lax.axis_index("mp")})
    if work is not None:
        work()
    copy.wait()
    return mine_ref[...].astype(jnp.float32) + theirs_ref[...].astype(jnp.float32)


def chat(kernel, results, operands, rows, channels, swaps, number, scratch=()):
    own = [
        pltpu.VMEM((swaps, rows, channels), jnp.bfloat16),
        pltpu.VMEM((swaps, rows, channels), jnp.bfloat16),
    ] + dma_sems(swaps, swaps)
    count = len(operands) + len(results)

    def whole(*refs):
        mine_ref, theirs_ref, send_sem, recv_sem = refs[count : count + 4]
        meet(twin_peers())

        def swap(index, partial_sum, work=None):
            return twin_sum(
                partial_sum,
                mine_ref.at[index],
                theirs_ref.at[index],
                send_sem.at[index],
                recv_sem.at[index],
                work,
            )

        kernel(swap, *refs[:count], *refs[count + 4 :])

    return talk(
        whole,
        tuple(results),
        operands,
        own + list(scratch),
        number,
        [VMEM] * len(operands),
        tuple([VMEM] * len(results)),
    )


def group_means(totals, count):
    channels = totals.shape[1]
    down = lax.broadcasted_iota(jnp.int32, (channels, channels), 0)
    across = lax.broadcasted_iota(jnp.int32, (channels, channels), 1)
    size = D // G
    same = (down // size == across // size).astype(jnp.float32)
    return dot_exact(totals, same) * (1.0 / (count * size))


def group_normal(source):
    count = source.shape[0]
    centered = source - group_means(jnp.sum(source, axis=0, keepdims=True), count)
    spread = group_means(jnp.sum(centered * centered, axis=0, keepdims=True), count)
    inverse = lax.rsqrt(spread + epsilon)
    return centered * inverse, inverse


def group_step(upstream, normal, inverse):
    count = upstream.shape[0]
    first = group_means(jnp.sum(upstream, axis=0, keepdims=True), count)
    second = group_means(jnp.sum(upstream * normal, axis=0, keepdims=True), count)
    return inverse * (upstream - first - normal * second)


def silu(value):
    return value * jax.nn.sigmoid(value)


def silu_slope(value):
    gate = jax.nn.sigmoid(value)
    return gate * (1.0 + value * (1.0 - gate))


def image_block(shape):
    return pl.BlockSpec((1,) + shape[1:], lambda i: (i, 0, 0))


def group_forward(source, scale, shift):
    def kernel(x_ref, scale_ref, shift_ref, out_ref):
        normal, _ = group_normal(x_ref[0].astype(jnp.float32))
        out_ref[0] = low(silu(normal * scale_ref[0] + shift_ref[0]))

    return local(
        kernel,
        jax.ShapeDtypeStruct(source.shape, jnp.bfloat16),
        (source, scale, shift),
        (source.shape[0],),
        [image_block(source.shape), image_block(scale.shape), image_block(shift.shape)],
        image_block(source.shape),
    )


def group_backward(source, scale, shift, upstream):
    def kernel(x_ref, scale_ref, shift_ref, up_ref, grad_ref, scale_grad_ref, shift_grad_ref):
        normal, inverse = group_normal(x_ref[0].astype(jnp.float32))
        grad = up_ref[0] * silu_slope(normal * scale_ref[0] + shift_ref[0])
        scale_grad_ref[0] = jnp.sum(grad * normal, axis=0, keepdims=True)
        shift_grad_ref[0] = jnp.sum(grad, axis=0, keepdims=True)
        grad_ref[0] = low(group_step(grad * scale_ref[0], normal, inverse))

    return local(
        kernel,
        (
            jax.ShapeDtypeStruct(source.shape, jnp.bfloat16),
            jax.ShapeDtypeStruct(scale.shape, jnp.float32),
            jax.ShapeDtypeStruct(shift.shape, jnp.float32),
        ),
        (source, scale, shift, upstream),
        (source.shape[0],),
        [
            image_block(source.shape),
            image_block(scale.shape),
            image_block(shift.shape),
            image_block(upstream.shape),
        ],
        (image_block(source.shape), image_block(scale.shape), image_block(shift.shape)),
    )


def flat_call(kernel, results, operands):
    return pl.pallas_call(
        kernel,
        out_shape=tuple(results),
        in_specs=[VMEM] * len(operands),
        out_specs=tuple([VMEM] * len(results)),
        compiler_params=pltpu.CompilerParams(vmem_limit_bytes=48 * 1024 * 1024),
    )(*operands)


def store_both(both_ref, value, owners, lines):
    both_ref[0] = value
    if (value.shape[1] // owners) % HDIM != 0:
        return
    size = value.shape[1] // owners
    frames = owners // lines
    both_ref[1] = jnp.concatenate(
        [
            value[:, (t * lines + s) * size : (t * lines + s + 1) * size]
            for s in range(lines)
            for t in range(frames)
        ],
        axis=1,
    )


def both_orders(rows, owners, lines):
    if (rows.shape[1] // owners) % HDIM != 0:
        return jnp.stack([rows, by_owner_line(rows, owners, lines)])

    def kernel(x_ref, both_ref):
        store_both(both_ref, x_ref[...], owners, lines)

    return flat_call(kernel, [jax.ShapeDtypeStruct((2,) + rows.shape, rows.dtype)], [rows])[0]


def first_norm(rows, branch, gain):
    def kernel(x_ref, branch_ref, gain_ref, one_ref, normed_ref):
        one = x_ref[...].astype(jnp.float32) + branch_ref[...].astype(jnp.float32)
        one_ref[...] = one
        normed_ref[...] = low(norm_forward(one, gain_ref[...]))

    return flat_call(
        kernel,
        [
            jax.ShapeDtypeStruct(rows.shape, jnp.float32),
            jax.ShapeDtypeStruct(rows.shape, jnp.bfloat16),
        ],
        [rows, branch, gain],
    )


def first_norm_backward(stream, gain, normed_grad, upstream, owners, lines):
    def kernel(x_ref, gain_ref, normed_ref, up_ref, grad_ref, both_ref, dg_ref):
        step, gain_grad = norm_backward(
            x_ref[...], gain_ref[...], normed_ref[...].astype(jnp.float32)
        )
        grad = up_ref[...] + step
        grad_ref[...] = grad
        dg_ref[...] = gain_grad
        store_both(both_ref, low(grad), owners, lines)

    grad, both, gain_grad = flat_call(
        kernel,
        [
            jax.ShapeDtypeStruct(stream.shape, jnp.float32),
            jax.ShapeDtypeStruct((2,) + stream.shape, jnp.bfloat16),
            jax.ShapeDtypeStruct(gain.shape, jnp.float32),
        ],
        [stream, gain, normed_grad, upstream],
    )
    if (stream.shape[1] // owners) % HDIM != 0:
        both = jnp.stack([both[0], by_owner_line(both[0], owners, lines)])
    return grad, both, gain_grad


def middle_forward(mix, stream, out_halves, in_halves, pairs, valid, gains, number):
    rows, channels = stream.shape
    width = mix.shape[1]
    slots = pairs.shape[0]
    part = rows // slots

    def kernel(
        swap, mix_ref, x_ref, out_ref, out_rest, in_ref, in_rest, pairs_ref, valid_ref, gain_ref,
        two_ref, normed_ref, query_ref, cross_ref, three_ref, last_ref, triple_ref,
    ):
        outs, ins = (out_ref, out_rest), (in_ref, in_rest)
        two = x_ref[...] + swap(0, dot(mix_ref[...], out_weight(outs, 0)))
        two_ref[...] = two
        normed_ref[...] = low(norm_forward(two, gain_ref[0:1, :]))
        query_ref[...] = low(dot(normed_ref[...], in_weight(ins, 0)))
        for slot in range(slots):
            here = slice(slot * part, (slot + 1) * part)
            good = valid_ref[slot] > 0.5
            for head in range(width // HDIM):
                at = head * HDIM
                cross = head_forward(
                    query_ref[here, at : at + HDIM],
                    pairs_ref[slot, :, at : at + HDIM],
                    pairs_ref[slot, :, width + at : width + at + HDIM],
                    None,
                    good,
                )
                cross_ref[here, at : at + HDIM] = low(cross)
        three = two_ref[...] + swap(1, dot(cross_ref[...], out_weight(outs, 1)))
        three_ref[...] = three
        last_ref[...] = low(norm_forward(three, gain_ref[1:2, :]))
        for j in range(3):
            triple_ref[:, j * width : (j + 1) * width] = low(dot(last_ref[...], in_weight(ins, 1 + j)))

    wide = jax.ShapeDtypeStruct((rows, channels), jnp.float32)
    wide_low = jax.ShapeDtypeStruct((rows, channels), jnp.bfloat16)
    thin = jax.ShapeDtypeStruct((rows, width), jnp.bfloat16)
    return chat(
        kernel,
        [wide, wide_low, thin, thin, wide, wide_low, jax.ShapeDtypeStruct((rows, 3 * width), jnp.bfloat16)],
        [mix, stream, *out_halves, *in_halves, pairs, valid, gains],
        rows,
        channels,
        2,
        number,
    )


def late_forward(mix, stream, out_halves, gain, number):
    rows, channels = stream.shape

    def kernel(swap, mix_ref, x_ref, out_ref, out_rest, gain_ref, four_ref, normed_ref):
        four = x_ref[...] + swap(0, dot(mix_ref[...], out_weight((out_ref, out_rest), 2)))
        four_ref[...] = four
        normed_ref[...] = low(norm_forward(four, gain_ref[...]))

    return chat(
        kernel,
        [
            jax.ShapeDtypeStruct((rows, channels), jnp.float32),
            jax.ShapeDtypeStruct((rows, channels), jnp.bfloat16),
        ],
        [mix, stream, *out_halves, gain],
        rows,
        channels,
        1,
        number,
    )


def late_backward(cot, normed_grad, stream, gain, mix, out_halves):
    rows, channels = stream.shape
    width = mix.shape[1]

    def kernel(
        cot_ref, up_ref, x_ref, gain_ref, mix_ref, out_ref, out_rest, grad_ref, mix_grad_ref, dw_ref, dg_ref
    ):
        step, gain_grad = norm_backward(
            x_ref[...], gain_ref[...], up_ref[...].astype(jnp.float32)
        )
        grad = cot_ref[...].astype(jnp.float32) + step
        grad_ref[...] = grad
        dg_ref[...] = gain_grad
        branch = low(grad)
        mix_grad_ref[...] = low(dot_nt(branch, out_weight((out_ref, out_rest), 2)))
        dw_ref[...] = low(dot_tn(branch, mix_ref[...]))

    return pl.pallas_call(
        kernel,
        out_shape=(
            jax.ShapeDtypeStruct((rows, channels), jnp.float32),
            jax.ShapeDtypeStruct((rows, width), jnp.bfloat16),
            jax.ShapeDtypeStruct((channels, width), jnp.bfloat16),
            jax.ShapeDtypeStruct((1, channels), jnp.float32),
        ),
        in_specs=[VMEM] * 7,
        out_specs=tuple([VMEM] * 4),
        compiler_params=pltpu.CompilerParams(vmem_limit_bytes=48 * 1024 * 1024),
    )(cot, normed_grad, stream, gain, mix, *out_halves)


def middle_backward(
    triple, upstream, three, two, last, normed, query, cross, mix, out_halves, in_halves, pairs, valid, gains, number
):
    rows, channels = three.shape
    width = mix.shape[1]
    slots, keys = pairs.shape[0], pairs.shape[1]
    part = rows // slots

    def kernel(
        swap, triple_ref, up_ref, three_ref, two_ref, last_ref, normed_ref, query_ref, cross_ref, mix_ref,
        out_ref, out_rest, in_ref, in_rest, pairs_ref, valid_ref, gain_ref,
        grad_ref, mix_grad_ref, pair_grad_ref, query_dw_ref, pair_dw_ref, cross_dw_ref, outs_dw_ref, dg_ref,
        cross_up_ref, dq_ref,
    ):
        outs, ins = (out_ref, out_rest), (in_ref, in_rest)

        def temporal_weights():
            query_dw_ref[...] = low(dot_tn(last_ref[...], triple_ref[:, :width]))
            pair_dw_ref[...] = low(dot_tn(last_ref[...], triple_ref[:, width:]))

        part_sum = dot_nt(triple_ref[:, :width], in_weight(ins, 1))
        part_sum = part_sum + dot_nt(triple_ref[:, width : 2 * width], in_weight(ins, 2))
        part_sum = part_sum + dot_nt(triple_ref[:, 2 * width :], in_weight(ins, 3))
        normed_grad = swap(0, part_sum, temporal_weights)
        step, gain_grad = norm_backward(three_ref[...], gain_ref[1:2, :], normed_grad)
        dg_ref[1:2, :] = gain_grad
        grad = up_ref[...] + step
        grad_ref[...] = grad
        branch = low(grad)
        cross_up_ref[...] = low(dot_nt(branch, out_weight(outs, 1)))
        for slot in range(slots):
            here = slice(slot * part, (slot + 1) * part)
            good = valid_ref[slot] > 0.5
            for head in range(width // HDIM):
                at = head * HDIM
                grads = head_backward(
                    query_ref[here, at : at + HDIM],
                    pairs_ref[slot, :, at : at + HDIM],
                    pairs_ref[slot, :, width + at : width + at + HDIM],
                    None,
                    good,
                    cross_up_ref[here, at : at + HDIM],
                )
                dq_ref[here, at : at + HDIM] = low(grads[0])
                pair_grad_ref[slot, :, at : at + HDIM] = low(grads[1])
                pair_grad_ref[slot, :, width + at : width + at + HDIM] = low(grads[2])

        def cross_weights():
            cross_dw_ref[...] = low(dot_tn(normed_ref[...], dq_ref[...]))
            outs_dw_ref[:, :width] = low(dot_tn(low(grad_ref[...]), cross_ref[...]))

        normed_grad = swap(1, dot_nt(dq_ref[...], in_weight(ins, 0)), cross_weights)
        step, gain_grad = norm_backward(two_ref[...], gain_ref[0:1, :], normed_grad)
        dg_ref[0:1, :] = gain_grad
        grad = grad_ref[...] + step
        grad_ref[...] = grad
        branch = low(grad)
        mix_grad_ref[...] = low(dot_nt(branch, out_weight(outs, 0)))
        outs_dw_ref[:, width:] = low(dot_tn(branch, mix_ref[...]))

    return chat(
        kernel,
        [
            jax.ShapeDtypeStruct((rows, channels), jnp.float32),
            jax.ShapeDtypeStruct((rows, width), jnp.bfloat16),
            jax.ShapeDtypeStruct((slots, keys, 2 * width), jnp.bfloat16),
            jax.ShapeDtypeStruct((channels, width), jnp.bfloat16),
            jax.ShapeDtypeStruct((channels, 2 * width), jnp.bfloat16),
            jax.ShapeDtypeStruct((channels, width), jnp.bfloat16),
            jax.ShapeDtypeStruct((channels, 2 * width), jnp.bfloat16),
            jax.ShapeDtypeStruct((2, channels), jnp.float32),
        ],
        [triple, upstream, three, two, last, normed, query, cross, mix, *out_halves, *in_halves, pairs, valid, gains],
        rows,
        channels,
        2,
        number,
        [pltpu.VMEM((rows, width), jnp.bfloat16), pltpu.VMEM((rows, width), jnp.bfloat16)],
    )


def on_device(
    video,
    cotangent,
    text,
    video_ids,
    timesteps,
    text_lengths,
    group_gain,
    group_bias,
    first_conv,
    film_weight,
    second_conv,
    spatial_norm,
    spatial_qkv,
    spatial_out,
    cross_norm,
    cross_query,
    cross_kv,
    cross_out,
    temporal_norm,
    temporal_qkv,
    temporal_out,
    offset_bias,
    feed_norm,
    feed_in,
    feed_out,
):
    frames_axis, lines, cores = (lax.axis_size(name) for name in ("tm", "space", "mp"))
    slots, frame_dev, row_dev, columns, channels = video.shape
    half_width = first_conv.shape[2]
    head_local = half_width // HDIM
    pixels_dev = row_dev * columns
    frames_all = frame_dev * frames_axis
    token_rows = slots * frame_dev * pixels_dev
    text_local = text.shape[1]
    images = slots * frame_dev
    frame_shape = (-1, frame_dev, H, W)
    everyone = ("tm", "space")
    owners = frames_axis * lines
    line_half = lines // 2
    feed_width = feed_in.shape[1] // lines
    text_rows = slots * text_local

    def wide(source):
        return source.reshape(frame_shape + source.shape[2:])

    out_piece = part_of(jnp.concatenate([spatial_out, cross_out, temporal_out], axis=1), "tm", 0)
    if frames_axis == 4:
        in_piece = jnp.concatenate([cross_query[None], temporal_qkv.transpose(1, 0, 2)], axis=0)
        in_piece = lax.dynamic_index_in_dim(in_piece, lax.axis_index("tm"), 0, keepdims=False)
    else:
        in_piece = jnp.concatenate([cross_query, temporal_qkv.reshape(-1, 3 * half_width)], axis=1)
        in_piece = part_of(in_piece, "tm", 1)
    qkv_piece = part_of(spatial_qkv.transpose(1, 0, 2), "tm", 1)
    qkv_piece = qkv_piece.reshape(3, -1, lines, half_width // lines).transpose(2, 0, 1, 3)
    in_quarter = part_of(feed_in, "tm", 0)
    in_quarter = in_quarter.reshape(-1, lines, feed_width).transpose(1, 0, 2)
    out_quarter = part_of(feed_out.reshape(lines, feed_width, -1), "tm", 1)
    cot_rows = cotangent.reshape(token_rows, channels)
    text_flat = text.reshape(text_rows, -1)
    cross_kv = cross_kv.reshape(cross_kv.shape[0], -1)

    video_rows = video.reshape(token_rows, channels)
    in_groups = (channels // owners) % (D // G) == 0
    video_both = both_orders(video_rows, owners, lines) if in_groups else video_rows
    video_lines, (text_line, qkv_piece, out_piece) = to_lines(
        video_both.reshape(-1, pixels_dev, channels),
        True,
        1,
        [
            LineColumns(text_flat),
            Exchange(qkv_piece, ("space",)),
            Share(out_piece, ("space",)),
        ],
    )

    def line_gains(whole):
        own = part_of(part_of(whole, "space", 0), "mp", 0)
        if not in_groups:
            return jnp.broadcast_to(own, (images, 1, own.shape[0]))
        owned = part_of(part_of(by_owner_line(whole, owners, lines), "space", 0), "mp", 0)
        return jnp.repeat(jnp.stack([own, owned]), images, axis=0)[:, None]

    gain_line, bias_line = line_gains(group_gain), line_gains(group_bias)
    first_in = group_forward(video_lines, gain_line, bias_line)
    text_part = jnp.dot(
        text_line.reshape(lines * text_rows, -1), cross_kv, preferred_element_type=jnp.float32
    )
    text_part = text_part.astype(jnp.bfloat16).reshape(lines, text_rows, -1)
    first_in, (text_part, in_piece) = gather_cores(
        first_in, 3, [Exchange(text_part, ("space",)), Share(in_piece, ("space",))]
    )
    if in_groups:
        first_in, first_owned = first_in[:images], first_in[images:]
    else:
        blocks = first_in.reshape(first_in.shape[:2] + (-1, lines, channels // owners))
        blocks = blocks.swapaxes(2, 3).reshape(first_in.shape)
        first_owned = lax.all_to_all(blocks, "space", split_axis=2, concat_axis=2, tiled=True)
    text_part = jnp.sum(text_part.astype(jnp.float32), axis=0).astype(jnp.bfloat16)
    hidden_part = conv_frames(wide(first_in), first_conv, "IHWO", False).astype(jnp.bfloat16)
    hidden, (out_first, text_part) = sum_lines(
        hidden_part.reshape(images, H * W, half_width),
        4,
        [Share(out_piece, ("tm",), 0, line_half), Share(text_part, ("space",))],
    )

    embed = sinusoid(timesteps).astype(jnp.bfloat16)
    film_part = jnp.einsum(
        "bvc,cjk->bvjk", part_of(embed, "space", 2), film_weight, preferred_element_type=jnp.float32
    )
    film = lax.psum_scatter(film_part, "space", scatter_dimension=3, tiled=True)
    frame_ids = part_of(video_ids, "tm", 1)
    choose = (frame_ids[:, :, None] == jnp.arange(VIDS, dtype=jnp.int32)[None, None, :]).astype(
        jnp.float32
    )
    frame_film = jnp.einsum("bfv,bvjk->jbfk", choose, film, precision=highest)
    frame_film = frame_film.reshape(2, images, 1, -1)
    film_scale, film_shift = 1.0 + frame_film[0], frame_film[1]
    second_in = group_forward(hidden, film_scale, film_shift)
    second_wide, (text_pairs, in_first) = gather_lines(
        second_in, 5, [Share(text_part, ("tm",)), Share(in_piece, ("tm",), 0, line_half)]
    )
    text_pairs = (
        text_pairs.reshape(owners, slots, text_local, 2 * half_width)
        .transpose(1, 0, 2, 3)
        .reshape(slots, TXT, 2 * half_width)
    )
    conv_part = conv_frames(wide(second_wide), second_conv, "IHWO", False).astype(jnp.bfloat16)
    conv_half, _ = sum_cores(conv_part.reshape(images, H * W, -1), 6)
    text_cols = text_flat.reshape(text_rows, owners, -1).transpose(1, 0, 2)
    conv_rows, (text_cols, qkv_piece) = from_lines(
        conv_half.astype(jnp.bfloat16),
        True,
        7,
        [Exchange(text_cols, everyone), Share(qkv_piece, ("tm",))],
    )
    spatial_qkv = qkv_piece.transpose(2, 1, 0, 3, 4).reshape(3, channels, -1)

    spatial_gain = spatial_norm[None]
    stream_one, spatial_in = first_norm(
        video_rows, conv_rows.reshape(token_rows, channels), spatial_gain
    )
    spatial_line, (in_rest,) = gather_tokens(
        spatial_in, 8, [Share(in_piece, ("tm",), line_half, lines - line_half)]
    )
    spatial_line = spatial_line.reshape(lines, images, pixels_dev, channels)
    spatial_triple, spatial_mix = spatial_forward(spatial_line, spatial_qkv)
    spatial_mix, (out_rest, cot_late) = from_lines(
        spatial_mix,
        False,
        9,
        [Share(out_piece, ("tm",), line_half, lines - line_half), Keep(cot_rows)],
    )
    cot_half = lax.all_gather(part_of(cot_late, "mp", 1), "space", axis=0, tiled=True)

    spatial_mix = spatial_mix.reshape(token_rows, half_width)
    out_all, in_all = (out_first, out_rest), (in_first, in_rest)
    text_valid = (jnp.arange(TXT, dtype=jnp.int32)[None, :] < text_lengths[:, None])[:, None, :]
    text_valid = text_valid.astype(jnp.float32)
    two_gains = jnp.stack([cross_norm, temporal_norm])
    stream_two, cross_in, cross_queries, cross_mix, stream_three, temporal_in, temporal_triple = (
        middle_forward(
            spatial_mix, stream_one, out_all, in_all, text_pairs, text_valid, two_gains, 34
        )
    )

    clip_triple, (in_quarter, out_quarter) = to_clips(
        temporal_triple.reshape(slots, frame_dev, pixels_dev, 3 * half_width),
        10,
        [Exchange(in_quarter, ("space",)), Exchange(out_quarter, ("space",))],
    )
    clip_pixels = clip_triple.shape[2]
    clip_rows = frames_all * clip_pixels
    clip_triple = clip_triple.reshape(slots, clip_rows, 3 * half_width)
    offset_table = offset_onehot(0, frames_all, frames_all)
    clip_frames = jnp.arange(clip_rows, dtype=jnp.int32)[:, None] // clip_pixels
    clip_frames = (clip_frames == jnp.arange(frames_all, dtype=jnp.int32)[None, :]).astype(
        jnp.float32
    )
    clip_bias = jnp.einsum("qkr,rh->hqk", offset_table, offset_bias, precision=highest)
    clip_bias = jnp.einsum("hqk,ck->hqc", clip_bias, clip_frames, precision=highest)
    clip_bias = jnp.einsum("rq,hqc->hrc", clip_frames, clip_bias, precision=highest)
    clip_ids = jnp.repeat(video_ids, clip_pixels, axis=1)
    clip_mix = temporal_forward(clip_triple, clip_bias, clip_ids, clip_pixels)
    temporal_mix, (cot_line,) = from_clips(
        clip_mix.reshape(slots, frames_all, clip_pixels, half_width), 11, [JoinCores(cot_half)]
    )
    temporal_mix = temporal_mix.reshape(token_rows, half_width)

    feed_gain = feed_norm[None]
    stream_four, feed_rows = late_forward(temporal_mix, stream_three, out_all, feed_gain, 35)
    feed_line, (feed_in, feed_out) = gather_tokens(
        feed_rows, 12, [Share(in_quarter, ("tm",)), Share(out_quarter, ("tm",))]
    )
    feed_in = feed_in.transpose(1, 0, 2, 3).reshape(channels, feed_width)
    feed_out = feed_out.transpose(0, 2, 1, 3).reshape(feed_width, channels)
    line_shape = (lines, token_rows, channels)
    final_part, feed_part, feed_grads = feed_both(
        feed_line.reshape(line_shape), cot_line.reshape(line_shape), feed_in, feed_out
    )
    normed_grad, (feed_grads,) = scatter_tokens(
        feed_part.reshape(lines * token_rows, channels), 14, [by_frames(feed_grads)]
    )

    upstream, mix_grad, temporal_out_grad, feed_norm_grad = late_backward(
        cot_rows, normed_grad, stream_four, feed_gain, temporal_mix, out_all
    )
    clip_up, (feed_grads,) = to_clips(
        mix_grad.reshape(slots, frame_dev, pixels_dev, half_width),
        15,
        [Exchange(feed_grads.reshape(lines, -1, 2 * feed_width), ("space",))],
    )
    clip_grads, score_total = temporal_backward(
        clip_triple,
        clip_bias,
        clip_ids,
        clip_pixels,
        clip_up.reshape(slots, clip_rows, half_width),
    )
    score_total = jnp.einsum("hqc,ck->hqk", score_total, clip_frames, precision=highest)
    offset_bias_grad = jnp.einsum("hqk,qkr->rh", score_total, offset_table, precision=highest)
    triple_grad, _ = from_clips(
        clip_grads.reshape(slots, frames_all, clip_pixels, 3 * half_width), 16
    )

    (
        upstream,
        mix_grad,
        pair_grad,
        temporal_query_grad,
        temporal_pair_grad,
        cross_query_grad,
        outs_grad,
        two_grads,
    ) = middle_backward(
        triple_grad.reshape(token_rows, 3 * half_width),
        upstream,
        stream_three,
        stream_two,
        temporal_in,
        cross_in,
        cross_queries,
        cross_mix,
        spatial_mix,
        out_all,
        in_all,
        text_pairs,
        text_valid,
        two_gains,
        36,
    )
    final_rows, (first_grads, second_grads) = scatter_tokens(
        final_part.reshape(lines * token_rows, channels),
        13,
        [by_frames(temporal_out_grad), by_frames(temporal_query_grad)],
    )
    mixed = (stream_four + final_rows.astype(jnp.float32)).astype(jnp.bfloat16)
    pair_grad = (
        pair_grad.reshape(slots, frames_axis, lines, text_local, 2 * half_width)
        .transpose(1, 2, 0, 3, 4)
        .reshape(frames_axis, lines * text_rows, 2 * half_width)
    )

    mix_line, (pair_grad,) = to_lines(
        mix_grad.reshape(images, pixels_dev, half_width), False, 17, [FrameSum(pair_grad)]
    )
    spatial_part, spatial_qkv_grad = spatial_backward(
        spatial_line, spatial_qkv, spatial_triple, mix_line
    )
    normed_grad, (pair_grad, third_grads) = scatter_tokens(
        spatial_part.reshape(lines * token_rows, channels),
        18,
        [
            Exchange(pair_grad.reshape(lines, text_rows, 2 * half_width), ("space",)),
            by_frames(temporal_pair_grad),
        ],
    )
    pair_grad = jnp.sum(pair_grad.astype(jnp.float32), axis=0).astype(jnp.bfloat16)
    upstream, branch_both, spatial_norm_grad = first_norm_backward(
        stream_one, spatial_gain, normed_grad, upstream, owners, lines
    )

    branch_line, (fourth_grads, pair_line) = to_lines(
        branch_both.reshape(-1, pixels_dev, channels),
        False,
        19,
        [by_frames(cross_query_grad), Share(pair_grad, ("space",))],
        join=True,
    )
    branch_line, branch_owned = branch_line[:images], branch_line[images:]
    second_conv_grad = conv_weight_grad(wide(second_wide), wide(branch_owned), "kc")
    second_part = conv_frames(wide(branch_line), second_conv, "OHWI", True).astype(jnp.bfloat16)
    second_in_grad, (fifth_grads, pair_all) = sum_lines(
        second_part.reshape(images, H * W, half_width),
        20,
        [by_frames(outs_grad), Share(pair_line, ("tm",))],
    )
    hidden_grad, scale_grad, shift_grad = group_backward(
        hidden, film_scale, film_shift, second_in_grad
    )
    frame_grads = jnp.stack([scale_grad, shift_grad], axis=1).reshape(slots, frame_dev, 2, -1)
    film_rows = jnp.einsum("bfv,bfjk->bvjk", choose, frame_grads, precision=highest)
    film_rows = film_rows.reshape(slots * VIDS * 2, -1)
    text_part = jnp.dot(
        pair_line.reshape(lines * text_rows, -1), cross_kv.T, preferred_element_type=jnp.float32
    )
    text_part = text_part.astype(jnp.bfloat16).reshape(lines, text_rows, -1)

    hidden_wide, (second_conv_grad, film_shares, text_part) = gather_lines(
        hidden_grad,
        21,
        [TapSum(second_conv_grad), Share(film_rows, everyone), Exchange(text_part, ("space",))],
    )
    first_conv_grad = conv_weight_grad(wide(first_owned), wide(hidden_wide), "ck")
    first_part = conv_frames(wide(hidden_wide), first_conv, "OHWI", True).astype(jnp.bfloat16)
    gathered_grads = jnp.concatenate(
        [first_grads, second_grads, third_grads, fourth_grads, fifth_grads], axis=1
    )
    first_in_grad, (first_conv_grad, spatial_qkv_grad, gathered_grads) = sum_cores(
        first_part.reshape(images, H * W, -1),
        22,
        [
            TapSum(first_conv_grad),
            by_frames(spatial_qkv_grad),
            Exchange(gathered_grads.reshape(lines, -1, gathered_grads.shape[1]), ("space",)),
        ],
    )
    video_line_grad, gain_grad, bias_grad = group_backward(
        video_lines[:images], gain_line[:images], bias_line[:images], first_in_grad
    )

    def placed(line_grad):
        whole = jnp.zeros((channels,), jnp.float32)
        size = line_grad.shape[2]
        place = (lax.axis_index("space") * cores + lax.axis_index("mp")) * size
        return lax.dynamic_update_slice_in_dim(whole, jnp.sum(line_grad, axis=(0, 1)), place, 0)

    small = jnp.concatenate(
        [
            item.reshape(owners, -1)
            for item in (
                placed(gain_grad),
                placed(bias_grad),
                spatial_norm_grad,
                two_grads[0],
                two_grads[1],
                feed_norm_grad,
                offset_bias_grad,
            )
        ],
        axis=1,
    )
    video_rows_grad, (small, qkv_part) = from_lines(
        video_line_grad,
        True,
        23,
        [
            Exchange(small[:, None], everyone),
            Exchange(spatial_qkv_grad.reshape(lines, -1, spatial_qkv_grad.shape[1]), ("space",)),
        ],
    )
    video_grad = upstream + video_rows_grad.reshape(token_rows, channels).astype(jnp.float32)

    film_shares = film_shares.reshape(frames_axis, lines, slots, VIDS, 2, -1)
    video_film_grad = (
        jnp.sum(film_shares, axis=0)
        .transpose(1, 2, 3, 0, 4)
        .reshape(slots, VIDS, 2, half_width)
    )
    film_weight_grad = jnp.einsum(
        "bvc,bvjk->cjk",
        part_of(part_of(embed, "tm", 2), "space", 2).astype(jnp.float32),
        video_film_grad,
        precision=highest,
    )
    cross_kv_grad = jnp.einsum(
        "prc,prk->ck",
        text_cols,
        pair_all.reshape(owners, text_rows, 2 * half_width),
        preferred_element_type=jnp.float32,
    )
    text_half = part_of(
        twin_add(text_part.transpose(1, 0, 2).reshape(text_rows, -1)), "mp", 1
    )
    small = jnp.sum(small, axis=(0, 1))
    small_twin = lax.ppermute(small, "mp", [(0, 1), (1, 0)])
    gain_size = channels // owners
    gains = [small[i * gain_size : (i + 1) * gain_size] for i in range(6)]
    for i in range(2):
        gains[i] = gains[i] + small_twin[i * gain_size : (i + 1) * gain_size]
    feed_grads, qkv_part = feed_grads.astype(jnp.float32), qkv_part.astype(jnp.float32)
    owner_rows = feed_grads.shape[1]
    gathered_grads = jnp.sum(gathered_grads.astype(jnp.float32), axis=0)
    owner_parts = [
        gathered_grads[:, i * half_width : (i + 1) * half_width] for i in range(7)
    ]
    return (
        mixed.reshape(video.shape),
        video_grad.reshape(video.shape),
        text_half.reshape(slots, text_local, -1),
        gains[0],
        gains[1],
        first_conv_grad.astype(jnp.float32).transpose(1, 0, 2),
        film_weight_grad,
        second_conv_grad.astype(jnp.float32).transpose(2, 0, 1),
        gains[2],
        qkv_part.reshape(lines, owner_rows, 3, -1)
        .transpose(1, 2, 0, 3)
        .reshape(owner_rows, 3, half_width),
        owner_parts[6].T,
        gains[3],
        owner_parts[4],
        cross_kv_grad.reshape(-1, 2, half_width),
        owner_parts[5].T,
        gains[4],
        gathered_grads[:, half_width : 4 * half_width].reshape(-1, 3, half_width),
        owner_parts[0].T,
        small[6 * gain_size :].reshape(R // owners, head_local),
        gains[5],
        feed_grads[:, :, :feed_width].transpose(1, 0, 2).reshape(owner_rows, -1),
        feed_grads[:, :, feed_width:].transpose(0, 2, 1).reshape(-1, owner_rows),
    )


def solution(mesh):
    return jax.shard_map(
        on_device,
        mesh=mesh,
        in_specs=(
            P(None, "tm", "space", None, None),
            P(None, "tm", "space", None, None),
            P(None, ("tm", "space"), None),
            P(),
            P(),
            P(),
            P(),
            P(),
            P("space", None, "mp"),
            P("space", None, "mp"),
            P("mp", None, "space"),
            P(),
            P("space", None, "mp"),
            P("mp", "space"),
            P(),
            P("space", "mp"),
            P("space", None, "mp"),
            P("mp", "space"),
            P(),
            P("space", None, "mp"),
            P("mp", "space"),
            P(None, "mp"),
            P(),
            P("space", "mp"),
            P("mp", "space"),
        ),
        out_specs=(
            P(None, "tm", "space", None, None),
            P(None, "tm", "space", None, None),
            P(None, ("tm", "space"), "mp"),
            P(("tm", "space")),
            P(("tm", "space")),
            P(("tm", "space"), None, "mp"),
            P(("tm", "space"), None, "mp"),
            P("mp", None, ("tm", "space")),
            P(("tm", "space")),
            P(("tm", "space"), None, "mp"),
            P("mp", ("tm", "space")),
            P(("tm", "space")),
            P(("tm", "space"), "mp"),
            P(("tm", "space"), None, "mp"),
            P("mp", ("tm", "space")),
            P(("tm", "space")),
            P(("tm", "space"), None, "mp"),
            P("mp", ("tm", "space")),
            P(("tm", "space"), "mp"),
            P(("tm", "space")),
            P(("tm", "space"), "mp"),
            P("mp", ("tm", "space")),
        ),
        check_vma=False,
    )
```

time: 1150 us -> 783 us (0.68)
  local copies, waits for them, and re-layouts: 226 us -> 97 us
  waiting for transfers between devices: 67.7 us -> 0.04 us
  matrix products: 101 us -> 33.7 us
  other arithmetic: 49.2 us -> 16 us
  Pallas kernels: 646 us -> 613 us
  starting transfers between devices: 28.3 us -> 0.58 us
    pallas_call x33 -> x25, Pallas kernels: 646 us -> 554 us  [talk(): pl.pallas_call(kernel, out_shape=result, in_specs=[ANY] * len(operands) i...]
    ppermute x8 -> x1, waiting for transfers between devices: 67.6 us -> 0.01 us  [twin_add(): other = lax.ppermute(mine, 'mp', [(0, 1), (1, 0)])]
    dot_general x46 -> x7, matrix products: 68.4 us -> 3.24 us  [the longest x1 0.89 us: on_device(): jnp.einsum('hqk,ck->hqc', clip_bias, clip_frames, precision=highest)]
    pallas_call x0 -> x13, Pallas kernels: none -> 59.1 us  [the longest x9 54.2 us: local(): pl.pallas_call(kernel, out_shape=results, grid=grid, in_specs=in_specs, o...]
    another operation x21 -> x9, local copies, waits for them, and re-layouts: 42.7 us -> 1.62 us  [the longest x3 0.73 us: line_gains(): return jnp.repeat(jnp.stack([own, owned]), images, axis=0)[:, None]]
    reshape x23 -> x16, local copies, waits for them, and re-layouts: 43.5 us -> 9.16 us  [the longest x3 3.05 us: on_device(): return (mixed.reshape(video.shape), video_grad.reshape(video.shape), text...]
    slice x13 -> x8, local copies, waits for them, and re-layouts: 36.4 us -> 3.45 us  [the longest x1 1.68 us: on_device(): video_lines[:images]]
    all_to_all x3 -> x0, starting transfers between devices: 20.3 us -> none  [space_to_all(): lax.all_to_all(source, 'space', split_axis=split, concat_axis=concat, til...]
  transfers between devices with their start and end apart: 17 -> 4, of which waited for: 4 -> 0; matrix products, arithmetic and copies ran while one was open for 24% -> 6% of each run, Pallas kernels for 47% -> 20%
where the time goes in v3:
time: 783 us; the launch traced here: 777 us
  Pallas kernels  613 us (78%)
  local copies, waits for them, and re-layouts  97 us (12%)
  matrix products  33.7 us (4%)
  between operations  16.3 us (2%)
  other arithmetic  16 us (2%)
    pallas_call x25, Pallas kernels, talk(): pl.pallas_call(kernel, out_shape=result, in_specs=[ANY] * len(operands) i...  554 us
    unnamed x318, local copies, waits for them, and re-layouts  69.7 us
    pallas_call x9, Pallas kernels, local(): pl.pallas_call(kernel, out_shape=results, grid=grid, in_specs=in_specs, o...  54.2 us
    conv_general_dilated x4, matrix products, conv_frames(): lax.conv_general_dilated(images, kernel, (1, 1), 'SAME', dimension_number...  18 us
  transfers between devices with their start and end apart: 4, of which 0 were waited for; matrix products, arithmetic and copies ran while one was open for 6% of the time, Pallas kernels for 20%

profile of v3, /device:TPU:2, one launch (start us, length us, event | category | flops | bytes accessed | tf_op | source)
XLA Modules:
  0.0 776.5 jit_solution(3453025456308640260)
XLA Ops:
  10.9 1.5 reshape.525
  14.8 3.5 copy.221
  21.3 39.8 %shard_map.409 = (bf16[8,256,128]{2,1,0:T(8,128)(2,1)S(1)}, bf16[4,16,1024]{2,1,0:T(8,128)(2,1)S(1)}, bf16[4,3,64,128]{3,2,1,0:T(8,128)(2,1)S(1)}, bf16[4,128,768]{2,1,0:T(8,128)(2,1)S(1)}) custom-call(bf16[8,64,1024]{2,1,0:T(8,128)(2,1)S(1)} %bitcast.503, bf16[16,4096]{1,0:T(8,128)(2,1)S(1)} %bitcast.542, ...), custom_call_target="tpu_custom_call" | custom-call | tf_op jit(solution)/shard_map/pallas_call | solution.py:83
  62.6 4.4 shard_map.410.refs_0_
  67.1 26.4 %shard_map.411 = (bf16[8,256,256]{2,1,0:T(8,128)(2,1)S(1)}, bf16[4,16,1024]{2,1,0:T(8,128)(2,1)S(1)}, bf16[4,256,512]{2,1,0:T(8,128)(2,1)S(1)}) custom-call(bf16[8,256,128]{2,1,0:T(8,128)(2,1)S(1)} %shard_map.410.refs_0_, bf16[4,16,1024]{2,1,0:T(8,128)(2,1)S(1)} %bitcast.541, bf16[256,512]{1,0:T(8,128)(2,1)S(1)} %fusion.64.refs_2_), custom_call_target="tpu_custom_call" | custom-call | tf_op jit(solution)/shard_map/pallas_call | solution.py:83
  97.0 6.6 convolution_convert_fusion.1
  105.3 1.6 reduce_sum.69.refs_2_
  108.7 28.4 %shard_map.412 = (f32[4,256,128]{2,1,0:T(8,128)S(1)}, bf16[4,2,128,768]{3,2,1,0:T(8,128)(2,1)S(1)}, bf16[4,16,1024]{2,1,0:T(8,128)(2,1)S(1)}) custom-call(bf16[4,256,512]{2,1,0:T(8,128)(2,1)S(1)} %bitcast.504, bf16[4,128,768]{2,1,0:T(8,128)(2,1)S(1)} %copy-done.23, bf16[16,1024]{1,0:T(8,128)(2,1)S(1)} %copy-done.97), custom_call_target="tpu_custom_call" | custom-call | tf_op jit(solution)/shard_map/pallas_call | solution.py:83
  142.1 2.2 shard_map.413.refs_0_
  146.5 35.5 %shard_map.414 = (bf16[4,256,512]{2,1,0:T(8,128)(2,1)S(1)}, bf16[4,4,16,1024]{3,2,1,0:T(8,128)(2,1)S(1)}, bf16[4,2,256,512]{3,2,1,0:T(8,128)(2,1)S(1)}) custom-call(bf16[4,256,128]{2,1,0:T(8,128)(2,1)S(1)} %shard_map.413.refs_0_, bf16[4,16,1024]{2,1,0:T(8,128)(2,1)S(1)} %copy-done.101, bf16[4,256,512]{2,1,0:T(8,128)(2,1)S(1)} %copy-done.16), custom_call_target="tpu_custom_call" | custom-call | tf_op jit(solution)/shard_map/pallas_call | solution.py:83
  182.9 3.9 convolution_convert_fusion.3
  187.0 1.6 shard_map.415
  188.7 15.2 %shard_map.416 = (bf16[4,64,1024]{2,1,0:T(8,128)(2,1)S(1)}, bf16[16,16,256]{2,1,0:T(8,128)(2,1)S(1)}, bf16[4,4,3,64,128]{4,3,2,1,0:T(8,128)(2,1)S(1)}) custom-call(bf16[4,256,128]{2,1,0:T(8,128)(2,1)S(1)} %convert_element_type.143.refs_0_, bf16[16,16,256]{2,1,0:T(8,128)(2,1)S(1)} %bitcast.549, bf16[4,3,64,128]{3,2,1,0:T(8,128)(2,1)S(1)} %copy-done.96), custom_call_target="tpu_custom_call" | custom-call | tf_op jit(solution)/shard_map/pallas_call | solution.py:83
  205.4 26.8 %shard_map.418 = (bf16[1,1024,1024]{2,1,0:T(8,128)(2,1)S(1)}, bf16[4,2,256,512]{3,2,1,0:T(8,128)(2,1)S(1)}) custom-call(bf16[1,256,1024]{2,1,0:T(8,128)(2,1)S(1)} %bitcast.539, bf16[4,256,512]{2,1,0:T(8,128)(2,1)S(1)} %copy-done.17), custom_call_target="tpu_custom_call" | custom-call | tf_op jit(solution)/shard_map/pallas_call | solution.py:83
  233.6 4.8 shard_map.419
  239.3 22.5 %shard_map.420 = (bf16[4,64,512]{2,1,0:T(8,128)(2,1)S(1)}, bf16[4,2,128,768]{3,2,1,0:T(8,128)(2,1)S(1)}, bf16[256,1024]{1,0:T(8,128)(2,1)S(1)}) custom-call(bf16[4,256,128]{2,1,0:T(8,128)(2,1)S(1)} %get-tuple-element.135.refs_0_, bf16[4,128,768]{2,1,0:T(8,128)(2,1)S(1)} %copy-done.24, bf16[256,1024]{1,0:T(8,128)(2,1)S(1)} %bitcast.512), custom_call_target="tpu_custom_call" | custom-call | tf_op jit(solution)/shard_map/pallas_call | solution.py:83
  267.8 1.7 slice.148.x_ref
  279.2 15.3 %shard_map.421 = (f32[256,1024]{1,0:T(8,128)S(1)}, bf16[256,1024]{1,0:T(8,128)(2,1)S(1)}, bf16[256,512]{1,0:T(8,128)(2,1)S(1)}, bf16[256,512]{1,0:T(8,128)(2,1)S...) custom-call(bf16[256,512]{1,0:T(8,128)(2,1)S(1)} %bitcast.523, ...), custom_call_target="tpu_custom_call" | custom-call | tf_op jit(solution)/shard_map/pallas_call | solution.py:83
  297.4 14.6 %shard_map.422 = (bf16[2,8,16,1536]{3,2,1,0:T(8,128)(2,1)S(1)}, bf16[4,64,512]{2,1,0:T(8,128)(2,1)S(1)}, bf16[4,128,256]{2,1,0:T(8,128)(2,1)S(1)}) custom-call(bf16[2,2,64,1536]{3,2,1,0:T(8,128)(2,1)S(1)} %bitcast.535, bf16[4,64,512]{2,1,0:T(8,128)(2,1)S(1)} %bitcast.527, bf16[4,128,256]{2,1,0:T(8,128)(2,1)S(1)} %constant_dynamic-slice_fusion.1.refs_2_), custom_call_target="tpu_custom_call" | custom-call | tf_op jit(solution)/shard_map/pallas_call | solution.py:83
  313.4 5.9 shard_map.423
  323.0 6.1 shard_map.424
  335.2 2.8 shard_map.425
  338.1 27.1 %shard_map.426 = (bf16[1,1024,1024]{2,1,0:T(8,128)(2,1)S(1)}, bf16[4,4,64,512]{3,2,1,0:T(8,128)(2,1)S(1)}, bf16[4,4,128,256]{3,2,1,0:T(8,128)(2,1)S(1)}) custom-call(bf16[1,256,1024]{2,1,0:T(8,128)(2,1)S(1)} %bitcast.548, bf16[4,64,512]{2,1,0:T(8,128)(2,1)S(1)} %copy-done.88, bf16[4,128,256]{2,1,0:T(8,128)(2,1)S(1)} %copy-done.90), custom_call_target="tpu_custom_call" | custom-call | tf_op jit(solution)/shard_map/pallas_call | solution.py:83
  366.8 11.2 %shard_map.427 = (bf16[4,256,1024]{2,1,0:T(8,128)(2,1)S(1)}, bf16[4,256,1024]{2,1,0:T(8,128)(2,1)}, bf16[1024,1024]{1,0:T(8,128)(2,1)}) custom-call(bf16[4,256,1024]{2,1,0:T(8,128)(2,1)} %bitcast.511, bf16[4,256,1024]{2,1,0:T(8,128)(2,1)} %bitcast.510, bf16[1024,512]{1,0:T(8,128)(2,1)S(1)} %bitcast.505, bf16[512,1024]{1,0:T(8,128)(2,1)S(1)} %bitcast.506), custom_call_target="tpu_custom_call" | custom-call | tf_op jit(solution)/shard_map/pallas_call | solution.py:802
  379.4 1.6 copy-done.37
  381.1 1.6 copy-done.38
  382.7 28.7 %shard_map.428 = (bf16[256,1024]{1,0:T(8,128)(2,1)S(1)}, bf16[256,1024]{1,0:T(8,128)(2,1)S(1)}) custom-call(bf16[4,256,1024]{2,1,0:T(8,128)(2,1)S(1)} %copy-done.37, bf16[4,256,1024]{2,1,0:T(8,128)(2,1)S(1)} %bitcast.519), custom_call_target="tpu_custom_call" | custom-call | tf_op jit(solution)/shard_map/pallas_call | solution.py:83
  411.4 3.3 shard_map.429
  416.4 15.2 %shard_map.430 = (bf16[2,8,16,512]{3,2,1,0:T(8,128)(2,1)S(1)}, bf16[4,64,1024]{2,1,0:T(8,128)(2,1)S(1)}) custom-call(bf16[2,2,64,512]{3,2,1,0:T(8,128)(2,1)S(1)} %bitcast.552, bf16[4,64,1024]{2,1,0:T(8,128)(2,1)S(1)} %bitcast.544), custom_call_target="tpu_custom_call" | custom-call | tf_op jit(solution)/shard_map/pallas_call | solution.py:83
  432.4 7.5 shard_map.431
  439.9 11.0 %shard_map.432 = bf16[2,2,64,1536]{3,2,1,0:T(8,128)(2,1)S(1)} custom-call(bf16[2,8,16,1536]{3,2,1,0:T(8,128)(2,1)S(1)} %bitcast.536), custom_call_target="tpu_custom_call" | custom-call | tf_op jit(solution)/shard_map/pallas_call | solution.py:83
  451.0 20.3 %shard_map.433 = (f32[256,1024]{1,0:T(8,128)S(1)}, bf16[256,512]{1,0:T(8,128)(2,1)S(1)}, bf16[2,128,1024]{2,1,0:T(8,128)(2,1)S(1)}, bf16[1024,512]{1,0:T(8,128)(...) custom-call(bf16[256,1536]{1,0:T(8,128)(2,1)S(1)} %bitcast.507, ...), custom_call_target="tpu_custom_call" | custom-call | tf_op jit(solution)/shard_map/pallas_call | solution.py:83
  473.3 13.3 %shard_map.435 = (bf16[4,256,128]{2,1,0:T(8,128)(2,1)S(1)}, bf16[64,1024]{1,0:T(8,128)(2,1)S(1)}) custom-call(bf16[4,64,512]{2,1,0:T(8,128)(2,1)S(1)} %bitcast.551, bf16[4,64,1024]{2,1,0:T(8,128)(2,1)S(1)} %bitcast.520), custom_call_target="tpu_custom_call" | custom-call | tf_op jit(solution)/shard_map/pallas_call | solution.py:83
  486.6 11.4 %shard_map.436 = (bf16[4,4,64,1024]{3,2,1,0:T(8,128)(2,1)S(1)}, bf16[1024,384]{1,0:T(8,128)(2,1)S(1)}) custom-call(bf16[4,4,64,1024]{3,2,1,0:T(8,128)(2,1)} %bitcast.497, bf16[3,1024,128]{2,1,0:T(8,128)(2,1)S(1)} %bitcast.499, bf16[4,3,256,128]{3,2,1,0:T(8,128)(2,1)S(1)} %copy-done.62, bf16[4,256,128]{2,1,0:T(8,128)(2,1)S(1)} %get-tuple-element.176.up_ref), custom_call_target="tpu_custom_call" | custom-call | tf_op jit(solution)/shard_map/pallas_call | solution.py:802
  499.0 27.0 %shard_map.437 = (bf16[256,1024]{1,0:T(8,128)(2,1)S(1)}, bf16[4,16,1024]{2,1,0:T(8,128)(2,1)S(1)}, bf16[256,1024]{1,0:T(8,128)(2,1)S(1)}) custom-call(bf16[4,256,1024]{2,1,0:T(8,128)(2,1)S(1)} %bitcast.518, bf16[4,16,1024]{2,1,0:T(8,128)(2,1)S(1)} %bitcast.555, bf16[4,256,1024]{2,1,0:T(8,128)(2,1)S(1)} %bitcast.517), custom_call_target="tpu_custom_call" | custom-call | tf_op jit(solution)/shard_map/pallas_call | solution.py:83
  533.4 20.8 %shard_map.439 = (bf16[8,256,256]{2,1,0:T(8,128)(2,1)S(1)}, bf16[256,512]{1,0:T(8,128)(2,1)S(1)}, bf16[4,16,1024]{2,1,0:T(8,128)(2,1)S(1)}) custom-call(bf16[8,64,1024]{2,1,0:T(8,128)(2,1)S(1)} %bitcast.529, bf16[4,256,512]{2,1,0:T(8,128)(2,1)S(1)} %bitcast.528, bf16[16,1024]{1,0:T(8,128)(2,1)S(1)} %reduce_sum.70.refs_2_), custom_call_target="tpu_custom_call" | custom-call | tf_op jit(solution)/shard_map/pallas_call | solution.py:83
  556.0 3.6 convolution_convert_fusion
  561.2 35.5 %shard_map.440 = (f32[4,256,128]{2,1,0:T(8,128)S(1)}, bf16[256,1024]{1,0:T(8,128)(2,1)S(1)}, bf16[4,4,16,1024]{3,2,1,0:T(8,128)(2,1)S(1)}) custom-call(bf16[4,256,512]{2,1,0:T(8,128)(2,1)S(1)} %bitcast.502, bf16[4,256,1024]{2,1,0:T(8,128)(2,1)S(1)} %bitcast.516, bf16[4,16,1024]{2,1,0:T(8,128)(2,1)S(1)} %get-tuple-element.188.refs_2_), custom_call_target="tpu_custom_call" | custom-call | tf_op jit(solution)/shard_map/pallas_call | solution.py:83
  596.7 3.4 shard_map.441
  603.5 26.1 %shard_map.434 = (bf16[256,1024]{1,0:T(8,128)(2,1)S(1)}, bf16[256,512]{1,0:T(8,128)(2,1)S(1)}, bf16[256,512]{1,0:T(8,128)(2,1)S(1)}) custom-call(bf16[4,256,1024]{2,1,0:T(8,128)(2,1)S(1)} %copy-done.34, bf16[4,256,512]{2,1,0:T(8,128)(2,1)S(1)} %bitcast.533, bf16[4,256,512]{2,1,0:T(8,128)(2,1)S(1)} %bitcast.534), custom_call_target="tpu_custom_call" | custom-call | tf_op jit(solution)/shard_map/pallas_call | solution.py:83
  634.4 34.8 %shard_map.442 = (bf16[4,256,512]{2,1,0:T(8,128)(2,1)S(1)}, bf16[9,64,512]{2,1,0:T(8,128)(2,1)S(1)}, f32[16,12,128]{2,1,0:T(8,128)S(1)}, bf16[4,16,1024]{2,1,0:T(8,128)(2,1)S(1)}) custom-call(bf16[4,256,128]{2,1,0:T(8,128)(2,1)S(1)} %copy-done.92, bf16[9,256,512]{2,1,0:T(8,128)(2,1)S(1)} %fusion.39.refs_1_, f32[12,128]{1,0:T(8,128)S(1)} %reshape.465.refs_2_, ...), custom_call_target="tpu_custom_call" | custom-call | tf_op jit(solution)/shard_map/pallas_call | solution.py:83
  669.2 3.9 convolution_convert_fusion.2
  681.1 38.5 %shard_map.443 = (f32[4,256,128]{2,1,0:T(8,128)S(1)}, bf16[9,64,512]{2,1,0:T(8,128)(2,1)S(1)}, bf16[256,384]{1,0:T(8,128)(2,1)S(1)}, bf16[4,64,3584]{2,1,0:T(8,128)(2,1)S(1)}) custom-call(bf16[4,256,256]{2,1,0:T(8,128)(2,1)S(1)} %bitcast.522, bf16[9,256,512]{2,1,0:T(8,128)(2,1)} %copy-done.128, bf16[4,256,384]{2,1,0:T(8,128)(2,1)S(1)} %bitcast.538, ...), custom_call_target="tpu_custom_call" | custom-call | tf_op jit(solution)/shard_map/pallas_call | solution.py:83
  727.6 1.8 copy.184
  731.4 3.3 shard_map.444
  736.5 20.5 %shard_map.445 = (bf16[4,64,1024]{2,1,0:T(8,128)(2,1)S(1)}, f32[16,1,448]{2,1,0:T(1,128)S(1)}, bf16[4,64,384]{2,1,0:T(8,128)(2,1)S(1)}) custom-call(bf16[4,256,128]{2,1,0:T(8,128)(2,1)S(1)} %get-tuple-element.201.refs_0_, f32[16,1,448]{2,1,0:T(1,128)S(1)} %broadcast_in_dim.40.refs_1_, bf16[4,64,384]{2,1,0:T(8,128)(2,1)S(1)} %bitcast.554), custom_call_target="tpu_custom_call" | custom-call | tf_op jit(solution)/shard_map/pallas_call | solution.py:83
  764.0 1.9 reshape.493
  768.0 1.5 add_bitcast_fusion
  (451 shorter events, 114.1 us)
Async XLA Ops:
  7.2 174.8 %copy-start = (bf16[512,9,256]{2,0,1:T(8,128)(2,1)S(1)}, bf16[512,9,256]{2,0,1:T(8,128)(2,1)}, u32[]{:S(2)}) copy-start(bf16[512,9,256]{2,0,1:T(8,128)(2,1)} %param.35) | copy-start | bytes 7077892
  7.2 132.5 %reduce-scatter.4.cloned.1.call-start = ((), (), s32[]{:S(2)}) async-start(), calls=%async_computation.2 | async-start | bytes 327680
  12.4 308.4 %all-gather.2.cloned.1.call-start = ((), (), s32[]{:S(2)}) async-start(), calls=%async_computation.1 | async-start | bytes 1310720 | tf_op jit(solution)/shard_map/all_gather | solution.py:1671
  12.5 251.3 %copy-start.139 = (s32[8,8]{0,1:T(8,128)}, s32[8,8]{0,1:T(8,128)S(1)}, u32[]{:S(2)}) copy-start(s32[8,8]{0,1:T(8,128)S(1)} %clamp_add_fusion) | copy-start | bytes 772
  18.4 43.6 %copy-start.124 = (bf16[128,8,2,512]{3,1,2,0:T(8,128)(2,1)S(1)}, bf16[128,8,2,512]{3,1,2,0:T(8,128)(2,1)}, u32[]{:S(2)}) copy-start(bf16[128,8,2,512]{3,1,2,0:T(8,128)(2,1)} %copy.221) | copy-start | bytes 6291460
  20.3 42.2 %copy-start.131 = (bf16[256,3,512]{2,0,1:T(8,128)(2,1)S(1)}, bf16[256,3,512]{2,0,1:T(8,128)(2,1)}, u32[]{:S(2)}) copy-start(bf16[256,3,512]{2,0,1:T(8,128)(2,1)} %param.44) | copy-start | bytes 2359300
  20.3 42.2 %copy-start.134 = (bf16[256,512]{1,0:T(8,128)(2,1)S(1)}, bf16[256,512]{1,0:T(8,128)(2,1)}, u32[]{:S(2)}) copy-start(bf16[256,512]{1,0:T(8,128)(2,1)} %param.40) | copy-start | bytes 786436
  103.7 37.1 %copy-start.143 = (s32[2,2]{1,0:T(2,128)}, s32[2,2]{1,0:T(2,128)S(1)}, u32[]{:S(2)}) copy-start(s32[2,2]{1,0:T(2,128)S(1)} %constant_dynamic-slice_fusion.3) | copy-start | bytes 52
  186.9 17.1 %copy-start.32 = (bf16[2,2,4,16,1024]{4,3,2,1,0:T(8,128)(2,1)S(1)}, bf16[2,2,4,16,1024]{4,3,2,1,0:T(8,128)(2,1)}, u32[]{:S(2)}) copy-start(bf16[2,2,4,16,1024]{4,3,2,1,0:T(8,128)(2,1)} %param.25) | copy-start | bytes 1572868
  187.0 18.4 %copy-start.17 = (bf16[4,256,512]{2,1,0:T(8,128)(2,1)S(1)}, bf16[4,256,512]{2,1,0:T(8,128)(2,1)}, u32[]{:S(2)}) copy-start(bf16[4,256,512]{2,1,0:T(8,128)(2,1)} %copy-done.15) | copy-start | bytes 3145732
  205.4 33.9 %copy-start.24 = (bf16[4,128,768]{2,1,0:T(8,128)(2,1)S(1)}, bf16[4,128,768]{2,1,0:T(8,128)(2,1)}, u32[]{:S(2)}) copy-start(bf16[4,128,768]{2,1,0:T(8,128)(2,1)} %copy-done.22) | copy-start | bytes 2359300
  205.4 33.9 %copy-start.29 = (bf16[2,2,4,16,1024]{4,3,2,1,0:T(8,128)(2,1)S(1)}, bf16[2,2,4,16,1024]{4,3,2,1,0:T(8,128)(2,1)}, u32[]{:S(2)}) copy-start(bf16[2,2,4,16,1024]{4,3,2,1,0:T(8,128)(2,1)} %param.26) | copy-start | bytes 1572868
  233.6 28.3 %copy-start.7 = (bf16[1,1024,1024]{2,1,0:T(8,128)(2,1)}, bf16[1,1024,1024]{2,1,0:T(8,128)(2,1)S(1)}, u32[]{:S(2)}) copy-start(bf16[1,1024,1024]{2,1,0:T(8,128)(2,1)S(1)} %get-tuple-element.133) | copy-start | bytes 6291460
  233.6 33.4 %copy-start.148 = (s32[2,8]{1,0:T(2,128)S(1)}, s32[2,8]{1,0:T(2,128)}, u32[]{:S(2)}) copy-start(s32[2,8]{1,0:T(2,128)} %param.28) | copy-start | bytes 196
  276.6 18.0 %copy-start.112 = (f32[2,1,128]{2,1,0:T(1,128)}, f32[2,1,128]{2,1,0:T(1,128)S(1)}, u32[]{:S(2)}) copy-start(f32[2,1,128]{2,1,0:T(1,128)S(1)} %compare_convert_fusion.refs_7_.refs_14_) | copy-start | bytes 3076
  277.9 35.5 %copy-start.9 = (f32[8,128,128]{2,1,0:T(8,128)}, f32[8,128,128]{2,1,0:T(8,128)S(1)}, u32[]{:S(2)}) copy-start(f32[8,128,128]{2,1,0:T(8,128)S(1)} %convolution_bitcast_fusion.19.bias_ref) | copy-start | bytes 1572868
  279.2 18.2 %copy-start.49 = (bf16[8,4,8,512]{3,2,0,1:T(8,128)(2,1)S(1)}, bf16[8,4,8,512]{3,2,0,1:T(8,128)(2,1)}, u32[]{:S(2)}) copy-start(bf16[8,4,8,512]{3,2,0,1:T(8,128)(2,1)} %copy.253) | copy-start | bytes 786436
  279.2 34.2 %copy-start.108 = (s32[2,1,128]{2,1,0:T(1,128)S(1)}, s32[2,1,128]{2,1,0:T(1,128)}, u32[]{:S(2)}) copy-start(s32[2,1,128]{2,1,0:T(1,128)} %broadcast_in_dim_reshape.17.turned_ref) | copy-start | bytes 3076
  338.1 73.3 %copy-start.18 = (f32[256,1024]{1,0:T(8,128)}, f32[256,1024]{1,0:T(8,128)S(1)}, u32[]{:S(2)}) copy-start(f32[256,1024]{1,0:T(8,128)S(1)} %get-tuple-element.148.x_ref) | copy-start | bytes 3145732
  366.8 44.6 %copy-start.105 = (f32[1024]{0:T(1024)S(1)}, f32[1024]{0:T(1024)}, u32[]{:S(2)}) copy-start(f32[1024]{0:T(1024)} %param.47) | copy-start | bytes 12292
  379.4 32.0 %copy-start.30 = (bf16[2,2,4,16,1024]{4,3,2,1,0:T(8,128)(2,1)S(1)}, bf16[2,2,4,16,1024]{4,3,2,1,0:T(8,128)(2,1)}, u32[]{:S(2)}) copy-start(bf16[2,2,4,16,1024]{4,3,2,1,0:T(8,128)(2,1)} %param.26) | copy-start | bytes 1572868
  411.4 21.0 %copy-start.10 = (f32[8,128,128]{2,1,0:T(8,128)S(1)}, f32[8,128,128]{2,1,0:T(8,128)}, u32[]{:S(2)}) copy-start(f32[8,128,128]{2,1,0:T(8,128)} %copy-done.9) | copy-start | bytes 1572868
  411.4 21.0 %copy-start.26 = (bf16[2,8,16,1536]{3,2,1,0:T(8,128)(2,1)S(1)}, bf16[2,8,16,1536]{3,2,1,0:T(8,128)(2,1)}, u32[]{:S(2)}) copy-start(bf16[2,8,16,1536]{3,2,1,0:T(8,128)(2,1)} %copy-done.25) | copy-start | bytes 2359300
  411.4 21.0 %copy-start.109 = (s32[2,1,128]{2,1,0:T(1,128)S(1)}, s32[2,1,128]{2,1,0:T(1,128)}, u32[]{:S(2)}) copy-start(s32[2,1,128]{2,1,0:T(1,128)} %broadcast_in_dim_reshape.17.turned_ref) | copy-start | bytes 3076
  416.3 34.6 %copy-start.57 = (bf16[1024,512]{1,0:T(8,128)(2,1)}, bf16[1024,512]{1,0:T(8,128)(2,1)S(1)}, u32[]{:S(2)}) copy-start(bf16[1024,512]{1,0:T(8,128)(2,1)S(1)} %get-tuple-element.160) | copy-start | bytes 3145732
  416.3 34.6 %copy-start.12 = (bf16[16,2,8,1024]{3,2,0,1:T(8,128)(2,1)S(1)}, bf16[16,2,8,1024]{3,2,0,1:T(8,128)(2,1)}, u32[]{:S(2)}) copy-start(bf16[16,2,8,1024]{3,2,0,1:T(8,128)(2,1)} %copy-done.11) | copy-start | bytes 1572868
  416.3 34.6 %copy-start.68 = (bf16[256,1024]{1,0:T(8,128)(2,1)S(1)}, bf16[256,1024]{1,0:T(8,128)(2,1)}, u32[]{:S(2)}) copy-start(bf16[256,1024]{1,0:T(8,128)(2,1)} %copy-done.67) | copy-start | bytes 1572868
  416.3 34.6 %copy-start.70 = (bf16[256,1024]{1,0:T(8,128)(2,1)S(1)}, bf16[256,1024]{1,0:T(8,128)(2,1)}, u32[]{:S(2)}) copy-start(bf16[256,1024]{1,0:T(8,128)(2,1)} %copy-done.69) | copy-start | bytes 1572868
  416.4 34.6 %copy-start.82 = (bf16[256,512]{1,0:T(8,128)(2,1)S(1)}, bf16[256,512]{1,0:T(8,128)(2,1)}, u32[]{:S(2)}) copy-start(bf16[256,512]{1,0:T(8,128)(2,1)} %copy-done.81) | copy-start | bytes 786436
  416.4 34.6 %copy-start.84 = (bf16[256,512]{1,0:T(8,128)(2,1)S(1)}, bf16[256,512]{1,0:T(8,128)(2,1)}, u32[]{:S(2)}) copy-start(bf16[256,512]{1,0:T(8,128)(2,1)} %copy-done.83) | copy-start | bytes 786436
  416.4 34.6 %copy-start.113 = (f32[2,1,128]{2,1,0:T(1,128)S(1)}, f32[2,1,128]{2,1,0:T(1,128)}, u32[]{:S(2)}) copy-start(f32[2,1,128]{2,1,0:T(1,128)} %copy-done.112) | copy-start | bytes 3076
  473.3 24.7 %copy-start.110 = (f32[2,1024]{1,0:T(2,128)}, f32[2,1024]{1,0:T(2,128)S(1)}, u32[]{:S(2)}) copy-start(f32[2,1024]{1,0:T(2,128)S(1)} %get-tuple-element.205) | copy-start | bytes 24580
  473.3 25.7 %copy-start.36 = (bf16[1024,1024]{1,0:T(8,128)(2,1)S(1)}, bf16[1024,1024]{1,0:T(8,128)(2,1)}, u32[]{:S(2)}) copy-start(bf16[1024,1024]{1,0:T(8,128)(2,1)} %get-tuple-element.179) | copy-start | bytes 6291460
  499.0 30.2 %copy-start.21 = (f32[256,1024]{1,0:T(8,128)S(1)}, f32[256,1024]{1,0:T(8,128)}, u32[]{:S(2)}) copy-start(f32[256,1024]{1,0:T(8,128)} %copy-done.20) | copy-start | bytes 3145732
  499.0 30.2 %copy-start.107 = (f32[1024]{0:T(1024)S(1)}, f32[1024]{0:T(1024)}, u32[]{:S(2)}) copy-start(f32[1024]{0:T(1024)} %param.36) | copy-start | bytes 12292
  531.5 22.8 %copy-start.125 = (bf16[128,8,2,512]{3,1,2,0:T(8,128)(2,1)S(1)}, bf16[128,8,2,512]{3,1,2,0:T(8,128)(2,1)}, u32[]{:S(2)}) copy-start(bf16[128,8,2,512]{3,1,2,0:T(8,128)(2,1)} %copy.221) | copy-start | bytes 6291460
  533.4 20.9 %copy-start.116 = (f32[1,1024]{1,0:T(1,128)}, f32[1,1024]{1,0:T(1,128)S(1)}, u32[]{:S(2)}) copy-start(f32[1,1024]{1,0:T(1,128)S(1)} %get-tuple-element.204) | copy-start | bytes 12292
  559.6 37.1 %copy-start.41 = (f32[4,256,128]{2,1,0:T(8,128)S(1)}, f32[4,256,128]{2,1,0:T(8,128)}, u32[]{:S(2)}) copy-start(f32[4,256,128]{2,1,0:T(8,128)} %copy-done.39) | copy-start | bytes 1572868
  559.8 40.9 %copy-start.144 = (s32[2,2]{1,0:T(2,128)S(1)}, s32[2,2]{1,0:T(2,128)}, u32[]{:S(2)}) copy-start(s32[2,2]{1,0:T(2,128)} %copy-done.143) | copy-start | bytes 52
  559.8 41.2 %copy-start.34 = (bf16[4,256,1024]{2,1,0:T(8,128)(2,1)S(1)}, bf16[4,256,1024]{2,1,0:T(8,128)(2,1)}, u32[]{:S(2)}) copy-start(bf16[4,256,1024]{2,1,0:T(8,128)(2,1)} %copy-done.33) | copy-start | bytes 6291460
  603.5 26.1 %copy-start.119 = (bf16[4,256,512]{2,1,0:T(8,128)(2,1)S(1)}, bf16[4,256,512]{2,1,0:T(8,128)(2,1)}, u32[]{:S(2)}) copy-start(bf16[4,256,512]{2,1,0:T(8,128)(2,1)} %copy-done.118) | copy-start | bytes 3145732
  603.5 26.1 %copy-start.133 = (bf16[4,256,256]{2,1,0:T(8,128)(2,1)S(1)}, bf16[4,256,256]{2,1,0:T(8,128)(2,1)}, u32[]{:S(2)}) copy-start(bf16[4,256,256]{2,1,0:T(8,128)(2,1)} %get-tuple-element.314) | copy-start | bytes 1572868
  633.9 35.2 %copy-start.151 = (bf16[256,9,512]{2,0,1:T(8,128)(2,1)S(1)}, bf16[256,9,512]{2,0,1:T(8,128)(2,1)}, u32[]{:S(2)}) copy-start(bf16[256,9,512]{2,0,1:T(8,128)(2,1)} %param.33) | copy-start | bytes 7077892
  730.1 37.9 %collective-permute-start = (bf16[16,4096]{1,0:T(8,128)(2,1)}, bf16[16,4096]{1,0:T(8,128)(2,1)}, u32[]{:S(2)}, u32[]{:S(2)}) collective-permute-start(bf16[16,4096]{1,0:T(8,128)(2,1)} %bitcast.213), channel_id=1, source_target_pairs={{0,1},{1,0},{2,3},{3,2},{4,5},{5,4},{6,7},{7,6},{8,9},{9,8},{10,11... | collective-permute-start | bytes 393224 | tf_op jit(solution)/shard_map/ppermute | solution.py:27
  730.2 28.5 %copy-start.53 = (f32[256,1024]{1,0:T(8,128)S(1)}, f32[256,1024]{1,0:T(8,128)}, u32[]{:S(2)}) copy-start(f32[256,1024]{1,0:T(8,128)} %copy-done.52) | copy-start | bytes 3145732
  736.5 23.4 %copy-start.136 = (bf16[2,3,512]{2,1,0:T(4,128)(2,1)S(1)}, bf16[2,3,512]{2,1,0:T(4,128)(2,1)}, u32[]{:S(2)}) copy-start(bf16[2,3,512]{2,1,0:T(4,128)(2,1)} %copy-done.135) | copy-start | bytes 18436
  736.5 23.4 %copy-start.138 = (bf16[2,3,512]{2,1,0:T(4,128)(2,1)S(1)}, bf16[2,3,512]{2,1,0:T(4,128)(2,1)}, u32[]{:S(2)}) copy-start(bf16[2,3,512]{2,1,0:T(4,128)(2,1)} %copy-done.137) | copy-start | bytes 18436
  757.0 9.7 %collective-permute-start.1 = (f32[448]{0:T(512)S(1)}, f32[448]{0:T(512)S(1)}, u32[]{:S(2)}, u32[]{:S(2)}) collective-permute-start(f32[448]{0:T(512)S(1)} %reduce_sum.73), channel_id=1, source_target_pairs={{0,1},{1,0},{2,3},{3,2},{4,5},{5,4},{6,7},{7,6},{8,9},{9,8},{10,11... | collective-permute-start | bytes 5384 | tf_op jit(solution)/shard_map/ppermute | solution.py:1903
  (109 other events, 346.1 us)
Sparse Core Ops, SparseCore 0:
  12.6 22.4 reduce-scatter.3
  263.9 26.8 all-gather.1

commit v4 on v3

--- a/solution.py
+++ b/solution.py
@@ -79,7 +79,7 @@
     return ref.at[:, pl.ds(pl.multiple_of(index * width, width), width), :]
 
 
-def talk(kernel, result, operands, scratch, number, specs=None, out_spec=ANY):
+def talk(kernel, result, operands, scratch, number, specs=None, out_spec=ANY, grant=32):
     return pl.pallas_call(
         kernel,
         out_shape=result,
@@ -87,7 +87,7 @@
         out_specs=out_spec,
         scratch_shapes=scratch,
         compiler_params=pltpu.CompilerParams(
-            collective_id=number, has_side_effects=True, vmem_limit_bytes=48 * 1024 * 1024
+            collective_id=number, has_side_effects=True, vmem_limit_bytes=grant * 1024 * 1024
         ),
     )(*operands)
 
@@ -119,62 +119,157 @@
 
 class Rider:
     scratch = ()
+    source_spec = ANY
     result_spec = ANY
 
     def peers(self):
         return [place for _, _, place in flat_peers(self.axes)]
 
+    def middle(self, *refs):
+        pass
+
+
+def square_places():
+    me = lax.axis_index("tm")
+    near = me + 1 - 2 * lax.rem(me, 2)
+    far = me + 2 - 4 * (me // 2)
+    return me, near, far, 3 - me
+
 
 class Exchange(Rider):
-    def __init__(self, source, axes):
-        self.source, self.axes = source, axes
-        count = source.shape[0]
-        self.result = jax.ShapeDtypeStruct(source.shape, source.dtype)
+    def __init__(self, source, axes, pick=None, cut=None):
+        self.source, self.axes, self.cut = source, axes, cut
+        self.pick = (lambda ref, place: ref.at[place]) if pick is None else pick
+        stack = source if cut is None else jax.eval_shape(cut, source)
+        count = math.prod(lax.axis_size(name) for name in axes)
+        self.result = jax.ShapeDtypeStruct(stack.shape, stack.dtype)
         self.scratch = dma_sems(count - 1, count - 1, 1)
 
     def plain(self):
-        return lax.all_to_all(self.source, self.axes, split_axis=0, concat_axis=0, tiled=True)
+        stack = self.source if self.cut is None else self.cut(self.source)
+        return lax.all_to_all(stack, self.axes, split_axis=0, concat_axis=0, tiled=True)
 
     def start(self, x_ref, out_ref, send_sem, recv_sem, own_sem):
         me = flat_index(self.axes)
         self.copies = [
-            send(x_ref.at[peer], out_ref.at[me], send_sem.at[i - 1], recv_sem.at[i - 1], place)
+            send(self.pick(x_ref, peer), out_ref.at[me], send_sem.at[i - 1], recv_sem.at[i - 1], place)
             for i, peer, place in flat_peers(self.axes)
         ]
-        self.copies.append(keep(x_ref.at[me], out_ref.at[me], own_sem.at[0]))
+        self.copies.append(keep(self.pick(x_ref, me), out_ref.at[me], own_sem.at[0]))
 
     def finish(self, *refs):
         for copy in self.copies:
             copy.wait()
 
 
+def span(index, size):
+    return pl.ds(pl.multiple_of(index * size, size), size)
+
+
+class LineSum(Rider):
+    axes = ("space",)
+    source_spec = VMEM
+    result_spec = VMEM
+
+    def __init__(self, source):
+        self.source = source
+        self.lines = lax.axis_size("space")
+        self.rows, self.width = source.shape[0] // self.lines, source.shape[1]
+        self.result = jax.ShapeDtypeStruct((self.rows, self.width), jnp.bfloat16)
+        self.scratch = [
+            pltpu.VMEM((self.lines - 1, self.rows, self.width), jnp.bfloat16)
+        ] + dma_sems(self.lines - 1, self.lines - 1)
+
+    def plain(self):
+        return lax.psum_scatter(self.source, "space", scatter_dimension=0, tiled=True)
+
+    def start(self, x_ref, out_ref, got_ref, send_sem, recv_sem):
+        self.copies = [
+            send(x_ref.at[span(peer, self.rows)], got_ref.at[i - 1], send_sem.at[i - 1], recv_sem.at[i - 1], {"space": peer})
+            for i, peer in others("space")
+        ]
+
+    def finish(self, x_ref, out_ref, got_ref, *sems):
+        for copy in self.copies:
+            copy.wait()
+        total = x_ref[span(lax.axis_index("space"), self.rows)].astype(jnp.float32)
+        for step in range(self.lines - 1):
+            total = total + got_ref[step].astype(jnp.float32)
+        out_ref[...] = total.astype(jnp.bfloat16)
+
+
 class Share(Rider):
-    def __init__(self, source, axes, first=0, size=None):
+    def __init__(self, source, axes, first=0, size=None, cols=None):
         self.source, self.axes = source, axes
-        self.first, self.size = first, size
+        self.first, self.size, self.cols = first, size, cols
         count = math.prod(lax.axis_size(name) for name in axes)
         shape = source.shape if size is None else (size,) + source.shape[1:]
+        if cols is not None:
+            shape = shape[:-1] + (cols[1] - cols[0],)
+        self.shape = shape
         self.result = jax.ShapeDtypeStruct((count,) + shape, source.dtype)
-        self.scratch = dma_sems(count - 1, count - 1, 1)
+        even = (len(shape) > 2 and shape[0] % 2 == 0) or shape[-2] % 32 == 0
+        self.square = axes == ("tm",) and count == 4 and even
+        copies = 4 if self.square else count - 1
+        self.scratch = dma_sems(copies, copies, 1)
 
     def plain(self):
         source = self.source
         if self.size is not None:
             source = source[self.first : self.first + self.size]
+        if self.cols is not None:
+            source = source[..., self.cols[0] : self.cols[1]]
         return lax.all_gather(source, self.axes, axis=0, tiled=False)
 
+    def half(self, ref, index):
+        if len(self.shape) > 2 and self.shape[0] % 2 == 0:
+            size = self.shape[0] // 2
+            return ref.at[pl.ds(index * size, size)]
+        size = self.shape[-2] // 2
+        rows = pl.ds(index * size, size)
+        return ref.at[:, rows] if len(self.shape) == 3 else ref.at[rows]
+
     def start(self, x_ref, out_ref, send_sem, recv_sem, own_sem):
-        me = flat_index(self.axes)
         part = x_ref if self.size is None else x_ref.at[pl.ds(self.first, self.size)]
-        self.copies = [
-            send(part, out_ref.at[me], send_sem.at[i - 1], recv_sem.at[i - 1], place)
-            for i, _, place in flat_peers(self.axes)
-        ]
-        self.copies.append(keep(part, out_ref.at[me], own_sem.at[0]))
+        if self.cols is not None:
+            part = part.at[:, :, pl.ds(self.cols[0], self.cols[1] - self.cols[0])]
+        if self.square:
+            me, near, far, _ = square_places()
+            self.copies = [
+                send(part, out_ref.at[me], send_sem.at[i], recv_sem.at[i], {"tm": peer})
+                for i, peer in enumerate((near, far))
+            ]
+        else:
+            me = flat_index(self.axes)
+            self.copies = [
+                send(part, out_ref.at[me], send_sem.at[i - 1], recv_sem.at[i - 1], place)
+                for i, _, place in flat_peers(self.axes)
+            ]
+        self.own = keep(part, out_ref.at[me], own_sem.at[0])
+
+    def middle(self, x_ref, out_ref, send_sem, recv_sem, own_sem):
+        if not self.square:
+            return
+        _, near, far, _ = square_places()
+        from_near, from_far = self.copies
+        from_far.wait_recv()
+        got = self.half(out_ref.at[far], 0)
+        to_near = send(got, got, send_sem.at[2], recv_sem.at[2], {"tm": near})
+        from_near.wait_recv()
+        got = self.half(out_ref.at[near], 1)
+        to_far = send(got, got, send_sem.at[3], recv_sem.at[3], {"tm": far})
+        self.passed = [to_near, to_far]
 
     def finish(self, *refs):
-        for copy in self.copies:
-            copy.wait()
+        if self.square:
+            for copy in self.copies:
+                copy.wait_send()
+            for copy in self.passed:
+                copy.wait()
+        else:
+            for copy in self.copies:
+                copy.wait()
+        self.own.wait()
 
 
 class JoinCores(Rider):
@@ -241,40 +336,167 @@
     axes = ("tm",)
     result_spec = VMEM
 
+    def __init__(self, source, taps=False):
+        self.taps = taps
+        self.count = lax.axis_size("tm")
+        if taps:
+            self.layers, all_rows, self.width = source.shape
+            self.rows = all_rows // self.count
+        else:
+            self.layers, (_, self.rows, self.width) = 1, source.shape
+        self.source = source
+        shape = (self.layers, self.rows, self.width)
+        self.result = jax.ShapeDtypeStruct(shape if taps else shape[1:], jnp.bfloat16)
+        self.square = self.count == 4 and self.rows % 32 == 0
+        self.split = self.rows // 2 if self.square else self.rows
+        half = (self.layers, self.split, self.width)
+        if self.square:
+            self.scratch = [
+                pltpu.VMEM((2, 2) + half, jnp.bfloat16),
+                pltpu.VMEM((2,) + half, jnp.bfloat16),
+                pltpu.VMEM((2, 2) + half, jnp.bfloat16),
+            ] + dma_sems(4, 6, 6)
+        else:
+            self.scratch = [
+                pltpu.VMEM((max(self.count - 1, 1),) + half, jnp.bfloat16),
+                pltpu.VMEM((1, 1) + half, jnp.bfloat16),
+            ] + dma_sems(1, self.count - 1, self.count - 1)
+
+    def plain(self):
+        dim = 1 if self.taps else 0
+        total = lax.psum_scatter(self.source, "tm", scatter_dimension=dim, tiled=True)
+        return total if self.taps else total[0]
+
+    def view(self, w_ref, place, half):
+        if self.taps:
+            start = pl.multiple_of(place * self.rows + half * self.split, self.split)
+            return w_ref.at[:, pl.ds(start, self.split)]
+        return w_ref.at[pl.ds(place, 1), pl.ds(half * self.split, self.split)]
+
+    def add(self, target_ref, first, *rest):
+        block = min(16, self.split)
+        steps = self.split // block
+
+        def some(index, carry):
+            layer = index // steps
+            rows = pl.ds(pl.multiple_of(lax.rem(index, steps) * block, block), block)
+            total = first[layer, rows].astype(jnp.float32)
+            for other in rest:
+                total = total + other[layer, rows].astype(jnp.float32)
+            target_ref[layer, rows] = total.astype(jnp.bfloat16)
+            return carry
+
+        lax.fori_loop(0, self.layers * steps, some, 0)
+
+    def out_view(self, out_ref, half):
+        rows = pl.ds(half * self.split, self.split)
+        if self.taps:
+            return out_ref.at[:, rows]
+        return out_ref.reshape(1, self.rows, self.width).at[:, rows]
+
+    def start(self, w_ref, out_ref, got_ref, *rest):
+        near_ref, own_sem, send_sem, recv_sem = rest[-4:]
+        if not self.square:
+            me = lax.axis_index("tm")
+            self.copies = [
+                send(self.view(w_ref, peer, 0), got_ref.at[i - 1], send_sem.at[i - 1], recv_sem.at[i - 1], {"tm": peer})
+                for i, peer in others("tm")
+            ]
+            self.own = [keep(self.view(w_ref, me, 0), near_ref.at[0, 0], own_sem.at[0])]
+            return
+        me, near, far, across = square_places()
+        self.copies = [
+            send(self.view(w_ref, place, half), got_ref.at[half, i], send_sem.at[2 * half + i], recv_sem.at[2 * half + i], {"tm": peer})
+            for half, peer in ((0, near), (1, far))
+            for i, place in ((1, across), (0, peer))
+        ]
+        self.own = [
+            keep(self.view(w_ref, place, half), near_ref.at[half, i], own_sem.at[2 * half + i])
+            for half, peer in ((0, far), (1, near))
+            for i, place in ((0, me), (1, peer))
+        ]
+
+    def middle(self, w_ref, out_ref, got_ref, *rest):
+        if not self.square:
+            return
+        last_ref, near_ref, _, send_sem, recv_sem = rest
+        _, near, far, _ = square_places()
+        self.passed = []
+        for half, peer in ((0, far), (1, near)):
+            self.copies[2 * half].wait_recv()
+            self.own[2 * half + 1].wait()
+            self.add(got_ref.at[half, 1], near_ref.at[half, 1], got_ref.at[half, 1])
+            self.passed.append(
+                send(got_ref.at[half, 1], last_ref.at[half], send_sem.at[4 + half], recv_sem.at[4 + half], {"tm": peer})
+            )
+
+    def finish(self, w_ref, out_ref, got_ref, *rest):
+        near_ref = rest[-4]
+        if not self.square:
+            for copy in self.copies + self.own:
+                copy.wait()
+            parts = [got_ref.at[i] for i in range(self.count - 1)]
+            self.add(self.out_view(out_ref, 0), near_ref.at[0, 0], *parts)
+            return
+        last_ref = rest[0]
+        for half in range(2):
+            self.copies[2 * half].wait_send()
+            self.copies[2 * half + 1].wait()
+            self.own[2 * half].wait()
+            self.passed[half].wait()
+            self.add(
+                self.out_view(out_ref, half),
+                near_ref.at[half, 0],
+                got_ref.at[half, 0],
+                last_ref.at[half],
+            )
+
+
+class SmallSum(Rider):
+    source_spec = VMEM
+    result_spec = VMEM
+
     def __init__(self, source):
-        self.count, self.rows, self.width = source.shape
         self.source = source
-        self.result = jax.ShapeDtypeStruct((self.rows, self.width), jnp.bfloat16)
+        self.frames, self.lines = source.shape[:2]
+        part = source.shape[1:]
+        self.result = jax.ShapeDtypeStruct(part[1:], source.dtype)
         self.scratch = [
-            pltpu.VMEM((max(self.count - 1, 1), self.rows, self.width), jnp.bfloat16),
-            pltpu.VMEM((self.rows, self.width), jnp.bfloat16),
-        ] + dma_sems(self.count - 1, self.count - 1, 1)
+            pltpu.VMEM((self.frames - 1,) + part, source.dtype),
+            pltpu.VMEM(part, source.dtype),
+            pltpu.VMEM((self.lines - 1,) + part[1:], source.dtype),
+        ] + dma_sems(self.frames - 1, self.frames - 1, self.lines - 1, self.lines - 1)
+
+    def peers(self):
+        return frame_peers() + line_peers()
 
     def plain(self):
-        return lax.psum_scatter(self.source, "tm", scatter_dimension=0, tiled=True)[0]
-
-    def start(self, w_ref, out_ref, got_ref, own_ref, send_sem, recv_sem, own_sem):
-        me = lax.axis_index("tm")
+        total = lax.psum_scatter(self.source, "tm", scatter_dimension=0, tiled=True)[0]
+        return lax.psum_scatter(total, "space", scatter_dimension=0, tiled=True)[0]
+
+    def start(self, x_ref, out_ref, got_ref, sum_ref, last_ref, send_sem, recv_sem, send2, recv2):
         self.copies = [
-            send(w_ref.at[peer], got_ref.at[i - 1], send_sem.at[i - 1], recv_sem.at[i - 1], {"tm": peer})
+            send(x_ref.at[peer], got_ref.at[i - 1], send_sem.at[i - 1], recv_sem.at[i - 1], {"tm": peer})
             for i, peer in others("tm")
         ]
-        self.copies.append(keep(w_ref.at[me], own_ref, own_sem.at[0]))
-
-    def finish(self, w_ref, out_ref, got_ref, own_ref, *sems):
-        for copy in self.copies:
+
+    def middle(self, x_ref, out_ref, got_ref, sum_ref, last_ref, send_sem, recv_sem, send2, recv2):
+        total = x_ref[lax.axis_index("tm")]
+        for i, copy in enumerate(self.copies):
             copy.wait()
-        block = min(16, self.rows)
-
-        def some(index, carry):
-            rows = pl.ds(pl.multiple_of(index * block, block), block)
-            total = own_ref[rows, :].astype(jnp.float32)
-            for step in range(self.count - 1):
-                total = total + got_ref[step, rows, :].astype(jnp.float32)
-            out_ref[rows, :] = total.astype(jnp.bfloat16)
-            return carry
-
-        lax.fori_loop(0, self.rows // block, some, 0)
+            total = total + got_ref[i]
+        sum_ref[...] = total
+        self.passed = [
+            send(sum_ref.at[peer], last_ref.at[i - 1], send2.at[i - 1], recv2.at[i - 1], {"space": peer})
+            for i, peer in others("space")
+        ]
+
+    def finish(self, x_ref, out_ref, got_ref, sum_ref, last_ref, *sems):
+        total = sum_ref[lax.axis_index("space")]
+        for i, copy in enumerate(self.passed):
+            copy.wait()
+            total = total + last_ref[i]
+        out_ref[...] = total
 
 
 class Keep(Rider):
@@ -298,6 +520,7 @@
 
 class TapSum(Rider):
     axes = ("tm",)
+    source_spec = VMEM
     result_spec = VMEM
 
     def __init__(self, source):
@@ -335,6 +558,40 @@
             return carry
 
         lax.fori_loop(0, self.taps, some, 0)
+
+
+class CoreSum(Rider):
+    source_spec = VMEM
+    result_spec = VMEM
+
+    def __init__(self, source):
+        self.source = source
+        rows, channels = source.shape
+        self.rows, self.width = rows, channels // lax.axis_size("mp")
+        self.result = jax.ShapeDtypeStruct((rows, self.width), jnp.bfloat16)
+        self.scratch = [pltpu.VMEM((rows, self.width), jnp.bfloat16)] + dma_sems(1, 1)
+
+    def peers(self):
+        return twin_peers()
+
+    def start(self, x_ref, out_ref, got_ref, send_sem, recv_sem):
+        core = lax.axis_index("mp")
+        theirs = pl.ds(pl.multiple_of((1 - core) * self.width, self.width), self.width)
+        self.copy = send(x_ref.at[:, theirs], got_ref, send_sem.at[0], recv_sem.at[0], {"mp": 1 - core})
+
+    def finish(self, x_ref, out_ref, got_ref, *sems):
+        self.copy.wait()
+        block = min(128, self.rows)
+        start = lax.axis_index("mp") * self.width
+        mine = pl.ds(pl.multiple_of(start, self.width), self.width)
+
+        def some(index, carry):
+            rows = pl.ds(pl.multiple_of(index * block, block), block)
+            total = x_ref[rows, mine].astype(jnp.float32) + got_ref[rows, :].astype(jnp.float32)
+            out_ref[rows, :] = total.astype(jnp.bfloat16)
+            return carry
+
+        lax.fori_loop(0, self.rows // block, some, 0)
 
 
 def plain_all(riders):
@@ -358,7 +615,15 @@
         meet(peers() + [peer for rider in riders for peer in rider.peers()])
         for rider, pack in zip(riders, packs):
             rider.start(*pack)
-        kernel(*ins, out_ref, *mine)
+        waiting = list(zip(riders, packs))
+
+        def hook():
+            while waiting:
+                rider, pack = waiting.pop(0)
+                rider.middle(*pack)
+
+        kernel(hook, *ins, out_ref, *mine)
+        hook()
         for rider, pack in zip(riders, packs):
             rider.finish(*pack)
 
@@ -368,7 +633,7 @@
         operands + [rider.source for rider in riders],
         scratch + [item for rider in riders for item in rider.scratch],
         number,
-        specs + [ANY] * count,
+        specs + [rider.source_spec for rider in riders],
         (out_spec,) + tuple(rider.result_spec for rider in riders),
     )
     return results[0], list(results[1:])
@@ -384,6 +649,119 @@
 
 def twin_peers():
     return [{"mp": 1 - lax.axis_index("mp")}]
+
+
+pieces_per_chunk = 2
+
+
+def relay_gather(lines, own, slot, sems, hook, arrived=None):
+    me = lax.axis_index("space")
+    right_send, right_recv, left_send, left_recv = sems
+    parts = pieces_per_chunk
+
+    def move(step, part, sign, send_sem, recv_sem):
+        place = slot(lax.rem(me - sign * step + lines, lines), part)
+        at = step * parts + part
+        return pltpu.make_async_remote_copy(
+            own(part) if step == 0 else place, place, send_sem.at[at], recv_sem.at[at],
+            device_id={"space": lax.rem(me + sign + lines, lines)}, device_id_type=MESH,
+        )
+
+    def came(step, part, sign, recv_sem, order):
+        place = slot(lax.rem(me - sign * (step + 1) + lines, lines), part)
+        at = step * parts + part
+        pltpu.make_async_remote_copy(
+            place, place, recv_sem.at[at], recv_sem.at[at],
+            device_id={"space": lax.rem(me + 1, lines)}, device_id_type=MESH,
+        ).wait_recv()
+        if arrived is not None:
+            arrived(place, order * parts + part)
+
+    ways = (
+        (1, me, right_send, right_recv, 0),
+        (-1, lines - 1 - me, left_send, left_recv, lines - 1),
+    )
+    for step in range(lines):
+        for part in range(parts):
+            for sign, rank, send_sem, recv_sem, order in ways:
+                if step > 0:
+
+                    @pl.when(rank >= step)
+                    def _():
+                        came(step - 1, part, sign, recv_sem, order + step - 1)
+
+                if step < lines - 1:
+
+                    @pl.when((rank >= step) & (rank + 1 < lines))
+                    def _():
+                        move(step, part, sign, send_sem, recv_sem).start()
+
+        if step == min(1, lines - 1):
+            hook()
+    for step in range(lines - 1):
+        for part in range(parts):
+            for sign, rank, send_sem, recv_sem, _ in ways:
+
+                @pl.when((rank >= step) & (rank + 1 < lines))
+                def _():
+                    move(step, part, sign, send_sem, recv_sem).wait_send()
+
+
+def relay_sum(lines, stage_ref, right_ref, left_ref, sems, hook, ready=None):
+    me = lax.axis_index("space")
+    right_send, right_recv, left_send, left_recv = sems
+    parts, last = pieces_per_chunk, lines - 1
+
+    def move(source, slots, sem_out, sem_in, step, part, peer):
+        at = step * parts + part
+        return pltpu.make_async_remote_copy(
+            source, slots.at[step, part], sem_out.at[at], sem_in.at[at],
+            device_id={"space": lax.rem(peer + lines, lines)}, device_id_type=MESH,
+        )
+
+    def add(slots, step, part, place):
+        total = slots[step, part].astype(jnp.float32) + stage_ref[place, part].astype(jnp.float32)
+        slots[step, part] = total.astype(jnp.bfloat16)
+
+    ways = (
+        (me, me + 1, right_ref, right_send, right_recv, lambda step: last - step + me),
+        (last - me, me - 1, left_ref, left_send, left_recv, lambda step: step - last + me),
+    )
+    for step in range(last):
+        if ready is not None:
+            ready(step)
+        for part in range(parts):
+            for rank, peer, slots, sem_out, sem_in, target in ways:
+                place = lax.rem(target(step) + 2 * lines, lines)
+
+                @pl.when(rank == 0)
+                def _():
+                    move(stage_ref.at[place, part], slots, sem_out, sem_in, step, part, peer).start()
+
+                if step > 0:
+
+                    @pl.when((rank > 0) & (rank <= step))
+                    def _():
+                        source = stage_ref.at[place, part]
+                        move(source, slots, sem_out, sem_in, step - 1, part, peer).wait_recv()
+                        add(slots, step - 1, part, place)
+                        source = slots.at[step - 1, part]
+                        move(source, slots, sem_out, sem_in, step, part, peer).start()
+
+        if step == min(1, last - 1):
+            hook()
+    for part in range(parts):
+        for rank, peer, slots, sem_out, sem_in, target in ways:
+
+            @pl.when(rank > 0)
+            def _():
+                move(stage_ref.at[0, part], slots, sem_out, sem_in, last - 1, part, peer).wait_recv()
+
+            for step in range(last):
+
+                @pl.when(rank <= step)
+                def _():
+                    move(stage_ref.at[0, part], slots, sem_out, sem_in, step, part, peer).wait_send()
 
 
 def to_lines(source, per_core, number, riders=(), join=False):
@@ -399,7 +777,7 @@
         moved = lax.all_to_all(source, "space", split_axis=2, concat_axis=1, tiled=True)
         return moved, plain_all(riders)
 
-    def kernel(x_ref, out_ref, send_sem, recv_sem, pass_sem, gain_sem, own_sem):
+    def kernel(hook, x_ref, out_ref, stage_ref, send_sem, recv_sem, pass_sem, gain_sem, own_sem):
         me, core = lax.axis_index("space"), lax.axis_index("mp")
         twin = {"mp": 1 - core}
         place = (lambda s: s * cores + core) if per_core or join else (lambda s: s)
@@ -408,10 +786,13 @@
             rows = rows_of(out_ref, origin, pixels)
             return cols_of(rows, core, width) if join else rows
 
-        copies = [
-            send(cols_of(x_ref, place(peer), width), spot(me), send_sem.at[i - 1], recv_sem.at[i - 1], {"space": peer})
-            for i, peer in others("space")
-        ]
+        copies = []
+        for i, peer in others("space"):
+            start = pl.multiple_of(place(peer) * width, width)
+            stage_ref[i - 1] = x_ref[:, :, pl.ds(start, width)]
+            copies.append(
+                send(stage_ref.at[i - 1], spot(me), send_sem.at[i - 1], recv_sem.at[i - 1], {"space": peer})
+            )
         if join:
             own_width = cores * width
             own = keep(cols_of(x_ref, me, own_width), rows_of(out_ref, me, pixels), own_sem.at[0])
@@ -434,8 +815,9 @@
 
     held = cores * width if join else width
     result = jax.ShapeDtypeStruct((images, lines * pixels, held), source.dtype)
-    sems = dma_sems(lines - 1, lines - 1, lines - 1, lines - 1, 1)
-    return talk_with(kernel, peers, result, [source], sems, number, riders)
+    scratch = [pltpu.VMEM((lines - 1, images, pixels, width), source.dtype)]
+    scratch = scratch + dma_sems(lines - 1, lines - 1, lines - 1, lines - 1, 1)
+    return talk_with(kernel, peers, result, [source], scratch, number, riders, [VMEM])
 
 
 def from_lines(source, per_core, number, riders=()):
@@ -450,37 +832,40 @@
             part = lax.all_gather(part, "mp", axis=3, tiled=True)
         return part.reshape(images, pixels, pieces * width), plain_all(riders)
 
-    def kernel(x_ref, out_ref, send_sem, recv_sem, pass_sem, gain_sem, own_sem):
+    def kernel(hook, x_ref, out_ref, got_ref, send_sem, recv_sem, pass_sem, gain_sem):
         me, core = lax.axis_index("space"), lax.axis_index("mp")
-        place = (lambda s: s * cores + core) if per_core else (lambda s: s)
         twin = {"mp": 1 - core}
-        target = cols_of(out_ref, place(me), width)
+        mine = core if per_core else 0
         copies = [
-            send(rows_of(x_ref, peer, pixels), target, send_sem.at[i - 1], recv_sem.at[i - 1], {"space": peer})
+            send(rows_of(x_ref, peer, pixels), got_ref.at[me, mine], send_sem.at[i - 1], recv_sem.at[i - 1], {"space": peer})
             for i, peer in others("space")
         ]
-        own = keep(rows_of(x_ref, me, pixels), target, own_sem.at[0])
         passed = []
         if per_core:
-            passed.append(send(rows_of(x_ref, me, pixels), target, pass_sem.at[0], gain_sem.at[0], twin))
+            passed.append(
+                send(rows_of(x_ref, me, pixels), got_ref.at[me, core], pass_sem.at[0], gain_sem.at[0], twin)
+            )
+        got_ref[me, mine] = x_ref[:, pl.ds(pl.multiple_of(me * pixels, pixels), pixels), :]
         for step in range(1, lines):
             copies[step - 1].wait_recv()
             if per_core:
-                origin = lax.rem(me - step + lines, lines)
-                got = cols_of(out_ref, place(origin), width)
+                got = got_ref.at[lax.rem(me - step + lines, lines), core]
                 passed.append(send(got, got, pass_sem.at[step], gain_sem.at[step], twin))
         for copy in copies:
             copy.wait_send()
-        own.wait()
         for copy in passed:
             copy.wait()
+        each = pieces // lines
+        for piece in range(pieces):
+            out_ref[:, :, piece * width : (piece + 1) * width] = got_ref[piece // each, piece % each]
 
     def peers():
         return line_peers() + ([{"mp": 1 - lax.axis_index("mp")}] if per_core else [])
 
     result = jax.ShapeDtypeStruct((images, pixels, pieces * width), source.dtype)
-    sems = dma_sems(lines - 1, lines - 1, lines, lines, 1)
-    return talk_with(kernel, peers, result, [source], sems, number, riders)
+    scratch = [pltpu.VMEM((lines, pieces // lines, images, pixels, width), source.dtype)]
+    scratch = scratch + dma_sems(lines - 1, lines - 1, lines, lines)
+    return talk_with(kernel, peers, result, [source], scratch, number, riders, [VMEM], VMEM)
 
 
 def gather_lines(source, number, riders=()):
@@ -489,20 +874,24 @@
     if width % lane != 0:
         return lax.all_gather(source, "space", axis=2, tiled=True), plain_all(riders)
 
-    def kernel(x_ref, out_ref, send_sem, recv_sem, own_sem):
-        me = lax.axis_index("space")
-        target = cols_of(out_ref, me, width)
-        copies = [
-            send(x_ref, target, send_sem.at[i - 1], recv_sem.at[i - 1], {"space": peer})
-            for i, peer in others("space")
-        ]
-        copies.append(keep(x_ref, target, own_sem.at[0]))
-        for copy in copies:
-            copy.wait()
+    def kernel(hook, x_ref, out_ref, got_ref, *sems):
+        some = images // pieces_per_chunk
+
+        def own(part):
+            return x_ref.at[pl.ds(part * some, some)]
+
+        def slot(index, part):
+            return got_ref.at[index, pl.ds(part * some, some)]
+
+        got_ref[lax.axis_index("space")] = x_ref[...]
+        relay_gather(lines, own, slot, sems, hook)
+        for line in range(lines):
+            out_ref[:, :, line * width : (line + 1) * width] = got_ref[line]
 
     result = jax.ShapeDtypeStruct((images, line_pixels, lines * width), source.dtype)
-    sems = dma_sems(lines - 1, lines - 1, 1)
-    return talk_with(kernel, line_peers, result, [source], sems, number, riders)
+    scratch = [pltpu.VMEM((lines,) + source.shape, source.dtype)]
+    scratch = scratch + dma_sems(*[pieces_per_chunk * (lines - 1)] * 4)
+    return talk_with(kernel, line_peers, result, [source], scratch, number, riders, [VMEM], VMEM)
 
 
 def gather_cores(source, number, riders=()):
@@ -511,7 +900,7 @@
     if width % lane != 0:
         return lax.all_gather(source, "mp", axis=2, tiled=True), plain_all(riders)
 
-    def kernel(x_ref, out_ref, send_sem, recv_sem, own_sem):
+    def kernel(hook, x_ref, out_ref, send_sem, recv_sem, own_sem):
         core = lax.axis_index("mp")
         twin = {"mp": 1 - core}
         target = cols_of(out_ref, core, width)
@@ -532,27 +921,34 @@
         total = lax.psum_scatter(source, "space", scatter_dimension=2, tiled=True)
         return total.astype(jnp.float32), plain_all(riders)
 
-    def kernel(x_ref, out_ref, got_ref, send_sem, recv_sem):
+    def kernel(hook, x_ref, out_ref, stage_ref, right_ref, left_ref, *sems):
         me = lax.axis_index("space")
-        copies = [
-            send(cols_of(x_ref, peer, width), got_ref.at[i - 1], send_sem.at[i - 1], recv_sem.at[i - 1], {"space": peer})
-            for i, peer in others("space")
-        ]
-        mine = pl.ds(pl.multiple_of(me * width, width), width)
-        for copy in copies:
-            copy.wait()
-        for image in range(images):
-            total = x_ref[image, :, mine].astype(jnp.float32)
-            for step in range(lines - 1):
-                total = total + got_ref[step, image].astype(jnp.float32)
-            out_ref[image] = total
+        for line in range(lines):
+            for part in range(pieces_per_chunk):
+                rows = slice(part * some, (part + 1) * some)
+                stage_ref[line, part] = x_ref[rows, :, line * width : (line + 1) * width]
+        relay_sum(lines, stage_ref, right_ref, left_ref, sems, hook)
+        for part in range(pieces_per_chunk):
+            rows = slice(part * some, (part + 1) * some)
+            out_ref[rows] = stage_ref[me, part].astype(jnp.float32)
+
+            @pl.when(me > 0)
+            def _():
+                out_ref[rows] += right_ref[lines - 2, part].astype(jnp.float32)
+
+            @pl.when(me < lines - 1)
+            def _():
+                out_ref[rows] += left_ref[lines - 2, part].astype(jnp.float32)
 
     result = jax.ShapeDtypeStruct((images, line_pixels, width), jnp.float32)
-    scratch = [pltpu.VMEM((lines - 1, images, line_pixels, width), source.dtype)]
-    scratch = scratch + dma_sems(lines - 1, lines - 1)
-    return talk_with(
-        kernel, line_peers, result, [source], scratch, number, riders, [VMEM], VMEM
-    )
+    some = images // pieces_per_chunk
+    chunk = (pieces_per_chunk, some, line_pixels, width)
+    scratch = [
+        pltpu.VMEM((lines,) + chunk, source.dtype),
+        pltpu.VMEM((lines - 1,) + chunk, source.dtype),
+        pltpu.VMEM((lines - 1,) + chunk, source.dtype),
+    ] + dma_sems(*[pieces_per_chunk * (lines - 1)] * 4)
+    return talk_with(kernel, line_peers, result, [source], scratch, number, riders, [VMEM], VMEM)
 
 
 def sum_cores(source, number, riders=()):
@@ -563,7 +959,7 @@
         total = lax.psum_scatter(source, "mp", scatter_dimension=2, tiled=True)
         return total.astype(jnp.float32), plain_all(riders)
 
-    def kernel(x_ref, out_ref, got_ref, send_sem, recv_sem):
+    def kernel(hook, x_ref, out_ref, got_ref, send_sem, recv_sem):
         core = lax.axis_index("mp")
         twin = {"mp": 1 - core}
         copy = send(cols_of(x_ref, 1 - core, width), got_ref, send_sem.at[0], recv_sem.at[0], twin)
@@ -588,36 +984,56 @@
     width = channels // cores
     source = rows.reshape(1, count, channels)
 
-    def kernel(x_ref, out_ref, send_sem, recv_sem, pass_sem, gain_sem, own_sem):
+    def kernel(hook, x_ref, out_ref, pass_sem, gain_sem, own_sem, *sems):
         me, core = lax.axis_index("space"), lax.axis_index("mp")
         twin = {"mp": 1 - core}
 
-        def spot(origin):
-            return cols_of(rows_of(out_ref, origin, count), core, width)
-
-        copies = [
-            send(cols_of(x_ref, core, width), spot(me), send_sem.at[i - 1], recv_sem.at[i - 1], {"space": peer})
-            for i, peer in others("space")
-        ]
+        some = count // pieces_per_chunk
+
+        def spot(origin, part):
+            start = pl.multiple_of(origin * count + part * some, some)
+            return cols_of(out_ref.at[:, pl.ds(start, some)], core, width)
+
+        def own_part(part):
+            return cols_of(x_ref.at[:, pl.ds(part * some, some)], core, width)
+
+        def hand(ref, order):
+            return pltpu.make_async_remote_copy(
+                ref, ref, pass_sem.at[order], gain_sem.at[order], device_id=twin, device_id_type=MESH
+            )
+
         own = keep(x_ref, rows_of(out_ref, me, count), own_sem.at[0])
-        passed = []
+        relay_gather(
+            lines,
+            own_part,
+            spot,
+            sems,
+            hook,
+            lambda ref, order: hand(ref, order).start(),
+        )
+        own.wait()
+        parts = pieces_per_chunk
         for step in range(1, lines):
-            copies[step - 1].wait_recv()
-            got = spot(lax.rem(me - step + lines, lines))
-            passed.append(send(got, got, pass_sem.at[step - 1], gain_sem.at[step - 1], twin))
-        for copy in copies:
-            copy.wait_send()
-        own.wait()
-        for copy in passed:
-            copy.wait()
+            for part in range(parts):
+
+                @pl.when(me - step >= 0)
+                def _():
+                    place = spot(lax.rem(me - step + lines, lines), part)
+                    hand(place, (step - 1) * parts + part).wait()
+
+                @pl.when(me + step < lines)
+                def _():
+                    place = spot(lax.rem(me + step, lines), part)
+                    hand(place, (lines + step - 2) * parts + part).wait()
 
     result = jax.ShapeDtypeStruct((1, lines * count, channels), rows.dtype)
-    sems = dma_sems(lines - 1, lines - 1, lines - 1, lines - 1, 1)
+    moves = pieces_per_chunk * (lines - 1)
+    sems = dma_sems(2 * moves, 2 * moves, 1, *[moves] * 4)
 
     def peers():
         return line_peers() + twin_peers()
 
-    line, others_done = talk_with(kernel, peers, result, [source], sems, number, riders)
+    line, others_done = talk_with(kernel, peers, result, [source], sems, number, riders, [VMEM], VMEM)
     return line.reshape(lines * count, channels), others_done
 
 
@@ -627,44 +1043,59 @@
     count, width = all_rows // lines, channels // cores
     source = partial_sum.astype(jnp.bfloat16).reshape(lines, count, channels)
 
-    def kernel(x_ref, out_ref, twin_ref, sum_ref, got_ref, s_sem, r_sem, s2_sem, r2_sem, s3_sem, r3_sem):
+    def kernel(
+        hook, x_ref, out_ref, twin_ref, stage_ref, right_ref, left_ref, sum_ref,
+        s_sem, r_sem, s3_sem, r3_sem, *sems,
+    ):
         me, core = lax.axis_index("space"), lax.axis_index("mp")
         twin = {"mp": 1 - core}
         theirs = pl.ds(pl.multiple_of((1 - core) * width, width), width)
         mine = pl.ds(pl.multiple_of(core * width, width), width)
-        order = [(i, peer) for i, peer in others("space")] + [(0, me)]
+        order = [lines - 1, 0] + list(range(1, lines - 1))
         first = [
-            send(x_ref.at[target, :, theirs], twin_ref.at[i], s_sem.at[i], r_sem.at[i], twin)
-            for i, target in order
+            send(x_ref.at[target, :, theirs], twin_ref.at[target], s_sem.at[target], r_sem.at[target], twin)
+            for target in order
         ]
-        second = []
-        for (i, target), copy in zip(order, first):
-            copy.wait_recv()
-            total = x_ref[target, :, mine].astype(jnp.float32) + twin_ref[i].astype(jnp.float32)
-            if i == 0:
-                own = total
-            else:
-                sum_ref[i - 1] = total.astype(jnp.bfloat16)
-                second.append(
-                    send(sum_ref.at[i - 1], got_ref.at[i - 1], s2_sem.at[i - 1], r2_sem.at[i - 1], {"space": target})
-                )
-        for copy in second:
-            copy.wait_recv()
-        for i in range(lines - 1):
-            own = own + got_ref[i].astype(jnp.float32)
-        out_ref[:, mine] = own.astype(jnp.bfloat16)
+
+        def ready(step):
+            turn = {0: zip(order[:2], first[:2]), 1: zip(order[2:], first[2:])}
+            for target, copy in turn.get(step, ()):
+                copy.wait_recv()
+                total = x_ref[target, :, mine].astype(jnp.float32)
+                total = total + twin_ref[target].astype(jnp.float32)
+                total = total.astype(jnp.bfloat16)
+                for part in range(pieces_per_chunk):
+                    stage_ref[target, part] = total[part * some : (part + 1) * some]
+
+        relay_sum(lines, stage_ref, right_ref, left_ref, sems, hook, ready)
+        for part in range(pieces_per_chunk):
+            sum_ref[part] = stage_ref[me, part].astype(jnp.float32)
+
+            @pl.when(me > 0)
+            def _():
+                sum_ref[part] += right_ref[lines - 2, part].astype(jnp.float32)
+
+            @pl.when(me < lines - 1)
+            def _():
+                sum_ref[part] += left_ref[lines - 2, part].astype(jnp.float32)
+
+            out_ref[part * some : (part + 1) * some, mine] = sum_ref[part].astype(jnp.bfloat16)
         third = send(out_ref.at[:, mine], out_ref.at[:, mine], s3_sem.at[0], r3_sem.at[0], twin)
-        for copy in first + second:
+        for copy in first:
             copy.wait_send()
         third.wait()
 
     result = jax.ShapeDtypeStruct((count, channels), jnp.bfloat16)
+    some = count // pieces_per_chunk
+    chunk = (pieces_per_chunk, some, width)
     scratch = [
         pltpu.VMEM((lines, count, width), jnp.bfloat16),
-        pltpu.VMEM((max(lines - 1, 1), count, width), jnp.bfloat16),
-        pltpu.VMEM((max(lines - 1, 1), count, width), jnp.bfloat16),
+        pltpu.VMEM((lines,) + chunk, jnp.bfloat16),
+        pltpu.VMEM((lines - 1,) + chunk, jnp.bfloat16),
+        pltpu.VMEM((lines - 1,) + chunk, jnp.bfloat16),
+        pltpu.VMEM(chunk, jnp.float32),
     ]
-    sems = dma_sems(lines, lines, lines - 1, lines - 1, 1, 1)
+    sems = dma_sems(lines, lines, 1, 1, *[pieces_per_chunk * (lines - 1)] * 4)
 
     def peers():
         return line_peers() + [{"mp": 1 - lax.axis_index("mp")}]
@@ -682,7 +1113,7 @@
     if few % 16 != 0:
         return lax.all_to_all(source, "tm", split_axis=2, concat_axis=1, tiled=True), plain_all(riders)
 
-    def kernel(x_ref, out_ref, send_sem, recv_sem, own_sem):
+    def kernel(hook, x_ref, out_ref, send_sem, recv_sem, own_sem):
         me = lax.axis_index("tm")
         target = out_ref.at[:, pl.ds(me * frames, frames)]
 
@@ -709,7 +1140,7 @@
     if few % 16 != 0:
         return lax.all_to_all(source, "tm", split_axis=1, concat_axis=2, tiled=True), plain_all(riders)
 
-    def kernel(x_ref, out_ref, send_sem, recv_sem, own_sem):
+    def kernel(hook, x_ref, out_ref, send_sem, recv_sem, own_sem):
         me = lax.axis_index("tm")
         target = out_ref.at[:, :, pl.ds(pl.multiple_of(me * few, few), few)]
 
@@ -762,11 +1193,11 @@
     return result.reshape(source.shape[:4] + (result.shape[-1],))
 
 
-def conv_weight_grad(source, upstream, form):
+def conv_weight_grad(source, upstream, form, taps=range(9)):
     padded = padded_rims(source)
     rows, cols = source.shape[2], source.shape[3]
     tap_list = []
-    for tap in range(9):
+    for tap in taps:
         i, j = tap // 3, tap % 3
         tap_list.append(
             jnp.einsum(
@@ -806,7 +1237,7 @@
         in_specs=in_specs,
         out_specs=out_specs,
         scratch_shapes=list(scratch),
-        compiler_params=pltpu.CompilerParams(vmem_limit_bytes=48 * 1024 * 1024),
+        compiler_params=pltpu.CompilerParams(vmem_limit_bytes=32 * 1024 * 1024),
     )(*operands)
 
 
@@ -872,28 +1303,54 @@
     return inverse * (scaled - first - normal * second), gain_grad
 
 
-def in_weight(halves, index):
-    per = halves[0].shape[0] // 4
+def in_weight(packs, index, width):
+    per = packs[0].shape[0] // 4
+    cols = width // per
     return jnp.concatenate(
         [
-            jnp.concatenate([half[t, s] for half in halves for s in range(half.shape[1])], axis=0)
+            jnp.concatenate(
+                [
+                    pack[t, s, :, i * cols : (i + 1) * cols]
+                    for pack in packs
+                    for s in range(pack.shape[1])
+                    for i in range(pack.shape[3] // cols)
+                ],
+                axis=0,
+            )
             for t in range(index * per, (index + 1) * per)
         ],
         axis=1,
     )
 
 
-def out_weight(halves, index):
-    frames, width = halves[0].shape[0], halves[0].shape[3] // 3
-    cols = slice(index * width, (index + 1) * width)
+def out_weight(pack, index, count):
+    width = pack.shape[3] // count
     return jnp.concatenate(
         [
-            jnp.concatenate([half[t, s, :, cols] for t in range(frames)], axis=0)
-            for half in halves
-            for s in range(half.shape[1])
+            jnp.concatenate(
+                [pack[t, s, :, index * width : (index + 1) * width] for t in range(pack.shape[0])],
+                axis=0,
+            )
+            for s in range(pack.shape[1])
         ],
         axis=1,
     )
+
+
+class Fetch:
+    def __init__(self, sources, targets, sem):
+        self.copies = [keep(*pair, sem.at[i]) for i, pair in enumerate(zip(sources, targets))]
+        self.targets, self.here = targets, set()
+
+    def __call__(self, index):
+        if index not in self.here:
+            self.here.add(index)
+            self.copies[index].wait()
+        return self.targets[index]
+
+
+def fetch_scratch(arrays):
+    return [pltpu.VMEM(item.shape, item.dtype) for item in arrays] + dma_sems(len(arrays))
 
 
 def spatial_forward(rows, weight):
@@ -1144,18 +1601,40 @@
     return mine_ref[...].astype(jnp.float32) + theirs_ref[...].astype(jnp.float32)
 
 
-def chat(kernel, results, operands, rows, channels, swaps, number, scratch=()):
-    own = [
-        pltpu.VMEM((swaps, rows, channels), jnp.bfloat16),
-        pltpu.VMEM((swaps, rows, channels), jnp.bfloat16),
-    ] + dma_sems(swaps, swaps)
-    count = len(operands) + len(results)
+def chat(kernel, results, operands, rows, channels, swaps, number, scratch=(), far=(), late=()):
+    own = []
+    if swaps > 0:
+        own = [
+            pltpu.VMEM((swaps, rows, channels), jnp.bfloat16),
+            pltpu.VMEM((swaps, rows, channels), jnp.bfloat16),
+        ] + dma_sems(swaps, swaps)
+    near, fetched = len(operands), len(far)
+    count = near + fetched + len(results)
+    late = list(late)
+    late_scratch = [pltpu.VMEM(results[i].shape, results[i].dtype) for i in late] + dma_sems(
+        len(late)
+    )
 
     def whole(*refs):
-        mine_ref, theirs_ref, send_sem, recv_sem = refs[count : count + 4]
-        meet(twin_peers())
+        ins, sources = refs[:near], refs[near : near + fetched]
+        outs = list(refs[near + fetched : count])
+        rest = refs[count:]
+        swapped, rest = rest[: len(own)], rest[len(own) :]
+        targets, sem, rest = rest[:fetched], rest[fetched], rest[fetched + 1 :]
+        held, late_sem, rest = rest[: len(late)], rest[len(late)], rest[len(late) + 1 :]
+        fetch = Fetch(sources, targets, sem)
+        ends = {place: outs[place] for place in late}
+        for place, ref in zip(late, held):
+            outs[place] = ref
+        written = []
+
+        def flush(*places):
+            for place in places:
+                index = late.index(place)
+                written.append(keep(held[index], ends[place], late_sem.at[index]))
 
         def swap(index, partial_sum, work=None):
+            mine_ref, theirs_ref, send_sem, recv_sem = swapped
             return twin_sum(
                 partial_sum,
                 mine_ref.at[index],
@@ -1165,17 +1644,27 @@
                 work,
             )
 
-        kernel(swap, *refs[:count], *refs[count + 4 :])
-
-    return talk(
+        if swaps > 0:
+            meet(twin_peers())
+        kernel(swap, fetch, flush, *ins, *outs, *rest)
+        for copy in written:
+            copy.wait()
+
+    specs = [VMEM] * near + [ANY] * fetched
+    out_specs = tuple(ANY if i in late else VMEM for i in range(len(results)))
+    scratch = own + fetch_scratch(far) + late_scratch + list(scratch)
+    if swaps > 0:
+        return talk(
+            whole, tuple(results), list(operands) + list(far), scratch, number, specs, out_specs, 56
+        )
+    return pl.pallas_call(
         whole,
-        tuple(results),
-        operands,
-        own + list(scratch),
-        number,
-        [VMEM] * len(operands),
-        tuple([VMEM] * len(results)),
-    )
+        out_shape=tuple(results),
+        in_specs=specs,
+        out_specs=out_specs,
+        scratch_shapes=scratch,
+        compiler_params=pltpu.CompilerParams(vmem_limit_bytes=56 * 1024 * 1024),
+    )(*operands, *far)
 
 
 def group_means(totals, count):
@@ -1263,7 +1752,7 @@
         out_shape=tuple(results),
         in_specs=[VMEM] * len(operands),
         out_specs=tuple([VMEM] * len(results)),
-        compiler_params=pltpu.CompilerParams(vmem_limit_bytes=48 * 1024 * 1024),
+        compiler_params=pltpu.CompilerParams(vmem_limit_bytes=32 * 1024 * 1024),
     )(*operands)
 
 
@@ -1294,60 +1783,72 @@
 
 
 def first_norm(rows, branch, gain):
-    def kernel(x_ref, branch_ref, gain_ref, one_ref, normed_ref):
-        one = x_ref[...].astype(jnp.float32) + branch_ref[...].astype(jnp.float32)
+    def kernel(swap, fetch, flush, branch_ref, gain_ref, one_ref, normed_ref):
+        one = fetch(0)[...].astype(jnp.float32) + branch_ref[...].astype(jnp.float32)
         one_ref[...] = one
+        flush(0)
         normed_ref[...] = low(norm_forward(one, gain_ref[...]))
 
-    return flat_call(
+    return chat(
         kernel,
         [
             jax.ShapeDtypeStruct(rows.shape, jnp.float32),
             jax.ShapeDtypeStruct(rows.shape, jnp.bfloat16),
         ],
-        [rows, branch, gain],
+        [branch, gain],
+        *rows.shape,
+        0,
+        0,
+        far=[rows],
+        late=[0],
     )
 
 
 def first_norm_backward(stream, gain, normed_grad, upstream, owners, lines):
-    def kernel(x_ref, gain_ref, normed_ref, up_ref, grad_ref, both_ref, dg_ref):
+    def kernel(swap, fetch, flush, gain_ref, normed_ref, grad_ref, both_ref, dg_ref):
         step, gain_grad = norm_backward(
-            x_ref[...], gain_ref[...], normed_ref[...].astype(jnp.float32)
+            fetch(0)[...], gain_ref[...], normed_ref[...].astype(jnp.float32)
         )
-        grad = up_ref[...] + step
+        grad = fetch(1)[...] + step
         grad_ref[...] = grad
+        flush(0)
         dg_ref[...] = gain_grad
         store_both(both_ref, low(grad), owners, lines)
 
-    grad, both, gain_grad = flat_call(
+    grad, both, gain_grad = chat(
         kernel,
         [
             jax.ShapeDtypeStruct(stream.shape, jnp.float32),
             jax.ShapeDtypeStruct((2,) + stream.shape, jnp.bfloat16),
             jax.ShapeDtypeStruct(gain.shape, jnp.float32),
         ],
-        [stream, gain, normed_grad, upstream],
+        [gain, normed_grad],
+        *stream.shape,
+        0,
+        0,
+        far=[stream, upstream],
+        late=[0],
     )
     if (stream.shape[1] // owners) % HDIM != 0:
         both = jnp.stack([both[0], by_owner_line(both[0], owners, lines)])
     return grad, both, gain_grad
 
 
-def middle_forward(mix, stream, out_halves, in_halves, pairs, valid, gains, number):
+def middle_forward(mix, stream, outs, ins, pairs, valid, gains, number):
     rows, channels = stream.shape
     width = mix.shape[1]
     slots = pairs.shape[0]
     part = rows // slots
 
     def kernel(
-        swap, mix_ref, x_ref, out_ref, out_rest, in_ref, in_rest, pairs_ref, valid_ref, gain_ref,
+        swap, fetch, flush, mix_ref, x_ref, pairs_ref, valid_ref, gain_ref,
         two_ref, normed_ref, query_ref, cross_ref, three_ref, last_ref, triple_ref,
     ):
-        outs, ins = (out_ref, out_rest), (in_ref, in_rest)
-        two = x_ref[...] + swap(0, dot(mix_ref[...], out_weight(outs, 0)))
+        two = x_ref[...] + swap(0, dot(mix_ref[...], out_weight(fetch(0), 0, 2)))
         two_ref[...] = two
         normed_ref[...] = low(norm_forward(two, gain_ref[0:1, :]))
-        query_ref[...] = low(dot(normed_ref[...], in_weight(ins, 0)))
+        flush(0, 1)
+        query_ref[...] = low(dot(normed_ref[...], in_weight((fetch(1), fetch(2)), 0, width)))
         for slot in range(slots):
             here = slice(slot * part, (slot + 1) * part)
             good = valid_ref[slot] > 0.5
@@ -1361,11 +1862,14 @@
                     good,
                 )
                 cross_ref[here, at : at + HDIM] = low(cross)
-        three = two_ref[...] + swap(1, dot(cross_ref[...], out_weight(outs, 1)))
+        flush(2, 3)
+        three = two_ref[...] + swap(1, dot(cross_ref[...], out_weight(fetch(0), 1, 2)))
         three_ref[...] = three
         last_ref[...] = low(norm_forward(three, gain_ref[1:2, :]))
+        flush(4, 5)
         for j in range(3):
-            triple_ref[:, j * width : (j + 1) * width] = low(dot(last_ref[...], in_weight(ins, 1 + j)))
+            weight = in_weight((fetch(1), fetch(2)), 1 + j, width)
+            triple_ref[:, j * width : (j + 1) * width] = low(dot(last_ref[...], weight))
 
     wide = jax.ShapeDtypeStruct((rows, channels), jnp.float32)
     wide_low = jax.ShapeDtypeStruct((rows, channels), jnp.bfloat16)
@@ -1373,20 +1877,24 @@
     return chat(
         kernel,
         [wide, wide_low, thin, thin, wide, wide_low, jax.ShapeDtypeStruct((rows, 3 * width), jnp.bfloat16)],
-        [mix, stream, *out_halves, *in_halves, pairs, valid, gains],
+        [mix, stream, pairs, valid, gains],
         rows,
         channels,
         2,
         number,
-    )
-
-
-def late_forward(mix, stream, out_halves, gain, number):
+        far=[outs, *ins],
+        late=range(6),
+    )
+
+
+def late_forward(mix, stream, out, gain, number):
     rows, channels = stream.shape
 
-    def kernel(swap, mix_ref, x_ref, out_ref, out_rest, gain_ref, four_ref, normed_ref):
-        four = x_ref[...] + swap(0, dot(mix_ref[...], out_weight((out_ref, out_rest), 2)))
+    def kernel(swap, fetch, flush, mix_ref, gain_ref, four_ref, normed_ref):
+        part = swap(0, dot(mix_ref[...], out_weight(fetch(0), 0, 1)))
+        four = fetch(1)[...] + part
         four_ref[...] = four
+        flush(0)
         normed_ref[...] = low(norm_forward(four, gain_ref[...]))
 
     return chat(
@@ -1395,47 +1903,53 @@
             jax.ShapeDtypeStruct((rows, channels), jnp.float32),
             jax.ShapeDtypeStruct((rows, channels), jnp.bfloat16),
         ],
-        [mix, stream, *out_halves, gain],
+        [mix, gain],
         rows,
         channels,
         1,
         number,
-    )
-
-
-def late_backward(cot, normed_grad, stream, gain, mix, out_halves):
+        far=[out, stream],
+        late=[0],
+    )
+
+
+def late_backward(cot, normed_grad, stream, gain, mix, out):
     rows, channels = stream.shape
     width = mix.shape[1]
 
-    def kernel(
-        cot_ref, up_ref, x_ref, gain_ref, mix_ref, out_ref, out_rest, grad_ref, mix_grad_ref, dw_ref, dg_ref
-    ):
+    def kernel(swap, fetch, flush, up_ref, gain_ref, grad_ref, mix_grad_ref, dw_ref, dg_ref):
         step, gain_grad = norm_backward(
-            x_ref[...], gain_ref[...], up_ref[...].astype(jnp.float32)
+            fetch(0)[...], gain_ref[...], up_ref[...].astype(jnp.float32)
         )
-        grad = cot_ref[...].astype(jnp.float32) + step
+        grad = fetch(1)[...].astype(jnp.float32) + step
         grad_ref[...] = grad
+        flush(0)
         dg_ref[...] = gain_grad
         branch = low(grad)
-        mix_grad_ref[...] = low(dot_nt(branch, out_weight((out_ref, out_rest), 2)))
-        dw_ref[...] = low(dot_tn(branch, mix_ref[...]))
-
-    return pl.pallas_call(
+        dw_ref[...] = low(dot_tn(branch, fetch(3)[...]))
+        flush(2)
+        mix_grad_ref[...] = low(dot_nt(branch, out_weight(fetch(2), 0, 1)))
+
+    return chat(
         kernel,
-        out_shape=(
+        [
             jax.ShapeDtypeStruct((rows, channels), jnp.float32),
             jax.ShapeDtypeStruct((rows, width), jnp.bfloat16),
             jax.ShapeDtypeStruct((channels, width), jnp.bfloat16),
             jax.ShapeDtypeStruct((1, channels), jnp.float32),
-        ),
-        in_specs=[VMEM] * 7,
-        out_specs=tuple([VMEM] * 4),
-        compiler_params=pltpu.CompilerParams(vmem_limit_bytes=48 * 1024 * 1024),
-    )(cot, normed_grad, stream, gain, mix, *out_halves)
+        ],
+        [normed_grad, gain],
+        rows,
+        channels,
+        0,
+        0,
+        far=[stream, cot, out, mix],
+        late=[0, 2],
+    )
 
 
 def middle_backward(
-    triple, upstream, three, two, last, normed, query, cross, mix, out_halves, in_halves, pairs, valid, gains, number
+    triple, upstream, three, two, last, normed, query, cross, mix, outs, ins, pairs, valid, gains, number
 ):
     rows, channels = three.shape
     width = mix.shape[1]
@@ -1443,27 +1957,32 @@
     part = rows // slots
 
     def kernel(
-        swap, triple_ref, up_ref, three_ref, two_ref, last_ref, normed_ref, query_ref, cross_ref, mix_ref,
-        out_ref, out_rest, in_ref, in_rest, pairs_ref, valid_ref, gain_ref,
+        swap, fetch, flush, pairs_ref, valid_ref, gain_ref,
         grad_ref, mix_grad_ref, pair_grad_ref, query_dw_ref, pair_dw_ref, cross_dw_ref, outs_dw_ref, dg_ref,
         cross_up_ref, dq_ref,
     ):
-        outs, ins = (out_ref, out_rest), (in_ref, in_rest)
+        def weight_in(index):
+            return in_weight((fetch(1), fetch(2)), index, width)
 
         def temporal_weights():
+            last_ref = fetch(3)
             query_dw_ref[...] = low(dot_tn(last_ref[...], triple_ref[:, :width]))
             pair_dw_ref[...] = low(dot_tn(last_ref[...], triple_ref[:, width:]))
-
-        part_sum = dot_nt(triple_ref[:, :width], in_weight(ins, 1))
-        part_sum = part_sum + dot_nt(triple_ref[:, width : 2 * width], in_weight(ins, 2))
-        part_sum = part_sum + dot_nt(triple_ref[:, 2 * width :], in_weight(ins, 3))
+            flush(3, 4)
+
+        triple_ref = fetch(9)
+        part_sum = dot_nt(triple_ref[:, :width], weight_in(1))
+        part_sum = part_sum + dot_nt(triple_ref[:, width : 2 * width], weight_in(2))
+        part_sum = part_sum + dot_nt(triple_ref[:, 2 * width :], weight_in(3))
         normed_grad = swap(0, part_sum, temporal_weights)
-        step, gain_grad = norm_backward(three_ref[...], gain_ref[1:2, :], normed_grad)
+        step, gain_grad = norm_backward(fetch(10)[...], gain_ref[1:2, :], normed_grad)
         dg_ref[1:2, :] = gain_grad
-        grad = up_ref[...] + step
+        grad = fetch(11)[...] + step
         grad_ref[...] = grad
         branch = low(grad)
-        cross_up_ref[...] = low(dot_nt(branch, out_weight(outs, 1)))
+        cross_up_ref[...] = low(dot_nt(branch, out_weight(fetch(0), 1, 2)))
+        query_ref, cross_ref, two_ref = fetch(4), fetch(5), fetch(6)
+        normed_ref, mix_ref = fetch(7), fetch(8)
         for slot in range(slots):
             here = slice(slot * part, (slot + 1) * part)
             good = valid_ref[slot] > 0.5
@@ -1483,16 +2002,19 @@
 
         def cross_weights():
             cross_dw_ref[...] = low(dot_tn(normed_ref[...], dq_ref[...]))
+            flush(5)
             outs_dw_ref[:, :width] = low(dot_tn(low(grad_ref[...]), cross_ref[...]))
 
-        normed_grad = swap(1, dot_nt(dq_ref[...], in_weight(ins, 0)), cross_weights)
+        normed_grad = swap(1, dot_nt(dq_ref[...], weight_in(0)), cross_weights)
         step, gain_grad = norm_backward(two_ref[...], gain_ref[0:1, :], normed_grad)
         dg_ref[0:1, :] = gain_grad
         grad = grad_ref[...] + step
         grad_ref[...] = grad
+        flush(0)
         branch = low(grad)
-        mix_grad_ref[...] = low(dot_nt(branch, out_weight(outs, 0)))
         outs_dw_ref[:, width:] = low(dot_tn(branch, mix_ref[...]))
+        flush(6)
+        mix_grad_ref[...] = low(dot_nt(branch, out_weight(fetch(0), 0, 2)))
 
     return chat(
         kernel,
@@ -1506,12 +2028,14 @@
             jax.ShapeDtypeStruct((channels, 2 * width), jnp.bfloat16),
             jax.ShapeDtypeStruct((2, channels), jnp.float32),
         ],
-        [triple, upstream, three, two, last, normed, query, cross, mix, *out_halves, *in_halves, pairs, valid, gains],
+        [pairs, valid, gains],
         rows,
         channels,
         2,
         number,
         [pltpu.VMEM((rows, width), jnp.bfloat16), pltpu.VMEM((rows, width), jnp.bfloat16)],
+        [outs, *ins, last, query, cross, two, normed, mix, triple, three, upstream],
+        [0, 3, 4, 5, 6],
     )
 
 
@@ -1568,28 +2092,74 @@
     else:
         in_piece = jnp.concatenate([cross_query, temporal_qkv.reshape(-1, 3 * half_width)], axis=1)
         in_piece = part_of(in_piece, "tm", 1)
-    qkv_piece = part_of(spatial_qkv.transpose(1, 0, 2), "tm", 1)
-    qkv_piece = qkv_piece.reshape(3, -1, lines, half_width // lines).transpose(2, 0, 1, 3)
-    in_quarter = part_of(feed_in, "tm", 0)
-    in_quarter = in_quarter.reshape(-1, lines, feed_width).transpose(1, 0, 2)
-    out_quarter = part_of(feed_out.reshape(lines, feed_width, -1), "tm", 1)
+    picks = channels % (16 * owners) == 0 and (half_width // lines) % lane == 0
+    turned_qkv = spatial_qkv.transpose(1, 0, 2)
+
+    def cut_qkv(whole):
+        piece = part_of(whole, "tm", 1)
+        return piece.reshape(3, -1, lines, half_width // lines).transpose(2, 0, 1, 3)
+
+    def pick_qkv(ref, place):
+        rows = span(lax.axis_index("tm"), channels // owners)
+        return ref.at[:, rows, span(place, half_width // lines)]
+
+    def cut_in(whole):
+        return part_of(whole, "tm", 0).reshape(-1, lines, feed_width).transpose(1, 0, 2)
+
+    def pick_in(ref, place):
+        return ref.at[span(lax.axis_index("tm"), channels // owners), span(place, feed_width)]
+
+    def cut_out(whole):
+        return part_of(whole.reshape(lines, feed_width, -1), "tm", 1)
+
+    def pick_out(ref, place):
+        return ref.at[span(place * frames_axis + lax.axis_index("tm"), feed_width // frames_axis)]
+
+    def cut_text(whole):
+        return whole.reshape(text_rows, frames_axis, -1).transpose(1, 0, 2)
+
+    def pick_text(ref, place):
+        return ref.at[:, span(place, ref.shape[1] // frames_axis)]
+
+    def cut_cols(whole):
+        return whole.reshape(frames_axis, text_rows, lines, -1).transpose(2, 0, 1, 3)
+
+    def pick_cols(ref, place):
+        return ref.at[:, :, span(place, ref.shape[2] // lines)]
+
+    def cut_and_send(source, axes, pick, cut):
+        return Exchange(source, axes, pick, cut) if picks else Exchange(cut(source), axes)
+
     cot_rows = cotangent.reshape(token_rows, channels)
     text_flat = text.reshape(text_rows, -1)
     cross_kv = cross_kv.reshape(cross_kv.shape[0], -1)
 
+    folds = in_piece.shape[0] // out_piece.shape[0]
+    in_piece = jnp.concatenate(jnp.split(in_piece, folds, axis=0), axis=1)
+    out_cols = out_piece.shape[1]
+    pack = jnp.concatenate([out_piece, in_piece], axis=1)
+    in_cols = (out_cols, pack.shape[1])
+    embed = sinusoid(timesteps).astype(jnp.bfloat16)
+    film_part = jnp.einsum(
+        "bvc,cjk->bvjk", part_of(embed, "space", 2), film_weight, preferred_element_type=jnp.float32
+    )
+    film_part = film_part.reshape(slots * VIDS * 2, lines, -1).transpose(1, 0, 2)
+
     video_rows = video.reshape(token_rows, channels)
     in_groups = (channels // owners) % (D // G) == 0
     video_both = both_orders(video_rows, owners, lines) if in_groups else video_rows
-    video_lines, (text_line, qkv_piece, out_piece) = to_lines(
+    video_lines, (text_line, qkv_piece, film, pack) = to_lines(
         video_both.reshape(-1, pixels_dev, channels),
         True,
         1,
         [
             LineColumns(text_flat),
-            Exchange(qkv_piece, ("space",)),
-            Share(out_piece, ("space",)),
+            cut_and_send(turned_qkv, ("space",), pick_qkv, cut_qkv),
+            Exchange(film_part, ("space",)),
+            Keep(pack),
         ],
     )
+    pack = lax.all_gather(pack, "space", axis=0, tiled=False)
 
     def line_gains(whole):
         own = part_of(part_of(whole, "space", 0), "mp", 0)
@@ -1604,9 +2174,7 @@
         text_line.reshape(lines * text_rows, -1), cross_kv, preferred_element_type=jnp.float32
     )
     text_part = text_part.astype(jnp.bfloat16).reshape(lines, text_rows, -1)
-    first_in, (text_part, in_piece) = gather_cores(
-        first_in, 3, [Exchange(text_part, ("space",)), Share(in_piece, ("space",))]
-    )
+    first_in, (text_part,) = gather_cores(first_in, 3, [Exchange(text_part, ("space",))])
     if in_groups:
         first_in, first_owned = first_in[:images], first_in[images:]
     else:
@@ -1615,17 +2183,13 @@
         first_owned = lax.all_to_all(blocks, "space", split_axis=2, concat_axis=2, tiled=True)
     text_part = jnp.sum(text_part.astype(jnp.float32), axis=0).astype(jnp.bfloat16)
     hidden_part = conv_frames(wide(first_in), first_conv, "IHWO", False).astype(jnp.bfloat16)
-    hidden, (out_first, text_part) = sum_lines(
+    hidden, (text_part, qkv_piece) = sum_lines(
         hidden_part.reshape(images, H * W, half_width),
         4,
-        [Share(out_piece, ("tm",), 0, line_half), Share(text_part, ("space",))],
-    )
-
-    embed = sinusoid(timesteps).astype(jnp.bfloat16)
-    film_part = jnp.einsum(
-        "bvc,cjk->bvjk", part_of(embed, "space", 2), film_weight, preferred_element_type=jnp.float32
-    )
-    film = lax.psum_scatter(film_part, "space", scatter_dimension=3, tiled=True)
+        [Share(text_part, ("space",)), Share(qkv_piece, ("tm",))],
+    )
+
+    film = jnp.sum(film, axis=0).reshape(slots, VIDS, 2, -1)
     frame_ids = part_of(video_ids, "tm", 1)
     choose = (frame_ids[:, :, None] == jnp.arange(VIDS, dtype=jnp.int32)[None, None, :]).astype(
         jnp.float32
@@ -1635,7 +2199,9 @@
     film_scale, film_shift = 1.0 + frame_film[0], frame_film[1]
     second_in = group_forward(hidden, film_scale, film_shift)
     second_wide, (text_pairs, in_first) = gather_lines(
-        second_in, 5, [Share(text_part, ("tm",)), Share(in_piece, ("tm",), 0, line_half)]
+        second_in,
+        5,
+        [Share(text_part, ("tm",)), Share(pack, ("tm",), 0, line_half, in_cols)],
     )
     text_pairs = (
         text_pairs.reshape(owners, slots, text_local, 2 * half_width)
@@ -1644,12 +2210,11 @@
     )
     conv_part = conv_frames(wide(second_wide), second_conv, "IHWO", False).astype(jnp.bfloat16)
     conv_half, _ = sum_cores(conv_part.reshape(images, H * W, -1), 6)
-    text_cols = text_flat.reshape(text_rows, owners, -1).transpose(1, 0, 2)
-    conv_rows, (text_cols, qkv_piece) = from_lines(
+    conv_rows, (outs_all,) = from_lines(
         conv_half.astype(jnp.bfloat16),
         True,
         7,
-        [Exchange(text_cols, everyone), Share(qkv_piece, ("tm",))],
+        [Share(pack, ("tm",), cols=(0, out_cols // 3 * 2))],
     )
     spatial_qkv = qkv_piece.transpose(2, 1, 0, 3, 4).reshape(3, channels, -1)
 
@@ -1658,33 +2223,40 @@
         video_rows, conv_rows.reshape(token_rows, channels), spatial_gain
     )
     spatial_line, (in_rest,) = gather_tokens(
-        spatial_in, 8, [Share(in_piece, ("tm",), line_half, lines - line_half)]
+        spatial_in, 8, [Share(pack, ("tm",), line_half, lines - line_half, in_cols)]
     )
     spatial_line = spatial_line.reshape(lines, images, pixels_dev, channels)
     spatial_triple, spatial_mix = spatial_forward(spatial_line, spatial_qkv)
-    spatial_mix, (out_rest, cot_late) = from_lines(
+    spatial_mix, (out_last, cot_late, text_cols) = from_lines(
         spatial_mix,
         False,
         9,
-        [Share(out_piece, ("tm",), line_half, lines - line_half), Keep(cot_rows)],
+        [
+            Share(pack, ("tm",), cols=(out_cols // 3 * 2, out_cols)),
+            Keep(cot_rows),
+            cut_and_send(text_flat, ("tm",), pick_text, cut_text),
+        ],
     )
     cot_half = lax.all_gather(part_of(cot_late, "mp", 1), "space", axis=0, tiled=True)
 
     spatial_mix = spatial_mix.reshape(token_rows, half_width)
-    out_all, in_all = (out_first, out_rest), (in_first, in_rest)
+    in_all = (in_first, in_rest)
     text_valid = (jnp.arange(TXT, dtype=jnp.int32)[None, :] < text_lengths[:, None])[:, None, :]
     text_valid = text_valid.astype(jnp.float32)
     two_gains = jnp.stack([cross_norm, temporal_norm])
     stream_two, cross_in, cross_queries, cross_mix, stream_three, temporal_in, temporal_triple = (
         middle_forward(
-            spatial_mix, stream_one, out_all, in_all, text_pairs, text_valid, two_gains, 34
+            spatial_mix, stream_one, outs_all, in_all, text_pairs, text_valid, two_gains, 34
         )
     )
 
     clip_triple, (in_quarter, out_quarter) = to_clips(
         temporal_triple.reshape(slots, frame_dev, pixels_dev, 3 * half_width),
         10,
-        [Exchange(in_quarter, ("space",)), Exchange(out_quarter, ("space",))],
+        [
+            cut_and_send(feed_in, ("space",), pick_in, cut_in),
+            cut_and_send(feed_out, ("space",), pick_out, cut_out),
+        ],
     )
     clip_pixels = clip_triple.shape[2]
     clip_rows = frames_all * clip_pixels
@@ -1699,13 +2271,15 @@
     clip_bias = jnp.einsum("rq,hqc->hrc", clip_frames, clip_bias, precision=highest)
     clip_ids = jnp.repeat(video_ids, clip_pixels, axis=1)
     clip_mix = temporal_forward(clip_triple, clip_bias, clip_ids, clip_pixels)
-    temporal_mix, (cot_line,) = from_clips(
-        clip_mix.reshape(slots, frames_all, clip_pixels, half_width), 11, [JoinCores(cot_half)]
+    temporal_mix, (cot_line, text_cols) = from_clips(
+        clip_mix.reshape(slots, frames_all, clip_pixels, half_width),
+        11,
+        [JoinCores(cot_half), cut_and_send(text_cols, ("space",), pick_cols, cut_cols)],
     )
     temporal_mix = temporal_mix.reshape(token_rows, half_width)
 
     feed_gain = feed_norm[None]
-    stream_four, feed_rows = late_forward(temporal_mix, stream_three, out_all, feed_gain, 35)
+    stream_four, feed_rows = late_forward(temporal_mix, stream_three, out_last, feed_gain, 35)
     feed_line, (feed_in, feed_out) = gather_tokens(
         feed_rows, 12, [Share(in_quarter, ("tm",)), Share(out_quarter, ("tm",))]
     )
@@ -1715,12 +2289,14 @@
     final_part, feed_part, feed_grads = feed_both(
         feed_line.reshape(line_shape), cot_line.reshape(line_shape), feed_in, feed_out
     )
-    normed_grad, (feed_grads,) = scatter_tokens(
-        feed_part.reshape(lines * token_rows, channels), 14, [by_frames(feed_grads)]
+    normed_grad, (feed_grads, final_half) = scatter_tokens(
+        feed_part.reshape(lines * token_rows, channels),
+        14,
+        [by_frames(feed_grads), CoreSum(final_part.reshape(lines * token_rows, channels))],
     )
 
     upstream, mix_grad, temporal_out_grad, feed_norm_grad = late_backward(
-        cot_rows, normed_grad, stream_four, feed_gain, temporal_mix, out_all
+        cot_rows, normed_grad, stream_four, feed_gain, temporal_mix, out_last
     )
     clip_up, (feed_grads,) = to_clips(
         mix_grad.reshape(slots, frame_dev, pixels_dev, half_width),
@@ -1736,8 +2312,10 @@
     )
     score_total = jnp.einsum("hqc,ck->hqk", score_total, clip_frames, precision=highest)
     offset_bias_grad = jnp.einsum("hqk,qkr->rh", score_total, offset_table, precision=highest)
-    triple_grad, _ = from_clips(
-        clip_grads.reshape(slots, frames_all, clip_pixels, 3 * half_width), 16
+    triple_grad, (first_grads, final_half) = from_clips(
+        clip_grads.reshape(slots, frames_all, clip_pixels, 3 * half_width),
+        16,
+        [by_frames(temporal_out_grad), LineSum(final_half)],
     )
 
     (
@@ -1759,28 +2337,26 @@
         cross_queries,
         cross_mix,
         spatial_mix,
-        out_all,
+        outs_all,
         in_all,
         text_pairs,
         text_valid,
         two_gains,
         36,
     )
-    final_rows, (first_grads, second_grads) = scatter_tokens(
-        final_part.reshape(lines * token_rows, channels),
-        13,
-        [by_frames(temporal_out_grad), by_frames(temporal_query_grad)],
-    )
-    mixed = (stream_four + final_rows.astype(jnp.float32)).astype(jnp.bfloat16)
     pair_grad = (
         pair_grad.reshape(slots, frames_axis, lines, text_local, 2 * half_width)
         .transpose(1, 2, 0, 3, 4)
         .reshape(frames_axis, lines * text_rows, 2 * half_width)
     )
 
-    mix_line, (pair_grad,) = to_lines(
-        mix_grad.reshape(images, pixels_dev, half_width), False, 17, [FrameSum(pair_grad)]
-    )
+    mix_line, (pair_grad, second_grads, final_rows) = to_lines(
+        mix_grad.reshape(images, pixels_dev, half_width),
+        False,
+        17,
+        [FrameSum(pair_grad), by_frames(temporal_query_grad), JoinCores(final_half)],
+    )
+    mixed = (stream_four + final_rows.astype(jnp.float32)).astype(jnp.bfloat16)
     spatial_part, spatial_qkv_grad = spatial_backward(
         spatial_line, spatial_qkv, spatial_triple, mix_line
     )
@@ -1792,6 +2368,12 @@
             by_frames(temporal_pair_grad),
         ],
     )
+    temporal_grads = lax.psum_scatter(
+        jnp.concatenate([first_grads, second_grads, third_grads], axis=1),
+        "space",
+        scatter_dimension=0,
+        tiled=True,
+    )
     pair_grad = jnp.sum(pair_grad.astype(jnp.float32), axis=0).astype(jnp.bfloat16)
     upstream, branch_both, spatial_norm_grad = first_norm_backward(
         stream_one, spatial_gain, normed_grad, upstream, owners, lines
@@ -1826,20 +2408,23 @@
     hidden_wide, (second_conv_grad, film_shares, text_part) = gather_lines(
         hidden_grad,
         21,
-        [TapSum(second_conv_grad), Share(film_rows, everyone), Exchange(text_part, ("space",))],
-    )
-    first_conv_grad = conv_weight_grad(wide(first_owned), wide(hidden_wide), "ck")
+        [FrameSum(second_conv_grad, True), Share(film_rows, ("tm",)), Exchange(text_part, ("space",))],
+    )
+    film_rows = jnp.sum(film_shares, axis=0)
+    first_conv_some, first_conv_rest = (
+        conv_weight_grad(wide(first_owned), wide(hidden_wide), "ck", taps)
+        for taps in (range(5), range(5, 9))
+    )
     first_part = conv_frames(wide(hidden_wide), first_conv, "OHWI", True).astype(jnp.bfloat16)
-    gathered_grads = jnp.concatenate(
-        [first_grads, second_grads, third_grads, fourth_grads, fifth_grads], axis=1
-    )
-    first_in_grad, (first_conv_grad, spatial_qkv_grad, gathered_grads) = sum_cores(
+    cross_grads = jnp.concatenate([fourth_grads, fifth_grads], axis=1)
+    first_in_grad, (first_conv_some, spatial_qkv_grad, cross_grads, film_shares) = sum_cores(
         first_part.reshape(images, H * W, -1),
         22,
         [
-            TapSum(first_conv_grad),
+            FrameSum(first_conv_some, True),
             by_frames(spatial_qkv_grad),
-            Exchange(gathered_grads.reshape(lines, -1, gathered_grads.shape[1]), ("space",)),
+            Exchange(cross_grads.reshape(lines, -1, cross_grads.shape[1]), ("space",)),
+            Share(film_rows, ("space",)),
         ],
     )
     video_line_grad, gain_grad, bias_grad = group_backward(
@@ -1867,20 +2452,20 @@
         ],
         axis=1,
     )
-    video_rows_grad, (small, qkv_part) = from_lines(
+    video_rows_grad, (small, qkv_part, first_conv_rest) = from_lines(
         video_line_grad,
         True,
         23,
         [
-            Exchange(small[:, None], everyone),
+            SmallSum(small.reshape(frames_axis, lines, 1, -1)),
             Exchange(spatial_qkv_grad.reshape(lines, -1, spatial_qkv_grad.shape[1]), ("space",)),
+            FrameSum(first_conv_rest, True),
         ],
     )
     video_grad = upstream + video_rows_grad.reshape(token_rows, channels).astype(jnp.float32)
 
-    film_shares = film_shares.reshape(frames_axis, lines, slots, VIDS, 2, -1)
     video_film_grad = (
-        jnp.sum(film_shares, axis=0)
+        film_shares.reshape(lines, slots, VIDS, 2, -1)
         .transpose(1, 2, 3, 0, 4)
         .reshape(slots, VIDS, 2, half_width)
     )
@@ -1892,14 +2477,14 @@
     )
     cross_kv_grad = jnp.einsum(
         "prc,prk->ck",
-        text_cols,
+        text_cols.transpose(1, 0, 2, 3).reshape(owners, text_rows, -1),
         pair_all.reshape(owners, text_rows, 2 * half_width),
         preferred_element_type=jnp.float32,
     )
     text_half = part_of(
         twin_add(text_part.transpose(1, 0, 2).reshape(text_rows, -1)), "mp", 1
     )
-    small = jnp.sum(small, axis=(0, 1))
+    small = small[0]
     small_twin = lax.ppermute(small, "mp", [(0, 1), (1, 0)])
     gain_size = channels // owners
     gains = [small[i * gain_size : (i + 1) * gain_size] for i in range(6)]
@@ -1907,10 +2492,9 @@
         gains[i] = gains[i] + small_twin[i * gain_size : (i + 1) * gain_size]
     feed_grads, qkv_part = feed_grads.astype(jnp.float32), qkv_part.astype(jnp.float32)
     owner_rows = feed_grads.shape[1]
-    gathered_grads = jnp.sum(gathered_grads.astype(jnp.float32), axis=0)
-    owner_parts = [
-        gathered_grads[:, i * half_width : (i + 1) * half_width] for i in range(7)
-    ]
+    temporal_grads = temporal_grads.astype(jnp.float32)
+    cross_grads = jnp.sum(cross_grads.astype(jnp.float32), axis=0)
+    first_conv_grad = jnp.concatenate([first_conv_some, first_conv_rest])
     return (
         mixed.reshape(video.shape),
         video_grad.reshape(video.shape),
@@ -1924,14 +2508,14 @@
         qkv_part.reshape(lines, owner_rows, 3, -1)
         .transpose(1, 2, 0, 3)
         .reshape(owner_rows, 3, half_width),
-        owner_parts[6].T,
+        cross_grads[:, 2 * half_width :].T,
         gains[3],
-        owner_parts[4],
+        cross_grads[:, :half_width],
         cross_kv_grad.reshape(-1, 2, half_width),
-        owner_parts[5].T,
+        cross_grads[:, half_width : 2 * half_width].T,
         gains[4],
-        gathered_grads[:, half_width : 4 * half_width].reshape(-1, 3, half_width),
-        owner_parts[0].T,
+        temporal_grads[:, half_width:].reshape(-1, 3, half_width),
+        temporal_grads[:, :half_width].T,
         small[6 * gain_size :].reshape(R // owners, head_local),
         gains[5],
         feed_grads[:, :, :feed_width].transpose(1, 0, 2).reshape(owner_rows, -1),

time: 783 us -> 699 us (0.89)
  Pallas kernels: 613 us -> 538 us
  local copies, waits for them, and re-layouts: 97 us -> 77.7 us
    pallas_call x25 -> x24, Pallas kernels: 554 us -> 472 us  [talk(): pl.pallas_call(kernel, out_shape=result, in_specs=[ANY] * len(operands) i...]
    unnamed x318 -> x267, local copies, waits for them, and re-layouts: 69.7 us -> 53.8 us
    pallas_call x1 -> x3, Pallas kernels: 3.32 us -> 14.7 us  [chat(): pl.pallas_call(whole, out_shape=tuple(results), in_specs=specs, out_specs...]
  transfers between devices with their start and end apart: 4 -> 5, of which waited for: 0 -> 0; matrix products, arithmetic and copies ran while one was open for 6% -> 8% of each run, Pallas kernels for 20% -> 20%
where the time goes in v4:
time: 699 us; the launch traced here: 691 us
  Pallas kernels  538 us (77%)
  local copies, waits for them, and re-layouts  77.7 us (11%)
  matrix products  37.6 us (5%)
  other arithmetic  21.8 us (3%)
  between operations  15.8 us (2%)
    pallas_call x24, Pallas kernels, talk(): pl.pallas_call(kernel, out_shape=result, in_specs=[ANY] * len(operands) i...  472 us
    unnamed x267, local copies, waits for them, and re-layouts  53.8 us
    pallas_call x9, Pallas kernels, local(): pl.pallas_call(kernel, out_shape=results, grid=grid, in_specs=in_specs, o...  50.4 us
    conv_general_dilated x4, matrix products, conv_frames(): lax.conv_general_dilated(images, kernel, (1, 1), 'SAME', dimension_number...  15.8 us
    pallas_call x3, Pallas kernels, chat(): pl.pallas_call(whole, out_shape=tuple(results), in_specs=specs, out_specs...  14.7 us
  transfers between devices with their start and end apart: 5, of which 0 were waited for; matrix products, arithmetic and copies ran while one was open for 8% of the time, Pallas kernels for 20%

profile of v4, /device:TPU:2, one launch (start us, length us, event | category | flops | bytes accessed | tf_op | source)
XLA Modules:
  0.0 691.1 jit_solution(2402241667314621137)
XLA Ops:
  15.2 21.2 %shard_map.409 = (bf16[8,256,128]{2,1,0:T(8,128)(2,1)S(1)}, bf16[4,16,1024]{2,1,0:T(8,128)(2,1)S(1)}, bf16[4,3,64,128]{3,2,1,0:T(8,128)(2,1)S(1)}, f32[4,12,128]{2,1,0:T(8,128)S(1)}, bf16[128,1792]{1,0:T(8,128)(2,1)S(1)}) custom-call(bf16[8,64,1024]{2,1,0:T(8,128)(2,1)S(1)} %bitcast.485, bf16[16,4096]{1,0:T(8,128)(2,1)S(1)} %bitcast.531, ...), custom_call_target="tpu_custom_call" | custom-call | tf_op jit(solution)/shard_map/pallas_call | solution.py:83
  41.2 3.5 copy.183
  45.0 4.4 shard_map.410.refs_0_
  49.5 2.4 convolution_convert_fusion.5
  51.8 10.0 %shard_map.411 = (bf16[8,256,256]{2,1,0:T(8,128)(2,1)S(1)}, bf16[4,16,1024]{2,1,0:T(8,128)(2,1)S(1)}) custom-call(bf16[8,256,128]{2,1,0:T(8,128)(2,1)S(1)} %shard_map.410.refs_0_, bf16[4,16,1024]{2,1,0:T(8,128)(2,1)S(1)} %bitcast.525), custom_call_target="tpu_custom_call" | custom-call | tf_op jit(solution)/shard_map/pallas_call | solution.py:83
  62.8 4.2 convolution_convert_fusion.1
  67.3 1.6 reduce_sum.69.refs_1_
  70.5 33.3 %shard_map.412 = (f32[4,256,128]{2,1,0:T(8,128)S(1)}, bf16[4,16,1024]{2,1,0:T(8,128)(2,1)S(1)}, bf16[4,4,3,64,128]{4,3,2,1,0:T(8,128)(2,1)S(1)}) custom-call(bf16[4,256,512]{2,1,0:T(8,128)(2,1)S(1)} %bitcast.487, bf16[16,1024]{1,0:T(8,128)(2,1)S(1)} %copy-done.88, bf16[4,3,64,128]{3,2,1,0:T(8,128)(2,1)S(1)} %copy-done.78), custom_call_target="tpu_custom_call" | custom-call | tf_op jit(solution)/shard_map/pallas_call | solution.py:83
  107.8 2.2 shard_map.413.refs_0_
  110.0 1.5 copy-done.2
  112.4 25.8 %shard_map.414 = (bf16[4,256,512]{2,1,0:T(8,128)(2,1)S(1)}, bf16[4,4,16,1024]{3,2,1,0:T(8,128)(2,1)S(1)}, bf16[4,2,128,1024]{3,2,1,0:T(8,128)(2,1)S(1)}) custom-call(bf16[4,256,128]{2,1,0:T(8,128)(2,1)S(1)} %shard_map.413.refs_0_, bf16[4,16,1024]{2,1,0:T(8,128)(2,1)S(1)} %copy-done.87, bf16[4,128,1792]{2,1,0:T(8,128)(2,1)S(1)} %bitcast.477), custom_call_target="tpu_custom_call" | custom-call | tf_op jit(solution)/shard_map/pallas_call | solution.py:83
  139.1 3.9 convolution_convert_fusion.3
  143.1 1.6 shard_map.415
  144.8 22.0 %shard_map.416 = (bf16[4,64,1024]{2,1,0:T(8,128)(2,1)S(1)}, bf16[4,4,128,512]{3,2,1,0:T(8,128)(2,1)S(1)}) custom-call(bf16[4,256,128]{2,1,0:T(8,128)(2,1)S(1)} %convert_element_type.147.refs_0_, bf16[4,128,1792]{2,1,0:T(8,128)(2,1)S(1)} %bitcast.478), custom_call_target="tpu_custom_call" | custom-call | tf_op jit(solution)/shard_map/pallas_call | solution.py:83
  169.0 4.0 shard_map.417
  174.0 20.8 %shard_map.418 = (bf16[1,1024,1024]{2,1,0:T(8,128)(2,1)S(1)}, bf16[4,2,128,1024]{3,2,1,0:T(8,128)(2,1)S(1)}) custom-call(bf16[1,256,1024]{2,1,0:T(8,128)(2,1)S(1)} %bitcast.530, bf16[4,128,1792]{2,1,0:T(8,128)(2,1)S(1)} %bitcast.479), custom_call_target="tpu_custom_call" | custom-call | tf_op jit(solution)/shard_map/pallas_call | solution.py:83
  196.2 4.8 shard_map.419
  202.0 14.4 %shard_map.420 = (bf16[4,64,512]{2,1,0:T(8,128)(2,1)S(1)}, bf16[4,4,128,256]{3,2,1,0:T(8,128)(2,1)S(1)}, bf16[256,1024]{1,0:T(8,128)(2,1)S(1)}, bf16[4,16,1024]{2,1,0:T(8,128)(2,1)S(1)}) custom-call(bf16[4,256,128]{2,1,0:T(8,128)(2,1)S(1)} %get-tuple-element.141.refs_0_, bf16[4,128,1792]{2,1,0:T(8,128)(2,1)S(1)} %bitcast.480, ...), custom_call_target="tpu_custom_call" | custom-call | tf_op jit(solution)/shard_map/pallas_call | solution.py:83
  229.2 2.1 copy.210
  231.3 15.9 %shard_map.421 = (f32[256,1024]{1,0:T(8,128)}, bf16[256,1024]{1,0:T(8,128)(2,1)}, bf16[256,512]{1,0:T(8,128)(2,1)}, bf16[256,512]{1,0:T(8,128)(2,1)}, f32[256,10...) custom-call(bf16[256,512]{1,0:T(8,128)(2,1)} %bitcast.507, ...), custom_call_target="tpu_custom_call" | custom-call | tf_op jit(solution)/shard_map/pallas_call | solution.py:83
  248.4 14.4 %shard_map.422 = (bf16[2,8,16,1536]{3,2,1,0:T(8,128)(2,1)S(1)}, bf16[4,64,512]{2,1,0:T(8,128)(2,1)S(1)}, bf16[4,128,256]{2,1,0:T(8,128)(2,1)S(1)}) custom-call(bf16[2,2,64,1536]{3,2,1,0:T(8,128)(2,1)S(1)} %bitcast.522, bf16[256,2048]{1,0:T(8,128)(2,1)S(1)} %copy-done.32, bf16[2048,256]{1,0:T(8,128)(2,1)S(1)} %copy-done.33), custom_call_target="tpu_custom_call" | custom-call | tf_op jit(solution)/shard_map/pallas_call | solution.py:83
  264.2 5.9 shard_map.423
  274.8 7.3 %shard_map.424 = (bf16[2,2,64,512]{3,2,1,0:T(8,128)(2,1)S(1)}, bf16[1024,1024]{1,0:T(8,128)(2,1)S(1)}, bf16[4,4,16,256]{3,2,1,0:T(8,128)(2,1)S(1)}) custom-call(bf16[2,8,16,512]{3,2,1,0:T(8,128)(2,1)S(1)} %bitcast.517, bf16[1024,512]{1,0:T(8,128)(2,1)S(1)} %copy-done.26, bf16[4,16,1024]{2,1,0:T(8,128)(2,1)S(1)} %copy-done.95), custom_call_target="tpu_custom_call" | custom-call | tf_op jit(solution)/shard_map/pallas_call | solution.py:83
  282.8 6.3 shard_map.425
  290.2 23.1 %shard_map.426 = (bf16[1,1024,1024]{2,1,0:T(8,128)(2,1)S(1)}, bf16[4,4,64,512]{3,2,1,0:T(8,128)(2,1)S(1)}, bf16[4,4,128,256]{3,2,1,0:T(8,128)(2,1)S(1)}) custom-call(bf16[1,256,1024]{2,1,0:T(8,128)(2,1)S(1)} %bitcast.528, bf16[4,64,512]{2,1,0:T(8,128)(2,1)S(1)} %copy-done.69, bf16[4,128,256]{2,1,0:T(8,128)(2,1)S(1)} %copy-done.71), custom_call_target="tpu_custom_call" | custom-call | tf_op jit(solution)/shard_map/pallas_call | solution.py:83
  314.5 8.5 %shard_map.427 = (bf16[4,256,1024]{2,1,0:T(8,128)(2,1)S(1)}, bf16[4,256,1024]{2,1,0:T(8,128)(2,1)S(1)}, bf16[1024,1024]{1,0:T(8,128)(2,1)S(1)}) custom-call(bf16[4,256,1024]{2,1,0:T(8,128)(2,1)S(1)} %bitcast.494, bf16[4,256,1024]{2,1,0:T(8,128)(2,1)S(1)} %bitcast.493, bf16[1024,512]{1,0:T(8,128)(2,1)S(1)} %bitcast.488, bf16[512,1024]{1,0:T(8,128)(2,1)S(1)} %bitcast.489), custom_call_target="tpu_custom_call" | custom-call | tf_op jit(solution)/shard_map/pallas_call | solution.py:1233
  323.1 25.5 %shard_map.428 = (bf16[256,1024]{1,0:T(8,128)(2,1)S(1)}, bf16[256,1024]{1,0:T(8,128)(2,1)S(1)}, bf16[1024,512]{1,0:T(8,128)(2,1)S(1)}) custom-call(bf16[4,256,1024]{2,1,0:T(8,128)(2,1)S(1)} %get-tuple-element.168.refs_0_, bf16[4,256,1024]{2,1,0:T(8,128)(2,1)S(1)} %bitcast.496, bf16[1024,1024]{1,0:T(8,128)(2,1)S(1)} %bitcast.495), custom_call_target="tpu_custom_call" | custom-call | tf_op jit(solution)/shard_map/pallas_call | solution.py:83
  349.4 5.4 shard_map.429
  355.8 14.0 %shard_map.430 = (bf16[2,8,16,512]{3,2,1,0:T(8,128)(2,1)S(1)}, bf16[4,64,1024]{2,1,0:T(8,128)(2,1)S(1)}) custom-call(bf16[2,2,64,512]{3,2,1,0:T(8,128)(2,1)S(1)} %bitcast.534, bf16[4,64,1024]{2,1,0:T(8,128)(2,1)S(1)} %bitcast.526), custom_call_target="tpu_custom_call" | custom-call | tf_op jit(solution)/shard_map/pallas_call | solution.py:83
  370.7 7.5 %shard_map.431 = (bf16[2,128,1536]{2,1,0:T(8,128)(2,1)S(1)}, f32[8,8,128]{2,1,0:T(8,128)S(1)}) custom-call(bf16[2,128,1536]{2,1,0:T(8,128)(2,1)S(1)} %bitcast.491, f32[8,128,128]{2,1,0:T(8,128)S(1)} %copy-done.10, s32[2,128,1]{2,1,0:T(8,128)S(1)} %broadcast_in_dim_reshape.18.ids_ref, s32[2,1,128]{2,1,0:T(1,128)S(1)} %broadcast_in_dim_reshape.17.turned_ref, ...), custom_call_target="tpu_custom_call" | custom-call | tf_op jit(solution)/shard_map/pallas_call | solution.py:1233
  378.8 25.0 %shard_map.432 = (bf16[2,2,64,1536]{3,2,1,0:T(8,128)(2,1)S(1)}, bf16[256,512]{1,0:T(8,128)(2,1)S(1)}, bf16[256,512]{1,0:T(8,128)(2,1)S(1)}) custom-call(bf16[2,8,16,1536]{3,2,1,0:T(8,128)(2,1)S(1)} %bitcast.521, bf16[4,256,512]{2,1,0:T(8,128)(2,1)S(1)} %bitcast.514, bf16[1024,512]{1,0:T(8,128)(2,1)S(1)} %get-tuple-element.177.refs_2_), custom_call_target="tpu_custom_call" | custom-call | tf_op jit(solution)/shard_map/pallas_call | solution.py:83
  404.7 22.4 %shard_map.433 = (f32[256,1024]{1,0:T(8,128)}, bf16[256,512]{1,0:T(8,128)(2,1)}, bf16[2,128,1024]{2,1,0:T(8,128)(2,1)}, bf16[1024,512]{1,0:T(8,128)(2,1)}, bf16[...) custom-call(bf16[2,128,1024]{2,1,0:T(8,128)(2,1)} %bitcast.574, ...), custom_call_target="tpu_custom_call" | custom-call | tf_op jit(solution)/shard_map/pallas_call | solution.py:83
  430.5 21.1 %shard_map.434 = (bf16[4,256,128]{2,1,0:T(8,128)(2,1)S(1)}, bf16[64,1024]{1,0:T(8,128)(2,1)S(1)}, bf16[256,512]{1,0:T(8,128)(2,1)S(1)}, bf16[256,1024]{1,0:T(8,128)(2,1)S(1)}) custom-call(bf16[4,64,512]{2,1,0:T(8,128)(2,1)S(1)} %bitcast.536, bf16[4,64,1024]{2,1,0:T(8,128)(2,1)S(1)} %bitcast.504, bf16[4,256,512]{2,1,0:T(8,128)(2,1)S(1)} %bitcast.510, ...), custom_call_target="tpu_custom_call" | custom-call | tf_op jit(solution)/shard_map/pallas_call | solution.py:83
  453.1 10.4 %shard_map.435 = (bf16[4,4,64,1024]{3,2,1,0:T(8,128)(2,1)S(1)}, bf16[1024,384]{1,0:T(8,128)(2,1)S(1)}) custom-call(bf16[4,4,64,1024]{3,2,1,0:T(8,128)(2,1)S(1)} %bitcast.482, bf16[3,1024,128]{2,1,0:T(8,128)(2,1)S(1)} %bitcast.484, bf16[4,3,256,128]{3,2,1,0:T(8,128)(2,1)S(1)} %copy-done.44, bf16[4,256,128]{2,1,0:T(8,128)(2,1)S(1)} %get-tuple-element.186.up_ref), custom_call_target="tpu_custom_call" | custom-call | tf_op jit(solution)/shard_map/pallas_call | solution.py:1233
  463.5 23.1 %shard_map.436 = (bf16[256,1024]{1,0:T(8,128)(2,1)S(1)}, bf16[4,16,1024]{2,1,0:T(8,128)(2,1)S(1)}, bf16[256,1024]{1,0:T(8,128)(2,1)S(1)}) custom-call(bf16[4,256,1024]{2,1,0:T(8,128)(2,1)S(1)} %bitcast.501, bf16[4,16,1024]{2,1,0:T(8,128)(2,1)S(1)} %bitcast.540, bf16[4,256,1024]{2,1,0:T(8,128)(2,1)S(1)} %bitcast.500), custom_call_target="tpu_custom_call" | custom-call | tf_op jit(solution)/shard_map/pallas_call | solution.py:83
  487.5 5.3 shard_map.437
  494.1 23.6 %shard_map.438 = (bf16[8,256,256]{2,1,0:T(8,128)(2,1)S(1)}, bf16[256,512]{1,0:T(8,128)(2,1)S(1)}, bf16[4,16,1024]{2,1,0:T(8,128)(2,1)S(1)}) custom-call(bf16[8,64,1024]{2,1,0:T(8,128)(2,1)S(1)} %bitcast.511, bf16[4,256,512]{2,1,0:T(8,128)(2,1)S(1)} %bitcast.509, bf16[16,1024]{1,0:T(8,128)(2,1)S(1)} %reduce_sum.71.refs_2_), custom_call_target="tpu_custom_call" | custom-call | tf_op jit(solution)/shard_map/pallas_call | solution.py:83
  519.3 3.6 convolution_convert_fusion
  524.5 27.3 %shard_map.439 = (f32[4,256,128]{2,1,0:T(8,128)S(1)}, bf16[256,1024]{1,0:T(8,128)(2,1)S(1)}, bf16[4,4,16,1024]{3,2,1,0:T(8,128)(2,1)S(1)}) custom-call(bf16[4,256,512]{2,1,0:T(8,128)(2,1)S(1)} %bitcast.486, bf16[4,256,1024]{2,1,0:T(8,128)(2,1)S(1)} %bitcast.499, bf16[4,16,1024]{2,1,0:T(8,128)(2,1)S(1)} %get-tuple-element.198.refs_2_), custom_call_target="tpu_custom_call" | custom-call | tf_op jit(solution)/shard_map/pallas_call | solution.py:83
  551.9 3.4 shard_map.440
  555.6 1.9 fusion.49
  562.1 22.8 %shard_map.441 = (bf16[4,256,512]{2,1,0:T(8,128)(2,1)S(1)}, bf16[9,64,512]{2,1,0:T(8,128)(2,1)S(1)}, f32[4,12,128]{2,1,0:T(8,128)S(1)}, bf16[4,16,1024]{2,1,0:T(8,128)(2,1)S(1)}) custom-call(bf16[4,256,128]{2,1,0:T(8,128)(2,1)S(1)} %get-tuple-element.200.refs_0_, bf16[9,256,512]{2,1,0:T(8,128)(2,1)S(1)} %fusion.35.refs_1_, f32[12,128]{1,0:T(8,128)S(1)} %reshape.477.refs_2_, ...), custom_call_target="tpu_custom_call" | custom-call | tf_op jit(solution)/shard_map/pallas_call | solution.py:83
  596.4 1.8 copy.151
  598.9 4.1 convolution_convert_fusion.2
  607.6 30.6 %shard_map.442 = (f32[4,256,128]{2,1,0:T(8,128)S(1)}, bf16[5,64,512]{2,1,0:T(8,128)(2,1)S(1)}, bf16[256,384]{1,0:T(8,128)(2,1)S(1)}, bf16[4,64,1536]{2,1,0:T(8,128)(2,1)S(1)}, f32[4,12,128]{2,1,0:T(8,128)S(1)}) custom-call(bf16[4,256,256]{2,1,0:T(8,128)(2,1)S(1)} %bitcast.503, bf16[5,256,512]{2,1,0:T(8,128)(2,1)S(1)} %fusion.19.refs_1_, ...), custom_call_target="tpu_custom_call" | custom-call | tf_op jit(solution)/shard_map/pallas_call | solution.py:83
  639.6 3.3 shard_map.443
  645.3 20.5 %shard_map.444 = (bf16[4,64,1024]{2,1,0:T(8,128)(2,1)S(1)}, f32[1,448]{1,0:T(1,128)S(1)}, bf16[4,64,384]{2,1,0:T(8,128)(2,1)S(1)}, bf16[4,64,512]{2,1,0:T(8,128)(2,1)S(1)}) custom-call(bf16[4,256,128]{2,1,0:T(8,128)(2,1)S(1)} %get-tuple-element.209.refs_0_, f32[4,4,1,448]{3,2,1,0:T(1,128)S(1)} %concatenate.53.refs_1_, bf16[4,64,384]{2,1,0:T(8,128)(2,1)S(1)} %bitcast.537, ...), custom_call_target="tpu_custom_call" | custom-call | tf_op jit(solution)/shard_map/pallas_call | solution.py:83
  679.4 1.5 add_bitcast_fusion
  (408 shorter events, 105.9 us)
Async XLA Ops:
  7.2 131.9 %copy-start = (bf16[512,9,256]{2,0,1:T(8,128)(2,1)S(1)}, bf16[512,9,256]{2,0,1:T(8,128)(2,1)}, u32[]{:S(2)}) copy-start(bf16[512,9,256]{2,0,1:T(8,128)(2,1)} %param.35) | copy-start | bytes 7077892
  7.2 102.8 %all-gather.6.cloned.1.call-start = ((), (), s32[]{:S(2)}) async-start(), calls=%async_computation.3 | async-start | bytes 2293760 | tf_op jit(solution)/shard_map/all_gather | solution.py:2162
  13.4 26.7 %copy-start.120 = (f32[1024]{0:T(1024)S(1)}, f32[1024]{0:T(1024)}, u32[]{:S(2)}) copy-start(f32[1024]{0:T(1024)} %param.31) | copy-start | bytes 12292
  13.4 26.8 %copy-start.121 = (f32[1024]{0:T(1024)S(1)}, f32[1024]{0:T(1024)}, u32[]{:S(2)}) copy-start(f32[1024]{0:T(1024)} %param.32) | copy-start | bytes 12292
  40.0 231.7 %all-gather.4.cloned.1.call-start = ((), (), s32[]{:S(2)}) async-start(), calls=%async_computation.1 | async-start | bytes 1310720 | tf_op jit(solution)/shard_map/all_gather | solution.py:2240
  41.2 8.3 %copy-start.85 = (bf16[4,16,1024]{2,1,0:T(8,128)(2,1)S(1)}, bf16[4,16,1024]{2,1,0:T(8,128)(2,1)}, u32[]{:S(2)}) copy-start(bf16[4,16,1024]{2,1,0:T(8,128)(2,1)} %copy-done.84) | copy-start | bytes 393220
  49.5 13.4 %copy-start.129 = (bf16[256,9,512]{2,0,1:T(8,128)(2,1)S(1)}, bf16[256,9,512]{2,0,1:T(8,128)(2,1)}, u32[]{:S(2)}) copy-start(bf16[256,9,512]{2,0,1:T(8,128)(2,1)} %param.33) | copy-start | bytes 7077892
  61.9 5.2 copy-start.24
  61.9 5.2 copy-start.89
  174.0 27.9 %copy-start.20 = (bf16[2,2,4,16,1024]{4,3,2,1,0:T(8,128)(2,1)S(1)}, bf16[2,2,4,16,1024]{4,3,2,1,0:T(8,128)(2,1)}, u32[]{:S(2)}) copy-start(bf16[2,2,4,16,1024]{4,3,2,1,0:T(8,128)(2,1)} %param.26) | copy-start | bytes 1572868
  196.2 20.2 %copy-start.4 = (bf16[1,1024,1024]{2,1,0:T(8,128)(2,1)}, bf16[1,1024,1024]{2,1,0:T(8,128)(2,1)S(1)}, u32[]{:S(2)}) copy-start(bf16[1,1024,1024]{2,1,0:T(8,128)(2,1)S(1)} %get-tuple-element.139) | copy-start | bytes 6291460
  202.0 19.1 %copy-start.122 = (s32[2,8]{1,0:T(2,128)S(1)}, s32[2,8]{1,0:T(2,128)}, u32[]{:S(2)}) copy-start(s32[2,8]{1,0:T(2,128)} %param.28) | copy-start | bytes 196
  219.5 461.5 %reduce-scatter.2.cloned.1.call-start = ((), (), s32[]{:S(2)}) async-start(), calls=%async_computation.2 | async-start | bytes 1310720 | tf_op jit(solution)/shard_map/reduce_scatter | solution.py:2371
  225.3 6.0 copy-start.118
  229.2 35.0 %copy-start.9 = (f32[8,128,128]{2,1,0:T(8,128)}, f32[8,128,128]{2,1,0:T(8,128)S(1)}, u32[]{:S(2)}) copy-start(f32[8,128,128]{2,1,0:T(8,128)S(1)} %convolution_bitcast_fusion.19.bias_ref) | copy-start | bytes 1572868
  231.3 15.9 %copy-start.32 = (bf16[256,2048]{1,0:T(8,128)(2,1)S(1)}, bf16[256,2048]{1,0:T(8,128)(2,1)}, u32[]{:S(2)}) copy-start(bf16[256,2048]{1,0:T(8,128)(2,1)} %refs_1_.1) | copy-start | bytes 3145732
  231.3 15.9 %copy-start.33 = (bf16[2048,256]{1,0:T(8,128)(2,1)S(1)}, bf16[2048,256]{1,0:T(8,128)(2,1)}, u32[]{:S(2)}) copy-start(bf16[2048,256]{1,0:T(8,128)(2,1)} %refs_2_.1) | copy-start | bytes 3145732
  274.8 14.4 %copy-start.69 = (bf16[4,64,512]{2,1,0:T(8,128)(2,1)S(1)}, bf16[4,64,512]{2,1,0:T(8,128)(2,1)}, u32[]{:S(2)}) copy-start(bf16[4,64,512]{2,1,0:T(8,128)(2,1)} %copy-done.68) | copy-start | bytes 786436
  274.8 14.4 %copy-start.71 = (bf16[4,128,256]{2,1,0:T(8,128)(2,1)S(1)}, bf16[4,128,256]{2,1,0:T(8,128)(2,1)}, u32[]{:S(2)}) copy-start(bf16[4,128,256]{2,1,0:T(8,128)(2,1)} %copy-done.70) | copy-start | bytes 786436
  282.8 6.4 copy-start.90
  349.4 21.3 %copy-start.10 = (f32[8,128,128]{2,1,0:T(8,128)S(1)}, f32[8,128,128]{2,1,0:T(8,128)}, u32[]{:S(2)}) copy-start(f32[8,128,128]{2,1,0:T(8,128)} %copy-done.9) | copy-start | bytes 1572868
  349.4 21.3 %copy-start.13 = (bf16[2,8,16,1536]{3,2,1,0:T(8,128)(2,1)S(1)}, bf16[2,8,16,1536]{3,2,1,0:T(8,128)(2,1)}, u32[]{:S(2)}) copy-start(bf16[2,8,16,1536]{3,2,1,0:T(8,128)(2,1)} %copy-done.12) | copy-start | bytes 2359300
  354.8 24.0 %copy-start.34 = (bf16[1024,512]{1,0:T(8,128)(2,1)S(1)}, bf16[1024,512]{1,0:T(8,128)(2,1)}, u32[]{:S(2)}) copy-start(bf16[1024,512]{1,0:T(8,128)(2,1)} %get-tuple-element.176) | copy-start | bytes 3145732
  404.7 22.4 %copy-start.72 = (bf16[256,512]{1,0:T(8,128)(2,1)}, bf16[256,512]{1,0:T(8,128)(2,1)S(1)}, u32[]{:S(2)}) copy-start(bf16[256,512]{1,0:T(8,128)(2,1)S(1)} %get-tuple-element.228) | copy-start | bytes 786436
  404.7 48.5 %copy-start.44 = (bf16[4,3,256,128]{3,2,1,0:T(8,128)(2,1)S(1)}, bf16[4,3,256,128]{3,2,1,0:T(8,128)(2,1)}, u32[]{:S(2)}) copy-start(bf16[4,3,256,128]{3,2,1,0:T(8,128)(2,1)} %copy-done.43) | copy-start | bytes 2359300
  427.1 26.0 %copy-start.5 = (bf16[1,1024,1024]{2,1,0:T(8,128)(2,1)S(1)}, bf16[1,1024,1024]{2,1,0:T(8,128)(2,1)}, u32[]{:S(2)}) copy-start(bf16[1,1024,1024]{2,1,0:T(8,128)(2,1)} %copy-done.4) | copy-start | bytes 6291460
  453.1 10.4 %copy-start.16 = (bf16[1024,1024]{1,0:T(8,128)(2,1)S(1)}, bf16[1024,1024]{1,0:T(8,128)(2,1)}, u32[]{:S(2)}) copy-start(bf16[1024,1024]{1,0:T(8,128)(2,1)} %get-tuple-element.189) | copy-start | bytes 6291460
  463.5 23.1 %copy-start.45 = (bf16[1024,384]{1,0:T(8,128)(2,1)}, bf16[1024,384]{1,0:T(8,128)(2,1)S(1)}, u32[]{:S(2)}) copy-start(bf16[1024,384]{1,0:T(8,128)(2,1)S(1)} %get-tuple-element.204) | copy-start | bytes 2359300
  487.5 5.3 copy-start.27
  494.1 23.6 %copy-start.107 = (bf16[128,8,2,512]{3,1,2,0:T(8,128)(2,1)S(1)}, bf16[128,8,2,512]{3,1,2,0:T(8,128)(2,1)}, u32[]{:S(2)}) copy-start(bf16[128,8,2,512]{3,1,2,0:T(8,128)(2,1)} %copy.183) | copy-start | bytes 6291460
  523.2 28.7 %copy-start.19 = (f32[4,256,128]{2,1,0:T(8,128)S(1)}, f32[4,256,128]{2,1,0:T(8,128)}, u32[]{:S(2)}) copy-start(f32[4,256,128]{2,1,0:T(8,128)} %copy-done.17) | copy-start | bytes 1572868
  524.5 30.7 %copy-start.126 = (s32[2,2]{1,0:T(2,128)S(1)}, s32[2,2]{1,0:T(2,128)}, u32[]{:S(2)}) copy-start(s32[2,2]{1,0:T(2,128)} %copy-done.125) | copy-start | bytes 52
  562.1 22.8 %copy-start.110 = (bf16[4,256,256]{2,1,0:T(8,128)(2,1)S(1)}, bf16[4,256,256]{2,1,0:T(8,128)(2,1)}, u32[]{:S(2)}) copy-start(bf16[4,256,256]{2,1,0:T(8,128)(2,1)} %get-tuple-element.302) | copy-start | bytes 1572868
  584.9 4.8 copy-start.103
  589.8 4.0 copy-start.73
  590.3 4.6 copy-start.50
  598.9 80.5 %collective-permute-start = (bf16[16,4096]{1,0:T(8,128)(2,1)}, bf16[16,4096]{1,0:T(8,128)(2,1)}, u32[]{:S(2)}, u32[]{:S(2)}) collective-permute-start(bf16[16,4096]{1,0:T(8,128)(2,1)} %bitcast.215), channel_id=1, source_target_pairs={{0,1},{1,0},{2,3},{3,2},{4,5},{5,4},{6,7},{7,6},{8,9},{9,8},{10,11... | collective-permute-start | bytes 393224 | tf_op jit(solution)/shard_map/ppermute | solution.py:27
  598.9 4.2 copy-start.111
  606.4 33.2 %copy-start.128 = (f32[128]{0:T(128)S(1)}, f32[128]{0:T(128)}, u32[]{:S(2)}) copy-start(f32[128]{0:T(128)} %dynamic_slice.50) | copy-start | bytes 1540
  606.4 33.2 %copy-start.127 = (f32[128]{0:T(128)S(1)}, f32[128]{0:T(128)}, u32[]{:S(2)}) copy-start(f32[128]{0:T(128)} %dynamic_slice.48) | copy-start | bytes 1540
  639.6 5.7 copy-start.80
  643.0 23.5 %copy-start.40 = (bf16[4,64,1536]{2,1,0:T(8,128)(2,1)S(1)}, bf16[4,64,1536]{2,1,0:T(8,128)(2,1)}, u32[]{:S(2)}) copy-start(bf16[4,64,1536]{2,1,0:T(8,128)(2,1)} %copy-done.39) | copy-start | bytes 2359300
  643.7 22.9 %copy-start.64 = (bf16[5,64,512]{2,1,0:T(8,128)(2,1)S(1)}, bf16[5,64,512]{2,1,0:T(8,128)(2,1)}, u32[]{:S(2)}) copy-start(bf16[5,64,512]{2,1,0:T(8,128)(2,1)} %copy-done.63) | copy-start | bytes 983044
  645.3 22.5 %copy-start.114 = (bf16[2,3,512]{2,1,0:T(4,128)(2,1)S(1)}, bf16[2,3,512]{2,1,0:T(4,128)(2,1)}, u32[]{:S(2)}) copy-start(bf16[2,3,512]{2,1,0:T(4,128)(2,1)} %copy-done.113) | copy-start | bytes 18436
  645.3 22.5 %copy-start.116 = (bf16[2,3,512]{2,1,0:T(4,128)(2,1)S(1)}, bf16[2,3,512]{2,1,0:T(4,128)(2,1)}, u32[]{:S(2)}) copy-start(bf16[2,3,512]{2,1,0:T(4,128)(2,1)} %copy-done.115) | copy-start | bytes 18436
  666.5 12.3 %collective-permute-start.1 = (f32[448]{0:T(512)S(1)}, f32[448]{0:T(512)S(1)}, u32[]{:S(2)}, u32[]{:S(2)}) collective-permute-start(f32[448]{0:T(512)S(1)} %bitcast.549), channel_id=1, source_target_pairs={{0,1},{1,0},{2,3},{3,2},{4,5},{5,4},{6,7},{7,6},{8,9},{9,8},{10,11... | collective-permute-start | bytes 5384 | tf_op jit(solution)/shard_map/ppermute | solution.py:2488
  672.5 5.0 copy-start.82
  677.6 6.7 copy-start.1
  (88 other events, 131.0 us)
Sparse Core Ops, SparseCore 0:
  40.1 51.8 all-gather.5
  219.6 26.7 all-gather.3
  595.1 34.8 reduce-scatter.1

commit v5 on v4

--- a/solution.py
+++ b/solution.py
@@ -162,6 +162,38 @@
             copy.wait()
 
 
+class ColumnJoin(Rider):
+    axes = ("space",)
+
+    def __init__(self, source, pick, cut):
+        self.source, self.pick, self.cut = source, pick, cut
+        stack = jax.eval_shape(cut, source)
+        self.lines, self.width = stack.shape[0], stack.shape[-1]
+        shape = stack.shape[1:-1] + (self.lines * self.width,)
+        self.result = jax.ShapeDtypeStruct(shape, stack.dtype)
+        self.scratch = dma_sems(self.lines - 1, self.lines - 1, 1)
+
+    def plain(self):
+        stack = lax.all_to_all(
+            self.cut(self.source), "space", split_axis=0, concat_axis=0, tiled=True
+        )
+        return jnp.concatenate([stack[i] for i in range(self.lines)], axis=-1)
+
+    def start(self, x_ref, out_ref, send_sem, recv_sem, own_sem):
+        me = lax.axis_index("space")
+        cols = span(me, self.width)
+        target = out_ref.at[:, cols] if len(self.result.shape) == 2 else out_ref.at[:, :, cols]
+        self.copies = [
+            send(self.pick(x_ref, peer), target, send_sem.at[i - 1], recv_sem.at[i - 1], {"space": peer})
+            for i, peer in others("space")
+        ]
+        self.copies.append(keep(self.pick(x_ref, me), target, own_sem.at[0]))
+
+    def finish(self, *refs):
+        for copy in self.copies:
+            copy.wait()
+
+
 def span(index, size):
     return pl.ds(pl.multiple_of(index * size, size), size)
 
@@ -171,17 +203,18 @@
     source_spec = VMEM
     result_spec = VMEM
 
-    def __init__(self, source):
+    def __init__(self, source, kind=jnp.bfloat16):
         self.source = source
         self.lines = lax.axis_size("space")
         self.rows, self.width = source.shape[0] // self.lines, source.shape[1]
-        self.result = jax.ShapeDtypeStruct((self.rows, self.width), jnp.bfloat16)
+        self.result = jax.ShapeDtypeStruct((self.rows, self.width), kind)
         self.scratch = [
             pltpu.VMEM((self.lines - 1, self.rows, self.width), jnp.bfloat16)
         ] + dma_sems(self.lines - 1, self.lines - 1)
 
     def plain(self):
-        return lax.psum_scatter(self.source, "space", scatter_dimension=0, tiled=True)
+        total = lax.psum_scatter(self.source, "space", scatter_dimension=0, tiled=True)
+        return total.astype(self.result.dtype)
 
     def start(self, x_ref, out_ref, got_ref, send_sem, recv_sem):
         self.copies = [
@@ -195,7 +228,7 @@
         total = x_ref[span(lax.axis_index("space"), self.rows)].astype(jnp.float32)
         for step in range(self.lines - 1):
             total = total + got_ref[step].astype(jnp.float32)
-        out_ref[...] = total.astype(jnp.bfloat16)
+        out_ref[...] = total.astype(out_ref.dtype)
 
 
 class Share(Rider):
@@ -336,17 +369,18 @@
     axes = ("tm",)
     result_spec = VMEM
 
-    def __init__(self, source, taps=False):
-        self.taps = taps
+    def __init__(self, source, taps=False, first=0, size=None, kind=jnp.bfloat16):
+        self.taps, self.first = taps, first
         self.count = lax.axis_size("tm")
         if taps:
             self.layers, all_rows, self.width = source.shape
+            self.layers = self.layers if size is None else size
             self.rows = all_rows // self.count
         else:
             self.layers, (_, self.rows, self.width) = 1, source.shape
         self.source = source
         shape = (self.layers, self.rows, self.width)
-        self.result = jax.ShapeDtypeStruct(shape if taps else shape[1:], jnp.bfloat16)
+        self.result = jax.ShapeDtypeStruct(shape if taps else shape[1:], kind)
         self.square = self.count == 4 and self.rows % 32 == 0
         self.split = self.rows // 2 if self.square else self.rows
         half = (self.layers, self.split, self.width)
@@ -364,13 +398,16 @@
 
     def plain(self):
         dim = 1 if self.taps else 0
-        total = lax.psum_scatter(self.source, "tm", scatter_dimension=dim, tiled=True)
-        return total if self.taps else total[0]
+        source = self.source
+        if self.taps:
+            source = source[self.first : self.first + self.layers]
+        total = lax.psum_scatter(source, "tm", scatter_dimension=dim, tiled=True)
+        return (total if self.taps else total[0]).astype(self.result.dtype)
 
     def view(self, w_ref, place, half):
         if self.taps:
             start = pl.multiple_of(place * self.rows + half * self.split, self.split)
-            return w_ref.at[:, pl.ds(start, self.split)]
+            return w_ref.at[pl.ds(self.first, self.layers), pl.ds(start, self.split)]
         return w_ref.at[pl.ds(place, 1), pl.ds(half * self.split, self.split)]
 
     def add(self, target_ref, first, *rest):
@@ -383,7 +420,7 @@
             total = first[layer, rows].astype(jnp.float32)
             for other in rest:
                 total = total + other[layer, rows].astype(jnp.float32)
-            target_ref[layer, rows] = total.astype(jnp.bfloat16)
+            target_ref[layer, rows] = total.astype(target_ref.dtype)
             return carry
 
         lax.fori_loop(0, self.layers * steps, some, 0)
@@ -518,48 +555,6 @@
         self.copy.wait()
 
 
-class TapSum(Rider):
-    axes = ("tm",)
-    source_spec = VMEM
-    result_spec = VMEM
-
-    def __init__(self, source):
-        self.taps, all_rows, self.width = source.shape
-        self.count = lax.axis_size("tm")
-        self.rows = all_rows // self.count
-        self.source = source
-        shape = (self.taps, self.rows, self.width)
-        self.result = jax.ShapeDtypeStruct(shape, jnp.bfloat16)
-        self.scratch = [
-            pltpu.VMEM((max(self.count - 1, 1),) + shape, jnp.bfloat16),
-            pltpu.VMEM(shape, jnp.bfloat16),
-        ] + dma_sems(self.count - 1, self.count - 1, 1)
-
-    def plain(self):
-        return lax.psum_scatter(self.source, "tm", scatter_dimension=1, tiled=True)
-
-    def start(self, w_ref, out_ref, got_ref, own_ref, send_sem, recv_sem, own_sem):
-        me = lax.axis_index("tm")
-        self.copies = [
-            send(rows_of(w_ref, peer, self.rows), got_ref.at[i - 1], send_sem.at[i - 1], recv_sem.at[i - 1], {"tm": peer})
-            for i, peer in others("tm")
-        ]
-        self.copies.append(keep(rows_of(w_ref, me, self.rows), own_ref, own_sem.at[0]))
-
-    def finish(self, w_ref, out_ref, got_ref, own_ref, *sems):
-        for copy in self.copies:
-            copy.wait()
-
-        def some(tap, carry):
-            total = own_ref[tap].astype(jnp.float32)
-            for step in range(self.count - 1):
-                total = total + got_ref[step, tap].astype(jnp.float32)
-            out_ref[tap] = total.astype(jnp.bfloat16)
-            return carry
-
-        lax.fori_loop(0, self.taps, some, 0)
-
-
 class CoreSum(Rider):
     source_spec = VMEM
     result_spec = VMEM
@@ -598,15 +593,14 @@
     return [rider.plain() for rider in riders]
 
 
-def talk_with(kernel, peers, result, operands, scratch, number, riders, specs=None, out_spec=ANY):
-    specs = [ANY] * len(operands) if specs is None else specs
-    inputs, own_scratch, count = len(operands), len(scratch), len(riders)
+def talk_many(kernel, peers, results, operands, scratch, number, riders, specs, out_specs):
+    inputs, outputs, own_scratch, count = len(operands), len(results), len(scratch), len(riders)
 
     def whole(*refs):
         ins, rider_ins = refs[:inputs], refs[inputs : inputs + count]
-        out_ref = refs[inputs + count]
-        rider_outs = refs[inputs + count + 1 : inputs + 2 * count + 1]
-        rest = refs[inputs + 2 * count + 1 :]
+        outs = refs[inputs + count : inputs + count + outputs]
+        rider_outs = refs[inputs + count + outputs : inputs + 2 * count + outputs]
+        rest = refs[inputs + 2 * count + outputs :]
         mine, rest = rest[:own_scratch], rest[own_scratch:]
         packs = []
         for rider, x_ref, y_ref in zip(riders, rider_ins, rider_outs):
@@ -622,21 +616,31 @@
                 rider, pack = waiting.pop(0)
                 rider.middle(*pack)
 
-        kernel(hook, *ins, out_ref, *mine)
+        kernel(hook, *ins, *outs, *mine)
         hook()
         for rider, pack in zip(riders, packs):
             rider.finish(*pack)
 
-    results = talk(
+    done = talk(
         whole,
-        (result,) + tuple(rider.result for rider in riders),
-        operands + [rider.source for rider in riders],
+        tuple(results) + tuple(rider.result for rider in riders),
+        list(operands) + [rider.source for rider in riders],
         scratch + [item for rider in riders for item in rider.scratch],
         number,
-        specs + [rider.source_spec for rider in riders],
-        (out_spec,) + tuple(rider.result_spec for rider in riders),
-    )
-    return results[0], list(results[1:])
+        list(specs) + [rider.source_spec for rider in riders],
+        tuple(out_specs) + tuple(rider.result_spec for rider in riders),
+    )
+    return list(done[:outputs]), list(done[outputs:])
+
+
+def talk_with(kernel, peers, result, operands, scratch, number, riders, specs=None, out_spec=ANY):
+    if number is None:
+        return kernel, peers, result, scratch
+    specs = [ANY] * len(operands) if specs is None else specs
+    done, others_done = talk_many(
+        kernel, peers, [result], operands, scratch, number, riders, specs, [out_spec]
+    )
+    return done[0], others_done
 
 
 def line_peers():
@@ -696,7 +700,7 @@
                     def _():
                         move(step, part, sign, send_sem, recv_sem).start()
 
-        if step == min(1, lines - 1):
+        if step == max(lines - 2, 0):
             hook()
     for step in range(lines - 1):
         for part in range(parts):
@@ -748,7 +752,7 @@
                         source = slots.at[step - 1, part]
                         move(source, slots, sem_out, sem_in, step, part, peer).start()
 
-        if step == min(1, last - 1):
+        if step == last - 1:
             hook()
     for part in range(parts):
         for rank, peer, slots, sem_out, sem_in, target in ways:
@@ -770,6 +774,8 @@
     pieces = lines * cores if per_core or join else lines
     width = channels // pieces
     if width % lane != 0 or pixels % 16 != 0:
+        if number is None:
+            return None
         if per_core:
             parts = source.reshape(images, pixels, lines, cores, width)
             parts = lax.dynamic_index_in_dim(parts, lax.axis_index("mp"), 3, keepdims=False)
@@ -798,6 +804,7 @@
             own = keep(cols_of(x_ref, me, own_width), rows_of(out_ref, me, pixels), own_sem.at[0])
         else:
             own = keep(cols_of(x_ref, place(me), width), spot(me), own_sem.at[0])
+        hook()
         passed = []
         for step in range(1, lines):
             copies[step - 1].wait_recv()
@@ -826,6 +833,8 @@
     pixels = line_pixels // lines
     pieces = lines * cores if per_core else lines
     if width % lane != 0 or pixels % 16 != 0:
+        if number is None:
+            return None
         part = lax.all_to_all(source, "space", split_axis=1, concat_axis=2, tiled=True)
         if per_core:
             part = part.reshape(images, pixels, lines, 1, width)
@@ -846,6 +855,7 @@
                 send(rows_of(x_ref, me, pixels), got_ref.at[me, core], pass_sem.at[0], gain_sem.at[0], twin)
             )
         got_ref[me, mine] = x_ref[:, pl.ds(pl.multiple_of(me * pixels, pixels), pixels), :]
+        hook()
         for step in range(1, lines):
             copies[step - 1].wait_recv()
             if per_core:
@@ -906,6 +916,7 @@
         target = cols_of(out_ref, core, width)
         copy = send(x_ref, target, send_sem.at[0], recv_sem.at[0], twin)
         own = keep(x_ref, target, own_sem.at[0])
+        hook()
         copy.wait()
         own.wait()
 
@@ -964,6 +975,7 @@
         twin = {"mp": 1 - core}
         copy = send(cols_of(x_ref, 1 - core, width), got_ref, send_sem.at[0], recv_sem.at[0], twin)
         mine = pl.ds(pl.multiple_of(core * width, width), width)
+        hook()
         copy.wait()
         for image in range(images):
             out_ref[image] = x_ref[image, :, mine].astype(jnp.float32) + got_ref[image].astype(
@@ -982,7 +994,7 @@
     count, channels = rows.shape
     lines, cores = lax.axis_size("space"), lax.axis_size("mp")
     width = channels // cores
-    source = rows.reshape(1, count, channels)
+    source = None if number is None else rows.reshape(1, count, channels)
 
     def kernel(hook, x_ref, out_ref, pass_sem, gain_sem, own_sem, *sems):
         me, core = lax.axis_index("space"), lax.axis_index("mp")
@@ -1033,6 +1045,8 @@
     def peers():
         return line_peers() + twin_peers()
 
+    if number is None:
+        return kernel, peers, result, sems
     line, others_done = talk_with(kernel, peers, result, [source], sems, number, riders, [VMEM], VMEM)
     return line.reshape(lines * count, channels), others_done
 
@@ -1041,7 +1055,9 @@
     all_rows, channels = partial_sum.shape
     lines, cores = lax.axis_size("space"), lax.axis_size("mp")
     count, width = all_rows // lines, channels // cores
-    source = partial_sum.astype(jnp.bfloat16).reshape(lines, count, channels)
+    source = None
+    if number is not None:
+        source = partial_sum.astype(jnp.bfloat16).reshape(lines, count, channels)
 
     def kernel(
         hook, x_ref, out_ref, twin_ref, stage_ref, right_ref, left_ref, sum_ref,
@@ -1100,10 +1116,9 @@
     def peers():
         return line_peers() + [{"mp": 1 - lax.axis_index("mp")}]
 
-    total, other = talk_with(
+    return talk_with(
         kernel, peers, result, [source], scratch + sems, number, riders, [VMEM], VMEM
     )
-    return total, other
 
 
 def to_clips(source, number, riders=()):
@@ -1111,6 +1126,8 @@
     count = lax.axis_size("tm")
     few = pixels // count
     if few % 16 != 0:
+        if number is None:
+            return None
         return lax.all_to_all(source, "tm", split_axis=2, concat_axis=1, tiled=True), plain_all(riders)
 
     def kernel(hook, x_ref, out_ref, send_sem, recv_sem, own_sem):
@@ -1125,6 +1142,7 @@
             for i, peer in others("tm")
         ]
         copies.append(keep(part(me), target, own_sem.at[0]))
+        hook()
         for copy in copies:
             copy.wait()
 
@@ -1138,6 +1156,8 @@
     count = lax.axis_size("tm")
     frames = all_frames // count
     if few % 16 != 0:
+        if number is None:
+            return None
         return lax.all_to_all(source, "tm", split_axis=1, concat_axis=2, tiled=True), plain_all(riders)
 
     def kernel(hook, x_ref, out_ref, send_sem, recv_sem, own_sem):
@@ -1152,6 +1172,7 @@
             for i, peer in others("tm")
         ]
         copies.append(keep(part(me), target, own_sem.at[0]))
+        hook()
         for copy in copies:
             copy.wait()
 
@@ -1355,32 +1376,33 @@
 
 def spatial_forward(rows, weight):
     lines, images, pixels, channels = rows.shape
-    width = weight.shape[2]
+    width = weight.shape[1] // 3
     count = lines * pixels
 
     def kernel(x_ref, w_ref, triple_ref, mix_ref):
         x = x_ref[...].reshape(count, channels)
-        for j in range(3):
-            triple_ref[0, j] = low(dot(x, w_ref[j]))
+        triple_ref[0] = low(dot(x, w_ref[...]))
         for head in range(width // HDIM):
-            cols = slice(head * HDIM, (head + 1) * HDIM)
-            query, key, value = (triple_ref[0, j, :, cols] for j in range(3))
-            mix_ref[0, :, cols] = low(head_forward(query, key, value, None, None))
+            at = head * HDIM
+            query, key, value = (
+                triple_ref[0, :, j * width + at : j * width + at + HDIM] for j in range(3)
+            )
+            mix_ref[0, :, at : at + HDIM] = low(head_forward(query, key, value, None, None))
 
     return local(
         kernel,
         (
-            jax.ShapeDtypeStruct((images, 3, count, width), jnp.bfloat16),
+            jax.ShapeDtypeStruct((images, count, 3 * width), jnp.bfloat16),
             jax.ShapeDtypeStruct((images, count, width), jnp.bfloat16),
         ),
         (rows, weight),
         (images,),
         [
             pl.BlockSpec((lines, 1, pixels, channels), lambda i: (0, i, 0, 0)),
-            pl.BlockSpec(weight.shape, lambda i: (0, 0, 0)),
+            pl.BlockSpec(weight.shape, lambda i: (0, 0)),
         ],
         (
-            pl.BlockSpec((1, 3, count, width), lambda i: (i, 0, 0, 0)),
+            pl.BlockSpec((1, count, 3 * width), lambda i: (i, 0, 0)),
             pl.BlockSpec((1, count, width), lambda i: (i, 0, 0)),
         ),
     )
@@ -1388,34 +1410,32 @@
 
 def spatial_backward(rows, weight, triple, upstream):
     lines, images, pixels, channels = rows.shape
-    width = weight.shape[2]
+    width = weight.shape[1] // 3
     count = lines * pixels
 
     def kernel(x_ref, w_ref, triple_ref, up_ref, grad_ref, dw_ref, grads_ref, total_ref):
         step = pl.program_id(0)
         x = x_ref[...].reshape(count, channels)
         for head in range(width // HDIM):
-            cols = slice(head * HDIM, (head + 1) * HDIM)
-            query, key, value = (triple_ref[0, j, :, cols] for j in range(3))
-            grads = head_backward(query, key, value, None, None, up_ref[0, :, cols])
+            at = head * HDIM
+            query, key, value = (
+                triple_ref[0, :, j * width + at : j * width + at + HDIM] for j in range(3)
+            )
+            grads = head_backward(query, key, value, None, None, up_ref[0, :, at : at + HDIM])
             for j in range(3):
-                grads_ref[j, :, cols] = low(grads[j])
-        part = dot_nt(grads_ref[0], w_ref[0])
-        part = part + dot_nt(grads_ref[1], w_ref[1])
-        part = part + dot_nt(grads_ref[2], w_ref[2])
+                grads_ref[:, j * width + at : j * width + at + HDIM] = low(grads[j])
+        part = dot_nt(grads_ref[...], w_ref[...])
         grad_ref[...] = low(part).reshape(lines, 1, pixels, channels)
 
         @pl.when(step == 0)
         def _():
             total_ref[...] = jnp.zeros_like(total_ref)
 
-        for j in range(3):
-            total_ref[j] += dot_tn(x, grads_ref[j])
+        total_ref[...] += dot_tn(x, grads_ref[...])
 
         @pl.when(step == images - 1)
         def _():
-            for j in range(3):
-                dw_ref[:, j * width : (j + 1) * width] = low(total_ref[j])
+            dw_ref[...] = low(total_ref[...])
 
     return local(
         kernel,
@@ -1427,8 +1447,8 @@
         (images,),
         [
             pl.BlockSpec((lines, 1, pixels, channels), lambda i: (0, i, 0, 0)),
-            pl.BlockSpec(weight.shape, lambda i: (0, 0, 0)),
-            pl.BlockSpec((1, 3, count, width), lambda i: (i, 0, 0, 0)),
+            pl.BlockSpec(weight.shape, lambda i: (0, 0)),
+            pl.BlockSpec((1, count, 3 * width), lambda i: (i, 0, 0)),
             pl.BlockSpec((1, count, width), lambda i: (i, 0, 0)),
         ],
         (
@@ -1436,8 +1456,8 @@
             pl.BlockSpec((channels, 3 * width), lambda i: (0, 0)),
         ),
         [
-            pltpu.VMEM((3, count, width), jnp.bfloat16),
-            pltpu.VMEM((3, channels, width), jnp.float32),
+            pltpu.VMEM((count, 3 * width), jnp.bfloat16),
+            pltpu.VMEM((channels, 3 * width), jnp.float32),
         ],
     )
 
@@ -1529,6 +1549,350 @@
             pl.BlockSpec((bias.shape[0], frames, rows), lambda i: (0, 0, 0)),
         ),
     )
+
+
+def later():
+    pass
+
+
+def like(*shape):
+    return jax.ShapeDtypeStruct(shape, jnp.bfloat16)
+
+
+def temporal_chain(triple, bias, ids, numbers, riders):
+    slots, frames, pixels, channels = triple.shape
+    width, count = channels // 3, lax.axis_size("tm")
+    few, all_frames = pixels // count, frames * count
+    rows = all_frames * few
+    first = to_clips(like(*triple.shape), None)
+    second = from_clips(like(slots, all_frames, few, width), None)
+    if first is None or second is None:
+        clip, done = to_clips(triple, numbers[0], riders)
+        mix = temporal_forward(clip.reshape(slots, rows, channels), bias, ids, few)
+        mix, _ = from_clips(mix.reshape(slots, all_frames, few, width), numbers[1])
+        return clip, mix, done
+
+    def kernel(hook, x_ref, bias_ref, ids_ref, turned_ref, clip_ref, out_ref, mix_ref, *scratch):
+        first[0](later, x_ref, clip_ref, *scratch[: len(first[3])])
+        for slot in range(slots):
+            valid = clip_masks(rows, few, ids_ref.at[pl.ds(slot, 1)], turned_ref.at[pl.ds(slot, 1)])
+            for head in range(width // HDIM):
+                at = head * HDIM
+                query, key, value = (
+                    clip_ref[slot, :, :, j * width + at : j * width + at + HDIM].reshape(rows, HDIM)
+                    for j in range(3)
+                )
+                mix = low(head_forward(query, key, value, bias_ref[head], valid))
+                mix_ref[slot, :, :, at : at + HDIM] = mix.reshape(all_frames, few, HDIM)
+        second[0](hook, mix_ref, out_ref, *scratch[len(first[3]) :])
+
+    (clip, mix), done = talk_many(
+        kernel,
+        frame_peers,
+        [first[2], second[2]],
+        [triple, bias, ids[:, :, None], ids[:, None, :]],
+        [pltpu.VMEM((slots, all_frames, few, width), jnp.bfloat16)] + first[3] + second[3],
+        numbers[0],
+        riders,
+        [VMEM] * 4,
+        [VMEM, VMEM],
+    )
+    return clip, mix, done
+
+
+def temporal_back_chain(clip, bias, ids, upstream, numbers, riders):
+    slots, all_frames, few, channels = clip.shape
+    width, rows = channels // 3, all_frames * few
+    first = to_clips(like(*upstream.shape), None)
+    second = from_clips(like(*clip.shape), None)
+    if first is None or second is None:
+        up, done = to_clips(upstream, numbers[0], riders)
+        grads, score = temporal_backward(
+            clip.reshape(slots, rows, channels), bias, ids, few, up.reshape(slots, rows, width)
+        )
+        grads, _ = from_clips(grads.reshape(clip.shape), numbers[1])
+        return grads, score, done
+
+    def kernel(
+        hook, up_ref, clip_ref, bias_ref, ids_ref, turned_ref, out_ref, score_ref, line_ref, grad_ref, *scratch
+    ):
+        first[0](later, up_ref, line_ref, *scratch[: len(first[3])])
+        frame = lax.broadcasted_iota(jnp.int32, (all_frames, rows), 0)
+        row = lax.broadcasted_iota(jnp.int32, (all_frames, rows), 1)
+        gather = low((row // few == frame).astype(jnp.float32))
+        score_ref[...] = jnp.zeros_like(score_ref)
+        for slot in range(slots):
+            valid = clip_masks(rows, few, ids_ref.at[pl.ds(slot, 1)], turned_ref.at[pl.ds(slot, 1)])
+            for head in range(width // HDIM):
+                at = head * HDIM
+                query, key, value = (
+                    clip_ref[slot, :, :, j * width + at : j * width + at + HDIM].reshape(rows, HDIM)
+                    for j in range(3)
+                )
+                up = line_ref[slot, :, :, at : at + HDIM].reshape(rows, HDIM)
+                grads = head_backward(query, key, value, bias_ref[head], valid, up)
+                for j in range(3):
+                    grad_ref[slot, :, :, j * width + at : j * width + at + HDIM] = low(
+                        grads[j]
+                    ).reshape(all_frames, few, HDIM)
+                score_ref[head] += dot(gather, grads[3])
+        second[0](hook, grad_ref, out_ref, *scratch[len(first[3]) :])
+
+    (grads, score), done = talk_many(
+        kernel,
+        frame_peers,
+        [second[2], jax.ShapeDtypeStruct((bias.shape[0], all_frames, rows), jnp.float32)],
+        [upstream, clip, bias, ids[:, :, None], ids[:, None, :]],
+        [pltpu.VMEM(first[2].shape, jnp.bfloat16), pltpu.VMEM(clip.shape, jnp.bfloat16)]
+        + first[3]
+        + second[3],
+        numbers[0],
+        riders,
+        [VMEM] * 5,
+        [VMEM, VMEM],
+    )
+    return grads, score, done
+
+
+def line_rows(line_ref, image, lines, images, pixels):
+    return jnp.concatenate(
+        [
+            line_ref[0, (s * images + image) * pixels : (s * images + image + 1) * pixels, :]
+            for s in range(lines)
+        ],
+        axis=0,
+    )
+
+
+def spatial_chain(rows, branch, gain, weight, images, numbers, riders):
+    count, channels = rows.shape
+    lines, width = lax.axis_size("space"), weight.shape[1] // 3
+    pixels = count // images
+    first = gather_tokens(like(*rows.shape), None)
+    second = from_lines(like(images, lines * pixels, width), False, None)
+    if second is None:
+        stream, normed = first_norm(rows, branch, gain)
+        line, done = gather_tokens(normed, numbers[0], riders)
+        line = line[None]
+        triple, mix = spatial_forward(line.reshape(lines, images, pixels, channels), weight)
+        mix, _ = from_lines(mix, False, numbers[1])
+        return stream, line, triple, mix, done
+
+    def kernel(
+        hook, branch_ref, gain_ref, w_ref, rows_ref, stream_ref, line_ref, triple_ref, out_ref,
+        mix_ref, normed_ref, one_ref, here_ref, sem, *scratch,
+    ):
+        fetch = Fetch([rows_ref], [here_ref], sem)
+        one = fetch(0)[...].astype(jnp.float32) + branch_ref[...].astype(jnp.float32)
+        one_ref[...] = one
+        written = keep(one_ref, stream_ref, sem.at[1])
+        normed_ref[0] = low(norm_forward(one, gain_ref[...]))
+        first[0](hook, normed_ref, line_ref, *scratch[: len(first[3])])
+        for image in range(images):
+            x = line_rows(line_ref, image, lines, images, pixels)
+            triple_ref[image] = low(dot(x, w_ref[...]))
+            for head in range(width // HDIM):
+                at = head * HDIM
+                query, key, value = (
+                    triple_ref[image, :, j * width + at : j * width + at + HDIM] for j in range(3)
+                )
+                mix = low(head_forward(query, key, value, None, None))
+                mix_ref[image, :, at : at + HDIM] = mix
+        second[0](hook, mix_ref, out_ref, *scratch[len(first[3]) :])
+        written.wait()
+
+    (stream, line, triple, mix), done = talk_many(
+        kernel,
+        lambda: line_peers() + twin_peers(),
+        [
+            jax.ShapeDtypeStruct(rows.shape, jnp.float32),
+            first[2],
+            like(images, lines * pixels, 3 * width),
+            second[2],
+        ],
+        [branch, gain, weight, rows],
+        [
+            pltpu.VMEM((images, lines * pixels, width), jnp.bfloat16),
+            pltpu.VMEM((1,) + rows.shape, jnp.bfloat16),
+            pltpu.VMEM(rows.shape, jnp.float32),
+            pltpu.VMEM(rows.shape, rows.dtype),
+        ]
+        + dma_sems(2)
+        + first[3]
+        + second[3],
+        numbers[0],
+        riders,
+        [VMEM, VMEM, VMEM, ANY],
+        [ANY, VMEM, VMEM, VMEM],
+    )
+    return stream, line, triple, mix, done
+
+
+def late_chain(mix, stream, out, gain, number, riders):
+    rows, channels = stream.shape
+    first = gather_tokens(like(*stream.shape), None)
+
+    def kernel(
+        hook, mix_ref, gain_ref, out_any, stream_any, four_any, line_ref,
+        normed_ref, four_ref, mine_ref, theirs_ref, out_ref, stream_ref, sem, end_sem, send_sem, recv_sem, *scratch,
+    ):
+        fetch = Fetch([out_any, stream_any], [out_ref, stream_ref], sem)
+        part = dot(mix_ref[...], out_weight(fetch(0), 0, 1))
+        part = twin_sum(part, mine_ref, theirs_ref, send_sem.at[0], recv_sem.at[0])
+        four = fetch(1)[...] + part
+        four_ref[...] = four
+        written = keep(four_ref, four_any, end_sem.at[0])
+        normed_ref[0] = low(norm_forward(four, gain_ref[...]))
+        first[0](hook, normed_ref, line_ref, *scratch)
+        written.wait()
+
+    (four, line), done = talk_many(
+        kernel,
+        lambda: line_peers() + twin_peers(),
+        [jax.ShapeDtypeStruct(stream.shape, jnp.float32), first[2]],
+        [mix, gain, out, stream],
+        [
+            pltpu.VMEM((1,) + stream.shape, jnp.bfloat16),
+            pltpu.VMEM(stream.shape, jnp.float32),
+            pltpu.VMEM(stream.shape, jnp.bfloat16),
+            pltpu.VMEM(stream.shape, jnp.bfloat16),
+            pltpu.VMEM(out.shape, out.dtype),
+            pltpu.VMEM(stream.shape, jnp.float32),
+        ]
+        + dma_sems(2, 1, 1, 1)
+        + first[3],
+        number,
+        riders,
+        [VMEM, VMEM, ANY, ANY],
+        [ANY, VMEM],
+    )
+    return four, line, done
+
+
+def first_back_chain(stream, gain, normed_grad, upstream, owners, images, numbers, riders):
+    count, channels = stream.shape
+    lines, pixels = lax.axis_size("space"), count // images
+    first = to_lines(like(2 * images, pixels, channels), False, None, join=True)
+    if first is None or (channels // owners) % HDIM != 0:
+        grad, both, gain_grad = first_norm_backward(
+            stream, gain, normed_grad, upstream, owners, lines
+        )
+        line, done = to_lines(
+            both.reshape(2 * images, pixels, channels), False, numbers[0], riders, join=True
+        )
+        return grad, line, gain_grad, done
+
+    def kernel(
+        hook, gain_ref, normed_ref, stream_any, up_any, grad_any, line_ref, dg_ref,
+        both_ref, rows_ref, grad_ref, stream_ref, up_ref, sem, *scratch,
+    ):
+        fetch = Fetch([stream_any, up_any], [stream_ref, up_ref], sem)
+        step, gain_grad = norm_backward(
+            fetch(0)[...], gain_ref[...], normed_ref[...].astype(jnp.float32)
+        )
+        grad = fetch(1)[...] + step
+        grad_ref[...] = grad
+        written = keep(grad_ref, grad_any, sem.at[2])
+        dg_ref[...] = gain_grad
+        store_both(rows_ref, low(grad), owners, lines)
+        for half in range(2):
+            for image in range(images):
+                both_ref[half * images + image] = rows_ref[
+                    half, image * pixels : (image + 1) * pixels, :
+                ]
+        first[0](hook, both_ref, line_ref, *scratch)
+        written.wait()
+
+    (grad, line, gain_grad), done = talk_many(
+        kernel,
+        first[1],
+        [
+            jax.ShapeDtypeStruct(stream.shape, jnp.float32),
+            first[2],
+            jax.ShapeDtypeStruct(gain.shape, jnp.float32),
+        ],
+        [gain, normed_grad, stream, upstream],
+        [
+            pltpu.VMEM((2 * images, pixels, channels), jnp.bfloat16),
+            pltpu.VMEM((2, count, channels), jnp.bfloat16),
+            pltpu.VMEM(stream.shape, jnp.float32),
+            pltpu.VMEM(stream.shape, jnp.float32),
+            pltpu.VMEM(stream.shape, jnp.float32),
+        ]
+        + dma_sems(3)
+        + first[3],
+        numbers[0],
+        riders,
+        [VMEM, VMEM, ANY, ANY],
+        [ANY, ANY, VMEM],
+    )
+    return grad, line, gain_grad, done
+
+
+def spatial_back_chain(upstream, line, weight, triple, numbers, riders):
+    images, pixels, _ = upstream.shape
+    lines, (channels, width) = lax.axis_size("space"), weight.shape
+    width = width // 3
+    count = images * pixels
+    first = to_lines(like(*upstream.shape), False, None)
+    second = scatter_tokens(like(lines * count, channels), None)
+    if first is None:
+        up, done = to_lines(upstream, False, numbers[0], riders)
+        part, grads = spatial_backward(
+            line.reshape(lines, images, pixels, channels), weight, triple, up
+        )
+        normed, _ = scatter_tokens(part.reshape(lines * count, channels), numbers[1])
+        return normed, jnp.stack(jnp.split(grads, 3, axis=1)), done
+
+    def kernel(
+        hook, up_ref, line_ref, w_ref, triple_ref, out_ref, dw_ref, upline_ref, part_ref, grads_ref, *scratch
+    ):
+        first[0](later, up_ref, upline_ref, *scratch[: len(first[3])])
+        for image in range(images):
+            for head in range(width // HDIM):
+                at = head * HDIM
+                query, key, value = (
+                    triple_ref[image, :, j * width + at : j * width + at + HDIM] for j in range(3)
+                )
+                up = upline_ref[image, :, at : at + HDIM]
+                grads = head_backward(query, key, value, None, None, up)
+                for j in range(3):
+                    grads_ref[image, :, j * width + at : j * width + at + HDIM] = low(grads[j])
+            part = low(dot_nt(grads_ref[image], w_ref[...]))
+            for s in range(lines):
+                here = slice(image * pixels, (image + 1) * pixels)
+                part_ref[s, here, :] = part[s * pixels : (s + 1) * pixels]
+
+        def weights():
+            total = None
+            for image in range(images):
+                x = line_rows(line_ref, image, lines, images, pixels)
+                one = dot_tn(x, grads_ref[image])
+                total = one if total is None else total + one
+            for j in range(3):
+                dw_ref[j] = low(total[:, j * width : (j + 1) * width])
+            hook()
+
+        second[0](weights, part_ref, out_ref, *scratch[len(first[3]) :])
+
+    (normed, grads), done = talk_many(
+        kernel,
+        lambda: line_peers() + twin_peers(),
+        [second[2], like(3, channels, width)],
+        [upstream, line, weight, triple],
+        [
+            pltpu.VMEM((images, lines * pixels, width), jnp.bfloat16),
+            pltpu.VMEM((lines, count, channels), jnp.bfloat16),
+            pltpu.VMEM((images, lines * pixels, 3 * width), jnp.bfloat16),
+        ]
+        + first[3]
+        + second[3],
+        numbers[0],
+        riders,
+        [VMEM] * 4,
+        [VMEM, VMEM],
+    )
+    return normed, grads, done
 
 
 def gelu_pair(upper):
@@ -1834,11 +2198,19 @@
     return grad, both, gain_grad
 
 
+def text_mask(rows, valid_ref):
+    slots, keys = valid_ref.shape
+    slot = lax.broadcasted_iota(jnp.int32, (rows, keys), 0) // (rows // slots)
+    good = None
+    for index in range(slots):
+        own = (slot == index) & (valid_ref[index : index + 1, :] > 0.5)
+        good = own if good is None else good | own
+    return good
+
+
 def middle_forward(mix, stream, outs, ins, pairs, valid, gains, number):
     rows, channels = stream.shape
     width = mix.shape[1]
-    slots = pairs.shape[0]
-    part = rows // slots
 
     def kernel(
         swap, fetch, flush, mix_ref, x_ref, pairs_ref, valid_ref, gain_ref,
@@ -1849,19 +2221,17 @@
         normed_ref[...] = low(norm_forward(two, gain_ref[0:1, :]))
         flush(0, 1)
         query_ref[...] = low(dot(normed_ref[...], in_weight((fetch(1), fetch(2)), 0, width)))
-        for slot in range(slots):
-            here = slice(slot * part, (slot + 1) * part)
-            good = valid_ref[slot] > 0.5
-            for head in range(width // HDIM):
-                at = head * HDIM
-                cross = head_forward(
-                    query_ref[here, at : at + HDIM],
-                    pairs_ref[slot, :, at : at + HDIM],
-                    pairs_ref[slot, :, width + at : width + at + HDIM],
-                    None,
-                    good,
-                )
-                cross_ref[here, at : at + HDIM] = low(cross)
+        good = text_mask(rows, valid_ref)
+        for head in range(width // HDIM):
+            at = head * HDIM
+            cross = head_forward(
+                query_ref[:, at : at + HDIM],
+                pairs_ref[:, at : at + HDIM],
+                pairs_ref[:, width + at : width + at + HDIM],
+                None,
+                good,
+            )
+            cross_ref[:, at : at + HDIM] = low(cross)
         flush(2, 3)
         three = two_ref[...] + swap(1, dot(cross_ref[...], out_weight(fetch(0), 1, 2)))
         three_ref[...] = three
@@ -1953,8 +2323,6 @@
 ):
     rows, channels = three.shape
     width = mix.shape[1]
-    slots, keys = pairs.shape[0], pairs.shape[1]
-    part = rows // slots
 
     def kernel(
         swap, fetch, flush, pairs_ref, valid_ref, gain_ref,
@@ -1983,22 +2351,21 @@
         cross_up_ref[...] = low(dot_nt(branch, out_weight(fetch(0), 1, 2)))
         query_ref, cross_ref, two_ref = fetch(4), fetch(5), fetch(6)
         normed_ref, mix_ref = fetch(7), fetch(8)
-        for slot in range(slots):
-            here = slice(slot * part, (slot + 1) * part)
-            good = valid_ref[slot] > 0.5
-            for head in range(width // HDIM):
-                at = head * HDIM
-                grads = head_backward(
-                    query_ref[here, at : at + HDIM],
-                    pairs_ref[slot, :, at : at + HDIM],
-                    pairs_ref[slot, :, width + at : width + at + HDIM],
-                    None,
-                    good,
-                    cross_up_ref[here, at : at + HDIM],
-                )
-                dq_ref[here, at : at + HDIM] = low(grads[0])
-                pair_grad_ref[slot, :, at : at + HDIM] = low(grads[1])
-                pair_grad_ref[slot, :, width + at : width + at + HDIM] = low(grads[2])
+        good = text_mask(rows, valid_ref)
+        for head in range(width // HDIM):
+            at = head * HDIM
+            grads = head_backward(
+                query_ref[:, at : at + HDIM],
+                pairs_ref[:, at : at + HDIM],
+                pairs_ref[:, width + at : width + at + HDIM],
+                None,
+                good,
+                cross_up_ref[:, at : at + HDIM],
+            )
+            dq_ref[:, at : at + HDIM] = low(grads[0])
+            pair_grad_ref[:, at : at + HDIM] = low(grads[1])
+            pair_grad_ref[:, width + at : width + at + HDIM] = low(grads[2])
+        flush(2)
 
         def cross_weights():
             cross_dw_ref[...] = low(dot_tn(normed_ref[...], dq_ref[...]))
@@ -2021,7 +2388,7 @@
         [
             jax.ShapeDtypeStruct((rows, channels), jnp.float32),
             jax.ShapeDtypeStruct((rows, width), jnp.bfloat16),
-            jax.ShapeDtypeStruct((slots, keys, 2 * width), jnp.bfloat16),
+            jax.ShapeDtypeStruct(pairs.shape, jnp.bfloat16),
             jax.ShapeDtypeStruct((channels, width), jnp.bfloat16),
             jax.ShapeDtypeStruct((channels, 2 * width), jnp.bfloat16),
             jax.ShapeDtypeStruct((channels, width), jnp.bfloat16),
@@ -2035,7 +2402,7 @@
         number,
         [pltpu.VMEM((rows, width), jnp.bfloat16), pltpu.VMEM((rows, width), jnp.bfloat16)],
         [outs, *ins, last, query, cross, two, normed, mix, triple, three, upstream],
-        [0, 3, 4, 5, 6],
+        [0, 2, 3, 4, 5, 6],
     )
 
 
@@ -2198,16 +2565,13 @@
     frame_film = frame_film.reshape(2, images, 1, -1)
     film_scale, film_shift = 1.0 + frame_film[0], frame_film[1]
     second_in = group_forward(hidden, film_scale, film_shift)
-    second_wide, (text_pairs, in_first) = gather_lines(
+    second_wide, (text_pairs, in_first, cot_late) = gather_lines(
         second_in,
         5,
-        [Share(text_part, ("tm",)), Share(pack, ("tm",), 0, line_half, in_cols)],
-    )
-    text_pairs = (
-        text_pairs.reshape(owners, slots, text_local, 2 * half_width)
-        .transpose(1, 0, 2, 3)
-        .reshape(slots, TXT, 2 * half_width)
-    )
+        [Share(text_part, ("tm",)), Share(pack, ("tm",), 0, line_half, in_cols), Keep(cot_rows)],
+    )
+    cot_half = lax.all_gather(part_of(cot_late, "mp", 1), "space", axis=0, tiled=True)
+    text_pairs = text_pairs.reshape(owners * text_rows, 2 * half_width)
     conv_part = conv_frames(wide(second_wide), second_conv, "IHWO", False).astype(jnp.bfloat16)
     conv_half, _ = sum_cores(conv_part.reshape(images, H * W, -1), 6)
     conv_rows, (outs_all,) = from_lines(
@@ -2216,33 +2580,32 @@
         7,
         [Share(pack, ("tm",), cols=(0, out_cols // 3 * 2))],
     )
-    spatial_qkv = qkv_piece.transpose(2, 1, 0, 3, 4).reshape(3, channels, -1)
+    spatial_qkv = qkv_piece.transpose(1, 0, 3, 2, 4).reshape(channels, -1)
 
     spatial_gain = spatial_norm[None]
-    stream_one, spatial_in = first_norm(
-        video_rows, conv_rows.reshape(token_rows, channels), spatial_gain
-    )
-    spatial_line, (in_rest,) = gather_tokens(
-        spatial_in, 8, [Share(pack, ("tm",), line_half, lines - line_half, in_cols)]
-    )
-    spatial_line = spatial_line.reshape(lines, images, pixels_dev, channels)
-    spatial_triple, spatial_mix = spatial_forward(spatial_line, spatial_qkv)
-    spatial_mix, (out_last, cot_late, text_cols) = from_lines(
-        spatial_mix,
-        False,
-        9,
-        [
-            Share(pack, ("tm",), cols=(out_cols // 3 * 2, out_cols)),
-            Keep(cot_rows),
-            cut_and_send(text_flat, ("tm",), pick_text, cut_text),
-        ],
-    )
-    cot_half = lax.all_gather(part_of(cot_late, "mp", 1), "space", axis=0, tiled=True)
+    stream_one, spatial_line, spatial_triple, spatial_mix, (in_rest, out_last, text_cols) = (
+        spatial_chain(
+            video_rows,
+            conv_rows.reshape(token_rows, channels),
+            spatial_gain,
+            spatial_qkv,
+            images,
+            (8, 9),
+            [
+                Share(pack, ("tm",), line_half, lines - line_half, in_cols),
+                Share(pack, ("tm",), cols=(out_cols // 3 * 2, out_cols)),
+                cut_and_send(text_flat, ("tm",), pick_text, cut_text),
+            ],
+        )
+    )
 
     spatial_mix = spatial_mix.reshape(token_rows, half_width)
     in_all = (in_first, in_rest)
-    text_valid = (jnp.arange(TXT, dtype=jnp.int32)[None, :] < text_lengths[:, None])[:, None, :]
-    text_valid = text_valid.astype(jnp.float32)
+    key = jnp.arange(owners * text_rows, dtype=jnp.int32)[None, :]
+    key_slot = key % text_rows // text_local
+    key_place = key // text_rows * text_local + key % text_local
+    own_slot = key_slot == jnp.arange(slots, dtype=jnp.int32)[:, None]
+    text_valid = (own_slot & (key_place < text_lengths[:, None])).astype(jnp.float32)
     two_gains = jnp.stack([cross_norm, temporal_norm])
     stream_two, cross_in, cross_queries, cross_mix, stream_three, temporal_in, temporal_triple = (
         middle_forward(
@@ -2250,17 +2613,8 @@
         )
     )
 
-    clip_triple, (in_quarter, out_quarter) = to_clips(
-        temporal_triple.reshape(slots, frame_dev, pixels_dev, 3 * half_width),
-        10,
-        [
-            cut_and_send(feed_in, ("space",), pick_in, cut_in),
-            cut_and_send(feed_out, ("space",), pick_out, cut_out),
-        ],
-    )
-    clip_pixels = clip_triple.shape[2]
+    clip_pixels = pixels_dev // frames_axis
     clip_rows = frames_all * clip_pixels
-    clip_triple = clip_triple.reshape(slots, clip_rows, 3 * half_width)
     offset_table = offset_onehot(0, frames_all, frames_all)
     clip_frames = jnp.arange(clip_rows, dtype=jnp.int32)[:, None] // clip_pixels
     clip_frames = (clip_frames == jnp.arange(frames_all, dtype=jnp.int32)[None, :]).astype(
@@ -2270,18 +2624,27 @@
     clip_bias = jnp.einsum("hqk,ck->hqc", clip_bias, clip_frames, precision=highest)
     clip_bias = jnp.einsum("rq,hqc->hrc", clip_frames, clip_bias, precision=highest)
     clip_ids = jnp.repeat(video_ids, clip_pixels, axis=1)
-    clip_mix = temporal_forward(clip_triple, clip_bias, clip_ids, clip_pixels)
-    temporal_mix, (cot_line, text_cols) = from_clips(
-        clip_mix.reshape(slots, frames_all, clip_pixels, half_width),
-        11,
-        [JoinCores(cot_half), cut_and_send(text_cols, ("space",), pick_cols, cut_cols)],
+    clip_triple, temporal_mix, (in_quarter, out_quarter, text_cols) = temporal_chain(
+        temporal_triple.reshape(slots, frame_dev, pixels_dev, 3 * half_width),
+        clip_bias,
+        clip_ids,
+        (10, 11),
+        [
+            cut_and_send(feed_in, ("space",), pick_in, cut_in),
+            cut_and_send(feed_out, ("space",), pick_out, cut_out),
+            cut_and_send(text_cols, ("space",), pick_cols, cut_cols),
+        ],
     )
     temporal_mix = temporal_mix.reshape(token_rows, half_width)
 
     feed_gain = feed_norm[None]
-    stream_four, feed_rows = late_forward(temporal_mix, stream_three, out_last, feed_gain, 35)
-    feed_line, (feed_in, feed_out) = gather_tokens(
-        feed_rows, 12, [Share(in_quarter, ("tm",)), Share(out_quarter, ("tm",))]
+    stream_four, feed_line, (feed_in, feed_out, cot_line) = late_chain(
+        temporal_mix,
+        stream_three,
+        out_last,
+        feed_gain,
+        12,
+        [Share(in_quarter, ("tm",)), Share(out_quarter, ("tm",)), JoinCores(cot_half)],
     )
     feed_in = feed_in.transpose(1, 0, 2, 3).reshape(channels, feed_width)
     feed_out = feed_out.transpose(0, 2, 1, 3).reshape(feed_width, channels)
@@ -2298,25 +2661,34 @@
     upstream, mix_grad, temporal_out_grad, feed_norm_grad = late_backward(
         cot_rows, normed_grad, stream_four, feed_gain, temporal_mix, out_last
     )
-    clip_up, (feed_grads,) = to_clips(
-        mix_grad.reshape(slots, frame_dev, pixels_dev, half_width),
-        15,
-        [Exchange(feed_grads.reshape(lines, -1, 2 * feed_width), ("space",))],
-    )
-    clip_grads, score_total = temporal_backward(
+
+    def cut_feed(half):
+        cols = slice(half * feed_width, (half + 1) * feed_width)
+        return lambda whole: whole[:, cols].reshape(lines, -1, feed_width)
+
+    def pick_feed(half):
+        cols = pl.ds(half * feed_width, feed_width)
+        return lambda ref, place: ref.at[span(place, channels // owners), cols]
+
+    (
+        triple_grad,
+        score_total,
+        (feed_in_grad, feed_out_grad, first_grads, final_half),
+    ) = temporal_back_chain(
         clip_triple,
         clip_bias,
         clip_ids,
-        clip_pixels,
-        clip_up.reshape(slots, clip_rows, half_width),
+        mix_grad.reshape(slots, frame_dev, pixels_dev, half_width),
+        (15, 16),
+        [
+            ColumnJoin(feed_grads, pick_feed(0), cut_feed(0)),
+            ColumnJoin(feed_grads, pick_feed(1), cut_feed(1)),
+            by_frames(temporal_out_grad),
+            LineSum(final_half),
+        ],
     )
     score_total = jnp.einsum("hqc,ck->hqk", score_total, clip_frames, precision=highest)
     offset_bias_grad = jnp.einsum("hqk,qkr->rh", score_total, offset_table, precision=highest)
-    triple_grad, (first_grads, final_half) = from_clips(
-        clip_grads.reshape(slots, frames_all, clip_pixels, 3 * half_width),
-        16,
-        [by_frames(temporal_out_grad), LineSum(final_half)],
-    )
 
     (
         upstream,
@@ -2344,55 +2716,54 @@
         two_gains,
         36,
     )
-    pair_grad = (
-        pair_grad.reshape(slots, frames_axis, lines, text_local, 2 * half_width)
-        .transpose(1, 2, 0, 3, 4)
-        .reshape(frames_axis, lines * text_rows, 2 * half_width)
-    )
-
-    mix_line, (pair_grad, second_grads, final_rows) = to_lines(
+    pair_grad = pair_grad.reshape(frames_axis, lines * text_rows, 2 * half_width)
+
+    (
+        normed_grad,
+        spatial_qkv_grad,
+        (pair_grad, second_grads, final_rows, temporal_out_grad, third_grads),
+    ) = spatial_back_chain(
         mix_grad.reshape(images, pixels_dev, half_width),
-        False,
-        17,
-        [FrameSum(pair_grad), by_frames(temporal_query_grad), JoinCores(final_half)],
-    )
-    mixed = (stream_four + final_rows.astype(jnp.float32)).astype(jnp.bfloat16)
-    spatial_part, spatial_qkv_grad = spatial_backward(
-        spatial_line, spatial_qkv, spatial_triple, mix_line
-    )
-    normed_grad, (pair_grad, third_grads) = scatter_tokens(
-        spatial_part.reshape(lines * token_rows, channels),
-        18,
-        [
-            Exchange(pair_grad.reshape(lines, text_rows, 2 * half_width), ("space",)),
+        spatial_line,
+        spatial_qkv,
+        spatial_triple,
+        (17, 18),
+        [
+            FrameSum(pair_grad),
+            by_frames(temporal_query_grad),
+            JoinCores(final_half),
+            LineSum(first_grads, jnp.float32),
             by_frames(temporal_pair_grad),
         ],
     )
-    temporal_grads = lax.psum_scatter(
-        jnp.concatenate([first_grads, second_grads, third_grads], axis=1),
-        "space",
-        scatter_dimension=0,
-        tiled=True,
-    )
+    mixed = (stream_four + final_rows.astype(jnp.float32)).astype(jnp.bfloat16)
+    (
+        upstream,
+        branch_line,
+        spatial_norm_grad,
+        (fourth_grads, pair_grad, temporal_query_grad),
+    ) = first_back_chain(
+        stream_one,
+        spatial_gain,
+        normed_grad,
+        upstream,
+        owners,
+        images,
+        (19,),
+        [
+            by_frames(cross_query_grad),
+            Exchange(pair_grad.reshape(lines, text_rows, 2 * half_width), ("space",)),
+            LineSum(second_grads, jnp.float32),
+        ],
+    )
+    branch_line, branch_owned = branch_line[:images], branch_line[images:]
     pair_grad = jnp.sum(pair_grad.astype(jnp.float32), axis=0).astype(jnp.bfloat16)
-    upstream, branch_both, spatial_norm_grad = first_norm_backward(
-        stream_one, spatial_gain, normed_grad, upstream, owners, lines
-    )
-
-    branch_line, (fourth_grads, pair_line) = to_lines(
-        branch_both.reshape(-1, pixels_dev, channels),
-        False,
-        19,
-        [by_frames(cross_query_grad), Share(pair_grad, ("space",))],
-        join=True,
-    )
-    branch_line, branch_owned = branch_line[:images], branch_line[images:]
     second_conv_grad = conv_weight_grad(wide(second_wide), wide(branch_owned), "kc")
     second_part = conv_frames(wide(branch_line), second_conv, "OHWI", True).astype(jnp.bfloat16)
-    second_in_grad, (fifth_grads, pair_all) = sum_lines(
+    second_in_grad, (fifth_grads, pair_line) = sum_lines(
         second_part.reshape(images, H * W, half_width),
         20,
-        [by_frames(outs_grad), Share(pair_line, ("tm",))],
+        [by_frames(outs_grad), Share(pair_grad, ("space",))],
     )
     hidden_grad, scale_grad, shift_grad = group_backward(
         hidden, film_scale, film_shift, second_in_grad
@@ -2405,25 +2776,25 @@
     )
     text_part = text_part.astype(jnp.bfloat16).reshape(lines, text_rows, -1)
 
-    hidden_wide, (second_conv_grad, film_shares, text_part) = gather_lines(
+    hidden_wide, (second_conv_grad, film_shares, text_part, pair_all) = gather_lines(
         hidden_grad,
         21,
-        [FrameSum(second_conv_grad, True), Share(film_rows, ("tm",)), Exchange(text_part, ("space",))],
+        [FrameSum(second_conv_grad, True, kind=jnp.float32), Share(film_rows, ("tm",)), Exchange(text_part, ("space",)), Share(pair_line, ("tm",))],
     )
     film_rows = jnp.sum(film_shares, axis=0)
-    first_conv_some, first_conv_rest = (
-        conv_weight_grad(wide(first_owned), wide(hidden_wide), "ck", taps)
-        for taps in (range(5), range(5, 9))
-    )
+    first_conv_grad = conv_weight_grad(wide(first_owned), wide(hidden_wide), "ck")
     first_part = conv_frames(wide(hidden_wide), first_conv, "OHWI", True).astype(jnp.bfloat16)
-    cross_grads = jnp.concatenate([fourth_grads, fifth_grads], axis=1)
-    first_in_grad, (first_conv_some, spatial_qkv_grad, cross_grads, film_shares) = sum_cores(
+    (
+        first_in_grad,
+        (first_conv_some, spatial_qkv_grad, cross_query_grad, outs_grad, film_shares),
+    ) = sum_cores(
         first_part.reshape(images, H * W, -1),
         22,
         [
-            FrameSum(first_conv_some, True),
-            by_frames(spatial_qkv_grad),
-            Exchange(cross_grads.reshape(lines, -1, cross_grads.shape[1]), ("space",)),
+            FrameSum(first_conv_grad, True, 0, 5),
+            FrameSum(spatial_qkv_grad, True),
+            LineSum(fourth_grads, jnp.float32),
+            LineSum(fifth_grads, jnp.float32),
             Share(film_rows, ("space",)),
         ],
     )
@@ -2452,14 +2823,24 @@
         ],
         axis=1,
     )
-    video_rows_grad, (small, qkv_part, first_conv_rest) = from_lines(
+    owner_rows = channels // owners
+
+    def cut_qkv_rows(whole):
+        return whole.reshape(3, lines, owner_rows, -1).transpose(1, 0, 2, 3)
+
+    video_rows_grad, (small, qkv_part, first_conv_rest, temporal_pair_grad) = from_lines(
         video_line_grad,
         True,
         23,
         [
             SmallSum(small.reshape(frames_axis, lines, 1, -1)),
-            Exchange(spatial_qkv_grad.reshape(lines, -1, spatial_qkv_grad.shape[1]), ("space",)),
-            FrameSum(first_conv_rest, True),
+            ColumnJoin(
+                spatial_qkv_grad,
+                lambda ref, place: ref.at[:, span(place, owner_rows)],
+                cut_qkv_rows,
+            ),
+            FrameSum(first_conv_grad, True, 5, 4),
+            LineSum(third_grads, jnp.float32),
         ],
     )
     video_grad = upstream + video_rows_grad.reshape(token_rows, channels).astype(jnp.float32)
@@ -2490,11 +2871,10 @@
     gains = [small[i * gain_size : (i + 1) * gain_size] for i in range(6)]
     for i in range(2):
         gains[i] = gains[i] + small_twin[i * gain_size : (i + 1) * gain_size]
-    feed_grads, qkv_part = feed_grads.astype(jnp.float32), qkv_part.astype(jnp.float32)
-    owner_rows = feed_grads.shape[1]
-    temporal_grads = temporal_grads.astype(jnp.float32)
-    cross_grads = jnp.sum(cross_grads.astype(jnp.float32), axis=0)
     first_conv_grad = jnp.concatenate([first_conv_some, first_conv_rest])
+    temporal_triple_grad = jnp.stack(
+        [temporal_query_grad, *jnp.split(temporal_pair_grad, 2, axis=1)], axis=1
+    )
     return (
         mixed.reshape(video.shape),
         video_grad.reshape(video.shape),
@@ -2503,23 +2883,21 @@
         gains[1],
         first_conv_grad.astype(jnp.float32).transpose(1, 0, 2),
         film_weight_grad,
-        second_conv_grad.astype(jnp.float32).transpose(2, 0, 1),
+        second_conv_grad.transpose(2, 0, 1),
         gains[2],
-        qkv_part.reshape(lines, owner_rows, 3, -1)
-        .transpose(1, 2, 0, 3)
-        .reshape(owner_rows, 3, half_width),
-        cross_grads[:, 2 * half_width :].T,
+        qkv_part.astype(jnp.float32).transpose(1, 0, 2),
+        outs_grad[:, half_width:].T,
         gains[3],
-        cross_grads[:, :half_width],
+        cross_query_grad,
         cross_kv_grad.reshape(-1, 2, half_width),
-        cross_grads[:, half_width : 2 * half_width].T,
+        outs_grad[:, :half_width].T,
         gains[4],
-        temporal_grads[:, half_width:].reshape(-1, 3, half_width),
-        temporal_grads[:, :half_width].T,
+        temporal_triple_grad,
+        temporal_out_grad.T,
         small[6 * gain_size :].reshape(R // owners, head_local),
         gains[5],
-        feed_grads[:, :, :feed_width].transpose(1, 0, 2).reshape(owner_rows, -1),
-        feed_grads[:, :, feed_width:].transpose(0, 2, 1).reshape(-1, owner_rows),
+        feed_in_grad.astype(jnp.float32),
+        feed_out_grad.astype(jnp.float32).T,
     )
 
 

time: 699 us -> 679 us (0.971)
  Pallas kernels: 538 us -> 501 us
  local copies, waits for them, and re-layouts: 77.7 us -> 95.6 us
    pallas_call x9 -> x5, Pallas kernels: 50.4 us -> 21.9 us  [local(): pl.pallas_call(kernel, out_shape=results, grid=grid, in_specs=in_specs, o...]
    unnamed x267 -> x298, local copies, waits for them, and re-layouts: 53.8 us -> 76.6 us
    pallas_call x3 -> x1, Pallas kernels: 14.7 us -> 5.42 us  [chat(): pl.pallas_call(whole, out_shape=tuple(results), in_specs=specs, out_specs...]
    reshape x8 -> x0, local copies, waits for them, and re-layouts: 7.04 us -> none  [the longest x1 2.06 us: on_device(): text_pairs.reshape(owners, slots, text_local, 2 * half_width)]
    pallas_call x24 -> x19, Pallas kernels: 472 us -> 473 us  [talk(): pl.pallas_call(kernel, out_shape=result, in_specs=[ANY] * len(operands) i...]
  transfers between devices with their start and end apart: 5 -> 4, of which waited for: 0 -> 0; matrix products, arithmetic and copies ran while one was open for 8% -> 8% of each run, Pallas kernels for 20% -> 30%
where the time goes in v5:
time: 679 us; the launch traced here: 670 us
  Pallas kernels  501 us (74%)
  local copies, waits for them, and re-layouts  95.6 us (14%)
  matrix products  36.1 us (5%)
  other arithmetic  21.4 us (3%)
  between operations  15.9 us (2%)
    pallas_call x19, Pallas kernels, talk(): pl.pallas_call(kernel, out_shape=result, in_specs=[ANY] * len(operands) i...  473 us
    unnamed x298, local copies, waits for them, and re-layouts  76.6 us
    pallas_call x5, Pallas kernels, local(): pl.pallas_call(kernel, out_shape=results, grid=grid, in_specs=in_specs, o...  21.9 us
    conv_general_dilated x4, matrix products, conv_frames(): lax.conv_general_dilated(images, kernel, (1, 1), 'SAME', dimension_number...  17.2 us
  transfers between devices with their start and end apart: 4, of which 0 were waited for; matrix products, arithmetic and copies ran while one was open for 8% of the time, Pallas kernels for 30%

profile of v5, /device:TPU:2, one launch (start us, length us, event | category | flops | bytes accessed | tf_op | source)
XLA Modules:
  0.0 670.3 jit_solution(4513456087372629004)
XLA Ops:
  16.2 21.2 %shard_map.409 = (bf16[8,256,128]{2,1,0:T(8,128)(2,1)S(1)}, bf16[4,16,1024]{2,1,0:T(8,128)(2,1)S(1)}, bf16[4,3,64,128]{3,2,1,0:T(8,128)(2,1)S(1)}, f32[4,12,128]{2,1,0:T(8,128)S(1)}, bf16[128,1792]{1,0:T(8,128)(2,1)S(1)}) custom-call(bf16[8,64,1024]{2,1,0:T(8,128)(2,1)S(1)} %bitcast.474, bf16[16,4096]{1,0:T(8,128)(2,1)S(1)} %bitcast.509, ...), custom_call_target="tpu_custom_call" | custom-call | tf_op jit(solution)/shard_map/pallas_call | solution.py:83
  42.2 3.5 copy.165
  45.9 4.4 shard_map.410.refs_0_
  50.4 2.4 convolution_convert_fusion.5
  52.8 10.0 %shard_map.411 = (bf16[8,256,256]{2,1,0:T(8,128)(2,1)S(1)}, bf16[4,16,1024]{2,1,0:T(8,128)(2,1)S(1)}) custom-call(bf16[8,256,128]{2,1,0:T(8,128)(2,1)S(1)} %shard_map.410.refs_0_, bf16[4,16,1024]{2,1,0:T(8,128)(2,1)S(1)} %bitcast.513), custom_call_target="tpu_custom_call" | custom-call | tf_op jit(solution)/shard_map/pallas_call | solution.py:83
  63.8 4.2 convolution_convert_fusion.1
  70.2 34.6 %shard_map.412 = (f32[4,256,128]{2,1,0:T(8,128)S(1)}, bf16[4,16,1024]{2,1,0:T(8,128)(2,1)S(1)}, bf16[4,4,3,64,128]{4,3,2,1,0:T(8,128)(2,1)S(1)}) custom-call(bf16[4,256,512]{2,1,0:T(8,128)(2,1)S(1)} %bitcast.476, bf16[16,1024]{1,0:T(8,128)(2,1)S(1)} %reduce_sum.60.refs_1_, bf16[4,3,64,128]{3,2,1,0:T(8,128)(2,1)S(1)} %copy-done.92), custom_call_target="tpu_custom_call" | custom-call | tf_op jit(solution)/shard_map/pallas_call | solution.py:83
  105.9 2.2 shard_map.413.refs_0_
  109.1 1.5 copy-done.2
  112.6 25.8 %shard_map.414 = (bf16[4,256,512]{2,1,0:T(8,128)(2,1)S(1)}, bf16[4,4,16,1024]{3,2,1,0:T(8,128)(2,1)S(1)}, bf16[4,2,128,1024]{3,2,1,0:T(8,128)(2,1)S(1)}, bf16[256,1024]{1,0:T(8,128)(2,1)S(1)}) custom-call(bf16[4,256,128]{2,1,0:T(8,128)(2,1)S(1)} %shard_map.413.refs_0_, bf16[4,16,1024]{2,1,0:T(8,128)(2,1)S(1)} %copy-done.110, ...), custom_call_target="tpu_custom_call" | custom-call | tf_op jit(solution)/shard_map/pallas_call | solution.py:83
  138.4 1.4 copy-done.4
  145.2 1.8 copy.111
  147.2 1.3 pad_maximum_fusion.2.refs_4_.refs_2_
  151.1 5.5 convolution_convert_fusion.3
  156.8 1.6 shard_map.415
  158.5 21.6 %shard_map.416 = (bf16[4,64,1024]{2,1,0:T(8,128)(2,1)S(1)}, bf16[4,4,128,512]{3,2,1,0:T(8,128)(2,1)S(1)}) custom-call(bf16[4,256,128]{2,1,0:T(8,128)(2,1)S(1)} %convert_element_type.140.refs_0_, bf16[4,128,1792]{2,1,0:T(8,128)(2,1)S(1)} %bitcast.469), custom_call_target="tpu_custom_call" | custom-call | tf_op jit(solution)/shard_map/pallas_call | solution.py:83
  180.1 1.4 copy-done.5
  181.5 32.7 %shard_map.417 = (f32[256,1024]{1,0:T(8,128)S(1)}, bf16[1,1024,1024]{2,1,0:T(8,128)(2,1)S(1)}, bf16[4,256,384]{2,1,0:T(8,128)(2,1)S(1)}, bf16[4,64,512]{2,1,0:T(...) custom-call(bf16[256,1024]{1,0:T(8,128)(2,1)S(1)} %bitcast.508, ...), custom_call_target="tpu_custom_call" | custom-call | tf_op jit(solution)/shard_map/pallas_call | solution.py:83
  214.3 1.3 copy-done.6
  219.2 13.4 %shard_map.418 = (f32[256,1024]{1,0:T(8,128)}, bf16[256,1024]{1,0:T(8,128)(2,1)}, bf16[256,512]{1,0:T(8,128)(2,1)}, bf16[256,512]{1,0:T(8,128)(2,1)}, f32[256,10...) custom-call(bf16[256,512]{1,0:T(8,128)(2,1)} %bitcast.501, f32[256,1024]{1,0:T(8,128)} %copy-done.14, ...), custom_call_target="tpu_custom_call" | custom-call | tf_op jit(solution)/shard_map/pallas_call | solution.py:83
  237.1 25.3 %shard_map.419 = (bf16[2,8,16,1536]{3,2,1,0:T(8,128)(2,1)S(1)}, bf16[2,2,64,512]{3,2,1,0:T(8,128)(2,1)S(1)}, bf16[4,64,512]{2,1,0:T(8,128)(2,1)S(1)}, bf16[4,128...) custom-call(bf16[2,2,64,1536]{3,2,1,0:T(8,128)(2,1)S(1)} %bitcast.506, ...), custom_call_target="tpu_custom_call" | custom-call | tf_op jit(solution)/shard_map/pallas_call | solution.py:83
  272.6 26.4 %shard_map.420 = (f32[256,1024]{1,0:T(8,128)S(1)}, bf16[1,1024,1024]{2,1,0:T(8,128)(2,1)S(1)}, bf16[4,4,64,512]{3,2,1,0:T(8,128)(2,1)S(1)}, bf16[4,4,128,256]{3,2,1,0:T(8,128)(2,1)S(1)}, bf16[1024,1024]{1,0:T(8,128)(2,1)S(1)}) custom-call(bf16[256,512]{1,0:T(8,128)(2,1)S(1)} %bitcast.499, f32[1,1024]{1,0:T(1,128)S(1)} %bitcast.528, ...), custom_call_target="tpu_custom_call" | custom-call | tf_op jit(solution)/shard_map/pallas_call | solution.py:83
  300.2 8.5 %shard_map.421 = (bf16[4,256,1024]{2,1,0:T(8,128)(2,1)S(1)}, bf16[4,256,1024]{2,1,0:T(8,128)(2,1)S(1)}, bf16[1024,1024]{1,0:T(8,128)(2,1)S(1)}) custom-call(bf16[4,256,1024]{2,1,0:T(8,128)(2,1)S(1)} %bitcast.479, bf16[4,256,1024]{2,1,0:T(8,128)(2,1)S(1)} %bitcast.480, bf16[1024,512]{1,0:T(8,128)(2,1)S(1)} %bitcast.477, bf16[512,1024]{1,0:T(8,128)(2,1)S(1)} %bitcast.478), custom_call_target="tpu_custom_call" | custom-call | tf_op jit(solution)/shard_map/pallas_call | solution.py:1254
  308.8 25.8 %shard_map.422 = (bf16[256,1024]{1,0:T(8,128)(2,1)S(1)}, bf16[256,1024]{1,0:T(8,128)(2,1)S(1)}, bf16[1024,512]{1,0:T(8,128)(2,1)S(1)}) custom-call(bf16[4,256,1024]{2,1,0:T(8,128)(2,1)S(1)} %get-tuple-element.160.refs_0_, bf16[4,256,1024]{2,1,0:T(8,128)(2,1)S(1)} %bitcast.482, bf16[1024,1024]{1,0:T(8,128)(2,1)S(1)} %bitcast.481), custom_call_target="tpu_custom_call" | custom-call | tf_op jit(solution)/shard_map/pallas_call | solution.py:83
  336.4 5.4 shard_map.423
  344.1 35.0 %shard_map.424 = (bf16[2,2,64,1536]{3,2,1,0:T(8,128)(2,1)S(1)}, f32[8,8,128]{2,1,0:T(8,128)S(1)}, bf16[64,2048]{1,0:T(8,128)(2,1)S(1)}, bf16[64,2048]{1,0:T(8,12...) custom-call(bf16[2,2,64,512]{3,2,1,0:T(8,128)(2,1)S(1)} %bitcast.515, ...), custom_call_target="tpu_custom_call" | custom-call | tf_op jit(solution)/shard_map/pallas_call | solution.py:83
  382.7 19.3 %shard_map.425 = (f32[256,1024]{1,0:T(8,128)}, bf16[256,512]{1,0:T(8,128)(2,1)}, bf16[256,1024]{1,0:T(8,128)(2,1)}, bf16[1024,512]{1,0:T(8,128)(2,1)}, bf16[1024...) custom-call(bf16[256,1024]{1,0:T(8,128)(2,1)} %bitcast.492, ...), custom_call_target="tpu_custom_call" | custom-call | tf_op jit(solution)/shard_map/pallas_call | solution.py:83
  402.1 1.6 copy-done.23
  408.8 47.9 %shard_map.426 = (bf16[256,1024]{1,0:T(8,128)(2,1)S(1)}, bf16[3,1024,128]{2,1,0:T(8,128)(2,1)S(1)}, bf16[64,1024]{1,0:T(8,128)(2,1)S(1)}, bf16[256,512]{1,0:T(8,...) custom-call(bf16[4,64,512]{2,1,0:T(8,128)(2,1)S(1)} %bitcast.514, ...), custom_call_target="tpu_custom_call" | custom-call | tf_op jit(solution)/shard_map/pallas_call | solution.py:83
  459.5 30.6 %shard_map.427 = (f32[256,1024]{1,0:T(8,128)S(1)}, bf16[8,256,256]{2,1,0:T(8,128)(2,1)S(1)}, f32[1,1024]{1,0:T(1,128)S(1)}, bf16[256,512]{1,0:T(8,128)(2,1)S(1)}...) custom-call(f32[1,1024]{1,0:T(1,128)S(1)} %bitcast.530, bf16[256,1024]{1,0:T(8,128)(2,1)S(1)} %get-tuple-element.180.refs_1_, ...), custom_call_target="tpu_custom_call" | custom-call | tf_op jit(solution)/shard_map/pallas_call | solution.py:83
  495.9 1.3 convolution_bitcast_fusion.21
  499.9 2.1 fusion.120
  501.9 3.6 convolution_convert_fusion
  505.8 1.3 copy-done.18
  507.2 25.2 %shard_map.428 = (f32[4,256,128]{2,1,0:T(8,128)S(1)}, bf16[256,1024]{1,0:T(8,128)(2,1)S(1)}, bf16[4,16,1024]{2,1,0:T(8,128)(2,1)S(1)}) custom-call(bf16[4,256,512]{2,1,0:T(8,128)(2,1)S(1)} %bitcast.475, bf16[4,256,1024]{2,1,0:T(8,128)(2,1)S(1)} %bitcast.486, bf16[16,1024]{1,0:T(8,128)(2,1)S(1)} %reduce_sum.62.refs_2_), custom_call_target="tpu_custom_call" | custom-call | tf_op jit(solution)/shard_map/pallas_call | solution.py:83
  533.2 3.4 shard_map.429
  536.9 1.8 fusion.53
  543.3 27.9 %shard_map.430 = (bf16[4,256,512]{2,1,0:T(8,128)(2,1)S(1)}, f32[9,64,512]{2,1,0:T(8,128)S(1)}, f32[4,12,128]{2,1,0:T(8,128)S(1)}, bf16[4,16,1024]{2,1,0:T(8,128)(2,1)S(1)}, bf16[4,4,16,1024]{3,2,1,0:T(8,128)(2,1)S(1)}) custom-call(bf16[4,256,128]{2,1,0:T(8,128)(2,1)S(1)} %get-tuple-element.190.refs_0_, bf16[9,256,512]{2,1,0:T(8,128)(2,1)S(1)} %fusion.39.refs_1_, ...), custom_call_target="tpu_custom_call" | custom-call | tf_op jit(solution)/shard_map/pallas_call | solution.py:83
  571.9 3.9 convolution_convert_fusion.2
  583.1 22.9 %shard_map.431 = (f32[4,256,128]{2,1,0:T(8,128)S(1)}, bf16[5,64,512]{2,1,0:T(8,128)(2,1)S(1)}, bf16[3,256,128]{2,1,0:T(8,128)(2,1)S(1)}, f32[64,512]{1,0:T(8,128...) custom-call(bf16[4,256,256]{2,1,0:T(8,128)(2,1)S(1)} %bitcast.485, ...), custom_call_target="tpu_custom_call" | custom-call | tf_op jit(solution)/shard_map/pallas_call | solution.py:83
  606.7 3.3 shard_map.432
  614.6 25.9 %shard_map.433 = (bf16[4,64,1024]{2,1,0:T(8,128)(2,1)S(1)}, f32[1,448]{1,0:T(1,128)S(1)}, bf16[3,64,512]{2,1,0:T(8,128)(2,1)S(1)}, bf16[4,64,512]{2,1,0:T(8,128)(2,1)S(1)}, f32[64,1024]{1,0:T(8,128)S(1)}) custom-call(bf16[4,256,128]{2,1,0:T(8,128)(2,1)S(1)} %copy-done.80, f32[4,4,1,448]{3,2,1,0:T(1,128)S(1)} %concatenate.46.refs_1_, ...), custom_call_target="tpu_custom_call" | custom-call | tf_op jit(solution)/shard_map/pallas_call | solution.py:83
  645.4 1.7 slice_bitcast_fusion.4
  647.1 1.7 convert_bitcast_fusion.2
  648.8 2.2 convert_add_fusion
  654.4 1.8 copy.137
  656.8 1.9 copy.136
  659.3 1.5 add_bitcast_fusion
  (414 shorter events, 103.2 us)
Async XLA Ops:
  7.2 143.9 %copy-start = (bf16[512,9,256]{2,0,1:T(8,128)(2,1)S(1)}, bf16[512,9,256]{2,0,1:T(8,128)(2,1)}, u32[]{:S(2)}) copy-start(bf16[512,9,256]{2,0,1:T(8,128)(2,1)} %param.35) | copy-start | bytes 7077892
  7.2 101.9 %all-gather.6.cloned.1.call-start = ((), (), s32[]{:S(2)}) async-start(), calls=%async_computation.1 | async-start | bytes 2293760 | tf_op jit(solution)/shard_map/all_gather | solution.py:2529
  13.4 27.6 %copy-start.134 = (f32[1024]{0:T(1024)S(1)}, f32[1024]{0:T(1024)}, u32[]{:S(2)}) copy-start(f32[1024]{0:T(1024)} %param.31) | copy-start | bytes 12292
  13.4 27.8 %copy-start.135 = (f32[1024]{0:T(1024)S(1)}, f32[1024]{0:T(1024)}, u32[]{:S(2)}) copy-start(f32[1024]{0:T(1024)} %param.32) | copy-start | bytes 12292
  41.0 225.1 %all-gather.4.cloned.1.call-start = ((), (), s32[]{:S(2)}) async-start(), calls=%async_computation | async-start | bytes 1310720 | tf_op jit(solution)/shard_map/all_gather | solution.py:2573
  42.2 8.2 %copy-start.98 = (bf16[4,16,1024]{2,1,0:T(8,128)(2,1)S(1)}, bf16[4,16,1024]{2,1,0:T(8,128)(2,1)}, u32[]{:S(2)}) copy-start(bf16[4,16,1024]{2,1,0:T(8,128)(2,1)} %copy-done.97) | copy-start | bytes 393220
  50.4 13.4 %copy-start.143 = (bf16[256,9,512]{2,0,1:T(8,128)(2,1)S(1)}, bf16[256,9,512]{2,0,1:T(8,128)(2,1)}, u32[]{:S(2)}) copy-start(bf16[256,9,512]{2,0,1:T(8,128)(2,1)} %param.33) | copy-start | bytes 7077892
  68.1 37.6 %copy-start.136 = (s32[2,8]{1,0:T(2,128)S(1)}, s32[2,8]{1,0:T(2,128)}, u32[]{:S(2)}) copy-start(s32[2,8]{1,0:T(2,128)} %param.28) | copy-start | bytes 196
  105.6 36.7 %copy-start.138 = (f32[128,8]{0,1:T(8,128)S(1)}, f32[128,8]{0,1:T(8,128)}, u32[]{:S(2)}) copy-start(f32[128,8]{0,1:T(8,128)} %param.46) | copy-start | bytes 12292
  105.6 38.9 %copy-start.30 = (bf16[8,256,128]{2,1,0:T(8,128)(2,1)S(1)}, bf16[8,256,128]{2,1,0:T(8,128)(2,1)}, u32[]{:S(2)}) copy-start(bf16[8,256,128]{2,1,0:T(8,128)(2,1)} %copy-done.28) | copy-start | bytes 1572868
  105.7 38.0 %copy-start.139 = (s32[2,2]{1,0:T(2,128)}, s32[2,2]{1,0:T(2,128)S(1)}, u32[]{:S(2)}) copy-start(s32[2,2]{1,0:T(2,128)S(1)} %constant_dynamic-slice_fusion.1) | copy-start | bytes 52
  109.0 33.3 %copy-start.130 = (s32[8,8]{0,1:T(8,128)}, s32[8,8]{0,1:T(8,128)S(1)}, u32[]{:S(2)}) copy-start(s32[8,8]{0,1:T(8,128)S(1)} %clamp_add_fusion) | copy-start | bytes 772
  151.1 81.5 %copy-start.7 = (f32[8,128,128]{2,1,0:T(8,128)}, f32[8,128,128]{2,1,0:T(8,128)S(1)}, u32[]{:S(2)}) copy-start(f32[8,128,128]{2,1,0:T(8,128)S(1)} %convolution_bitcast_fusion.19.refs_1_.refs_2_) | copy-start | bytes 1572868
  156.7 24.9 %copy-start.17 = (bf16[2,2,4,16,1024]{4,3,2,1,0:T(8,128)(2,1)S(1)}, bf16[2,2,4,16,1024]{4,3,2,1,0:T(8,128)(2,1)}, u32[]{:S(2)}) copy-start(bf16[2,2,4,16,1024]{4,3,2,1,0:T(8,128)(2,1)} %param.25) | copy-start | bytes 1572868
  156.7 24.8 %copy-start.66 = (bf16[2,8,4096]{2,1,0:T(8,128)(2,1)S(1)}, bf16[2,8,4096]{2,1,0:T(8,128)(2,1)}, u32[]{:S(2)}) copy-start(bf16[2,8,4096]{2,1,0:T(8,128)(2,1)} %param.27) | copy-start | bytes 393220
  156.7 24.8 %copy-start.115 = (f32[1024]{0:T(1024)S(1)}, f32[1024]{0:T(1024)}, u32[]{:S(2)}) copy-start(f32[1024]{0:T(1024)} %param.36) | copy-start | bytes 12292
  219.2 13.4 %copy-start.21 = (bf16[1,1024,1024]{2,1,0:T(8,128)(2,1)}, bf16[1,1024,1024]{2,1,0:T(8,128)(2,1)S(1)}, u32[]{:S(2)}) copy-start(bf16[1,1024,1024]{2,1,0:T(8,128)(2,1)S(1)} %get-tuple-element.172.refs_1_) | copy-start | bytes 6291460
  219.2 13.4 %copy-start.99 = (bf16[4,16,1024]{2,1,0:T(8,128)(2,1)}, bf16[4,16,1024]{2,1,0:T(8,128)(2,1)S(1)}, u32[]{:S(2)}) copy-start(bf16[4,16,1024]{2,1,0:T(8,128)(2,1)S(1)} %get-tuple-element.143.refs_6_) | copy-start | bytes 393220
  219.2 13.5 %copy-start.116 = (s32[2,1,128]{2,1,0:T(1,128)S(1)}, s32[2,1,128]{2,1,0:T(1,128)}, u32[]{:S(2)}) copy-start(s32[2,1,128]{2,1,0:T(1,128)} %broadcast_in_dim_reshape.17.refs_3_.refs_4_) | copy-start | bytes 3076
  232.6 33.5 %copy-start.114 = (f32[1024]{0:T(1024)S(1)}, f32[1024]{0:T(1024)}, u32[]{:S(2)}) copy-start(f32[1024]{0:T(1024)} %param.47) | copy-start | bytes 12292
  382.7 19.3 %copy-start.111 = (f32[8,8,128]{2,1,0:T(8,128)}, f32[8,8,128]{2,1,0:T(8,128)S(1)}, u32[]{:S(2)}) copy-start(f32[8,8,128]{2,1,0:T(8,128)S(1)} %get-tuple-element.206) | copy-start | bytes 98308
  382.7 19.3 %copy-start.22 = (bf16[1,1024,1024]{2,1,0:T(8,128)(2,1)S(1)}, bf16[1,1024,1024]{2,1,0:T(8,128)(2,1)}, u32[]{:S(2)}) copy-start(bf16[1,1024,1024]{2,1,0:T(8,128)(2,1)} %copy-done.21) | copy-start | bytes 6291460
  382.7 19.3 %copy-start.58 = (bf16[4,256,384]{2,1,0:T(8,128)(2,1)S(1)}, bf16[4,256,384]{2,1,0:T(8,128)(2,1)}, u32[]{:S(2)}) copy-start(bf16[4,256,384]{2,1,0:T(8,128)(2,1)} %copy-done.57) | copy-start | bytes 2359300
  408.8 48.8 %copy-start.13 = (f32[256,1024]{1,0:T(8,128)S(1)}, f32[256,1024]{1,0:T(8,128)}, u32[]{:S(2)}) copy-start(f32[256,1024]{1,0:T(8,128)} %copy-done.12) | copy-start | bytes 3145732
  408.8 49.8 %copy-start.33 = (bf16[1024,512]{1,0:T(8,128)(2,1)S(1)}, bf16[1024,512]{1,0:T(8,128)(2,1)}, u32[]{:S(2)}) copy-start(bf16[1024,512]{1,0:T(8,128)(2,1)} %get-tuple-element.182) | copy-start | bytes 3145732
  457.5 32.6 %copy-start.59 = (bf16[256,1024]{1,0:T(8,128)(2,1)}, bf16[256,1024]{1,0:T(8,128)(2,1)S(1)}, u32[]{:S(2)}) copy-start(bf16[256,1024]{1,0:T(8,128)(2,1)S(1)} %get-tuple-element.208.refs_4_) | copy-start | bytes 1572868
  457.5 32.6 %copy-start.103 = (f32[64,512]{1,0:T(8,128)}, f32[64,512]{1,0:T(8,128)S(1)}, u32[]{:S(2)}) copy-start(f32[64,512]{1,0:T(8,128)S(1)} %get-tuple-element.223) | copy-start | bytes 393220
  458.5 36.1 %copy-start.137 = (f32[1,1024]{1,0:T(1,128)S(1)}, f32[1,1024]{1,0:T(1,128)}, u32[]{:S(2)}) copy-start(f32[1,1024]{1,0:T(1,128)} %get-tuple-element.205) | copy-start | bytes 12292
  458.5 37.0 %copy-start.131 = (f32[2,1024]{1,0:T(2,128)S(1)}, f32[2,1024]{1,0:T(2,128)}, u32[]{:S(2)}) copy-start(f32[2,1024]{1,0:T(2,128)} %get-tuple-element.204) | copy-start | bytes 24580
  458.5 37.1 %copy-start.112 = (f32[8,8,128]{2,1,0:T(8,128)S(1)}, f32[8,8,128]{2,1,0:T(8,128)}, u32[]{:S(2)}) copy-start(f32[8,8,128]{2,1,0:T(8,128)} %copy-done.111) | copy-start | bytes 98308
  458.5 37.1 %copy-start.133 = (s32[128]{0:T(128)S(1)}, s32[128]{0:T(128)}, u32[]{:S(2)}) copy-start(s32[128]{0:T(128)} %copy-done.132) | copy-start | bytes 1540
  459.5 38.7 %copy-start.74 = (bf16[64,2048]{1,0:T(8,128)(2,1)S(1)}, bf16[64,2048]{1,0:T(8,128)(2,1)}, u32[]{:S(2)}) copy-start(bf16[64,2048]{1,0:T(8,128)(2,1)} %copy-done.73) | copy-start | bytes 786436
  459.5 39.5 %copy-start.72 = (bf16[64,2048]{1,0:T(8,128)(2,1)S(1)}, bf16[64,2048]{1,0:T(8,128)(2,1)}, u32[]{:S(2)}) copy-start(bf16[64,2048]{1,0:T(8,128)(2,1)} %copy-done.71) | copy-start | bytes 786436
  505.6 26.9 %copy-start.122 = (bf16[128,8,2,512]{3,1,2,0:T(8,128)(2,1)S(1)}, bf16[128,8,2,512]{3,1,2,0:T(8,128)(2,1)}, u32[]{:S(2)}) copy-start(bf16[128,8,2,512]{3,1,2,0:T(8,128)(2,1)} %copy.165) | copy-start | bytes 6291460
  507.2 26.0 %copy-start.20 = (f32[4,256,128]{2,1,0:T(8,128)S(1)}, f32[4,256,128]{2,1,0:T(8,128)}, u32[]{:S(2)}) copy-start(f32[4,256,128]{2,1,0:T(8,128)} %copy-done.19) | copy-start | bytes 1572868
  543.3 28.6 %copy-start.144 = (bf16[256,9,512]{2,0,1:T(8,128)(2,1)S(1)}, bf16[256,9,512]{2,0,1:T(8,128)(2,1)}, u32[]{:S(2)}) copy-start(bf16[256,9,512]{2,0,1:T(8,128)(2,1)} %param.33) | copy-start | bytes 7077892
  571.9 87.5 %collective-permute-start = (bf16[16,4096]{1,0:T(8,128)(2,1)}, bf16[16,4096]{1,0:T(8,128)(2,1)}, u32[]{:S(2)}, u32[]{:S(2)}) collective-permute-start(bf16[16,4096]{1,0:T(8,128)(2,1)} %bitcast.195), channel_id=1, source_target_pairs={{0,1},{1,0},{2,3},{3,2},{4,5},{5,4},{6,7},{7,6},{8,9},{9,8},{10,11... | collective-permute-start | bytes 393224 | tf_op jit(solution)/shard_map/ppermute | solution.py:27
  580.9 25.8 %copy-start.142 = (f32[128]{0:T(128)S(1)}, f32[128]{0:T(128)}, u32[]{:S(2)}) copy-start(f32[128]{0:T(128)} %dynamic_slice.50) | copy-start | bytes 1540
  580.9 25.8 %copy-start.141 = (f32[128]{0:T(128)S(1)}, f32[128]{0:T(128)}, u32[]{:S(2)}) copy-start(f32[128]{0:T(128)} %dynamic_slice.48) | copy-start | bytes 1540
  614.6 34.2 %copy-start.37 = (f32[256,1024]{1,0:T(8,128)S(1)}, f32[256,1024]{1,0:T(8,128)}, u32[]{:S(2)}) copy-start(f32[256,1024]{1,0:T(8,128)} %copy-done.36) | copy-start | bytes 3145732
  643.4 7.6 %copy-start.127 = (bf16[2,3,512]{2,1,0:T(4,128)(2,1)S(1)}, bf16[2,3,512]{2,1,0:T(4,128)(2,1)}, u32[]{:S(2)}) copy-start(bf16[2,3,512]{2,1,0:T(4,128)(2,1)} %copy-done.126) | copy-start | bytes 18436
  643.4 7.6 %copy-start.129 = (bf16[2,3,512]{2,1,0:T(4,128)(2,1)S(1)}, bf16[2,3,512]{2,1,0:T(4,128)(2,1)}, u32[]{:S(2)}) copy-start(bf16[2,3,512]{2,1,0:T(4,128)(2,1)} %copy-done.128) | copy-start | bytes 18436
  643.4 8.8 %copy-start.70 = (bf16[5,64,512]{2,1,0:T(8,128)(2,1)S(1)}, bf16[5,64,512]{2,1,0:T(8,128)(2,1)}, u32[]{:S(2)}) copy-start(bf16[5,64,512]{2,1,0:T(8,128)(2,1)} %copy-done.69) | copy-start | bytes 983044
  643.4 8.8 %copy-start.82 = (bf16[4,64,512]{2,1,0:T(8,128)(2,1)S(1)}, bf16[4,64,512]{2,1,0:T(8,128)(2,1)}, u32[]{:S(2)}) copy-start(bf16[4,64,512]{2,1,0:T(8,128)(2,1)} %copy-done.81) | copy-start | bytes 786436
  644.0 14.7 %collective-permute-start.1 = (f32[448]{0:T(512)S(1)}, f32[448]{0:T(512)S(1)}, u32[]{:S(2)}, u32[]{:S(2)}) collective-permute-start(f32[448]{0:T(512)S(1)} %bitcast.533), channel_id=1, source_target_pairs={{0,1},{1,0},{2,3},{3,2},{4,5},{5,4},{6,7},{7,6},{8,9},{9,8},{10,11... | collective-permute-start | bytes 5384 | tf_op jit(solution)/shard_map/ppermute | solution.py:2869
  654.4 6.5 copy-start.27
  654.4 8.8 %copy-start.1 = (bf16[512,9,256]{2,0,1:T(8,128)(2,1)S(1)}, bf16[512,9,256]{2,0,1:T(8,128)(2,1)}, u32[]{:S(2)}) copy-start(bf16[512,9,256]{2,0,1:T(8,128)(2,1)} %param.35) | copy-start | bytes 7077892
  656.8 5.7 copy-start.104
  (101 other events, 185.1 us)
Sparse Core Ops, SparseCore 0:
  41.1 53.1 all-gather.5
  142.4 32.7 all-gather.3

commit v6 on v5

--- a/solution.py
+++ b/solution.py
@@ -593,7 +593,9 @@
     return [rider.plain() for rider in riders]
 
 
-def talk_many(kernel, peers, results, operands, scratch, number, riders, specs, out_specs):
+def talk_many(
+    kernel, peers, results, operands, scratch, number, riders, specs, out_specs, grant=32
+):
     inputs, outputs, own_scratch, count = len(operands), len(results), len(scratch), len(riders)
 
     def whole(*refs):
@@ -629,16 +631,19 @@
         number,
         list(specs) + [rider.source_spec for rider in riders],
         tuple(out_specs) + tuple(rider.result_spec for rider in riders),
+        grant,
     )
     return list(done[:outputs]), list(done[outputs:])
 
 
-def talk_with(kernel, peers, result, operands, scratch, number, riders, specs=None, out_spec=ANY):
+def talk_with(
+    kernel, peers, result, operands, scratch, number, riders, specs=None, out_spec=ANY, grant=32
+):
     if number is None:
         return kernel, peers, result, scratch
     specs = [ANY] * len(operands) if specs is None else specs
     done, others_done = talk_many(
-        kernel, peers, [result], operands, scratch, number, riders, specs, [out_spec]
+        kernel, peers, [result], operands, scratch, number, riders, specs, [out_spec], grant
     )
     return done[0], others_done
 
@@ -824,7 +829,7 @@
     result = jax.ShapeDtypeStruct((images, lines * pixels, held), source.dtype)
     scratch = [pltpu.VMEM((lines - 1, images, pixels, width), source.dtype)]
     scratch = scratch + dma_sems(lines - 1, lines - 1, lines - 1, lines - 1, 1)
-    return talk_with(kernel, peers, result, [source], scratch, number, riders, [VMEM])
+    return talk_with(kernel, peers, result, [source], scratch, number, riders, [VMEM], ANY, 58)
 
 
 def from_lines(source, per_core, number, riders=()):
@@ -1596,6 +1601,7 @@
         riders,
         [VMEM] * 4,
         [VMEM, VMEM],
+        58,
     )
     return clip, mix, done
 
@@ -1617,6 +1623,7 @@
         hook, up_ref, clip_ref, bias_ref, ids_ref, turned_ref, out_ref, score_ref, line_ref, grad_ref, *scratch
     ):
         first[0](later, up_ref, line_ref, *scratch[: len(first[3])])
+        hook()
         frame = lax.broadcasted_iota(jnp.int32, (all_frames, rows), 0)
         row = lax.broadcasted_iota(jnp.int32, (all_frames, rows), 1)
         gather = low((row // few == frame).astype(jnp.float32))
@@ -1650,6 +1657,7 @@
         riders,
         [VMEM] * 5,
         [VMEM, VMEM],
+        58,
     )
     return grads, score, done
 
@@ -1687,7 +1695,8 @@
         one_ref[...] = one
         written = keep(one_ref, stream_ref, sem.at[1])
         normed_ref[0] = low(norm_forward(one, gain_ref[...]))
-        first[0](hook, normed_ref, line_ref, *scratch[: len(first[3])])
+        first[0](later, normed_ref, line_ref, *scratch[: len(first[3])])
+        hook()
         for image in range(images):
             x = line_rows(line_ref, image, lines, images, pixels)
             triple_ref[image] = low(dot(x, w_ref[...]))
@@ -1724,6 +1733,7 @@
         riders,
         [VMEM, VMEM, VMEM, ANY],
         [ANY, VMEM, VMEM, VMEM],
+        58,
     )
     return stream, line, triple, mix, done
 
@@ -1825,6 +1835,7 @@
         riders,
         [VMEM, VMEM, ANY, ANY],
         [ANY, ANY, VMEM],
+        58,
     )
     return grad, line, gain_grad, done
 
@@ -1871,8 +1882,8 @@
                 total = one if total is None else total + one
             for j in range(3):
                 dw_ref[j] = low(total[:, j * width : (j + 1) * width])
-            hook()
-
+
+        hook()
         second[0](weights, part_ref, out_ref, *scratch[len(first[3]) :])
 
     (normed, grads), done = talk_many(
@@ -1891,6 +1902,7 @@
         riders,
         [VMEM] * 4,
         [VMEM, VMEM],
+        58,
     )
     return normed, grads, done
 

time: 679 us -> 655 us (0.965)
  local copies, waits for them, and re-layouts: 95.6 us -> 66.6 us
  Pallas kernels: 501 us -> 508 us
    unnamed x298 -> x182, local copies, waits for them, and re-layouts: 76.6 us -> 42.7 us
    pallas_call x19, Pallas kernels: 473 us -> 481 us  [talk(): pl.pallas_call(kernel, out_shape=result, in_specs=[ANY] * len(operands) i...]
  transfers between devices with their start and end apart: 4 -> 4, of which waited for: 0 -> 0; matrix products, arithmetic and copies ran while one was open for 8% -> 8% of each run, Pallas kernels for 30% -> 31%
where the time goes in v6:
time: 655 us; the launch traced here: 646 us
  Pallas kernels  508 us (78%)
  local copies, waits for them, and re-layouts  66.6 us (10%)
  matrix products  34 us (5%)
  other arithmetic  21.1 us (3%)
  between operations  15.6 us (2%)
    pallas_call x19, Pallas kernels, talk(): pl.pallas_call(kernel, out_shape=result, in_specs=[ANY] * len(operands) i...  481 us
    unnamed x182, local copies, waits for them, and re-layouts  42.7 us
    pallas_call x5, Pallas kernels, local(): pl.pallas_call(kernel, out_shape=results, grid=grid, in_specs=in_specs, o...  21.9 us
    conv_general_dilated x4, matrix products, conv_frames(): lax.conv_general_dilated(images, kernel, (1, 1), 'SAME', dimension_number...  15.6 us
  transfers between devices with their start and end apart: 4, of which 0 were waited for; matrix products, arithmetic and copies ran while one was open for 8% of the time, Pallas kernels for 31%

profile of v6, /device:TPU:2, one launch (start us, length us, event | category | flops | bytes accessed | tf_op | source)
XLA Modules:
  0.0 646.2 jit_solution(276240223087587652)
XLA Ops:
  8.3 1.2 fusion.58
  14.3 22.9 %shard_map.409 = (bf16[8,256,128]{2,1,0:T(8,128)(2,1)}, bf16[4,16,1024]{2,1,0:T(8,128)(2,1)}, bf16[4,3,64,128]{3,2,1,0:T(8,128)(2,1)}, f32[4,12,128]{2,1,0:T(8,128)}, bf16[128,1792]{1,0:T(8,128)(2,1)}) custom-call(bf16[8,64,1024]{2,1,0:T(8,128)(2,1)} %bitcast.472, bf16[16,4096]{1,0:T(8,128)(2,1)} %bitcast.550, bf16[3,256,512]{2,1,0:T(8,128)(2,1)} %bitcast.547, ...), custom_call_target="tpu_custom_call" | custom-call | tf_op jit(solution)/shard_map/pallas_call | solution.py:83
  38.4 3.5 copy.165
  42.2 4.4 shard_map.410.refs_0_
  46.7 2.4 convolution_convert_fusion.5
  49.0 9.9 %shard_map.411 = (bf16[8,256,256]{2,1,0:T(8,128)(2,1)S(1)}, bf16[4,16,1024]{2,1,0:T(8,128)(2,1)S(1)}) custom-call(bf16[8,256,128]{2,1,0:T(8,128)(2,1)S(1)} %shard_map.410.refs_0_, bf16[4,16,1024]{2,1,0:T(8,128)(2,1)S(1)} %bitcast.499), custom_call_target="tpu_custom_call" | custom-call | tf_op jit(solution)/shard_map/pallas_call | solution.py:83
  60.0 4.2 convolution_convert_fusion.1
  66.4 34.6 %shard_map.412 = (f32[4,256,128]{2,1,0:T(8,128)S(1)}, bf16[4,16,1024]{2,1,0:T(8,128)(2,1)S(1)}, bf16[4,4,3,64,128]{4,3,2,1,0:T(8,128)(2,1)S(1)}) custom-call(bf16[4,256,512]{2,1,0:T(8,128)(2,1)S(1)} %bitcast.474, bf16[16,1024]{1,0:T(8,128)(2,1)S(1)} %reduce_sum.60.refs_1_, bf16[4,3,64,128]{3,2,1,0:T(8,128)(2,1)S(1)} %copy-done.44), custom_call_target="tpu_custom_call" | custom-call | tf_op jit(solution)/shard_map/pallas_call | solution.py:83
  102.2 2.2 shard_map.413.refs_0_
  105.4 1.5 copy-done.2
  108.8 25.7 %shard_map.414 = (bf16[4,256,512]{2,1,0:T(8,128)(2,1)S(1)}, bf16[4,4,16,1024]{3,2,1,0:T(8,128)(2,1)S(1)}, bf16[4,2,128,1024]{3,2,1,0:T(8,128)(2,1)S(1)}, bf16[256,1024]{1,0:T(8,128)(2,1)S(1)}) custom-call(bf16[4,256,128]{2,1,0:T(8,128)(2,1)S(1)} %shard_map.413.refs_0_, bf16[4,16,1024]{2,1,0:T(8,128)(2,1)S(1)} %copy-done.52, ...), custom_call_target="tpu_custom_call" | custom-call | tf_op jit(solution)/shard_map/pallas_call | solution.py:83
  134.5 1.3 copy-done.4
  141.9 1.9 copy.111
  147.5 3.9 convolution_convert_fusion.3
  151.5 1.6 shard_map.415
  153.2 21.6 %shard_map.416 = (bf16[4,64,1024]{2,1,0:T(8,128)(2,1)S(1)}, bf16[4,4,128,512]{3,2,1,0:T(8,128)(2,1)S(1)}) custom-call(bf16[4,256,128]{2,1,0:T(8,128)(2,1)S(1)} %convert_element_type.140.refs_0_, bf16[4,128,1792]{2,1,0:T(8,128)(2,1)S(1)} %bitcast.471), custom_call_target="tpu_custom_call" | custom-call | tf_op jit(solution)/shard_map/pallas_call | solution.py:83
  174.9 1.3 copy-done.5
  177.0 37.0 %shard_map.417 = (f32[256,1024]{1,0:T(8,128)}, bf16[1,1024,1024]{2,1,0:T(8,128)(2,1)}, bf16[4,256,384]{2,1,0:T(8,128)(2,1)}, bf16[4,64,512]{2,1,0:T(8,128)(2,1)}...) custom-call(bf16[256,1024]{1,0:T(8,128)(2,1)} %bitcast.496, ...), custom_call_target="tpu_custom_call" | custom-call | tf_op jit(solution)/shard_map/pallas_call | solution.py:83
  213.9 12.7 %shard_map.418 = (f32[256,1024]{1,0:T(8,128)}, bf16[256,1024]{1,0:T(8,128)(2,1)}, bf16[256,512]{1,0:T(8,128)(2,1)}, bf16[256,512]{1,0:T(8,128)(2,1)}, f32[256,10...) custom-call(bf16[256,512]{1,0:T(8,128)(2,1)} %bitcast.543, ...), custom_call_target="tpu_custom_call" | custom-call | tf_op jit(solution)/shard_map/pallas_call | solution.py:83
  226.7 25.2 %shard_map.419 = (bf16[2,8,16,1536]{3,2,1,0:T(8,128)(2,1)}, bf16[2,2,64,512]{3,2,1,0:T(8,128)(2,1)}, bf16[4,64,512]{2,1,0:T(8,128)(2,1)}, bf16[4,128,256]{2,1,0:T(8,128)(2,1)}, bf16[4,4,16,256]{3,2,1,0:T(8,128)(2,1)}) custom-call(bf16[2,2,64,1536]{3,2,1,0:T(8,128)(2,1)} %bitcast.548, f32[8,128,128]{2,1,0:T(8,128)} %convolution_bitcast_fusion.19.refs_1_.refs_2_, ...), custom_call_target="tpu_custom_call" | custom-call | tf_op jit(solution)/shard_map/pallas_call | solution.py:83
  251.9 1.6 copy.134
  258.7 27.4 %shard_map.420 = (f32[256,1024]{1,0:T(8,128)S(1)}, bf16[1,1024,1024]{2,1,0:T(8,128)(2,1)S(1)}, bf16[4,4,64,512]{3,2,1,0:T(8,128)(2,1)S(1)}, bf16[4,4,128,256]{3,2,1,0:T(8,128)(2,1)S(1)}, bf16[1024,1024]{1,0:T(8,128)(2,1)S(1)}) custom-call(bf16[256,512]{1,0:T(8,128)(2,1)S(1)} %bitcast.494, f32[1,1024]{1,0:T(1,128)S(1)} %bitcast.506, ...), custom_call_target="tpu_custom_call" | custom-call | tf_op jit(solution)/shard_map/pallas_call | solution.py:83
  287.3 8.5 %shard_map.421 = (bf16[4,256,1024]{2,1,0:T(8,128)(2,1)S(1)}, bf16[4,256,1024]{2,1,0:T(8,128)(2,1)S(1)}, bf16[1024,1024]{1,0:T(8,128)(2,1)S(1)}) custom-call(bf16[4,256,1024]{2,1,0:T(8,128)(2,1)S(1)} %bitcast.477, bf16[4,256,1024]{2,1,0:T(8,128)(2,1)S(1)} %bitcast.478, bf16[1024,512]{1,0:T(8,128)(2,1)S(1)} %bitcast.475, bf16[512,1024]{1,0:T(8,128)(2,1)S(1)} %bitcast.476), custom_call_target="tpu_custom_call" | custom-call | tf_op jit(solution)/shard_map/pallas_call | solution.py:1259
  295.9 25.0 %shard_map.422 = (bf16[256,1024]{1,0:T(8,128)(2,1)S(1)}, bf16[256,1024]{1,0:T(8,128)(2,1)S(1)}, bf16[1024,512]{1,0:T(8,128)(2,1)S(1)}) custom-call(bf16[4,256,1024]{2,1,0:T(8,128)(2,1)S(1)} %get-tuple-element.160.refs_0_, bf16[4,256,1024]{2,1,0:T(8,128)(2,1)S(1)} %bitcast.480, bf16[1024,1024]{1,0:T(8,128)(2,1)S(1)} %bitcast.479), custom_call_target="tpu_custom_call" | custom-call | tf_op jit(solution)/shard_map/pallas_call | solution.py:83
  323.5 5.3 shard_map.423
  328.8 38.1 %shard_map.424 = (bf16[2,2,64,1536]{3,2,1,0:T(8,128)(2,1)}, f32[8,8,128]{2,1,0:T(8,128)}, bf16[64,2048]{1,0:T(8,128)(2,1)}, bf16[64,2048]{1,0:T(8,128)(2,1)}, bf...) custom-call(bf16[2,2,64,512]{3,2,1,0:T(8,128)(2,1)} %bitcast.573, bf16[2,8,16,1536]{3,2,1,0:T(8,128)(2,1)} %get-tuple-element.165.refs_1_, ...), custom_call_target="tpu_custom_call" | custom-call | tf_op jit(solution)/shard_map/pallas_call | solution.py:83
  366.9 19.2 %shard_map.425 = (f32[256,1024]{1,0:T(8,128)}, bf16[256,512]{1,0:T(8,128)(2,1)}, bf16[256,1024]{1,0:T(8,128)(2,1)}, bf16[1024,512]{1,0:T(8,128)(2,1)}, bf16[1024...) custom-call(bf16[256,1024]{1,0:T(8,128)(2,1)} %bitcast.489, ...), custom_call_target="tpu_custom_call" | custom-call | tf_op jit(solution)/shard_map/pallas_call | solution.py:83
  386.1 51.3 %shard_map.426 = (bf16[256,1024]{1,0:T(8,128)(2,1)}, bf16[3,1024,128]{2,1,0:T(8,128)(2,1)}, bf16[64,1024]{1,0:T(8,128)(2,1)}, bf16[256,512]{1,0:T(8,128)(2,1)}, ...) custom-call(bf16[4,64,512]{2,1,0:T(8,128)(2,1)} %bitcast.572, ...), custom_call_target="tpu_custom_call" | custom-call | tf_op jit(solution)/shard_map/pallas_call | solution.py:83
  437.4 2.0 add_convert_fusion
  439.4 27.4 %shard_map.427 = (f32[256,1024]{1,0:T(8,128)}, bf16[8,256,256]{2,1,0:T(8,128)(2,1)}, f32[1,1024]{1,0:T(1,128)}, bf16[256,512]{1,0:T(8,128)(2,1)}, bf16[4,16,1024]{2,1,0:T(8,128)(2,1)}, /*index=5*/f32[64,512]{1,0:T(8,128)}) custom-call(f32[1,1024]{1,0:T(1,128)} %bitcast.586, bf16[256,1024]{1,0:T(8,128)(2,1)} %get-tuple-element.180.refs_1_, ...), custom_call_target="tpu_custom_call" | custom-call | tf_op jit(solution)/shard_map/pallas_call | solution.py:83
  467.4 1.3 reduce.20
  476.3 2.1 fusion.120
  478.3 3.6 convolution_convert_fusion
  482.2 1.3 copy-done.12
  483.5 25.5 %shard_map.428 = (f32[4,256,128]{2,1,0:T(8,128)S(1)}, bf16[256,1024]{1,0:T(8,128)(2,1)S(1)}, bf16[4,16,1024]{2,1,0:T(8,128)(2,1)S(1)}) custom-call(bf16[4,256,512]{2,1,0:T(8,128)(2,1)S(1)} %bitcast.473, bf16[4,256,1024]{2,1,0:T(8,128)(2,1)S(1)} %bitcast.484, bf16[16,1024]{1,0:T(8,128)(2,1)S(1)} %reduce_sum.62.refs_2_), custom_call_target="tpu_custom_call" | custom-call | tf_op jit(solution)/shard_map/pallas_call | solution.py:83
  509.8 3.4 shard_map.429
  513.5 1.9 fusion.53
  520.0 27.7 %shard_map.430 = (bf16[4,256,512]{2,1,0:T(8,128)(2,1)S(1)}, f32[9,64,512]{2,1,0:T(8,128)S(1)}, f32[4,12,128]{2,1,0:T(8,128)S(1)}, bf16[4,16,1024]{2,1,0:T(8,128)(2,1)S(1)}, bf16[4,4,16,1024]{3,2,1,0:T(8,128)(2,1)S(1)}) custom-call(bf16[4,256,128]{2,1,0:T(8,128)(2,1)S(1)} %get-tuple-element.190.refs_0_, bf16[9,256,512]{2,1,0:T(8,128)(2,1)S(1)} %fusion.39.refs_1_, ...), custom_call_target="tpu_custom_call" | custom-call | tf_op jit(solution)/shard_map/pallas_call | solution.py:83
  548.4 3.9 convolution_convert_fusion.2
  560.7 22.3 %shard_map.431 = (f32[4,256,128]{2,1,0:T(8,128)S(1)}, bf16[5,64,512]{2,1,0:T(8,128)(2,1)S(1)}, bf16[3,256,128]{2,1,0:T(8,128)(2,1)S(1)}, f32[64,512]{1,0:T(8,128...) custom-call(bf16[4,256,256]{2,1,0:T(8,128)(2,1)S(1)} %bitcast.483, ...), custom_call_target="tpu_custom_call" | custom-call | tf_op jit(solution)/shard_map/pallas_call | solution.py:83
  583.1 3.3 shard_map.432
  591.8 25.8 %shard_map.433 = (bf16[4,64,1024]{2,1,0:T(8,128)(2,1)S(1)}, f32[1,448]{1,0:T(1,128)S(1)}, bf16[3,64,512]{2,1,0:T(8,128)(2,1)S(1)}, bf16[4,64,512]{2,1,0:T(8,128)(2,1)S(1)}, f32[64,1024]{1,0:T(8,128)S(1)}) custom-call(bf16[4,256,128]{2,1,0:T(8,128)(2,1)S(1)} %copy-done.37, f32[4,4,1,448]{3,2,1,0:T(1,128)S(1)} %concatenate.46.refs_1_, ...), custom_call_target="tpu_custom_call" | custom-call | tf_op jit(solution)/shard_map/pallas_call | solution.py:83
  621.7 1.7 slice_bitcast_fusion.4
  623.4 1.7 convert_bitcast_fusion.2
  629.7 1.8 copy.137
  632.1 1.9 copy.136
  634.0 1.3 bitcast_add_fusion
  635.3 1.5 add_bitcast_fusion
  (298 shorter events, 73.6 us)
Async XLA Ops:
  7.2 140.3 %copy-start = (bf16[512,9,256]{2,0,1:T(8,128)(2,1)S(1)}, bf16[512,9,256]{2,0,1:T(8,128)(2,1)}, u32[]{:S(2)}) copy-start(bf16[512,9,256]{2,0,1:T(8,128)(2,1)} %param.35) | copy-start | bytes 7077892
  7.2 4.1 copy-start.11
  7.2 5.4 copy-start.64
  7.2 98.1 %all-gather.6.cloned.1.call-start = ((), (), s32[]{:S(2)}) async-start(), calls=%async_computation.1 | async-start | bytes 2293760 | tf_op jit(solution)/shard_map/all_gather | solution.py:2541
  8.3 5.2 copy-start.71
  12.6 24.7 %copy-start.75 = (f32[1024]{0:T(1024)S(1)}, f32[1024]{0:T(1024)}, u32[]{:S(2)}) copy-start(f32[1024]{0:T(1024)} %param.31) | copy-start | bytes 12292
  12.6 24.9 %copy-start.76 = (f32[1024]{0:T(1024)S(1)}, f32[1024]{0:T(1024)}, u32[]{:S(2)}) copy-start(f32[1024]{0:T(1024)} %param.32) | copy-start | bytes 12292
  37.2 5.0 copy-start.20
  37.3 216.2 %all-gather.4.cloned.1.call-start = ((), (), s32[]{:S(2)}) async-start(), calls=%async_computation | async-start | bytes 1310720 | tf_op jit(solution)/shard_map/all_gather | solution.py:2585
  38.4 8.2 %copy-start.67 = (bf16[4,16,1024]{2,1,0:T(8,128)(2,1)S(1)}, bf16[4,16,1024]{2,1,0:T(8,128)(2,1)}, u32[]{:S(2)}) copy-start(bf16[4,16,1024]{2,1,0:T(8,128)(2,1)} %get-tuple-element.125) | copy-start | bytes 393220
  46.7 13.4 %copy-start.85 = (bf16[256,9,512]{2,0,1:T(8,128)(2,1)S(1)}, bf16[256,9,512]{2,0,1:T(8,128)(2,1)}, u32[]{:S(2)}) copy-start(bf16[256,9,512]{2,0,1:T(8,128)(2,1)} %param.33) | copy-start | bytes 7077892
  59.0 5.3 copy-start.24
  59.0 5.3 copy-start.48
  64.3 37.6 %copy-start.77 = (s32[2,8]{1,0:T(2,128)S(1)}, s32[2,8]{1,0:T(2,128)}, u32[]{:S(2)}) copy-start(s32[2,8]{1,0:T(2,128)} %param.28) | copy-start | bytes 196
  101.9 36.4 %copy-start.81 = (f32[128,8]{0,1:T(8,128)S(1)}, f32[128,8]{0,1:T(8,128)}, u32[]{:S(2)}) copy-start(f32[128,8]{0,1:T(8,128)} %param.46) | copy-start | bytes 12292
  101.9 39.2 %copy-start.21 = (bf16[8,256,128]{2,1,0:T(8,128)(2,1)S(1)}, bf16[8,256,128]{2,1,0:T(8,128)(2,1)}, u32[]{:S(2)}) copy-start(bf16[8,256,128]{2,1,0:T(8,128)(2,1)} %get-tuple-element.124.x_ref) | copy-start | bytes 1572868
  138.3 6.6 %copy-start.79 = (f32[1024]{0:T(1024)S(1)}, f32[1024]{0:T(1024)}, u32[]{:S(2)}) copy-start(f32[1024]{0:T(1024)} %param.43) | copy-start | bytes 12292
  138.3 6.6 %copy-start.80 = (f32[1024]{0:T(1024)S(1)}, f32[1024]{0:T(1024)}, u32[]{:S(2)}) copy-start(f32[1024]{0:T(1024)} %param.39) | copy-start | bytes 12292
  138.3 7.2 %copy-start.82 = (s32[2]{0:T(128)S(1)}, s32[2]{0:T(128)}, u32[]{:S(2)}) copy-start(s32[2]{0:T(128)} %param.30) | copy-start | bytes 28
  141.8 5.6 copy-start.55
  226.7 26.8 %copy-start.6 = (f32[256,1024]{1,0:T(8,128)S(1)}, f32[256,1024]{1,0:T(8,128)}, u32[]{:S(2)}) copy-start(f32[256,1024]{1,0:T(8,128)} %get-tuple-element.146.refs_3_.refs_13_) | copy-start | bytes 3145732
  226.7 26.8 %copy-start.53 = (f32[1024]{0:T(1024)S(1)}, f32[1024]{0:T(1024)}, u32[]{:S(2)}) copy-start(f32[1024]{0:T(1024)} %param.47) | copy-start | bytes 12292
  386.1 51.3 %copy-start.10 = (f32[256,1024]{1,0:T(8,128)S(1)}, f32[256,1024]{1,0:T(8,128)}, u32[]{:S(2)}) copy-start(f32[256,1024]{1,0:T(8,128)} %copy-done.9) | copy-start | bytes 3145732
  439.4 29.3 %copy-start.78 = (f32[1,1024]{1,0:T(1,128)S(1)}, f32[1,1024]{1,0:T(1,128)}, u32[]{:S(2)}) copy-start(f32[1,1024]{1,0:T(1,128)} %get-tuple-element.205) | copy-start | bytes 12292
  439.4 31.4 %copy-start.74 = (f32[2,1024]{1,0:T(2,128)S(1)}, f32[2,1024]{1,0:T(2,128)}, u32[]{:S(2)}) copy-start(f32[2,1024]{1,0:T(2,128)} %get-tuple-element.204) | copy-start | bytes 24580
  439.4 32.7 %copy-start.73 = (f32[8,8,128]{2,1,0:T(8,128)S(1)}, f32[8,8,128]{2,1,0:T(8,128)}, u32[]{:S(2)}) copy-start(f32[8,8,128]{2,1,0:T(8,128)} %get-tuple-element.206) | copy-start | bytes 98308
  439.4 35.2 %copy-start.66 = (bf16[64,2048]{1,0:T(8,128)(2,1)S(1)}, bf16[64,2048]{1,0:T(8,128)(2,1)}, u32[]{:S(2)}) copy-start(bf16[64,2048]{1,0:T(8,128)(2,1)} %get-tuple-element.224) | copy-start | bytes 786436
  439.4 36.0 %copy-start.65 = (bf16[64,2048]{1,0:T(8,128)(2,1)S(1)}, bf16[64,2048]{1,0:T(8,128)(2,1)}, u32[]{:S(2)}) copy-start(bf16[64,2048]{1,0:T(8,128)(2,1)} %get-tuple-element.225) | copy-start | bytes 786436
  482.0 27.1 %copy-start.59 = (bf16[128,8,2,512]{3,1,2,0:T(8,128)(2,1)S(1)}, bf16[128,8,2,512]{3,1,2,0:T(8,128)(2,1)}, u32[]{:S(2)}) copy-start(bf16[128,8,2,512]{3,1,2,0:T(8,128)(2,1)} %copy.165) | copy-start | bytes 6291460
  483.5 26.3 %copy-start.14 = (f32[4,256,128]{2,1,0:T(8,128)S(1)}, f32[4,256,128]{2,1,0:T(8,128)}, u32[]{:S(2)}) copy-start(f32[4,256,128]{2,1,0:T(8,128)} %copy-done.13) | copy-start | bytes 1572868
  509.0 4.2 copy-start.31
  520.0 28.4 %copy-start.86 = (bf16[256,9,512]{2,0,1:T(8,128)(2,1)S(1)}, bf16[256,9,512]{2,0,1:T(8,128)(2,1)}, u32[]{:S(2)}) copy-start(bf16[256,9,512]{2,0,1:T(8,128)(2,1)} %param.33) | copy-start | bytes 7077892
  547.7 4.7 copy-start.18
  547.7 4.7 copy-start.57
  548.4 86.9 %collective-permute-start = (bf16[16,4096]{1,0:T(8,128)(2,1)}, bf16[16,4096]{1,0:T(8,128)(2,1)}, u32[]{:S(2)}, u32[]{:S(2)}) collective-permute-start(bf16[16,4096]{1,0:T(8,128)(2,1)} %bitcast.195), channel_id=1, source_target_pairs={{0,1},{1,0},{2,3},{3,2},{4,5},{5,4},{6,7},{7,6},{8,9},{9,8},{10,11... | collective-permute-start | bytes 393224 | tf_op jit(solution)/shard_map/ppermute | solution.py:27
  557.0 26.0 %copy-start.84 = (f32[128]{0:T(128)S(1)}, f32[128]{0:T(128)}, u32[]{:S(2)}) copy-start(f32[128]{0:T(128)} %dynamic_slice.50) | copy-start | bytes 1540
  557.0 26.1 %copy-start.83 = (f32[128]{0:T(128)S(1)}, f32[128]{0:T(128)}, u32[]{:S(2)}) copy-start(f32[128]{0:T(128)} %dynamic_slice.48) | copy-start | bytes 1540
  557.5 25.6 %copy-start.23 = (bf16[4,256,128]{2,1,0:T(8,128)(2,1)S(1)}, bf16[4,256,128]{2,1,0:T(8,128)(2,1)}, u32[]{:S(2)}) copy-start(bf16[4,256,128]{2,1,0:T(8,128)(2,1)} %slice.146.x_ref) | copy-start | bytes 786436
  619.7 5.4 copy-start.60
  619.7 6.6 %copy-start.72 = (bf16[2,3,512]{2,1,0:T(4,128)(2,1)S(1)}, bf16[2,3,512]{2,1,0:T(4,128)(2,1)}, u32[]{:S(2)}) copy-start(bf16[2,3,512]{2,1,0:T(4,128)(2,1)} %copy-done.71) | copy-start | bytes 18436
  619.7 7.7 %copy-start.39 = (bf16[4,64,512]{2,1,0:T(8,128)(2,1)S(1)}, bf16[4,64,512]{2,1,0:T(8,128)(2,1)}, u32[]{:S(2)}) copy-start(bf16[4,64,512]{2,1,0:T(8,128)(2,1)} %copy-done.38) | copy-start | bytes 786436
  620.3 13.7 %collective-permute-start.1 = (f32[448]{0:T(512)S(1)}, f32[448]{0:T(512)}, u32[]{:S(2)}, u32[]{:S(2)}) collective-permute-start(f32[448]{0:T(512)S(1)} %bitcast.509), channel_id=1, source_target_pairs={{0,1},{1,0},{2,3},{3,2},{4,5},{5,4},{6,7},{7,6},{8,9},{9,8},{10,11... | collective-permute-start | bytes 5384 | tf_op jit(solution)/shard_map/ppermute | solution.py:2881
  625.1 4.2 copy-start.58
  625.1 4.2 copy-start.68
  629.6 7.2 %copy-start.19 = (f32[9,64,512]{2,1,0:T(8,128)S(1)}, f32[9,64,512]{2,1,0:T(8,128)}, u32[]{:S(2)}) copy-start(f32[9,64,512]{2,1,0:T(8,128)} %copy-done.18) | copy-start | bytes 3538948
  629.6 9.5 %copy-start.1 = (bf16[512,9,256]{2,0,1:T(8,128)(2,1)S(1)}, bf16[512,9,256]{2,0,1:T(8,128)(2,1)}, u32[]{:S(2)}) copy-start(bf16[512,9,256]{2,0,1:T(8,128)(2,1)} %param.35) | copy-start | bytes 7077892
  632.1 5.8 copy-start.50
  632.1 6.4 copy-start.69
  (43 other events, 60.2 us)
Sparse Core Ops, SparseCore 0:
  37.4 53.1 all-gather.5
  138.4 33.0 all-gather.3
